TPU v7x, 32 devices: a whole 2x2x4 slice. The times are simulated.
32 devices in a mesh: dp: 8 (over z, y), tensor: 4 (over x, core).
Axes of the slice: x: 2, y: 2, z: 4, core: 2. Of those that a mesh axis runs over, the one named last changes fastest.
Arguments:
- tokens: bfloat16 [8, 1024, 1024], P('dp', 'tensor'), may hold values from -6 to 6
- segments: int32 [8, 1024], P('dp'), may hold values from 0 to 4, as said below
- routes: int32 [8, 1024, 8], P('dp'), may hold values from 0 to 31, all different within a row
- priority: int32 [8, 1024], P('dp'), may hold values from 0 to 1023, as said below
- norm_attn: bfloat16 [1024], P('dp'), may hold values from 0.5 to 1.5
- w_query: bfloat16 [1024, 1024], P('dp', 'tensor'), may hold values from -0.1875 to 0.1875
- w_key: bfloat16 [1024, 512], P('dp', 'tensor'), may hold values from -0.1875 to 0.1875
- w_value: bfloat16 [1024, 512], P('dp', 'tensor'), may hold values from -0.1875 to 0.1875
- w_out: bfloat16 [1024, 1024], P('dp', 'tensor'), may hold values from -1 to 1
- norm_moe: bfloat16 [1024], P('dp'), may hold values from 0.5 to 1.5
- w_router: bfloat16 [1024, 32], P('dp'), may hold values from -0.09375 to 0.09375
- w_gate: bfloat16 [32, 1024, 512], P(None, 'dp', 'tensor'), may hold values from -0.1875 to 0.1875
- w_up: bfloat16 [32, 1024, 512], P(None, 'dp', 'tensor'), may hold values from -0.1875 to 0.1875
- w_down: bfloat16 [32, 1024, 512], P(None, 'dp', 'tensor'), may hold values from -1 to 1
- cotangent: bfloat16 [8, 1024, 1024], P('dp', 'tensor'), may hold values from -6 to 6
Outputs:
- block_out: bfloat16 [8, 1024, 1024], P('dp', 'tensor')
- tokens_grad: float32 [8, 1024, 1024], P('dp', 'tensor')
- norm_attn_grad: float32 [1024], P('dp')
- query_grad: float32 [1024, 1024], P('dp', 'tensor')
- key_grad: float32 [1024, 512], P('dp', 'tensor')
- value_grad: float32 [1024, 512], P('dp', 'tensor')
- out_grad: float32 [1024, 1024], P('dp', 'tensor')
- norm_moe_grad: float32 [1024], P('dp')
- router_grad: float32 [1024, 32], P('dp')
- gate_grad: float32 [32, 1024, 512], P(None, 'dp', 'tensor')
- up_grad: float32 [32, 1024, 512], P(None, 'dp', 'tensor')
- down_grad: float32 [32, 1024, 512], P(None, 'dp', 'tensor')
Inputs may be any that keep to these rules, and one draw needn't show every extreme that they name: `segments`: numbers start at 0 in each sequence, never fall along it, and end at 4 in every sequence. `priority`: each run of 1 sequence of one data group holds every number once.
All inputs are finite; a program needn't handle non-finite values.
Results may differ from a plain program's by a relative error of at most 0.014.
Values may be sent and summed in bfloat16 or wider, within the bound.
No kernel may reach another device: no remote copies, remote signals or barrier semaphores. Data moves between devices by JAX's collectives and lax.ppermute only.
A program may use at most 192 MiB of HBM per device.

v0:
```python
import math

import jax
import jax.numpy as jnp
from jax import lax
from jax.sharding import PartitionSpec as P

HEAD_SIZE = 64


EPSILON = 1e-06
TOP_PRECISION = lax.Precision.HIGHEST
FLOOR_SCORE = -1e30


def contract(left, right, left_dims, right_dims):
    return lax.dot_general(
        left, right, ((left_dims, right_dims), ((), ())), preferred_element_type=jnp.float32
    )


def contract_exact(left, right, left_dims, right_dims):
    return lax.dot_general(
        left,
        right,
        ((left_dims, right_dims), ((), ())),
        precision=TOP_PRECISION,
        preferred_element_type=jnp.float32,
    )


def normalize(value_rows):
    factor = lax.rsqrt(jnp.mean(value_rows * value_rows, axis=-1, keepdims=True) + EPSILON)
    return (value_rows * factor, factor)


def norm_back(upstream, normed, factor, gain):
    scaled = upstream * gain
    gain_part = jnp.sum(upstream * normed, axis=(0, 1))
    inward = factor * (scaled - normed * jnp.mean(scaled * normed, axis=-1, keepdims=True))
    return (inward, gain_part)


def positions(segments):
    complete_length = segments.shape[-1]
    spots = jnp.broadcast_to(jnp.arange(complete_length, dtype=jnp.int32), segments.shape)
    change = jnp.concatenate(
        [
            jnp.ones(segments.shape[:-1] + (1,), dtype=jnp.bool_),
            segments[..., 1:] != segments[..., :-1],
        ],
        axis=-1,
    )
    starts = lax.cummax(jnp.where(change, spots, 0), axis=segments.ndim - 1)
    return spots - starts


def rope_tables(places, head_dim):
    half_dim = head_dim // 2
    inverse = jnp.exp(
        jnp.arange(half_dim, dtype=jnp.float32) * (-2.0 * math.log(10000.0) / head_dim)
    )
    angle = places.astype(jnp.float32)[..., None] * inverse
    return (jnp.cos(angle)[..., None, :], jnp.sin(angle)[..., None, :])


def rotate(value_rows, cosine, sine):
    half_dim = value_rows.shape[-1] // 2
    front = value_rows[..., :half_dim]
    rear = value_rows[..., half_dim:]
    return jnp.concatenate([front * cosine - rear * sine, rear * cosine + front * sine], axis=-1)


def unrotate(value_rows, cosine, sine):
    half_dim = value_rows.shape[-1] // 2
    front = value_rows[..., :half_dim]
    rear = value_rows[..., half_dim:]
    return jnp.concatenate([front * cosine + rear * sine, rear * cosine - front * sine], axis=-1)


def slot_plan(routes_flat, priority_flat, expert_count, capacity):
    token_count = routes_flat.shape[0]
    labels = jnp.arange(expert_count, dtype=jnp.int32)
    hit_counts = jnp.sum(
        (routes_flat[:, :, None] == labels).astype(jnp.int32), axis=1, dtype=jnp.int32
    )
    by_priority = (
        jnp.zeros((token_count,), jnp.int32)
        .at[priority_flat]
        .set(jnp.arange(token_count, dtype=jnp.int32))
    )
    ordered_hits = hit_counts[by_priority]
    earlier = jnp.cumsum(ordered_hits, axis=0, dtype=jnp.int32) - ordered_hits
    pair_rank = jnp.take_along_axis(earlier[priority_flat], routes_flat, axis=1)
    kept_pairs = pair_rank < capacity
    slot_place = jnp.where(kept_pairs, pair_rank, capacity)
    owners = jnp.broadcast_to(jnp.arange(token_count, dtype=jnp.int32)[:, None], routes_flat.shape)
    slot_table = (
        jnp.full((expert_count, capacity), token_count, jnp.int32)
        .at[routes_flat, slot_place]
        .set(owners, mode="drop")
    )
    return (kept_pairs, jnp.minimum(pair_rank, capacity - 1), slot_place, slot_table)


def block_view(block_id, block_count, block_rows, query_rows, key_rot, value_rows, segments):
    which = block_id // block_count
    offset = block_id % block_count * block_rows
    query_seq = lax.dynamic_index_in_dim(query_rows, which, 0, keepdims=False)
    query_blk = lax.dynamic_slice_in_dim(query_seq, offset, block_rows, 0)
    key_seq = lax.dynamic_index_in_dim(key_rot, which, 0, keepdims=False)
    value_seq = lax.dynamic_index_in_dim(value_rows, which, 0, keepdims=False)
    seg_seq = lax.dynamic_index_in_dim(segments, which, 0, keepdims=False)
    seg_blk = lax.dynamic_slice_in_dim(seg_seq, offset, block_rows, 0)
    row_ids = offset + jnp.arange(block_rows, dtype=jnp.int32)
    col_ids = jnp.arange(seg_seq.shape[0], dtype=jnp.int32)
    allowed = (seg_blk[:, None] == seg_seq[None, :]) & (row_ids[:, None] >= col_ids[None, :])
    return (which, offset, query_blk, key_seq, value_seq, allowed)


def local(
    tokens,
    segments,
    routes,
    priority,
    norm_attn,
    w_query,
    w_key,
    w_value,
    w_out,
    norm_moe,
    w_router,
    w_gate,
    w_up,
    w_down,
    cotangent,
):
    sequence_count, local_len, model_dim = tokens.shape
    complete_length = local_len * lax.axis_size("tensor")
    token_count = sequence_count * complete_length
    top_count = routes.shape[2]
    expert_count = w_gate.shape[0]
    capacity = token_count * top_count // expert_count
    head_dim = HEAD_SIZE
    kv_heads = w_key.shape[1] // head_dim
    query_heads = w_query.shape[1] // head_dim
    group_size = query_heads // kv_heads
    scale = 1.0 / math.sqrt(head_dim)
    block_rows = min(512, complete_length)
    block_count = complete_length // block_rows
    own_start = lax.axis_index("tensor") * local_len
    attn_set = (
        lax.all_gather(norm_attn, "dp", axis=0, tiled=True),
        lax.all_gather(w_query, "dp", axis=0, tiled=True),
        lax.all_gather(w_key, "dp", axis=0, tiled=True),
        lax.all_gather(w_value, "dp", axis=0, tiled=True),
        lax.all_gather(w_out, "dp", axis=0, tiled=True),
    )
    gain_attn = attn_set[0].astype(jnp.float32)
    inputs = tokens.astype(jnp.float32)
    normed_one, factor_one = normalize(inputs)
    attn_local = (normed_one * gain_attn).astype(jnp.bfloat16)
    attention_input = lax.all_gather(attn_local, "tensor", axis=1, tiled=True)
    cosine, sine = rope_tables(positions(segments), head_dim)
    query_rows = rotate(
        jnp.dot(attention_input, attn_set[1], preferred_element_type=jnp.float32).reshape(
            sequence_count, complete_length, query_heads, head_dim
        ),
        cosine,
        sine,
    )
    query_rows = query_rows.astype(jnp.bfloat16).reshape(
        sequence_count, complete_length, kv_heads, group_size, head_dim
    )
    key_rot = rotate(
        jnp.dot(attention_input, attn_set[2], preferred_element_type=jnp.float32).reshape(
            sequence_count, complete_length, kv_heads, head_dim
        ),
        cosine,
        sine,
    ).astype(jnp.bfloat16)
    value_rows = (
        jnp.dot(attention_input, attn_set[3], preferred_element_type=jnp.float32)
        .astype(jnp.bfloat16)
        .reshape(sequence_count, complete_length, kv_heads, head_dim)
    )

    def forward_block(block_id):
        which, offset, query_blk, key_seq, value_seq, allowed = block_view(
            block_id, block_count, block_rows, query_rows, key_rot, value_rows, segments
        )
        scores = scale * jnp.einsum(
            "qkgd,tkd->kgqt", query_blk, key_seq, preferred_element_type=jnp.float32
        )
        masked = jnp.where(allowed, scores, FLOOR_SCORE)
        top_score = jnp.max(masked, axis=-1, keepdims=True)
        lifted = jnp.exp(masked - top_score)
        summed = jnp.sum(lifted, axis=-1, keepdims=True)
        shares = (lifted / summed).astype(jnp.bfloat16)
        mixed_result = jnp.einsum(
            "kgqt,tkd->qkgd", shares, value_seq, preferred_element_type=jnp.float32
        )
        return (
            mixed_result.astype(jnp.bfloat16).reshape(block_rows, query_heads * head_dim),
            top_score + jnp.log(summed),
        )

    blended_all, log_totals = lax.map(
        forward_block, jnp.arange(sequence_count * block_count, dtype=jnp.int32)
    )
    attn_mix = blended_all.reshape(sequence_count, complete_length, query_heads * head_dim)
    attn_part = contract(attn_mix, attn_set[4], (2,), (1,))
    attention_output = lax.psum_scatter(attn_part, "tensor", scatter_dimension=1, tiled=True)
    after_attn = inputs + attention_output
    moe_set = (
        lax.all_gather(norm_moe, "dp", axis=0, tiled=True),
        lax.all_gather(w_router, "dp", axis=0, tiled=True),
        lax.all_gather(w_gate, "dp", axis=1, tiled=True),
        lax.all_gather(w_up, "dp", axis=1, tiled=True),
        lax.all_gather(w_down, "dp", axis=1, tiled=True),
    )
    gain_moe = moe_set[0].astype(jnp.float32)
    normed_two, factor_two = normalize(after_attn)
    moe_local = (normed_two * gain_moe).astype(jnp.bfloat16)
    moe_in = lax.all_gather(moe_local, "tensor", axis=1, tiled=True).reshape(token_count, model_dim)
    logits = jnp.dot(moe_in, moe_set[1], preferred_element_type=jnp.float32)
    routes_flat = routes.reshape(token_count, top_count)
    chosen = jnp.take_along_axis(logits, routes_flat, axis=1)
    gate_lift = jnp.exp(chosen - jnp.max(chosen, axis=1, keepdims=True))
    gates = gate_lift / jnp.sum(gate_lift, axis=1, keepdims=True)
    kept_pairs, pair_slot, slot_place, slot_table = slot_plan(
        routes_flat, priority.reshape(token_count), expert_count, capacity
    )
    slot_weights = (
        jnp.zeros((expert_count, capacity), jnp.float32)
        .at[routes_flat, slot_place]
        .set(gates, mode="drop")
    )
    padded = jnp.concatenate([moe_in, jnp.zeros((1, model_dim), jnp.bfloat16)], axis=0)

    def expert_forward(combined, inputs_e):
        gate_mat, up_mat, down_mat, row_ids, weight_row = inputs_e
        picked = padded[row_ids]
        gate_pre = jnp.dot(picked, gate_mat, preferred_element_type=jnp.float32)
        up_pre = jnp.dot(picked, up_mat, preferred_element_type=jnp.float32)
        hidden = (jax.nn.silu(gate_pre) * up_pre).astype(jnp.bfloat16)
        expert_out = contract(hidden, down_mat, (1,), (1,))
        combined = combined.at[row_ids].add(weight_row[:, None] * expert_out)
        return (combined, (gate_pre, up_pre))

    combined, (gate_kept, up_kept) = lax.scan(
        expert_forward,
        jnp.zeros((token_count + 1, model_dim), jnp.float32),
        (moe_set[2], moe_set[3], moe_set[4], slot_table, slot_weights),
    )
    moe_part = combined[:token_count].reshape(sequence_count, complete_length, model_dim)
    moe_out = lax.psum_scatter(moe_part, "tensor", scatter_dimension=1, tiled=True)
    block_out = (after_attn + moe_out).astype(jnp.bfloat16)
    refetched = (
        lax.all_gather(norm_attn, "dp", axis=0, tiled=True),
        lax.all_gather(w_query, "dp", axis=0, tiled=True),
        lax.all_gather(w_key, "dp", axis=0, tiled=True),
        lax.all_gather(w_value, "dp", axis=0, tiled=True),
        lax.all_gather(w_out, "dp", axis=0, tiled=True),
        lax.all_gather(norm_moe, "dp", axis=0, tiled=True),
        lax.all_gather(w_router, "dp", axis=0, tiled=True),
        lax.all_gather(w_gate, "dp", axis=1, tiled=True),
        lax.all_gather(w_up, "dp", axis=1, tiled=True),
        lax.all_gather(w_down, "dp", axis=1, tiled=True),
    )
    attn_back = refetched[:5]
    moe_back = refetched[5:]
    out_grad_all = lax.all_gather(cotangent, "tensor", axis=1, tiled=True).reshape(
        token_count, model_dim
    )
    grad_padded = jnp.concatenate([out_grad_all, jnp.zeros((1, model_dim), jnp.bfloat16)], axis=0)

    def expert_backward(accum, inputs_e):
        gate_mat, up_mat, down_mat, row_ids, weight_row, gate_saved, up_saved = inputs_e
        picked = padded[row_ids]
        sigma = jax.nn.sigmoid(gate_saved)
        active = gate_saved * sigma
        hidden = (active * up_saved).astype(jnp.bfloat16)
        expert_out = contract(hidden, down_mat, (1,), (1,))
        slot_dy = grad_padded[row_ids].astype(jnp.float32)
        gate_share = jnp.sum(slot_dy * expert_out, axis=1)
        slot_grad = (weight_row[:, None] * slot_dy).astype(jnp.bfloat16)
        hidden_grad = jnp.dot(slot_grad, down_mat, preferred_element_type=jnp.float32)
        gate_pre_grad = (
            hidden_grad * up_saved * sigma * (1.0 + gate_saved * (1.0 - sigma))
        ).astype(jnp.bfloat16)
        up_pre_grad = (hidden_grad * active).astype(jnp.bfloat16)
        picked_grad = contract(gate_pre_grad, gate_mat, (1,), (1,)) + contract(
            up_pre_grad, up_mat, (1,), (1,)
        )
        gate_mat_grad = contract(picked, gate_pre_grad, (0,), (0,))
        up_mat_grad = contract(picked, up_pre_grad, (0,), (0,))
        down_mat_grad = contract(slot_grad, hidden, (0,), (0,))
        accum = accum.at[row_ids].add(picked_grad)
        return (accum, (gate_mat_grad, up_mat_grad, down_mat_grad, gate_share))

    accum, (gate_grad, up_grad, down_grad, gate_shares) = lax.scan(
        expert_backward,
        jnp.zeros((token_count + 1, model_dim), jnp.float32),
        (moe_back[2], moe_back[3], moe_back[4], slot_table, slot_weights, gate_kept, up_kept),
    )
    gate_part = jnp.where(kept_pairs, gate_shares[routes_flat, pair_slot], 0.0)
    gate_dot = lax.psum(gate_part, "tensor")
    chosen_grad = gates * (gate_dot - jnp.sum(gates * gate_dot, axis=1, keepdims=True))
    labels = jnp.arange(expert_count, dtype=jnp.int32)
    logit_grad = jnp.sum(
        jnp.where(routes_flat[:, :, None] == labels, chosen_grad[:, :, None], 0.0), axis=1
    )
    router_grad = contract_exact(moe_in.astype(jnp.float32), logit_grad, (0,), (0,))
    own_logit_grad = lax.dynamic_slice_in_dim(
        logit_grad.reshape(sequence_count, complete_length, expert_count), own_start, local_len, 1
    )
    router_back = contract_exact(own_logit_grad, moe_back[1].astype(jnp.float32), (2,), (1,))
    moe_in_part = accum[:token_count].reshape(sequence_count, complete_length, model_dim)
    moe_in_grad = (
        lax.psum_scatter(moe_in_part, "tensor", scatter_dimension=1, tiled=True) + router_back
    )
    inward_two, gain_two_part = norm_back(
        moe_in_grad, normed_two, factor_two, moe_back[0].astype(jnp.float32)
    )
    after_grad = cotangent.astype(jnp.float32) + inward_two
    attn_out_grad = lax.all_gather(after_grad.astype(jnp.bfloat16), "tensor", axis=1, tiled=True)
    mix_grad = jnp.dot(attn_out_grad, attn_back[4], preferred_element_type=jnp.float32).astype(
        jnp.bfloat16
    )
    out_grad = contract(attn_out_grad, attn_mix, (0, 1), (0, 1))
    mix_grad = mix_grad.reshape(sequence_count, complete_length, kv_heads, group_size, head_dim)

    def attend_backward(carry, block_id):
        key_accum, value_accum = carry
        which, offset, query_blk, key_seq, value_seq, allowed = block_view(
            block_id, block_count, block_rows, query_rows, key_rot, value_rows, segments
        )
        log_total = lax.dynamic_index_in_dim(log_totals, block_id, 0, keepdims=False)
        scores = scale * jnp.einsum(
            "qkgd,tkd->kgqt", query_blk, key_seq, preferred_element_type=jnp.float32
        )
        masked = jnp.where(allowed, scores, FLOOR_SCORE)
        shares = jnp.exp(masked - log_total)
        shares_low = shares.astype(jnp.bfloat16)
        grad_seq = lax.dynamic_index_in_dim(mix_grad, which, 0, keepdims=False)
        grad_blk = lax.dynamic_slice_in_dim(grad_seq, offset, block_rows, 0)
        share_grad = jnp.einsum(
            "qkgd,tkd->kgqt", grad_blk, value_seq, preferred_element_type=jnp.float32
        )
        value_part = jnp.einsum(
            "kgqt,qkgd->tkd", shares_low, grad_blk, preferred_element_type=jnp.float32
        )
        inner = jnp.sum(shares * share_grad, axis=-1, keepdims=True)
        score_grad = (shares * (share_grad - inner)).astype(jnp.bfloat16)
        query_part = scale * jnp.einsum(
            "kgqt,tkd->qkgd", score_grad, key_seq, preferred_element_type=jnp.float32
        )
        key_part = scale * jnp.einsum(
            "kgqt,qkgd->tkd", score_grad, query_blk, preferred_element_type=jnp.float32
        )
        key_accum = lax.dynamic_update_index_in_dim(
            key_accum,
            lax.dynamic_index_in_dim(key_accum, which, 0, keepdims=False) + key_part,
            which,
            0,
        )
        value_accum = lax.dynamic_update_index_in_dim(
            value_accum,
            lax.dynamic_index_in_dim(value_accum, which, 0, keepdims=False) + value_part,
            which,
            0,
        )
        return ((key_accum, value_accum), query_part)

    kv_zero = jnp.zeros((sequence_count, complete_length, kv_heads, head_dim), jnp.float32)
    (key_sum, value_sum), query_parts = lax.scan(
        attend_backward,
        (kv_zero, kv_zero),
        jnp.arange(sequence_count * block_count, dtype=jnp.int32),
    )
    query_rot_grad = query_parts.reshape(sequence_count, complete_length, query_heads, head_dim)
    query_in_grad = (
        unrotate(query_rot_grad, cosine, sine)
        .astype(jnp.bfloat16)
        .reshape(sequence_count, complete_length, query_heads * head_dim)
    )
    key_in_grad = (
        unrotate(key_sum, cosine, sine)
        .astype(jnp.bfloat16)
        .reshape(sequence_count, complete_length, kv_heads * head_dim)
    )
    value_in_grad = value_sum.astype(jnp.bfloat16).reshape(
        sequence_count, complete_length, kv_heads * head_dim
    )
    query_grad = contract(attention_input, query_in_grad, (0, 1), (0, 1))
    key_grad = contract(attention_input, key_in_grad, (0, 1), (0, 1))
    value_grad = contract(attention_input, value_in_grad, (0, 1), (0, 1))
    attn_in_part = (
        contract(query_in_grad, attn_back[1], (2,), (1,))
        + contract(key_in_grad, attn_back[2], (2,), (1,))
        + contract(value_in_grad, attn_back[3], (2,), (1,))
    )
    attn_in_grad = lax.psum_scatter(attn_in_part, "tensor", scatter_dimension=1, tiled=True)
    inward_one, gain_one_part = norm_back(
        attn_in_grad, normed_one, factor_one, attn_back[0].astype(jnp.float32)
    )
    tokens_grad = after_grad + inward_one
    reduced = (
        lax.psum_scatter(gain_one_part, "dp", scatter_dimension=0, tiled=True),
        lax.psum_scatter(query_grad, "dp", scatter_dimension=0, tiled=True),
        lax.psum_scatter(key_grad, "dp", scatter_dimension=0, tiled=True),
        lax.psum_scatter(value_grad, "dp", scatter_dimension=0, tiled=True),
        lax.psum_scatter(out_grad, "dp", scatter_dimension=0, tiled=True),
        lax.psum_scatter(gain_two_part, "dp", scatter_dimension=0, tiled=True),
        lax.psum_scatter(router_grad, "dp", scatter_dimension=0, tiled=True),
        lax.psum_scatter(gate_grad, "dp", scatter_dimension=1, tiled=True),
        lax.psum_scatter(up_grad, "dp", scatter_dimension=1, tiled=True),
        lax.psum_scatter(down_grad, "dp", scatter_dimension=1, tiled=True),
    )
    gain_one, gain_two = lax.psum((reduced[0], reduced[5]), "tensor")
    return (
        block_out,
        tokens_grad,
        gain_one,
        reduced[1],
        reduced[2],
        reduced[3],
        reduced[4],
        gain_two,
        reduced[6],
        reduced[7],
        reduced[8],
        reduced[9],
    )


def solution(mesh):
    in_specs = (
        P("dp", "tensor", None),
        P("dp", None),
        P("dp", None, None),
        P("dp", None),
        P("dp"),
        P("dp", "tensor"),
        P("dp", "tensor"),
        P("dp", "tensor"),
        P("dp", "tensor"),
        P("dp"),
        P("dp", None),
        P(None, "dp", "tensor"),
        P(None, "dp", "tensor"),
        P(None, "dp", "tensor"),
        P("dp", "tensor", None),
    )
    out_specs = (
        P("dp", "tensor", None),
        P("dp", "tensor", None),
        P("dp"),
        P("dp", "tensor"),
        P("dp", "tensor"),
        P("dp", "tensor"),
        P("dp", "tensor"),
        P("dp"),
        P("dp", None),
        P(None, "dp", "tensor"),
        P(None, "dp", "tensor"),
        P(None, "dp", "tensor"),
    )
    return jax.shard_map(local, mesh=mesh, in_specs=in_specs, out_specs=out_specs, check_vma=False)
```

profile of v0, /device:TPU:0, one launch (start us, length us, event | category | flops | bytes accessed | tf_op | source)
XLA Modules:
  0.0 3328.2 jit_solution(5488753400322305656)
XLA Ops:
  8.5 22.3 all-gather
  35.1 30.9 all_gather.55
  66.9 31.5 all_gather.54
  98.7 30.8 all_gather.56
  129.5 31.2 all_gather.57
  167.6 20.7 while.62
  192.5 16.4 all-gather.1
  209.0 24.6 reduce-scatter.13.cloned.1.call-done
  247.4 9.0 reduce-window.16
  260.4 52.9 %gather_fusion.6 = s32[8192]{0:T(1024)S(1)} fusion(s32[1024,32]{1,0:T(8,128)S(1)} %gather_fusion.4, s32[8192]{0:T(1024)S(1)} %reshape.809), kind=kCustom, calls=%fused_computation.6 | custom fusion | bytes 131072 | tf_op jit(solution)/shard_map/jit(take_along_axis)/gather | solution.py:94
  316.2 30.5 scatter_custom_fusion.3
  347.3 28.7 all_gather.60
  381.5 65.5 %gather_fusion.7 = f32[8192]{0:T(1024)S(1)} fusion(f32[1024,32]{0,1:T(8,128)S(1)} %fusion.164, s32[8192]{0:T(1024)S(1)} %reshape.809), kind=kCustom, calls=%fused_computation.7 | custom fusion | bytes 131072 | tf_op jit(solution)/shard_map/jit(take_along_axis)/gather | solution.py:228
  448.1 30.8 scatter_custom_fusion.4
  480.7 55.7 %all-gather.16.cloned.1.call-done = bf16[32,1024,128]{2,1,0:T(8,128)(2,1)} async-done(((bf16[32,128,128]{2,1,0:T(8,128)(2,1)}), bf16[32,1024,128]{2,1,0:T(8,128)(2,1)}) %all-gather.16.cloned.1.call-update) | async-done | bytes 8388624 | tf_op jit(solution)/shard_map/all_gather | solution.py:219
  536.5 125.5 %all-gather.18.cloned.1.call-done = bf16[32,1024,128]{2,1,0:T(8,128)(2,1)} async-done(((bf16[32,128,128]{2,1,0:T(8,128)(2,1)}), bf16[32,1024,128]{2,1,0:T(8,128)(2,1)}) %all-gather.18.cloned.1.call-update) | async-done | bytes 8388624 | tf_op jit(solution)/shard_map/all_gather | solution.py:220
  664.5 437.5 %while.63 = (s32[]{:T(128)}, f32[1025,1024]{1,0:T(8,128)}, f32[32,256,128]{2,1,0:T(8,128)}, f32[32,256,128]{2,1,0:T(8,128)}, s32[32,256]{1,0:T(8,128)}, /*index=...) while((s32[]{:T(128)}, f32[1025,1024]{1,0:T(8,128)}, ...), condition=%wide.region_19.20_spmd, body=%wide.region_17.19_spmd.sunk | while | flops 202049280 | bytes 7878785 | solution.py:251
  1104.5 759.1 %while.64 = (s32[]{:T(128)}, f32[1025,1024]{1,0:T(8,128)}, f32[32,1024,128]{2,1,0:T(8,128)}, f32[32,1024,128]{2,1,0:T(8,128)}, f32[32,1024,128]{2,1,0:T(8,128)},...) while((s32[]{:T(128)}, f32[1025,1024]{1,0:T(8,128)}, ...), condition=%wide.region_24.25_spmd, body=%wide.region_21.24_spmd.sunk | while | flops 473466368 | bytes 14831809 | solution.py:302
  1163.7 7.4 scatter_fusion.1
  1211.1 7.4 scatter_fusion.1
  1305.9 7.4 scatter_fusion.1
  1329.6 7.4 scatter_fusion.1
  1353.3 7.4 scatter_fusion.1
  1448.2 7.4 scatter_fusion.1
  1471.9 7.4 scatter_fusion.1
  1638.1 7.4 scatter_fusion.1
  1661.8 7.4 scatter_fusion.1
  1709.3 7.4 scatter_fusion.1
  1780.5 7.4 scatter_fusion.1
  1804.2 7.4 scatter_fusion.1
  1851.7 7.4 scatter_fusion.1
  1870.7 65.0 %gather_fusion.5 = f32[8192]{0:T(1024)S(1)} fusion(f32[32,256]{1,0:T(8,128)S(1)} %get-tuple-element.395, s32[8192]{0:T(1024)S(1)} %reshape.803), kind=kCustom, calls=%fused_computation.5 | custom fusion | bytes 131072 | tf_op jit(solution)/shard_map/gather | solution.py:307
  1936.2 10.9 psum.21
  1951.7 20.6 all-gather.22.cloned.1.call-done
  1976.6 60.3 %while.65 = (s32[]{:T(128)}, f32[1,1024,2,64]{1,3,2,0:T(8,128)S(1)}, f32[1,1024,2,64]{1,3,2,0:T(8,128)}, f32[2,512,2,2,64]{1,0,4,3,2:T(2,128)}, s32[2]{0:T(128)S...) while((s32[]{:T(128)}, ...), condition=%wide.region_32.33_spmd, body=%wide.region_30.32_spmd.sunk | while | flops 1375730176 | bytes 71637368 | solution.py:377
  1996.2 10.4 dynamic_update_slice.69
  2026.2 10.4 dynamic_update_slice.69
  2067.4 22.1 reduce-scatter.19.cloned.1.call-done
  2091.2 21.6 all-reduce.4
  2119.7 17.2 reduce-scatter.15.cloned.1.call-done
  2140.1 61.8 %reduce-scatter.29.cloned.1.call-done = f32[128,32]{0,1:T(8,128)} async-done(((f32[1024,32]{0,1:T(8,128)}), f32[128,32]{0,1:T(8,128)}) %reduce-scatter.29.cloned.1.call-update) | async-done | bytes 16400 | tf_op jit(solution)/shard_map/reduce_scatter | solution.py:416
  2201.9 64.9 %reduce-scatter.25.cloned.1.call-done = f32[128,128]{1,0:T(8,128)} async-done(((f32[1024,128]{1,0:T(8,128)}), f32[128,128]{1,0:T(8,128)}) %reduce-scatter.25.cloned.1.call-update) | async-done | bytes 65552 | tf_op jit(solution)/shard_map/reduce_scatter | solution.py:413
  2266.7 65.1 %reduce-scatter.23.cloned.1.call-done = f32[128,128]{1,0:T(8,128)} async-done(((f32[1024,128]{1,0:T(8,128)}), f32[128,128]{1,0:T(8,128)}) %reduce-scatter.23.cloned.1.call-update) | async-done | bytes 65552 | tf_op jit(solution)/shard_map/reduce_scatter | solution.py:412
  2331.8 66.4 %reduce-scatter.27.cloned.1.call-done = f32[128,256]{1,0:T(8,128)} async-done(((f32[1024,256]{1,0:T(8,128)}), f32[128,256]{1,0:T(8,128)}) %reduce-scatter.27.cloned.1.call-update) | async-done | bytes 131088 | tf_op jit(solution)/shard_map/reduce_scatter | solution.py:414
  2398.2 66.7 %reduce-scatter.21.cloned.1.call-done = f32[128,256]{1,0:T(8,128)} async-done(((f32[1024,256]{1,0:T(8,128)}), f32[128,256]{1,0:T(8,128)}) %reduce-scatter.21.cloned.1.call-update) | async-done | bytes 131088 | tf_op jit(solution)/shard_map/reduce_scatter | solution.py:411
  2464.9 285.3 %reduce-scatter.31.cloned.1.call-done = f32[32,128,128]{2,1,0:T(8,128)} async-done(((f32[32,1024,128]{2,1,0:T(8,128)}), f32[32,128,128]{2,1,0:T(8,128)}) %reduce-scatter.31.cloned.1.call-update) | async-done | bytes 2097168 | tf_op jit(solution)/shard_map/reduce_scatter | solution.py:417
  2750.2 285.6 %reduce-scatter.33.cloned.1.call-done = f32[32,128,128]{2,1,0:T(8,128)} async-done(((f32[32,1024,128]{2,1,0:T(8,128)}), f32[32,128,128]{2,1,0:T(8,128)}) %reduce-scatter.33.cloned.1.call-update) | async-done | bytes 2097168 | tf_op jit(solution)/shard_map/reduce_scatter | solution.py:418
  3035.8 285.4 %reduce-scatter.35.cloned.1.call-done = f32[32,128,128]{2,1,0:T(8,128)} async-done(((f32[32,1024,128]{2,1,0:T(8,128)}), f32[32,128,128]{2,1,0:T(8,128)}) %reduce-scatter.35.cloned.1.call-update) | async-done | bytes 2097168 | tf_op jit(solution)/shard_map/reduce_scatter | solution.py:419
  (1038 shorter events, 1256.5 us)
Async XLA Ops:
  7.2 91.5 %copy-start.56 = (bf16[128,128]{1,0:T(8,128)(2,1)S(1)}, bf16[128,128]{1,0:T(8,128)(2,1)}, u32[]{:S(2)}) copy-start(bf16[128,128]{1,0:T(8,128)(2,1)} %param.30) | copy-start | bytes 98308
  7.2 122.4 %copy-start.55 = (bf16[128,256]{1,0:T(8,128)(2,1)S(1)}, bf16[128,256]{1,0:T(8,128)(2,1)}, u32[]{:S(2)}) copy-start(bf16[128,256]{1,0:T(8,128)(2,1)} %param.31) | copy-start | bytes 196612
  7.2 154.1 %all-gather.10.cloned.1.call-start = ((), (), s32[]{:S(2)}) async-start(), calls=%async_computation.12 | async-start | bytes 2621440 | tf_op jit(solution)/shard_map/all_gather | solution.py:163
  33.5 200.1 %reduce-scatter.13.cloned.1.call-start = ((), (), s32[]{:S(2)}) async-start(), calls=%async_computation.13 | async-start | bytes 5242880 | tf_op jit(solution)/shard_map/reduce_scatter | solution.py:213
  98.5 68.0 %copy-start.18 = (bf16[1024,256]{1,0:T(8,128)(2,1)}, bf16[1024,256]{1,0:T(8,128)(2,1)S(1)}, u32[]{:S(2)}) copy-start(bf16[1024,256]{1,0:T(8,128)(2,1)S(1)} %all_gather.54) | copy-start | bytes 1572868
  129.5 37.2 %copy-start.28 = (bf16[1024,128]{1,0:T(8,128)(2,1)}, bf16[1024,128]{1,0:T(8,128)(2,1)S(1)}, u32[]{:S(2)}) copy-start(bf16[1024,128]{1,0:T(8,128)(2,1)S(1)} %all_gather.56) | copy-start | bytes 786436
  160.7 28.2 copy-start.33
  189.0 44.6 %copy-start.9 = (bf16[1,256,1024]{2,1,0:T(8,128)(2,1)S(1)}, bf16[1,256,1024]{2,1,0:T(8,128)(2,1)}, u32[]{:S(2)}) copy-start(bf16[1,256,1024]{2,1,0:T(8,128)(2,1)} %param.23) | copy-start | bytes 1572868
  191.7 47.3 %copy-start.43 = (s32[1,1024,8]{1,2,0:T(8,128)S(1)}, s32[1,1024,8]{1,2,0:T(8,128)}, u32[]{:S(2)}) copy-start(s32[1,1024,8]{1,2,0:T(8,128)} %param.25) | copy-start | bytes 98308
  191.8 184.3 %all-gather.20.cloned.1.call-start = ((), (), s32[]{:S(2)}) async-start(), calls=%async_computation.19 | async-start | bytes 2621440 | tf_op jit(solution)/shard_map/all_gather | solution.py:273
  192.5 186.7 %all-gather.12.cloned.1.call-start = ((), (), s32[]{:S(2)}) async-start(), calls=%async_computation.14 | async-start | bytes 2621440 | tf_op jit(solution)/shard_map/all_gather | solution.py:225
  209.0 30.2 copy-start.49
  209.0 30.6 copy-start.63
  237.0 243.8 %all-gather.14.cloned.1.call-start = ((), (), s32[]{:S(2)}) async-start(), calls=%async_computation.15 | async-start | bytes 9437184 | tf_op jit(solution)/shard_map/all_gather | solution.py:218
  237.6 298.9 %all-gather.16.cloned.1.call-start = ((), (), s32[]{:S(2)}) async-start(), calls=%async_computation.16 | async-start | bytes 9437184 | tf_op jit(solution)/shard_map/all_gather | solution.py:219
  238.1 423.9 %all-gather.18.cloned.1.call-start = ((), (), s32[]{:S(2)}) async-start(), calls=%async_computation.17 | async-start | bytes 9437184 | tf_op jit(solution)/shard_map/all_gather | solution.py:220
  238.9 1708.4 %reduce-scatter.17.cloned.1.call-start = ((), (), s32[]{:S(2)}) async-start(), calls=%async_computation.20 | async-start | bytes 5242880 | tf_op jit(solution)/shard_map/reduce_scatter | solution.py:321
  260.4 53.5 %copy-start.21 = (s32[1,1024,8]{2,1,0:T(8,128)S(1)}, s32[1,1024,8]{2,1,0:T(8,128)}, u32[]{:S(2)}) copy-start(s32[1,1024,8]{2,1,0:T(8,128)} %copy-done.20) | copy-start | bytes 98308
  313.3 65.8 %copy-start.11 = (s32[8192]{0:T(1024)}, s32[8192]{0:T(1024)S(1)}, u32[]{:S(2)}) copy-start(s32[8192]{0:T(1024)S(1)} %gather_fusion.6) | copy-start | bytes 98308
  313.4 34.0 %copy-start.62 = (bf16[128,32]{0,1:T(8,128)(2,1)S(1)}, bf16[128,32]{0,1:T(8,128)(2,1)}, u32[]{:S(2)}) copy-start(bf16[128,32]{0,1:T(8,128)(2,1)} %param.33) | copy-start | bytes 24580
  316.2 65.3 %copy-start.57 = (s32[8192]{0:T(1024)}, s32[8192]{0:T(1024)S(1)}, u32[]{:S(2)}) copy-start(s32[8192]{0:T(1024)S(1)} %reshape.845) | copy-start | bytes 98308
  381.5 66.0 %copy-start.44 = (s32[1,1024,8]{1,2,0:T(8,128)S(1)}, s32[1,1024,8]{1,2,0:T(8,128)}, u32[]{:S(2)}) copy-start(s32[1,1024,8]{1,2,0:T(8,128)} %param.25) | copy-start | bytes 98308
  447.5 31.4 copy-start.47
  447.6 31.3 copy-start.41
  1868.5 103.9 %all-gather.22.cloned.1.call-start = ((), (), s32[]{:S(2)}) async-start(), calls=%async_computation.21 | async-start | bytes 2621440 | tf_op jit(solution)/shard_map/all_gather | solution.py:327
  1870.6 65.6 %copy-start.46 = (s32[1024,8]{0,1:T(8,128)S(1)}, s32[1024,8]{0,1:T(8,128)}, u32[]{:S(2)}) copy-start(s32[1024,8]{0,1:T(8,128)} %copy.99) | copy-start | bytes 98308
  1870.6 65.6 %copy-start.48 = (pred[1024,8]{0,1:T(8,128)(4,1)S(1)}, pred[1024,8]{0,1:T(8,128)(4,1)}, u32[]{:S(2)}) copy-start(pred[1024,8]{0,1:T(8,128)(4,1)} %copy-done.47) | copy-start | bytes 24580
  1870.6 76.5 %copy-start.42 = (f32[1024,8]{0,1:T(8,128)S(1)}, f32[1024,8]{0,1:T(8,128)}, u32[]{:S(2)}) copy-start(f32[1024,8]{0,1:T(8,128)} %copy-done.41) | copy-start | bytes 98308
  1870.6 76.6 %copy-start.45 = (s32[1,1024,8]{1,2,0:T(8,128)S(1)}, s32[1,1024,8]{1,2,0:T(8,128)}, u32[]{:S(2)}) copy-start(s32[1,1024,8]{1,2,0:T(8,128)} %param.25) | copy-start | bytes 98308
  1870.6 76.7 %copy-start.6 = (f32[1,256,1024]{2,1,0:T(8,128)S(1)}, f32[1,256,1024]{2,1,0:T(8,128)}, u32[]{:S(2)}) copy-start(f32[1,256,1024]{2,1,0:T(8,128)} %copy-done.5) | copy-start | bytes 3145732
  1870.6 76.7 %copy-start.39 = (bf16[1024,32]{0,1:T(8,128)(2,1)S(1)}, bf16[1024,32]{0,1:T(8,128)(2,1)}, u32[]{:S(2)}) copy-start(bf16[1024,32]{0,1:T(8,128)(2,1)} %copy-done.38) | copy-start | bytes 196612
  1870.6 76.7 %copy-start.50 = (f32[8,1,128]{2,1,0:T(1,128)S(1)}, f32[8,1,128]{2,1,0:T(1,128)}, u32[]{:S(2)}) copy-start(f32[8,1,128]{2,1,0:T(1,128)} %copy-done.49) | copy-start | bytes 12292
  1870.6 76.7 %copy-start.59 = (f32[256]{0:T(256)S(1)}, f32[256]{0:T(256)}, u32[]{:S(2)}) copy-start(f32[256]{0:T(256)} %copy-done.58) | copy-start | bytes 3076
  1947.3 28.3 copy-start.37
  1951.7 137.9 %reduce-scatter.19.cloned.1.call-start = ((), (), s32[]{:S(2)}) async-start(), calls=%async_computation.22 | async-start | bytes 5242880 | tf_op jit(solution)/shard_map/reduce_scatter | solution.py:404
  1976.6 62.5 %copy-start.25 = (f32[1024,32]{0,1:T(8,128)S(1)}, f32[1024,32]{0,1:T(8,128)}, u32[]{:S(2)}) copy-start(f32[1024,32]{0,1:T(8,128)} %copy-done.24) | copy-start | bytes 393220
  1976.6 62.5 %copy-start.27 = (f32[1024,32]{0,1:T(8,128)S(1)}, f32[1024,32]{0,1:T(8,128)}, u32[]{:S(2)}) copy-start(f32[1024,32]{0,1:T(8,128)} %copy-done.26) | copy-start | bytes 393220
  2044.8 92.0 %reduce-scatter.15.cloned.1.call-start = ((), (), s32[]{:S(2)}) async-start(), calls=%async_computation.18 | async-start | bytes 5242880 | tf_op jit(solution)/shard_map/reduce_scatter | solution.py:257
  2049.8 152.1 %reduce-scatter.29.cloned.1.call-start = ((), (), s32[]{:S(2)}) async-start(), calls=%async_computation.27 | async-start | bytes 147456 | tf_op jit(solution)/shard_map/reduce_scatter | solution.py:416
  2053.7 213.1 %reduce-scatter.25.cloned.1.call-start = ((), (), s32[]{:S(2)}) async-start(), calls=%async_computation.25 | async-start | bytes 589824 | tf_op jit(solution)/shard_map/reduce_scatter | solution.py:413
  2055.3 276.5 %reduce-scatter.23.cloned.1.call-start = ((), (), s32[]{:S(2)}) async-start(), calls=%async_computation.24 | async-start | bytes 589824 | tf_op jit(solution)/shard_map/reduce_scatter | solution.py:412
  2057.9 340.3 %reduce-scatter.27.cloned.1.call-start = ((), (), s32[]{:S(2)}) async-start(), calls=%async_computation.26 | async-start | bytes 1179648 | tf_op jit(solution)/shard_map/reduce_scatter | solution.py:414
  2061.3 403.6 %reduce-scatter.21.cloned.1.call-start = ((), (), s32[]{:S(2)}) async-start(), calls=%async_computation.23 | async-start | bytes 1179648 | tf_op jit(solution)/shard_map/reduce_scatter | solution.py:411
  2064.2 685.9 %reduce-scatter.31.cloned.1.call-start = ((), (), s32[]{:S(2)}) async-start(), calls=%async_computation.28 | async-start | bytes 18874368 | tf_op jit(solution)/shard_map/reduce_scatter | solution.py:417
  2064.8 971.0 %reduce-scatter.33.cloned.1.call-start = ((), (), s32[]{:S(2)}) async-start(), calls=%async_computation.29 | async-start | bytes 18874368 | tf_op jit(solution)/shard_map/reduce_scatter | solution.py:418
  2065.4 1255.8 %reduce-scatter.35.cloned.1.call-start = ((), (), s32[]{:S(2)}) async-start(), calls=%async_computation.30 | async-start | bytes 18874368 | tf_op jit(solution)/shard_map/reduce_scatter | solution.py:419
  2065.5 71.4 %copy-start.16 = (f32[1,256,1024]{2,1,0:T(8,128)S(1)}, f32[1,256,1024]{2,1,0:T(8,128)}, u32[]{:S(2)}) copy-start(f32[1,256,1024]{2,1,0:T(8,128)} %copy-done.15) | copy-start | bytes 3145732
  2065.5 71.4 %copy-start.23 = (bf16[1,256,1024]{2,1,0:T(8,128)(2,1)S(1)}, bf16[1,256,1024]{2,1,0:T(8,128)(2,1)}, u32[]{:S(2)}) copy-start(bf16[1,256,1024]{2,1,0:T(8,128)(2,1)} %param.37) | copy-start | bytes 1572868
  (39 other events, 335.3 us)
Sparse Core Ops, SparseCore 0:
  33.6 19.8 all-gather.9
  191.8 41.7 reduce-scatter.12
  235.2 22.6 all-gather.19
  260.0 22.5 all-gather.11
  284.9 126.1 all-gather.13
  413.3 123.1 all-gather.15
  538.9 123.0 all-gather.17
  1868.6 42.6 reduce-scatter.16
  1951.8 20.5 all-gather.21
  2045.0 44.5 reduce-scatter.18
  2092.2 44.6 reduce-scatter.14
  2140.6 61.1 reduce-scatter.28
  2205.8 60.9 reduce-scatter.24
  2270.9 60.8 reduce-scatter.22
  2335.6 62.4 reduce-scatter.26
  2402.4 62.4 reduce-scatter.20
  2469.1 281.0 reduce-scatter.30
  2754.9 280.9 reduce-scatter.32
  3040.1 281.0 reduce-scatter.34
where the time goes:
time: 3350 us; the launch traced here: 3330 us
  waiting for transfers between devices  1450 us (43%)
  matrix products  578 us (17%)
  other arithmetic  538 us (16%)
  local copies, waits for them, and re-layouts  500 us (15%)
  blocking collectives  231 us (7%)
    dot_general x232, matrix products, contract(): lax.dot_general(left, right, ((left_dims, right_dims), ((), ())), preferr...  361 us
    reduce_scatter x1, waiting for transfers between devices, local(): lax.psum_scatter(up_grad, 'dp', scatter_dimension=1, tiled=True)  286 us
    reduce_scatter x1, waiting for transfers between devices, local(): lax.psum_scatter(down_grad, 'dp', scatter_dimension=1, tiled=True)  285 us
    reduce_scatter x1, waiting for transfers between devices, local(): lax.psum_scatter(gate_grad, 'dp', scatter_dimension=1, tiled=True)  285 us
    scatter-add x32, other arithmetic, expert_backward(): accum = accum.at[row_ids].add(picked_grad)  238 us
    scatter-add x32, other arithmetic, expert_forward(): combined = combined.at[row_ids].add(weight_row[:, None] * expert_out)  216 us
    all_gather x1, waiting for transfers between devices, local(): lax.all_gather(w_down, 'dp', axis=1, tiled=True)  126 us
    gather x32, local copies, waits for them, and re-layouts, expert_backward(): slot_dy = grad_padded[row_ids].astype(jnp.float32)  110 us
  transfers between devices with their start and end apart: 19, of which 14 were waited for; matrix products, arithmetic and copies ran while one was open for 9% of the time, Pallas kernels for 0%

commit v1 on v0

v1 whole, which is shorter than its diff:
```python
import functools
import math

import jax
import jax.numpy as jnp
from jax import lax
from jax.experimental import pallas as pl
from jax.experimental.pallas import tpu as pltpu
from jax.sharding import Mesh, PartitionSpec as P

HEAD_SIZE = 64
EPSILON = 1e-06
FLOOR_SCORE = -1e30
VMEM_LIMIT = 60 * 1024 * 1024
DP = ("o", "u", "y")
POOL = ("u", "y", "x", "c")
ORDERS = (("u", "y", "x"), ("y", "x", "u"), ("x", "u", "y"))
PIECE = 384
BLK = 256
BF = jnp.bfloat16
F32 = jnp.float32


def swap(value, axis):
    return lax.ppermute(value, axis, [(0, 1), (1, 0)])


def mm(left, right):
    return lax.dot_general(left, right, (((1,), (0,)), ((), ())), preferred_element_type=F32)


def mm_nt(left, right):
    return lax.dot_general(left, right, (((1,), (1,)), ((), ())), preferred_element_type=F32)


def mm_tn(left, right):
    return lax.dot_general(left, right, (((0,), (0,)), ((), ())), preferred_element_type=F32)


def lanes(shape):
    return lax.broadcasted_iota(jnp.int32, shape, 1)


def turn_halves(value):
    first = lanes(value.shape) % HEAD_SIZE < HEAD_SIZE // 2
    half = HEAD_SIZE // 2
    return jnp.where(first, pltpu.roll(value, 128 - half, 1), pltpu.roll(value, half, 1))


def both_halves(value, which):
    low = lanes(value.shape) < HEAD_SIZE
    turned = pltpu.roll(value, HEAD_SIZE, 1)
    return jnp.where(low, value, turned) if which == 0 else jnp.where(low, turned, value)


def stack_heads(pair):
    low = lanes(pair.shape) < HEAD_SIZE
    zero = jnp.zeros_like(pair)
    return jnp.concatenate([jnp.where(low, pair, zero), jnp.where(low, zero, pair)], axis=0)


def join_heads(stacked):
    rows = stacked.shape[0] // 2
    low = lanes((rows, stacked.shape[1])) < HEAD_SIZE
    return jnp.where(low, stacked[:rows], stacked[rows:])


def allowed_keys(start_col, block, width):
    rows = start_col.shape[0]
    cols = lax.broadcasted_iota(jnp.int32, (rows, width), 1)
    row_ids = block * rows + lax.broadcasted_iota(jnp.int32, (rows, width), 0)
    keep = (cols >= start_col) & (cols <= row_ids)
    return jnp.concatenate([keep, keep], axis=0)


def attend_forward_kernel(
    table, offs, t0, t1, t2, t3, wa, wb, gain, cosine, sine, start,
    ain_o, wqkv_o, wob_o, q_o, kd_o, vd_o, mix_o, lse_o, keep_o, send_o,
):
    blocks, shard = wb.shape[0], wb.shape[1]
    for b in range(blocks):
        at = pl.multiple_of(table[b] * shard, shard)
        wqkv_o[pl.ds(at, shard), :] = wa[b, :shard, :]
        wob_o[pl.ds(at, shard), :] = wb[b]
    for r, piece in enumerate((t0, t1, t2, t3)):
        at = pl.multiple_of(offs[r], BLK)
        rows = pl.ds(at, BLK)
        value = piece[...].astype(F32)
        factor = lax.rsqrt(jnp.mean(value * value, axis=-1, keepdims=True) + EPSILON)
        normed = (value * factor * gain[...]).astype(BF)
        ain_o[rows, :] = normed
        qkv = mm(normed, wqkv_o[...])
        cos_b, sin_b = cosine[rows, :], sine[rows, :]
        for part in range(3):
            raw = qkv[:, part * 128 : part * 128 + 128]
            turned = (raw * cos_b + turn_halves(raw) * sin_b).astype(BF)
            if part < 2:
                q_o[rows, part * 128 : part * 128 + 128] = turned * 0.125
            else:
                wide = turned.astype(F32)
                for kv in range(2):
                    kd_o[kv, rows, :] = both_halves(wide, kv).astype(BF)
        value_rows = qkv[:, 384:512].astype(BF).astype(F32)
        for kv in range(2):
            vd_o[kv, rows, :] = both_halves(value_rows, kv).astype(BF)
    total = ain_o.shape[0]
    for block in range(total // BLK):
        width = (block + 1) * BLK
        rows = pl.ds(block * BLK, BLK)
        keep = allowed_keys(start[rows, :], block, width)
        logs = jnp.zeros((BLK, 128), F32)
        for kv in range(2):
            query = stack_heads(q_o[rows, kv * 128 : kv * 128 + 128])
            scores = jnp.where(keep, mm_nt(query, kd_o[kv, :width, :]), FLOOR_SCORE)
            top = jnp.max(scores, axis=-1, keepdims=True)
            lifted = jnp.exp(scores - top)
            summed = jnp.sum(lifted, axis=-1, keepdims=True)
            shares = (lifted * (1.0 / summed)).astype(BF)
            mixed = join_heads(mm(shares, vd_o[kv, :width, :]))
            mix_o[rows, kv * 128 : kv * 128 + 128] = mixed.astype(BF)
            log_total = top + jnp.log(summed)
            lane = lanes(logs.shape)
            logs = jnp.where(lane == 2 * kv, log_total[:BLK], logs)
            logs = jnp.where(lane == 2 * kv + 1, log_total[BLK:], logs)
        lse_o[rows, :] = logs
    for r in range(4):
        rows = pl.ds(pl.multiple_of(offs[r], BLK), BLK)
        part = mm_nt(mix_o[rows, :], wob_o[:, :256])
        if r % 2 == 0:
            keep_o[r // 2] = part
        else:
            send_o[r // 2] = part.astype(BF)


def attend_backward_kernel(
    offs, a0, a1, a2, a3, wqkv, wob, q, kd, vd, mix, lse, start, ain, cosine, sine,
    keep_o, send_o, wg_o, og_o, gcol_o, aog, mgrad, dqkv, dk, dv,
):
    total = ain.shape[0]
    for r, piece in enumerate((a0, a1, a2, a3)):
        aog[pl.ds(pl.multiple_of(offs[r], BLK), BLK), :] = piece[...]
    mgrad[...] = mm(aog[...], wob[:, :256]).astype(BF)
    og_o[...] = mm_tn(aog[...], mix[...])
    dk[...] = jnp.zeros_like(dk)
    dv[...] = jnp.zeros_like(dv)
    for block in range(total // BLK):
        width = (block + 1) * BLK
        rows = pl.ds(block * BLK, BLK)
        keep = allowed_keys(start[rows, :], block, width)
        logs = lse[rows, :]
        lane = lanes(logs.shape)
        cos_b, sin_b = cosine[rows, :], sine[rows, :]
        for kv in range(2):
            cols = slice(kv * 128, kv * 128 + 128)
            query = stack_heads(q[rows, cols])
            out_grad = stack_heads(mgrad[rows, cols])
            log_total = jnp.concatenate(
                [
                    jnp.sum(jnp.where(lane == 2 * kv + h, logs, 0.0), axis=1, keepdims=True)
                    for h in range(2)
                ],
                axis=0,
            )
            keys = kd[kv, :width, :]
            scores = jnp.where(keep, mm_nt(query, keys), FLOOR_SCORE)
            shares = jnp.exp(scores - log_total)
            share_grad = mm_nt(out_grad, vd[kv, :width, :])
            inner = jnp.sum(shares * share_grad, axis=-1, keepdims=True)
            score_grad = (shares * (share_grad - inner)).astype(BF)
            query_grad = join_heads(mm(score_grad, keys)) * 0.125
            query_grad = query_grad * cos_b - turn_halves(query_grad) * sin_b
            dqkv[rows, cols] = query_grad.astype(BF)
            dk[kv, :width, :] += mm_tn(score_grad, query)
            dv[kv, :width, :] += mm_tn(shares.astype(BF), out_grad)
    joined = []
    for acc in (dk, dv):
        pair = [acc[kv] + pltpu.roll(acc[kv], HEAD_SIZE, 1) for kv in range(2)]
        joined.append(jnp.where(lanes(pair[0].shape) < HEAD_SIZE, pair[0], pair[1]))
    key_grad = joined[0] * cosine[...] - turn_halves(joined[0]) * sine[...]
    dqkv[:, 256:384] = key_grad.astype(BF)
    dqkv[:, 384:512] = joined[1].astype(BF)
    wg_o[...] = mm_tn(ain[...], dqkv[...]).astype(BF)
    ones = jnp.ones((BLK, 128), BF)
    gain_sum = jnp.zeros(gcol_o.shape, F32)
    for r in range(4):
        rows = pl.ds(pl.multiple_of(offs[r], BLK), BLK)
        part = mm_nt(dqkv[rows, :], wqkv[...])
        gain_sum += mm_tn((part * ain[rows, :].astype(F32)).astype(BF), ones)
        if r % 2 == 0:
            keep_o[r // 2] = part
        else:
            send_o[r // 2] = part.astype(BF)
    gcol_o[...] = gain_sum.astype(BF)


def route_kernel(tok, keep, got, cross, gain, wr, routes, after_o, ma_o, mb_o, mc_o, gates_o):
    after = tok[...].astype(F32) + (keep[0] + got[0].astype(F32) + cross[...].astype(F32))
    after_o[...] = after
    factor = lax.rsqrt(jnp.mean(after * after, axis=-1, keepdims=True) + EPSILON)
    moe_in = (after * factor * gain[...]).astype(BF)
    logits = mm(moe_in, wr[...])
    lane = lanes(logits.shape)
    routed = lane < 0
    for k in range(routes.shape[1]):
        routed = routed | (routes[:, k : k + 1] == lane)
    top = jnp.max(jnp.where(routed, logits, FLOOR_SCORE), axis=1, keepdims=True)
    lifted = jnp.where(routed, jnp.exp(jnp.where(routed, logits - top, 0.0)), 0.0)
    gates = lifted / jnp.sum(lifted, axis=1, keepdims=True)
    gates_o[...] = gates
    high = gates.astype(BF).astype(F32)
    middle = (gates - high).astype(BF).astype(F32)
    low = gates - high - middle
    extra = high + pltpu.roll(middle, 32, 1) + pltpu.roll(low, 64, 1)
    ma_o[...] = moe_in[:, :PIECE]
    mb_o[...] = moe_in[:, PIECE : 2 * PIECE]
    mc_o[:, : PIECE - 128] = moe_in[:, 2 * PIECE :]
    mc_o[:, PIECE - 128 :] = extra.astype(BF)


def expert_kernel(n_weights, n_sends, first, meta, *refs):
    refs = list(refs)
    take = lambda n: [refs.pop(0) for _ in range(n)]
    tok_k, tok_c = take(3), take(3)
    dy_k, dy_c = take(3), take(3)
    (rank,) = take(1)
    weights = take(n_weights)
    prev = [] if first else take(12)
    outs = take(12)
    grads = take(n_sends)
    mat, acc, pick_s, dy_s, pre_s = take(5)
    step = pl.program_id(0)
    shard = weights[0].shape[2]
    hidden = mat.shape[1] // 3
    own_expert = meta[0]

    @pl.when(step == 0)
    def _():
        for i, buf in enumerate(weights):
            for b in range(buf.shape[0]):
                at = pl.multiple_of(meta[1 + i] + b // 4 * shard, shard)
                for m in range(3):
                    col = m * hidden + b % 4 * 128
                    mat[pl.ds(at, shard), col : col + 128] = buf[b, m]
        acc[...] = jnp.zeros_like(acc)

    slots = BLK
    row_ids = lax.broadcasted_iota(jnp.int32, (slots, rank.shape[-1]), 0)
    pick = jnp.where(rank[0] == row_ids, 1.0, 0.0).astype(BF)
    half = rank.shape[-1] // 2
    pick_k, pick_c = pick[:, :half], pick[:, half:]

    def gather(kept, other):
        flat = lambda ref: ref[...].reshape(half, ref.shape[-1])
        return mm(pick_k, flat(kept)) + mm(pick_c, flat(other))

    last = None
    for i in range(3):
        got = gather(tok_k[i], tok_c[i])
        width = min(PIECE, pick_s.shape[1] - i * PIECE)
        pick_s[:, i * PIECE : i * PIECE + width] = got[:, :width].astype(BF)
        last = got
        got = gather(dy_k[i], dy_c[i])
        dy_s[:, i * PIECE : i * PIECE + width] = got[:, :width].astype(BF)
    extra = last[:, PIECE - 128 :]
    lane = lanes(extra.shape)
    mine = (lane % 32 == own_expert) & (lane < 96)
    gate = jnp.sum(jnp.where(mine, extra, 0.0), axis=1, keepdims=True)
    picked, dy = pick_s[...], dy_s[...]
    gate_pre = mm(picked, mat[:, :hidden])
    up_pre = mm(picked, mat[:, hidden : 2 * hidden])
    back = mm(dy, mat[:, 2 * hidden :])
    sigma = 1.0 / (1.0 + jnp.exp(-gate_pre))
    active = gate_pre * sigma
    hid = active * up_pre
    gate_dot = jnp.sum(hid.astype(BF).astype(F32) * back, axis=1, keepdims=True)
    weighted = (gate * hid).astype(BF)
    back = back * gate
    pre_s[:, :hidden] = (back * up_pre * sigma * (1.0 + gate_pre * (1.0 - sigma))).astype(BF)
    pre_s[:, hidden:] = (back * active).astype(BF)
    pre_grad = pre_s[...]
    picked_grad = mm_nt(pre_grad, mat[:, : 2 * hidden]).astype(BF)
    expert_out = mm_nt(weighted, mat[:, 2 * hidden :]).astype(BF)
    acc[:, : 2 * hidden] += mm_tn(picked, pre_grad)
    acc[:, 2 * hidden :] += mm_tn(dy, weighted)
    dot_high = gate_dot.astype(BF).astype(F32)
    dot_low = gate_dot - dot_high
    note = jnp.where(lane == own_expert, dot_high, 0.0)
    note = jnp.where(lane == own_expert + 32, dot_low, note).astype(BF)

    def put(place, side, chosen, value):
        index = place + 3 * side
        summed = mm_tn(chosen, value)
        if not first:
            summed += prev[index][...].reshape(summed.shape).astype(F32)
        outs[index][...] = summed.astype(BF).reshape(outs[index].shape)

    for side, chosen in ((1, pick_c), (0, pick_k)):
        for i in range(3):
            part = picked_grad[:, i * PIECE : (i + 1) * PIECE]
            if i == 2:
                part = jnp.concatenate([part, note], axis=1)
            put(i, side, chosen, part)
            put(6 + i, side, chosen, expert_out[:, i * PIECE : (i + 1) * PIECE])

    @pl.when(step == pl.num_programs(0) - 1)
    def _():
        for i, buf in enumerate(grads):
            for b in range(buf.shape[0]):
                at = pl.multiple_of(meta[1 + i] + b // 4 * shard, shard)
                for m in range(3):
                    col = m * hidden + b % 4 * 128
                    buf[b, m] = acc[pl.ds(at, shard), col : col + 128].astype(BF)


def back_kernel(
    after, ak, ar, bk, br, ck, cr, gain, wr, gates, cot, after_grad_o, aog_o, small_o
):
    both = lambda a, b: a[...].astype(F32) + b[...].astype(F32)
    last = both(ck, cr)
    upstream = jnp.concatenate([both(ak, ar), both(bk, br), last[:, : PIECE - 128]], axis=1)
    extra = last[:, PIECE - 128 :]
    lane = lanes(extra.shape)
    gate_dot = jnp.where(lane < 32, extra + pltpu.roll(extra, 96, 1), 0.0)
    share = gates[...]
    logit_grad = share * (gate_dot - jnp.sum(share * gate_dot, axis=1, keepdims=True))
    high = logit_grad.astype(BF)
    low = (logit_grad - high.astype(F32)).astype(BF)
    router = wr[...]
    upstream += mm_nt(high, router) + mm_nt(low, router)
    value = after[...]
    factor = lax.rsqrt(jnp.mean(value * value, axis=-1, keepdims=True) + EPSILON)
    normed = value * factor
    moe_in = (normed * gain[...]).astype(BF)
    scaled = upstream * gain[...]
    inward = factor * (scaled - normed * jnp.mean(scaled * normed, axis=-1, keepdims=True))
    after_grad = cot[...].astype(F32) + inward
    after_grad_o[...] = after_grad
    aog_o[...] = after_grad.astype(BF)
    column = jnp.where(lane == 32, 1.0, 0.0).astype(BF)
    small_o[...] = (
        mm_tn(moe_in, high) + mm_tn(moe_in, low) + mm_tn((upstream * normed).astype(BF), column)
    )


def finish_kernel(tok, keep, got, cross, gain, after_grad, out):
    upstream = keep[0] + got[0].astype(F32) + cross[...].astype(F32)
    value = tok[...].astype(F32)
    factor = lax.rsqrt(jnp.mean(value * value, axis=-1, keepdims=True) + EPSILON)
    normed = value * factor
    scaled = upstream * gain[...]
    inward = factor * (scaled - normed * jnp.mean(scaled * normed, axis=-1, keepdims=True))
    out[...] = after_grad[...] + inward


def spec_of(space):
    return pl.BlockSpec(memory_space=space)


def simple_call(kernel, outs, n_scalar, n_in, scratch=(), flops=0, moved=0):
    return pl.pallas_call(
        kernel,
        out_shape=[jax.ShapeDtypeStruct(s, d) for s, d in outs],
        in_specs=[spec_of(pltpu.SMEM)] * n_scalar + [spec_of(pltpu.VMEM)] * n_in,
        out_specs=[spec_of(pltpu.VMEM)] * len(outs),
        scratch_shapes=list(scratch),
        compiler_params=pltpu.CompilerParams(vmem_limit_bytes=VMEM_LIMIT),
        cost_estimate=pl.CostEstimate(flops=flops, bytes_accessed=moved, transcendentals=0),
    )


def gather_dp(value, count):
    me = lax.axis_index(DP)
    if count <= 8:
        parts = [value]
        for s in range(1, count):
            parts.append(lax.ppermute(value, DP, [((i + s) % count, i) for i in range(count)]))
        return jnp.stack(parts), (me + jnp.arange(count, dtype=jnp.int32)) % count
    return lax.all_gather(value, DP, axis=0), jnp.arange(count, dtype=jnp.int32)


def gather_pool(pieces):
    kept, other = [], []
    for piece, order in zip(pieces, ORDERS):
        buf = piece
        for axis in order:
            buf = jnp.stack([buf, swap(buf, axis)])
        kept.append(buf)
        other.append(swap(buf, "c"))
    return kept, other


def scatter_pool(kept, other):
    pairs = []
    for keep, send, order in zip(kept, other, ORDERS):
        buf = keep.astype(F32) + swap(send, "c").astype(F32)
        for axis in reversed(order[1:]):
            buf = buf[0] + swap(buf[1].astype(BF), axis).astype(F32)
        pairs.append((buf[0].astype(BF), swap(buf[1].astype(BF), order[0])))
    return pairs


def gather_tensor(value):
    cross = swap(value, "x")
    return [value, swap(value, "c"), cross, swap(cross, "c")]


def sum_tensor(keep, send):
    got = swap(send, "c")
    cross = swap((keep[1] + got[1].astype(F32)).astype(BF), "x")
    return got, cross


def pool_spec(order, width):
    shape = tuple(2 if axis == "x" else 1 for axis in reversed(order)) + (BLK, width)
    zero = jnp.int32(0)

    def index(g):
        place = {"x": 0, "u": g // 2, "y": g % 2}
        return tuple(place[axis] for axis in reversed(order)) + (0, 0)

    del zero
    return pl.BlockSpec(shape, index)


def local(
    tokens, segments, routes, priority, norm_attn, w_query, w_key, w_value, w_out, norm_moe,
    w_router, w_gate, w_up, w_down, cotangent,
):
    _, rows, dim = tokens.shape
    n_outer = lax.axis_size("o")
    n_dp = 4 * n_outer
    shard = w_query.shape[0]
    length = 4 * rows
    top = routes.shape[2]
    experts = w_gate.shape[0]
    per_device = experts // 16
    capacity = length * top // experts
    hidden = 4 * w_gate.shape[2]
    at_x, at_c = lax.axis_index("x"), lax.axis_index("c")
    at_t = at_x * 2 + at_c
    at_o = lax.axis_index("o")
    at_pool = lax.axis_index(POOL)

    tok = tokens[0]
    cot = cotangent[0]
    tok_parts = gather_tensor(tok)
    gains = jnp.zeros((16, 512), BF)
    gains = gains.at[0, :shard].set(norm_attn).at[0, shard : 2 * shard].set(norm_moe)
    pack_a = jnp.concatenate([jnp.concatenate([w_query, w_key, w_value], axis=1), gains], axis=0)
    pack_b = jnp.concatenate([w_out, w_router, jnp.zeros((shard, 128 - experts), BF)], axis=1)
    wa, table = gather_dp(pack_a, n_dp)
    wb, _ = gather_dp(pack_b, n_dp)
    both_gains = wa[:, shard, : 2 * shard].astype(F32)
    if n_dp <= 8:
        both_gains = lax.dynamic_slice_in_dim(
            jnp.concatenate([both_gains, both_gains], axis=0), n_dp - table[0], n_dp, 0
        )
    gain_attn = both_gains[:, :shard].reshape(1, dim)
    gain_moe = both_gains[:, shard:].reshape(1, dim)

    expert_mats, bases = [], None
    for j in range(per_device):
        part = jnp.stack([w[j * 16 : (j + 1) * 16] for w in (w_gate, w_up, w_down)], axis=1)
        part = lax.all_to_all(part, POOL, 0, 0, tiled=True)
        if n_outer == 2:
            expert_mats.append([part, swap(part, "o")])
            bases = [at_o * 4 * shard, (1 - at_o) * 4 * shard]
        else:
            expert_mats.append([lax.all_gather(part, "o", axis=0, tiled=True)])
            bases = [jnp.int32(0)]

    seg = segments[0]
    start = jnp.zeros_like(seg)
    for s in range(1, 5):
        start = jnp.where(seg >= s, jnp.sum((seg < s).astype(jnp.int32)), start)
    place = (jnp.arange(length, dtype=jnp.int32) - start).astype(F32)
    lane = jnp.arange(128, dtype=jnp.int32)
    half = HEAD_SIZE // 2
    inverse = jnp.exp((lane % half).astype(F32) * (-2.0 * math.log(10000.0) / HEAD_SIZE))
    angle = place[:, None] * inverse[None, :]
    cosine = jnp.cos(angle)
    sine = jnp.sin(angle) * jnp.where(lane % HEAD_SIZE < half, -1.0, 1.0)
    start_col = start[:, None]

    plan = jnp.concatenate([routes[0].T, priority], axis=0)
    plan = plan.reshape(top + 1, 2, 2, rows)
    plan = jnp.where(at_x == 1, plan[:, ::-1], plan)
    plan = jnp.where(at_c == 1, plan[:, :, ::-1], plan)
    plan = plan.swapaxes(1, 2).reshape(top + 1, length)
    plan = jnp.stack([plan, swap(plan, "y")])
    plan = jnp.concatenate([plan, swap(plan, "u")], axis=0)
    own = [j * 16 + at_pool for j in range(per_device)]
    hits = jnp.stack([jnp.any(plan[:, :top] == e, axis=1) for e in own], axis=1)
    first = plan[:, top]
    less = (first[:, :, None] < first[:, None, :]).astype(BF)
    rank = jnp.einsum("gjs,gst->gjt", hits.astype(BF), less, preferred_element_type=F32)
    rank = rank.astype(jnp.int32)
    rank = jnp.where(hits & (rank < capacity), rank, -1)

    table = table.astype(jnp.int32)
    offs = (jnp.bitwise_xor(at_t, jnp.arange(4, dtype=jnp.int32)) * rows).astype(jnp.int32)
    heads = w_query.shape[1]
    ain, wqkv, wob, q, kd, vd, mix, lse, keep, send = simple_call(
        attend_forward_kernel,
        [
            ((length, dim), BF),
            ((dim, 512), BF),
            ((dim, PIECE), BF),
            ((length, heads), BF),
            ((2, length, 128), BF),
            ((2, length, 128), BF),
            ((length, heads), BF),
            ((length, 128), F32),
            ((2, rows, dim), F32),
            ((2, rows, dim), BF),
        ],
        2,
        10,
        flops=3 * 10**9,
        moved=16 * 2**20,
    )(table, offs, *tok_parts, wa, wb, gain_attn, cosine, sine, start_col)

    got, cross = sum_tensor(keep, send)
    route_col = lax.dynamic_slice_in_dim(routes[0], at_t * rows, rows, 0)
    router = wob[:, 256:]
    after, ma, mb, mc, gates = simple_call(
        route_kernel,
        [
            ((rows, dim), F32),
            ((rows, PIECE), BF),
            ((rows, PIECE), BF),
            ((rows, PIECE), BF),
            ((rows, 128), F32),
        ],
        0,
        7,
        flops=10**8,
        moved=4 * 2**20,
    )(tok, keep, got, cross, gain_moe, router, route_col)

    dy_kept, dy_other = gather_pool([cot[:, i * PIECE : (i + 1) * PIECE] for i in range(3)])
    tok_kept, tok_other = gather_pool([ma, mb, mc])

    widths = [PIECE, PIECE, PIECE]
    dy_widths = [PIECE, PIECE, dim - 2 * PIECE]
    tok_specs = [pool_spec(o, w) for o, w in zip(ORDERS, widths)]
    dy_specs = [pool_spec(o, w) for o, w in zip(ORDERS, dy_widths)]
    out_specs = tok_specs * 2 + dy_specs * 2
    out_shapes = [jax.ShapeDtypeStruct((2, 2, 2, rows, w), BF) for w in widths * 2 + dy_widths * 2]
    prev = []
    weight_grads = []
    for j in range(per_device):
        mats = expert_mats[j]
        whole = [pl.BlockSpec(m.shape, lambda g: (0, 0, 0, 0), pipeline_mode=pl.Buffered(1)) for m in mats]
        meta = jnp.stack([own[j]] + bases).astype(jnp.int32)
        result = pl.pallas_call(
            functools.partial(expert_kernel, len(mats), len(mats), j == 0),
            grid=(4,),
            in_specs=[spec_of(pltpu.SMEM)]
            + tok_specs * 2
            + dy_specs * 2
            + [pl.BlockSpec((1, 1, length), lambda g: (g, 0, 0))]
            + whole
            + (out_specs if prev else []),
            out_specs=out_specs + whole,
            out_shape=out_shapes + [jax.ShapeDtypeStruct(m.shape, BF) for m in mats],
            scratch_shapes=[
                pltpu.VMEM((dim, 3 * hidden), BF),
                pltpu.VMEM((dim, 3 * hidden), F32),
                pltpu.VMEM((capacity, dim), BF),
                pltpu.VMEM((capacity, dim), BF),
                pltpu.VMEM((capacity, 2 * hidden), BF),
            ],
            compiler_params=pltpu.CompilerParams(vmem_limit_bytes=VMEM_LIMIT),
            cost_estimate=pl.CostEstimate(flops=19 * 10**9, bytes_accessed=48 * 2**20, transcendentals=0),
        )(meta, *tok_kept, *tok_other, *dy_kept, *dy_other, rank[:, j : j + 1], *mats, *prev)
        prev = result[:12]
        weight_grads.append(result[12:])

    pairs = scatter_pool(prev[:3], prev[3:6])
    out_pairs = scatter_pool(prev[6:9], prev[9:12])

    after_grad, aog, small = simple_call(
        back_kernel,
        [((rows, dim), F32), ((rows, dim), BF), ((dim, 128), F32)],
        0,
        11,
        flops=10**9,
        moved=6 * 2**20,
    )(after, *pairs[0], *pairs[1], *pairs[2], gain_moe, router, gates, cot)
    aog_parts = gather_tensor(aog)

    keep, send, wg, og, gcol = simple_call(
        attend_backward_kernel,
        [
            ((2, rows, dim), F32),
            ((2, rows, dim), BF),
            ((dim, 512), BF),
            ((dim, 256), F32),
            ((dim, 128), BF),
        ],
        1,
        15,
        scratch=[
            pltpu.VMEM((length, dim), BF),
            pltpu.VMEM((length, heads), BF),
            pltpu.VMEM((length, 512), BF),
            pltpu.VMEM((2, length, 128), F32),
            pltpu.VMEM((2, length, 128), F32),
        ],
        flops=9 * 10**9,
        moved=20 * 2**20,
    )(offs, *aog_parts, wqkv, wob, q, kd, vd, mix, lse, start_col, ain, cosine, sine)

    got, cross = sum_tensor(keep, send)
    tokens_grad = simple_call(
        finish_kernel, [((rows, dim), F32)], 0, 6, flops=10**7, moved=6 * 2**20
    )(tok, keep, got, cross, gain_attn, after_grad)[0]

    moe_out = jnp.concatenate([a.astype(F32) + b.astype(F32) for a, b in out_pairs], axis=1)
    block_out = (after + moe_out).astype(BF)

    side = lax.psum_scatter(
        jnp.concatenate([og, small], axis=1), DP, scatter_dimension=0, tiled=True
    )
    tail = jnp.concatenate([wg, gcol], axis=1).reshape(n_dp, shard, 640)
    tail = jnp.sum(lax.all_to_all(tail, DP, 0, 0, tiled=True).astype(F32), axis=0)
    narrow = jnp.concatenate([side[:, 256 : 256 + experts + 1], tail[:, 512:513]], axis=1)
    narrow = narrow + swap(narrow, "x")
    narrow = narrow + swap(narrow, "c")
    moved = []
    for j in range(per_device):
        if n_outer == 2:
            mine, sent = weight_grads[j]
            summed = (mine.astype(F32) + swap(sent, "o").astype(F32)).astype(BF)
        else:
            summed = lax.psum_scatter(weight_grads[j][0], "o", scatter_dimension=0, tiled=True)
        moved.append(lax.all_to_all(summed, POOL, 0, 0, tiled=True))
    gate_grad, up_grad, down_grad = (
        jnp.concatenate([part[:, m] for part in moved], axis=0).astype(F32) for m in range(3)
    )
    return (
        block_out[None],
        tokens_grad[None],
        narrow[:, experts + 1] / norm_attn.astype(F32),
        tail[:, :256],
        tail[:, 256:384],
        tail[:, 384:512],
        side[:, :256],
        narrow[:, experts],
        narrow[:, :experts],
        gate_grad,
        up_grad,
        down_grad,
    )


def solution(mesh):
    devices = mesh.devices
    fine = Mesh(devices.reshape(devices.shape[0] // 4, 2, 2, 2, 2), ("o", "u", "y", "x", "c"))
    dp, tensor = DP, ("x", "c")
    in_specs = (
        P(dp, tensor, None),
        P(dp, None),
        P(dp, None, None),
        P(dp, None),
        P(dp),
        P(dp, tensor),
        P(dp, tensor),
        P(dp, tensor),
        P(dp, tensor),
        P(dp),
        P(dp, None),
        P(None, dp, tensor),
        P(None, dp, tensor),
        P(None, dp, tensor),
        P(dp, tensor, None),
    )
    out_specs = (
        P(dp, tensor, None),
        P(dp, tensor, None),
        P(dp),
        P(dp, tensor),
        P(dp, tensor),
        P(dp, tensor),
        P(dp, tensor),
        P(dp),
        P(dp, None),
        P(None, dp, tensor),
        P(None, dp, tensor),
        P(None, dp, tensor),
    )
    return jax.shard_map(local, mesh=fine, in_specs=in_specs, out_specs=out_specs, check_vma=False)
```

time: 3350 us -> 828 us (0.25)
  waiting for transfers between devices: 1450 us -> 432 us
  matrix products: 578 us -> 2.91 us
  local copies, waits for them, and re-layouts: 500 us -> 43.5 us
  other arithmetic: 538 us -> 85.3 us
  blocking collectives: 231 us -> 0 us
  starting transfers between devices: 0.77 us -> 129 us
  Pallas kernels: 0 us -> 114 us
    reduce_scatter x12 -> x1, waiting for transfers between devices: 1250 us -> 27 us  [local(): lax.psum_scatter(jnp.concatenate([og, small], axis=1), DP, scatter_dimens...]
    dot_general x349 -> x1, matrix products: 578 us -> 2.91 us  [local(): jnp.einsum('gjs,gst->gjt', hits.astype(BF), less, preferred_element_type=...]
    scatter-add x64 -> x0, other arithmetic: 454 us -> none  [the longest x32 238 us: expert_backward(): accum = accum.at[row_ids].add(picked_grad)]
    ppermute x0 -> x80, waiting for transfers between devices: none -> 392 us  [the longest x66 348 us: swap(): return lax.ppermute(value, axis, [(0, 1), (1, 0)])]
    gather x109 -> x0, local copies, waits for them, and re-layouts: 376 us -> none  [the longest x32 110 us: expert_backward(): slot_dy = grad_padded[row_ids].astype(jnp.float32)]
    all_gather x7 -> x0, waiting for transfers between devices: 202 us -> none  [the longest x1 126 us: local(): lax.all_gather(w_down, 'dp', axis=1, tiled=True)]
    all_gather x7 -> x0, blocking collectives: 192 us -> none  [the longest x1 31.5 us: local(): lax.all_gather(w_query, 'dp', axis=0, tiled=True)]
    pallas_call x0 -> x7, Pallas kernels: none -> 114 us  [the longest x2 66.3 us: local(): pl.pallas_call(functools.partial(expert_kernel, len(mats), len(mats), j =...]
  transfers between devices with their start and end apart: 19 -> 86, of which waited for: 14 -> 28; matrix products, arithmetic and copies ran while one was open for 9% -> 14% of each run, Pallas kernels for 0% -> 10%
where the time goes in v1:
time: 828 us; the launch traced here: 822 us
  waiting for transfers between devices  432 us (52%)
  starting transfers between devices  129 us (16%)
  Pallas kernels  114 us (14%)
  other arithmetic  85.3 us (10%)
  local copies, waits for them, and re-layouts  43.5 us (5%)
  between operations  15.6 us (2%)
    ppermute x66, waiting for transfers between devices, swap(): return lax.ppermute(value, axis, [(0, 1), (1, 0)])  348 us
    ppermute x66, starting transfers between devices, swap(): return lax.ppermute(value, axis, [(0, 1), (1, 0)])  82.7 us
    pallas_call x2, Pallas kernels, local(): pl.pallas_call(functools.partial(expert_kernel, len(mats), len(mats), j =...  66.3 us
    ppermute x14, waiting for transfers between devices, gather_dp(): lax.ppermute(value, DP, [((i + s) % count, i) for i in range(count)])  43.2 us
    another operation x18, other arithmetic, gather_pool(): buf = jnp.stack([buf, swap(buf, axis)])  29.3 us
    reduce_scatter x1, waiting for transfers between devices, local(): lax.psum_scatter(jnp.concatenate([og, small], axis=1), DP, scatter_dimens...  27 us
    ppermute x14, starting transfers between devices, gather_dp(): lax.ppermute(value, DP, [((i + s) % count, i) for i in range(count)])  22.4 us
    pallas_call x1, Pallas kernels, local(): simple_call(attend_backward_kernel, [((2, rows, dim), F32), ((2, rows, di...  21.2 us
  transfers between devices with their start and end apart: 86, of which 28 were waited for; matrix products, arithmetic and copies ran while one was open for 14% of the time, Pallas kernels for 10%

profile of v1, /device:TPU:0, one launch (start us, length us, event | category | flops | bytes accessed | tf_op | source)
XLA Modules:
  0.0 822.2 jit_solution(3804865525075943053)
XLA Ops:
  9.8 2.7 broadcast_select_fusion.1
  14.8 6.1 collective-permute-start.3
  21.3 3.0 collective-permute-start.6
  33.6 4.5 all-to-all-start.1
  46.0 3.1 fusion.29
  50.0 10.5 %collective-permute-done.11 = bf16[128,384]{1,0:T(8,128)(2,1)S(1)} collective-permute-done((bf16[128,384]{1,0:T(8,128)(2,1)S(1)}, bf16[128,384]{1,0:T(8,128)(2,1)S(1)}, u32[]{:S(2)}, u32[]{:S(2)}) %collective-permute-start.11) | collective-permute-done | bytes 98336 | tf_op jit(solution)/shard_map/ppermute | solution.py:376
  61.7 4.3 collective-permute-done.12
  68.5 4.9 collective-permute-done.13
  74.8 6.0 collective-permute-done.14
  80.9 6.4 collective-permute-done.15
  87.2 3.0 collective-permute-start.16
  90.3 4.3 collective-permute-done.16
  96.8 3.6 collective-permute-start.1
  100.5 6.8 collective-permute-done.7
  110.3 13.8 %shard_map.238 = (bf16[1024,1024]{1,0:T(8,128)(2,1)}, bf16[1024,512]{1,0:T(8,128)(2,1)}, bf16[1024,384]{1,0:T(8,128)(2,1)}, bf16[1024,256]{1,0:T(8,128)(2,1)}, b...) custom-call(s32[8]{0:T(128)} %copy-done.58, ...), custom_call_target="tpu_custom_call" | custom-call | flops 3000000000 | bytes 16777216 | tf_op jit(solution)/shard_map/pallas_call | solution.py:503
  128.1 5.2 collective-permute-start.31
  146.7 3.8 collective-permute-done.32
  160.9 4.0 shard_map.239
  169.3 12.4 %collective-permute-done.35 = bf16[2,256,384]{2,1,0:T(8,128)(2,1)} collective-permute-done((bf16[2,256,384]{2,1,0:T(8,128)(2,1)}, bf16[2,256,384]{2,1,0:T(8,128)(2,1)}, u32[]{:S(2)}, u32[]{:S(2)}) %collective-permute-start.35) | collective-permute-done | bytes 393248 | tf_op jit(solution)/shard_map/ppermute | solution.py:25
  196.4 4.4 all-to-all-start
  210.7 14.7 %collective-permute-done.20 = bf16[2,256,384]{2,1,0:T(8,128)(2,1)S(1)} collective-permute-done((bf16[2,256,384]{2,1,0:T(8,128)(2,1)}, bf16[2,256,384]{2,1,0:T(8,128)(2,1)S(1)}, u32[]{:S(2)}, u32[]{:S(2)}) %collective-permute-start.20) | collective-permute-done | bytes 393248 | tf_op jit(solution)/shard_map/ppermute | solution.py:25
  226.4 3.2 collective-permute-start.21
  232.1 14.0 %collective-permute-done.27 = bf16[2,2,256,384]{3,2,1,0:T(8,128)(2,1)} collective-permute-done((bf16[2,2,256,384]{3,2,1,0:T(8,128)(2,1)}, bf16[2,2,256,384]{3,2,1,0:T(8,128)(2,1)}, u32[]{:S(2)}, u32[]{:S(2)}) %collective-permute-start.27) | collective-permute-done | bytes 786464 | tf_op jit(solution)/shard_map/ppermute | solution.py:25
  257.1 2.9 and_select_fusion
  262.9 94.7 %collective-permute-done.46.refs_14_ = bf16[16,3,128,128]{3,2,1,0:T(8,128)(2,1)} collective-permute-done((bf16[16,3,128,128]{3,2,1,0:T(8,128)(2,1)}, bf16[16,3,128,128]{3,2,1,0:T(8,128)(2,1)}, u32[]{:S(2)}, u32[]{:S(2)}) %collective-permute-start.46) | collective-permute-done | bytes 1572896 | tf_op jit(solution)/shard_map/ppermute | solution.py:25
  357.6 32.3 %shard_map.240 = (bf16[2,2,2,256,384]{4,3,2,1,0:T(8,128)(2,1)}, bf16[2,2,2,256,384]{4,3,2,1,0:T(8,128)(2,1)}, bf16[2,2,2,256,384]{4,3,2,1,0:T(8,128)(2,1)}, bf16...) custom-call(s32[3]{0:T(128)} %add_add_fusion.1.meta, ...), custom_call_target="tpu_custom_call" | custom-call | flops 19000000512 | bytes 50331648 | tf_op jit(solution)/shard_map/pallas_call | solution.py:556
  392.0 34.0 %shard_map.241 = (bf16[2,2,2,256,384]{4,3,2,1,0:T(8,128)(2,1)}, bf16[2,2,2,256,384]{4,3,2,1,0:T(8,128)(2,1)}, bf16[2,2,2,256,384]{4,3,2,1,0:T(8,128)(2,1)}, bf16...) custom-call(s32[3]{0:T(128)} %add_add_fusion.meta, ...), custom_call_target="tpu_custom_call" | custom-call | flops 19000000512 | bytes 50331648 | tf_op jit(solution)/shard_map/pallas_call | solution.py:556
  426.8 2.8 collective-permute-start.79
  431.3 98.3 %collective-permute-done.78 = bf16[16,3,128,128]{3,2,1,0:T(8,128)(2,1)S(1)} collective-permute-done((bf16[16,3,128,128]{3,2,1,0:T(8,128)(2,1)}, bf16[16,3,128,128]{3,2,1,0:T(8,128)(2,1)S(1)}, u32[]{:S(2)}, u32[]{:S(2)}) %collective-permute-start.78) | collective-permute-done | bytes 1572896 | tf_op jit(solution)/shard_map/ppermute | solution.py:25
  531.2 4.4 all-to-all-start.3
  542.1 16.3 %collective-permute-done.56 = bf16[2,2,256,256]{3,2,1,0:T(8,128)(2,1)S(1)} collective-permute-done((bf16[2,2,256,256]{3,2,1,0:T(8,128)(2,1)S(1)}, bf16[2,2,256,256]{3,2,1,0:T(8,128)(2,1)S(1)}, u32[]{:S(2)}, u32[]{:S(2)}) %collective-permute-start.56) | collective-permute-done | bytes 524320 | tf_op jit(solution)/shard_map/ppermute | solution.py:25
  558.8 10.2 %collective-permute-start.64 = (bf16[2,2,256,384]{3,2,1,0:T(8,128)(2,1)S(1)}, bf16[2,2,256,384]{3,2,1,0:T(8,128)(2,1)S(1)}, u32[]{:S(2)}, u32[]{:S(2)}) collective-permute-start(bf16[2,2,256,384]{3,2,1,0:T(8,128)(2,1)S(1)} %fusion.17), channel_id=1, source_target_pairs={{0,8},{8,0},{1,9},{9,1},{2,10},{10,2},{3,11},{11,3},{4,12},{12,4},... | collective-permute-start | bytes 2359304 | tf_op jit(solution)/shard_map/ppermute | solution.py:25
  578.1 3.2 add_convert_fusion
  582.3 20.4 %collective-permute-done.57 = bf16[2,256,256]{2,1,0:T(8,128)(2,1)S(1)} collective-permute-done((bf16[2,256,256]{2,1,0:T(8,128)(2,1)S(1)}, bf16[2,256,256]{2,1,0:T(8,128)(2,1)S(1)}, u32[]{:S(2)}, u32[]{:S(2)}) %collective-permute-start.57) | collective-permute-done | bytes 262176 | tf_op jit(solution)/shard_map/ppermute | solution.py:25
  602.8 3.7 collective-permute-start.58
  609.7 21.3 %collective-permute-done.69 = bf16[2,256,384]{2,1,0:T(8,128)(2,1)S(1)} collective-permute-done((bf16[2,256,384]{2,1,0:T(8,128)(2,1)S(1)}, bf16[2,256,384]{2,1,0:T(8,128)(2,1)S(1)}, u32[]{:S(2)}, u32[]{:S(2)}) %collective-permute-start.69) | collective-permute-done | bytes 393248 | tf_op jit(solution)/shard_map/ppermute | solution.py:25
  636.3 5.5 collective-permute-done.61
  644.5 4.4 all-to-all-start.4
  652.6 20.7 %collective-permute-done.62.ar = bf16[256,384]{1,0:T(8,128)(2,1)S(1)} collective-permute-done((bf16[256,384]{1,0:T(8,128)(2,1)}, bf16[256,384]{1,0:T(8,128)(2,1)S(1)}, u32[]{:S(2)}, u32[]{:S(2)}) %collective-permute-start.62) | collective-permute-done | bytes 196640 | tf_op jit(solution)/shard_map/ppermute | solution.py:25
  674.0 4.5 shard_map.242
  678.5 2.7 collective-permute-start.72
  684.7 8.5 %collective-permute-done.72.a2 = bf16[256,1024]{1,0:T(8,128)(2,1)S(1)} collective-permute-done((bf16[256,1024]{1,0:T(8,128)(2,1)}, bf16[256,1024]{1,0:T(8,128)(2,1)S(1)}, u32[]{:S(2)}, u32[]{:S(2)}) %collective-permute-start.72) | collective-permute-done | bytes 524320 | tf_op jit(solution)/shard_map/ppermute | solution.py:25
  699.3 21.2 %shard_map.243 = (f32[2,256,1024]{2,1,0:T(8,128)}, bf16[2,256,1024]{2,1,0:T(8,128)(2,1)}, bf16[1024,512]{1,0:T(8,128)(2,1)}, f32[1024,256]{1,0:T(8,128)}, bf16[1024,128]{1,0:T(8,128)(2,1)}) custom-call(s32[4]{0:T(128)} %xor_multiply_fusion.offs, bf16[256,1024]{1,0:T(8,128)(2,1)} %get-tuple-element.119.a0, bf16[256,1024]{1,0:T(8,128)(2,1)} %copy-done.54, ...), custom_call_target="tpu_custom_call" | custom-call | flops 8999999488 | bytes 20971520 | tf_op jit(solution)/shard_map/pallas_call | solution.py:593
  727.4 5.7 all-to-all-start.2
  737.5 12.5 %collective-permute-done.54 = bf16[256,384]{1,0:T(8,128)(2,1)S(1)} collective-permute-done((bf16[256,384]{1,0:T(8,128)(2,1)S(1)}, bf16[256,384]{1,0:T(8,128)(2,1)S(1)}, u32[]{:S(2)}, u32[]{:S(2)}) %collective-permute-start.54) | collective-permute-done | bytes 196640 | tf_op jit(solution)/shard_map/ppermute | solution.py:25
  761.4 13.6 %all-to-all-done.2 = bf16[8,128,640]{2,1,0:T(8,128)(2,1)S(1)} async-done(((bf16[8,128,640]{2,1,0:T(8,128)(2,1)}), bf16[8,128,640]{2,1,0:T(8,128)(2,1)S(1)}, u32[]{:S(2)}, u32[]{:S(2)}) %all-to-all-start.2) | async-done | bytes 1310752 | tf_op jit(solution)/shard_map/all_to_all | solution.py:627
  775.3 27.0 %reduce-scatter.2.cloned.1.call-done = f32[128,384]{1,0:T(8,128)} async-done(((f32[1024,384]{1,0:T(8,128)}), f32[128,384]{1,0:T(8,128)}) %reduce-scatter.2.cloned.1.call-update) | async-done | bytes 196624 | tf_op jit(solution)/shard_map/reduce_scatter | solution.py:623
  807.1 4.1 shard_map.244
  (400 shorter events, 187.0 us)
Async XLA Ops:
  14.8 79.8 %collective-permute-start.3 = (bf16[144,512]{1,0:T(8,128)(2,1)S(1)}, bf16[144,512]{1,0:T(8,128)(2,1)S(1)}, u32[]{:S(2)}, u32[]{:S(2)}) collective-permute-start(bf16[144,512]{1,0:T(8,128)(2,1)S(1)} %pad_maximum_fusion.22), channel_id=1, source_target_pairs={{4,0},{8,4},{12,8},{16,12},{20,16},{24,20},{28,24},{0,28},{5,1},{9... | collective-permute-start | bytes 442376 | tf_op jit(solution)/shard_map/ppermute | solution.py:376
  20.9 74.4 %collective-permute-start.4 = (bf16[144,512]{1,0:T(8,128)(2,1)S(1)}, bf16[144,512]{1,0:T(8,128)(2,1)S(1)}, u32[]{:S(2)}, u32[]{:S(2)}) collective-permute-start(bf16[144,512]{1,0:T(8,128)(2,1)S(1)} %pad_maximum_fusion.22), channel_id=1, source_target_pairs={{8,0},{12,4},{16,8},{20,12},{24,16},{28,20},{0,24},{4,28},{9,1},{1... | collective-permute-start | bytes 442376 | tf_op jit(solution)/shard_map/ppermute | solution.py:376
  21.3 75.5 %collective-permute-start.5 = (bf16[144,512]{1,0:T(8,128)(2,1)S(1)}, bf16[144,512]{1,0:T(8,128)(2,1)S(1)}, u32[]{:S(2)}, u32[]{:S(2)}) collective-permute-start(bf16[144,512]{1,0:T(8,128)(2,1)S(1)} %pad_maximum_fusion.22), channel_id=1, source_target_pairs={{12,0},{16,4},{20,8},{24,12},{28,16},{0,20},{4,24},{8,28},{13,1},{... | collective-permute-start | bytes 442376 | tf_op jit(solution)/shard_map/ppermute | solution.py:376
  21.3 79.1 %collective-permute-start.6 = (bf16[144,512]{1,0:T(8,128)(2,1)S(1)}, bf16[144,512]{1,0:T(8,128)(2,1)S(1)}, u32[]{:S(2)}, u32[]{:S(2)}) collective-permute-start(bf16[144,512]{1,0:T(8,128)(2,1)S(1)} %pad_maximum_fusion.22), channel_id=1, source_target_pairs={{16,0},{20,4},{24,8},{28,12},{0,16},{4,20},{8,24},{12,28},{17,1},{... | collective-permute-start | bytes 442376 | tf_op jit(solution)/shard_map/ppermute | solution.py:376
  26.7 22.9 %collective-permute-start.10 = (bf16[128,384]{1,0:T(8,128)(2,1)S(1)}, bf16[128,384]{1,0:T(8,128)(2,1)S(1)}, u32[]{:S(2)}, u32[]{:S(2)}) collective-permute-start(bf16[128,384]{1,0:T(8,128)(2,1)S(1)} %get-tuple-element.181), channel_id=1, source_target_pairs={{4,0},{8,4},{12,8},{16,12},{20,16},{24,20},{28,24},{0,28},{5,1},{9... | collective-permute-start | bytes 294920 | tf_op jit(solution)/shard_map/ppermute | solution.py:376
  33.6 162.8 %all-to-all-start.1 = ((bf16[16,3,128,128]{3,2,1,0:T(8,128)(2,1)}), bf16[16,3,128,128]{3,2,1,0:T(8,128)(2,1)}, u32[]{:S(2)}, u32[]{:S(2)}) async-start(bf16[16,3,128,128]{3,2,1,0:T(8,128)(2,1)} %pad_maximum_fusion.6), calls=%async_computation.1 | async-start | bytes 3145728 | tf_op jit(solution)/shard_map/all_to_all | solution.py:464
  125.7 64.4 %collective-permute-start.43 = (s32[9,1024]{1,0:T(8,128)}, s32[9,1024]{1,0:T(8,128)S(1)}, u32[]{:S(2)}, u32[]{:S(2)}) collective-permute-start(s32[9,1024]{1,0:T(8,128)} %reshape.281), channel_id=1, source_target_pairs={{0,4},{4,0},{1,5},{5,1},{2,6},{6,2},{3,7},{7,3},{8,12},{12,8},{9,1... | collective-permute-start | bytes 110600 | tf_op jit(solution)/shard_map/ppermute | solution.py:25
  145.0 22.0 %collective-permute-start.38 = (bf16[2,256,256]{2,1,0:T(8,128)(2,1)}, bf16[2,256,256]{2,1,0:T(8,128)(2,1)}, u32[]{:S(2)}, u32[]{:S(2)}) collective-permute-start(bf16[2,256,256]{2,1,0:T(8,128)(2,1)} %get-tuple-element.231), channel_id=1, source_target_pairs={{0,8},{8,0},{1,9},{9,1},{2,10},{10,2},{3,11},{11,3},{4,12},{12,4},... | collective-permute-start | bytes 786440 | tf_op jit(solution)/shard_map/ppermute | solution.py:25
  151.6 39.4 %collective-permute-start.33 = (bf16[2,2,256,384]{3,2,1,0:T(8,128)(2,1)}, bf16[2,2,256,384]{3,2,1,0:T(8,128)(2,1)}, u32[]{:S(2)}, u32[]{:S(2)}) collective-permute-start(bf16[2,2,256,384]{3,2,1,0:T(8,128)(2,1)} %get-tuple-element.197), channel_id=1, source_target_pairs={{0,2},{2,0},{1,3},{3,1},{4,6},{6,4},{5,7},{7,5},{8,10},{10,8},{9,1... | collective-permute-start | bytes 2359304 | tf_op jit(solution)/shard_map/ppermute | solution.py:25
  155.4 26.4 %collective-permute-start.35 = (bf16[2,256,384]{2,1,0:T(8,128)(2,1)}, bf16[2,256,384]{2,1,0:T(8,128)(2,1)}, u32[]{:S(2)}, u32[]{:S(2)}) collective-permute-start(bf16[2,256,384]{2,1,0:T(8,128)(2,1)} %get-tuple-element.219), channel_id=1, source_target_pairs={{0,2},{2,0},{1,3},{3,1},{4,6},{6,4},{5,7},{7,5},{8,10},{10,8},{9,1... | collective-permute-start | bytes 1179656 | tf_op jit(solution)/shard_map/ppermute | solution.py:25
  168.8 38.1 %collective-permute-start.39 = (bf16[2,2,256,256]{3,2,1,0:T(8,128)(2,1)}, bf16[2,2,256,256]{3,2,1,0:T(8,128)(2,1)}, u32[]{:S(2)}, u32[]{:S(2)}) collective-permute-start(bf16[2,2,256,256]{3,2,1,0:T(8,128)(2,1)} %get-tuple-element.205), channel_id=1, source_target_pairs={{0,4},{4,0},{1,5},{5,1},{2,6},{6,2},{3,7},{7,3},{8,12},{12,8},{9,1... | collective-permute-start | bytes 1572872 | tf_op jit(solution)/shard_map/ppermute | solution.py:25
  190.0 36.4 %collective-permute-start.36 = (bf16[2,2,256,384]{3,2,1,0:T(8,128)(2,1)}, bf16[2,2,256,384]{3,2,1,0:T(8,128)(2,1)}, u32[]{:S(2)}, u32[]{:S(2)}) collective-permute-start(bf16[2,2,256,384]{3,2,1,0:T(8,128)(2,1)} %get-tuple-element.195), channel_id=1, source_target_pairs={{0,8},{8,0},{1,9},{9,1},{2,10},{10,2},{3,11},{11,3},{4,12},{12,4},... | collective-permute-start | bytes 2359304 | tf_op jit(solution)/shard_map/ppermute | solution.py:25
  195.5 59.8 %collective-permute-start.40 = (bf16[2,2,2,256,384]{4,3,2,1,0:T(8,128)(2,1)}, bf16[2,2,2,256,384]{4,3,2,1,0:T(8,128)(2,1)}, u32[]{:S(2)}, u32[]{:S(2)}) collective-permute-start(bf16[2,2,2,256,384]{4,3,2,1,0:T(8,128)(2,1)} %pad_maximum_fusion.3.refs_6_), channel_id=1, source_target_pairs={{0,1},{1,0},{2,3},{3,2},{4,5},{5,4},{6,7},{7,6},{8,9},{9,8},{10,11... | collective-permute-start | bytes 4718600 | tf_op jit(solution)/shard_map/ppermute | solution.py:25
  196.4 64.3 %all-to-all-start = ((bf16[16,3,128,128]{3,2,1,0:T(8,128)(2,1)}), bf16[16,3,128,128]{3,2,1,0:T(8,128)(2,1)}, u32[]{:S(2)}, u32[]{:S(2)}) async-start(bf16[16,3,128,128]{3,2,1,0:T(8,128)(2,1)} %pad_maximum_fusion.5), calls=%async_computation | async-start | bytes 3145728 | tf_op jit(solution)/shard_map/all_to_all | solution.py:464
  201.8 23.6 %collective-permute-start.20 = (bf16[2,256,384]{2,1,0:T(8,128)(2,1)}, bf16[2,256,384]{2,1,0:T(8,128)(2,1)S(1)}, u32[]{:S(2)}, u32[]{:S(2)}) collective-permute-start(bf16[2,256,384]{2,1,0:T(8,128)(2,1)} %get-tuple-element.227), channel_id=1, source_target_pairs={{0,4},{4,0},{1,5},{5,1},{2,6},{6,2},{3,7},{7,3},{8,12},{12,8},{9,1... | collective-permute-start | bytes 1179656 | tf_op jit(solution)/shard_map/ppermute | solution.py:25
  203.7 42.4 %collective-permute-start.27 = (bf16[2,2,256,384]{3,2,1,0:T(8,128)(2,1)}, bf16[2,2,256,384]{3,2,1,0:T(8,128)(2,1)}, u32[]{:S(2)}, u32[]{:S(2)}) collective-permute-start(bf16[2,2,256,384]{3,2,1,0:T(8,128)(2,1)} %get-tuple-element.199), channel_id=1, source_target_pairs={{0,4},{4,0},{1,5},{5,1},{2,6},{6,2},{3,7},{7,3},{8,12},{12,8},{9,1... | collective-permute-start | bytes 2359304 | tf_op jit(solution)/shard_map/ppermute | solution.py:25
  206.8 43.6 %collective-permute-start.24 = (bf16[2,2,256,384]{3,2,1,0:T(8,128)(2,1)}, bf16[2,2,256,384]{3,2,1,0:T(8,128)(2,1)}, u32[]{:S(2)}, u32[]{:S(2)}) collective-permute-start(bf16[2,2,256,384]{3,2,1,0:T(8,128)(2,1)} %get-tuple-element.201), channel_id=1, source_target_pairs={{0,8},{8,0},{1,9},{9,1},{2,10},{10,2},{3,11},{11,3},{4,12},{12,4},... | collective-permute-start | bytes 2359304 | tf_op jit(solution)/shard_map/ppermute | solution.py:25
  225.4 29.9 %collective-permute-start.42 = (bf16[2,2,2,256,256]{4,3,2,1,0:T(8,128)(2,1)}, bf16[2,2,2,256,256]{4,3,2,1,0:T(8,128)(2,1)}, u32[]{:S(2)}, u32[]{:S(2)}) collective-permute-start(bf16[2,2,2,256,256]{4,3,2,1,0:T(8,128)(2,1)} %pad_maximum_fusion.9.refs_8_), channel_id=1, source_target_pairs={{0,1},{1,0},{2,3},{3,2},{4,5},{5,4},{6,7},{7,6},{8,9},{9,8},{10,11... | collective-permute-start | bytes 3145736 | tf_op jit(solution)/shard_map/ppermute | solution.py:25
  226.4 25.3 %collective-permute-start.21 = (bf16[2,2,256,384]{3,2,1,0:T(8,128)(2,1)}, bf16[2,2,256,384]{3,2,1,0:T(8,128)(2,1)}, u32[]{:S(2)}, u32[]{:S(2)}) collective-permute-start(bf16[2,2,256,384]{3,2,1,0:T(8,128)(2,1)} %get-tuple-element.203), channel_id=1, source_target_pairs={{0,2},{2,0},{1,3},{3,1},{4,6},{6,4},{5,7},{7,5},{8,10},{10,8},{9,1... | collective-permute-start | bytes 2359304 | tf_op jit(solution)/shard_map/ppermute | solution.py:25
  251.7 105.9 %collective-permute-start.46 = (bf16[16,3,128,128]{3,2,1,0:T(8,128)(2,1)}, bf16[16,3,128,128]{3,2,1,0:T(8,128)(2,1)}, u32[]{:S(2)}, u32[]{:S(2)}) collective-permute-start(bf16[16,3,128,128]{3,2,1,0:T(8,128)(2,1)} %all-to-all-done.1.refs_13_), channel_id=1, source_target_pairs={{0,16},{16,0},{1,17},{17,1},{2,18},{18,2},{3,19},{19,3},{4,20},{20... | collective-permute-start | bytes 4718600 | tf_op jit(solution)/shard_map/ppermute | solution.py:25
  254.8 102.8 %collective-permute-start.30 = (bf16[2,2,2,256,384]{4,3,2,1,0:T(8,128)(2,1)}, bf16[2,2,2,256,384]{4,3,2,1,0:T(8,128)(2,1)}, u32[]{:S(2)}, u32[]{:S(2)}) collective-permute-start(bf16[2,2,2,256,384]{4,3,2,1,0:T(8,128)(2,1)} %pad_maximum_fusion.2.refs_2_), channel_id=1, source_target_pairs={{0,1},{1,0},{2,3},{3,2},{4,5},{5,4},{6,7},{7,6},{8,9},{9,8},{10,11... | collective-permute-start | bytes 4718600 | tf_op jit(solution)/shard_map/ppermute | solution.py:25
  255.2 102.4 %collective-permute-start.29 = (bf16[2,2,2,256,384]{4,3,2,1,0:T(8,128)(2,1)S(1)}, bf16[2,2,2,256,384]{4,3,2,1,0:T(8,128)(2,1)}, u32[]{:S(2)}, u32[]{:S(2)}) collective-permute-start(bf16[2,2,2,256,384]{4,3,2,1,0:T(8,128)(2,1)S(1)} %pad_maximum_fusion.1.refs_1_), channel_id=1, source_target_pairs={{0,1},{1,0},{2,3},{3,2},{4,5},{5,4},{6,7},{7,6},{8,9},{9,8},{10,11... | collective-permute-start | bytes 4718600 | tf_op jit(solution)/shard_map/ppermute | solution.py:25
  255.3 102.3 %collective-permute-start.28 = (bf16[2,2,2,256,384]{4,3,2,1,0:T(8,128)(2,1)}, bf16[2,2,2,256,384]{4,3,2,1,0:T(8,128)(2,1)}, u32[]{:S(2)}, u32[]{:S(2)}) collective-permute-start(bf16[2,2,2,256,384]{4,3,2,1,0:T(8,128)(2,1)} %pad_maximum_fusion.refs_0_), channel_id=1, source_target_pairs={{0,1},{1,0},{2,3},{3,2},{4,5},{5,4},{6,7},{7,6},{8,9},{9,8},{10,11... | collective-permute-start | bytes 4718600 | tf_op jit(solution)/shard_map/ppermute | solution.py:25
  260.7 130.1 %collective-permute-start.45 = (bf16[16,3,128,128]{3,2,1,0:T(8,128)(2,1)}, bf16[16,3,128,128]{3,2,1,0:T(8,128)(2,1)S(1)}, u32[]{:S(2)}, u32[]{:S(2)}) collective-permute-start(bf16[16,3,128,128]{3,2,1,0:T(8,128)(2,1)} %all-to-all-done.refs_13_), channel_id=1, source_target_pairs={{0,16},{16,0},{1,17},{17,1},{2,18},{18,2},{3,19},{19,3},{4,20},{20... | collective-permute-start | bytes 4718600 | tf_op jit(solution)/shard_map/ppermute | solution.py:25
  426.1 103.4 %collective-permute-start.78 = (bf16[16,3,128,128]{3,2,1,0:T(8,128)(2,1)}, bf16[16,3,128,128]{3,2,1,0:T(8,128)(2,1)S(1)}, u32[]{:S(2)}, u32[]{:S(2)}) collective-permute-start(bf16[16,3,128,128]{3,2,1,0:T(8,128)(2,1)} %get-tuple-element.135), channel_id=1, source_target_pairs={{0,16},{16,0},{1,17},{17,1},{2,18},{18,2},{3,19},{19,3},{4,20},{20... | collective-permute-start | bytes 4718600 | tf_op jit(solution)/shard_map/ppermute | solution.py:25
  426.2 109.5 %collective-permute-start.67 = (bf16[2,2,2,256,384]{4,3,2,1,0:T(8,128)(2,1)}, bf16[2,2,2,256,384]{4,3,2,1,0:T(8,128)(2,1)}, u32[]{:S(2)}, u32[]{:S(2)}) collective-permute-start(bf16[2,2,2,256,384]{4,3,2,1,0:T(8,128)(2,1)} %get-tuple-element.117), channel_id=1, source_target_pairs={{0,1},{1,0},{2,3},{3,2},{4,5},{5,4},{6,7},{7,6},{8,9},{9,8},{10,11... | collective-permute-start | bytes 4718600 | tf_op jit(solution)/shard_map/ppermute | solution.py:25
  426.6 111.8 %collective-permute-start.63 = (bf16[2,2,2,256,384]{4,3,2,1,0:T(8,128)(2,1)}, bf16[2,2,2,256,384]{4,3,2,1,0:T(8,128)(2,1)}, u32[]{:S(2)}, u32[]{:S(2)}) collective-permute-start(bf16[2,2,2,256,384]{4,3,2,1,0:T(8,128)(2,1)} %get-tuple-element.115), channel_id=1, source_target_pairs={{0,1},{1,0},{2,3},{3,2},{4,5},{5,4},{6,7},{7,6},{8,9},{9,8},{10,11... | collective-permute-start | bytes 4718600 | tf_op jit(solution)/shard_map/ppermute | solution.py:25
  426.8 150.3 %collective-permute-start.79 = (bf16[16,3,128,128]{3,2,1,0:T(8,128)(2,1)}, bf16[16,3,128,128]{3,2,1,0:T(8,128)(2,1)}, u32[]{:S(2)}, u32[]{:S(2)}) collective-permute-start(bf16[16,3,128,128]{3,2,1,0:T(8,128)(2,1)} %get-tuple-element.137), channel_id=1, source_target_pairs={{0,16},{16,0},{1,17},{17,1},{2,18},{18,2},{3,19},{19,3},{4,20},{20... | collective-permute-start | bytes 4718600 | tf_op jit(solution)/shard_map/ppermute | solution.py:25
  429.6 129.2 %collective-permute-start.59 = (bf16[2,2,2,256,384]{4,3,2,1,0:T(8,128)(2,1)}, bf16[2,2,2,256,384]{4,3,2,1,0:T(8,128)(2,1)}, u32[]{:S(2)}, u32[]{:S(2)}) collective-permute-start(bf16[2,2,2,256,384]{4,3,2,1,0:T(8,128)(2,1)} %get-tuple-element.113), channel_id=1, source_target_pairs={{0,1},{1,0},{2,3},{3,2},{4,5},{5,4},{6,7},{7,6},{8,9},{9,8},{10,11... | collective-permute-start | bytes 4718600 | tf_op jit(solution)/shard_map/ppermute | solution.py:25
  529.5 41.4 %collective-permute-start.47 = (bf16[2,2,2,256,384]{4,3,2,1,0:T(8,128)(2,1)}, bf16[2,2,2,256,384]{4,3,2,1,0:T(8,128)(2,1)}, u32[]{:S(2)}, u32[]{:S(2)}) collective-permute-start(bf16[2,2,2,256,384]{4,3,2,1,0:T(8,128)(2,1)} %get-tuple-element.107), channel_id=1, source_target_pairs={{0,1},{1,0},{2,3},{3,2},{4,5},{5,4},{6,7},{7,6},{8,9},{9,8},{10,11... | collective-permute-start | bytes 4718600 | tf_op jit(solution)/shard_map/ppermute | solution.py:25
  531.2 113.2 %all-to-all-start.3 = ((bf16[16,3,128,128]{3,2,1,0:T(8,128)(2,1)}), bf16[16,3,128,128]{3,2,1,0:T(8,128)(2,1)}, u32[]{:S(2)}, u32[]{:S(2)}) async-start(bf16[16,3,128,128]{3,2,1,0:T(8,128)(2,1)} %add_convert_fusion.1), calls=%async_computation.4 | async-start | bytes 3145728 | tf_op jit(solution)/shard_map/all_to_all | solution.py:638
  535.7 39.5 %collective-permute-start.51 = (bf16[2,2,2,256,384]{4,3,2,1,0:T(8,128)(2,1)}, bf16[2,2,2,256,384]{4,3,2,1,0:T(8,128)(2,1)S(1)}, u32[]{:S(2)}, u32[]{:S(2)}) collective-permute-start(bf16[2,2,2,256,384]{4,3,2,1,0:T(8,128)(2,1)} %get-tuple-element.109), channel_id=1, source_target_pairs={{0,1},{1,0},{2,3},{3,2},{4,5},{5,4},{6,7},{7,6},{8,9},{9,8},{10,11... | collective-permute-start | bytes 4718600 | tf_op jit(solution)/shard_map/ppermute | solution.py:25
  558.4 44.4 %collective-permute-start.68 = (bf16[2,2,256,384]{3,2,1,0:T(8,128)(2,1)S(1)}, bf16[2,2,256,384]{3,2,1,0:T(8,128)(2,1)S(1)}, u32[]{:S(2)}, u32[]{:S(2)}) collective-permute-start(bf16[2,2,256,384]{3,2,1,0:T(8,128)(2,1)S(1)} %fusion.18), channel_id=1, source_target_pairs={{0,4},{4,0},{1,5},{5,1},{2,6},{6,2},{3,7},{7,3},{8,12},{12,8},{9,1... | collective-permute-start | bytes 2359304 | tf_op jit(solution)/shard_map/ppermute | solution.py:25
  558.8 47.9 %collective-permute-start.64 = (bf16[2,2,256,384]{3,2,1,0:T(8,128)(2,1)S(1)}, bf16[2,2,256,384]{3,2,1,0:T(8,128)(2,1)S(1)}, u32[]{:S(2)}, u32[]{:S(2)}) collective-permute-start(bf16[2,2,256,384]{3,2,1,0:T(8,128)(2,1)S(1)} %fusion.17), channel_id=1, source_target_pairs={{0,8},{8,0},{1,9},{9,1},{2,10},{10,2},{3,11},{11,3},{4,12},{12,4},... | collective-permute-start | bytes 2359304 | tf_op jit(solution)/shard_map/ppermute | solution.py:25
  570.9 38.1 %collective-permute-start.60 = (bf16[2,2,256,384]{3,2,1,0:T(8,128)(2,1)S(1)}, bf16[2,2,256,384]{3,2,1,0:T(8,128)(2,1)S(1)}, u32[]{:S(2)}, u32[]{:S(2)}) collective-permute-start(bf16[2,2,256,384]{3,2,1,0:T(8,128)(2,1)S(1)} %fusion.16), channel_id=1, source_target_pairs={{0,2},{2,0},{1,3},{3,1},{4,6},{6,4},{5,7},{7,5},{8,10},{10,8},{9,1... | collective-permute-start | bytes 2359304 | tf_op jit(solution)/shard_map/ppermute | solution.py:25
  575.1 106.1 %collective-permute-start.48 = (bf16[2,2,256,384]{3,2,1,0:T(8,128)(2,1)}, bf16[2,2,256,384]{3,2,1,0:T(8,128)(2,1)}, u32[]{:S(2)}, u32[]{:S(2)}) collective-permute-start(bf16[2,2,256,384]{3,2,1,0:T(8,128)(2,1)} %fusion.14), channel_id=1, source_target_pairs={{0,2},{2,0},{1,3},{3,1},{4,6},{6,4},{5,7},{7,5},{8,10},{10,8},{9,1... | collective-permute-start | bytes 2359304 | tf_op jit(solution)/shard_map/ppermute | solution.py:25
  577.0 25.6 %collective-permute-start.57 = (bf16[2,256,256]{2,1,0:T(8,128)(2,1)S(1)}, bf16[2,256,256]{2,1,0:T(8,128)(2,1)S(1)}, u32[]{:S(2)}, u32[]{:S(2)}) collective-permute-start(bf16[2,256,256]{2,1,0:T(8,128)(2,1)S(1)} %fusion.41), channel_id=1, source_target_pairs={{0,8},{8,0},{1,9},{9,1},{2,10},{10,2},{3,11},{11,3},{4,12},{12,4},... | collective-permute-start | bytes 786440 | tf_op jit(solution)/shard_map/ppermute | solution.py:25
  602.7 90.5 %collective-permute-start.52 = (bf16[2,2,256,384]{3,2,1,0:T(8,128)(2,1)}, bf16[2,2,256,384]{3,2,1,0:T(8,128)(2,1)}, u32[]{:S(2)}, u32[]{:S(2)}) collective-permute-start(bf16[2,2,256,384]{3,2,1,0:T(8,128)(2,1)} %fusion.15), channel_id=1, source_target_pairs={{0,8},{8,0},{1,9},{9,1},{2,10},{10,2},{3,11},{11,3},{4,12},{12,4},... | collective-permute-start | bytes 2359304 | tf_op jit(solution)/shard_map/ppermute | solution.py:25
  602.8 46.4 %collective-permute-start.58 = (bf16[256,256]{1,0:T(8,128)(2,1)S(1)}, bf16[256,256]{1,0:T(8,128)(2,1)S(1)}, u32[]{:S(2)}, u32[]{:S(2)}) collective-permute-start(bf16[256,256]{1,0:T(8,128)(2,1)S(1)} %slice_bitcast_fusion.34), channel_id=1, source_target_pairs={{0,2},{2,0},{1,3},{3,1},{4,6},{6,4},{5,7},{7,5},{8,10},{10,8},{9,1... | collective-permute-start | bytes 393224 | tf_op jit(solution)/shard_map/ppermute | solution.py:25
  606.7 24.3 %collective-permute-start.69 = (bf16[2,256,384]{2,1,0:T(8,128)(2,1)S(1)}, bf16[2,256,384]{2,1,0:T(8,128)(2,1)S(1)}, u32[]{:S(2)}, u32[]{:S(2)}) collective-permute-start(bf16[2,256,384]{2,1,0:T(8,128)(2,1)S(1)} %fusion.40), channel_id=1, source_target_pairs={{0,8},{8,0},{1,9},{9,1},{2,10},{10,2},{3,11},{11,3},{4,12},{12,4},... | collective-permute-start | bytes 1179656 | tf_op jit(solution)/shard_map/ppermute | solution.py:25
  609.0 25.1 %collective-permute-start.65 = (bf16[2,256,384]{2,1,0:T(8,128)(2,1)S(1)}, bf16[2,256,384]{2,1,0:T(8,128)(2,1)S(1)}, u32[]{:S(2)}, u32[]{:S(2)}) collective-permute-start(bf16[2,256,384]{2,1,0:T(8,128)(2,1)S(1)} %fusion.39), channel_id=1, source_target_pairs={{0,2},{2,0},{1,3},{3,1},{4,6},{6,4},{5,7},{7,5},{8,10},{10,8},{9,1... | collective-permute-start | bytes 1179656 | tf_op jit(solution)/shard_map/ppermute | solution.py:25
  644.5 82.9 %all-to-all-start.4 = ((bf16[16,3,128,128]{3,2,1,0:T(8,128)(2,1)}), bf16[16,3,128,128]{3,2,1,0:T(8,128)(2,1)}, u32[]{:S(2)}, u32[]{:S(2)}) async-start(bf16[16,3,128,128]{3,2,1,0:T(8,128)(2,1)} %add_convert_fusion), calls=%async_computation.5 | async-start | bytes 3145728 | tf_op jit(solution)/shard_map/all_to_all | solution.py:638
  648.9 153.5 %reduce-scatter.2.cloned.1.call-start = ((), (), s32[]{:S(2)}) async-start(), calls=%async_computation.6 | async-start | bytes 1769472 | tf_op jit(solution)/shard_map/reduce_scatter | solution.py:623
  649.8 23.5 %collective-permute-start.62 = (bf16[256,384]{1,0:T(8,128)(2,1)}, bf16[256,384]{1,0:T(8,128)(2,1)S(1)}, u32[]{:S(2)}, u32[]{:S(2)}) collective-permute-start(bf16[256,384]{1,0:T(8,128)(2,1)} %get-tuple-element.216), channel_id=1, source_target_pairs={{0,8},{8,0},{1,9},{9,1},{2,10},{10,2},{3,11},{11,3},{4,12},{12,4},... | collective-permute-start | bytes 589832 | tf_op jit(solution)/shard_map/ppermute | solution.py:25
  683.8 39.1 %collective-permute-start.49 = (bf16[2,256,384]{2,1,0:T(8,128)(2,1)}, bf16[2,256,384]{2,1,0:T(8,128)(2,1)}, u32[]{:S(2)}, u32[]{:S(2)}) collective-permute-start(bf16[2,256,384]{2,1,0:T(8,128)(2,1)} %fusion.36), channel_id=1, source_target_pairs={{0,4},{4,0},{1,5},{5,1},{2,6},{6,2},{3,7},{7,3},{8,12},{12,8},{9,1... | collective-permute-start | bytes 1179656 | tf_op jit(solution)/shard_map/ppermute | solution.py:25
  696.6 36.5 %collective-permute-start.53 = (bf16[2,256,384]{2,1,0:T(8,128)(2,1)}, bf16[2,256,384]{2,1,0:T(8,128)(2,1)}, u32[]{:S(2)}, u32[]{:S(2)}) collective-permute-start(bf16[2,256,384]{2,1,0:T(8,128)(2,1)} %fusion.37), channel_id=1, source_target_pairs={{0,2},{2,0},{1,3},{3,1},{4,6},{6,4},{5,7},{7,5},{8,10},{10,8},{9,1... | collective-permute-start | bytes 1179656 | tf_op jit(solution)/shard_map/ppermute | solution.py:25
  727.4 47.7 %all-to-all-start.2 = ((bf16[8,128,640]{2,1,0:T(8,128)(2,1)}), bf16[8,128,640]{2,1,0:T(8,128)(2,1)S(1)}, u32[]{:S(2)}, u32[]{:S(2)}) async-start(bf16[8,128,640]{2,1,0:T(8,128)(2,1)} %bitcast.121), calls=%async_computation.3 | async-start | bytes 2621440 | tf_op jit(solution)/shard_map/all_to_all | solution.py:627
  759.0 47.3 %collective-permute-start.75 = (bf16[256,1024]{1,0:T(8,128)(2,1)}, bf16[256,1024]{1,0:T(8,128)(2,1)S(1)}, u32[]{:S(2)}, u32[]{:S(2)}) collective-permute-start(bf16[256,1024]{1,0:T(8,128)(2,1)} %fusion.31), channel_id=1, source_target_pairs={{0,2},{2,0},{1,3},{3,1},{4,6},{6,4},{5,7},{7,5},{8,10},{10,8},{9,1... | collective-permute-start | bytes 1572872 | tf_op jit(solution)/shard_map/ppermute | solution.py:25
  (97 other events, 1171.1 us)
Sparse Core Ops, SparseCore 0:
  723.1 79.2 reduce-scatter.1

commit v2 on v1

v2 whole, which is shorter than its diff:
```python
import functools
import math

import jax
import jax.numpy as jnp
from jax import lax
from jax.experimental import pallas as pl
from jax.experimental.pallas import tpu as pltpu
from jax.sharding import Mesh, PartitionSpec as P

HEAD_SIZE = 64
EPSILON = 1e-06
FLOOR_SCORE = -1e30
VMEM_LIMIT = 60 * 1024 * 1024
DP = ("o", "u", "y")
POOL = ("u", "y", "x", "c")
ORDERS = (("u", "y", "x"), ("y", "x", "u"), ("x", "u", "y"))
TOK = (512, 256, 256)
SECOND = (384, 256, 384)
NOTES = 128
BLK = 256
BF = jnp.bfloat16
F32 = jnp.float32


def after_all(value, *others):
    return lax.optimization_barrier((value,) + others)[0]


def together(values, *others):
    return lax.optimization_barrier((*values, *others))[: len(values)]


def cuts(dim):
    found, a, b = [], 0, 0
    for i, (first, second) in enumerate(zip(TOK, SECOND)):
        found.append((a, a + first, b, b + second, first + (NOTES if i == 2 else 0)))
        a, b = a + first, b + second
    assert a == b == dim
    return found


def swap(value, axis):
    return lax.ppermute(value, axis, [(0, 1), (1, 0)])


def mm(left, right):
    return lax.dot_general(left, right, (((1,), (0,)), ((), ())), preferred_element_type=F32)


def mm_nt(left, right):
    return lax.dot_general(left, right, (((1,), (1,)), ((), ())), preferred_element_type=F32)


def mm_tn(left, right):
    return lax.dot_general(left, right, (((0,), (0,)), ((), ())), preferred_element_type=F32)


def lanes(shape):
    return lax.broadcasted_iota(jnp.int32, shape, 1)


def turn_halves(value):
    first = lanes(value.shape) % HEAD_SIZE < HEAD_SIZE // 2
    half = HEAD_SIZE // 2
    return jnp.where(first, pltpu.roll(value, 128 - half, 1), pltpu.roll(value, half, 1))


def both_halves(value, which):
    low = lanes(value.shape) < HEAD_SIZE
    turned = pltpu.roll(value, HEAD_SIZE, 1)
    return jnp.where(low, value, turned) if which == 0 else jnp.where(low, turned, value)


def stack_heads(pair):
    low = lanes(pair.shape) < HEAD_SIZE
    zero = jnp.zeros_like(pair)
    return jnp.concatenate([jnp.where(low, pair, zero), jnp.where(low, zero, pair)], axis=0)


def join_heads(stacked):
    rows = stacked.shape[0] // 2
    low = lanes((rows, stacked.shape[1])) < HEAD_SIZE
    return jnp.where(low, stacked[:rows], stacked[rows:])


def allowed_keys(start_col, block, width):
    rows = start_col.shape[0]
    cols = lax.broadcasted_iota(jnp.int32, (rows, width), 1)
    row_ids = block * rows + lax.broadcasted_iota(jnp.int32, (rows, width), 0)
    keep = (cols >= start_col) & (cols <= row_ids)
    return jnp.concatenate([keep, keep], axis=0)


def attend_forward_kernel(n_parts, shard, table, offs, t0, t1, t2, t3, *refs):
    parts, refs = refs[:n_parts], refs[n_parts:]
    gain_in, cosine, sine, start, ain_o, wqkv_o, gains_o, q_o, kd_o, vd_o, mix_o, lse_o = refs
    gains_o[...] = gain_in[...]
    base = 0
    for part in parts:
        for b in range(part.shape[0]):
            at = pl.multiple_of(table[base + b] * shard, shard)
            wqkv_o[pl.ds(at, shard), :] = part[b, :shard, :]
            if shard == 128:
                note = part[b, shard:, :].astype(F32)
                for row in range(2):
                    gains_o[row : row + 1, pl.ds(at, 128)] = note[row : row + 1, :128]
        base += part.shape[0]
    gain = gains_o[0:1, :]
    for r, piece in enumerate((t0, t1, t2, t3)):
        at = pl.multiple_of(offs[r], BLK)
        rows = pl.ds(at, BLK)
        value = piece[...].astype(F32)
        factor = lax.rsqrt(jnp.mean(value * value, axis=-1, keepdims=True) + EPSILON)
        normed = (value * factor * gain).astype(BF)
        ain_o[rows, :] = normed
        qkv = mm(normed, wqkv_o[...])
        cos_b, sin_b = cosine[rows, :], sine[rows, :]
        for part in range(3):
            raw = qkv[:, part * 128 : part * 128 + 128]
            turned = (raw * cos_b + turn_halves(raw) * sin_b).astype(BF)
            if part < 2:
                q_o[rows, part * 128 : part * 128 + 128] = turned * 0.125
            else:
                wide = turned.astype(F32)
                for kv in range(2):
                    kd_o[kv, rows, :] = both_halves(wide, kv).astype(BF)
        value_rows = qkv[:, 384:512].astype(BF).astype(F32)
        for kv in range(2):
            vd_o[kv, rows, :] = both_halves(value_rows, kv).astype(BF)
    total = ain_o.shape[0]
    for block in range(total // BLK):
        width = (block + 1) * BLK
        rows = pl.ds(block * BLK, BLK)
        keep = allowed_keys(start[rows, :], block, width)
        logs = jnp.zeros((BLK, 128), F32)
        for kv in range(2):
            query = stack_heads(q_o[rows, kv * 128 : kv * 128 + 128])
            scores = jnp.where(keep, mm_nt(query, kd_o[kv, :width, :]), FLOOR_SCORE)
            top = jnp.max(scores, axis=-1, keepdims=True)
            lifted = jnp.exp(scores - top)
            summed = jnp.sum(lifted, axis=-1, keepdims=True)
            shares = (lifted * (1.0 / summed)).astype(BF)
            mixed = join_heads(mm(shares, vd_o[kv, :width, :]))
            mix_o[rows, kv * 128 : kv * 128 + 128] = mixed.astype(BF)
            log_total = top + jnp.log(summed)
            lane = lanes(logs.shape)
            logs = jnp.where(lane == 2 * kv, log_total[:BLK], logs)
            logs = jnp.where(lane == 2 * kv + 1, log_total[BLK:], logs)
        lse_o[rows, :] = logs


def project_kernel(n_parts, table, offs, mix, *refs):
    parts, (keep_o, send_o, wob) = refs[:n_parts], refs[n_parts:]
    base = 0
    for part in parts:
        shard = part.shape[1]
        for b in range(part.shape[0]):
            wob[pl.ds(pl.multiple_of(table[base + b] * shard, shard), shard), :] = part[b]
        base += part.shape[0]
    for r in range(4):
        rows = pl.ds(pl.multiple_of(offs[r], BLK), BLK)
        part = mm_nt(mix[rows, :], wob[:, :256])
        if r % 2 == 0:
            keep_o[r // 2] = part
        else:
            send_o[r // 2] = part.astype(BF)


def attend_backward_kernel(
    n_blocks, dests, offs, a0, a1, a2, a3, wqkv, wob, q, kd, vd, lse, start, ain, cosine, sine,
    keep_o, send_o, *refs,
):
    wg_o, (aog, mgrad, dqkv, dk, dv, flat) = refs[:n_blocks], refs[n_blocks:]
    total = ain.shape[0]
    for r, piece in enumerate((a0, a1, a2, a3)):
        aog[pl.ds(pl.multiple_of(offs[r], BLK), BLK), :] = piece[...]
    mgrad[...] = mm(aog[...], wob[:, :256]).astype(BF)
    dk[...] = jnp.zeros_like(dk)
    dv[...] = jnp.zeros_like(dv)
    for block in range(total // BLK):
        width = (block + 1) * BLK
        rows = pl.ds(block * BLK, BLK)
        keep = allowed_keys(start[rows, :], block, width)
        logs = lse[rows, :]
        lane = lanes(logs.shape)
        cos_b, sin_b = cosine[rows, :], sine[rows, :]
        for kv in range(2):
            cols = slice(kv * 128, kv * 128 + 128)
            query = stack_heads(q[rows, cols])
            out_grad = stack_heads(mgrad[rows, cols])
            log_total = jnp.concatenate(
                [
                    jnp.sum(jnp.where(lane == 2 * kv + h, logs, 0.0), axis=1, keepdims=True)
                    for h in range(2)
                ],
                axis=0,
            )
            keys = kd[kv, :width, :]
            scores = jnp.where(keep, mm_nt(query, keys), FLOOR_SCORE)
            shares = jnp.exp(scores - log_total)
            share_grad = mm_nt(out_grad, vd[kv, :width, :])
            inner = jnp.sum(shares * share_grad, axis=-1, keepdims=True)
            score_grad = (shares * (share_grad - inner)).astype(BF)
            query_grad = join_heads(mm(score_grad, keys)) * 0.125
            query_grad = query_grad * cos_b - turn_halves(query_grad) * sin_b
            dqkv[rows, cols] = query_grad.astype(BF)
            dk[kv, :width, :] += mm_tn(score_grad, query)
            dv[kv, :width, :] += mm_tn(shares.astype(BF), out_grad)
    joined = []
    for acc in (dk, dv):
        pair = [acc[kv] + pltpu.roll(acc[kv], HEAD_SIZE, 1) for kv in range(2)]
        joined.append(jnp.where(lanes(pair[0].shape) < HEAD_SIZE, pair[0], pair[1]))
    key_grad = joined[0] * cosine[...] - turn_halves(joined[0]) * sine[...]
    dqkv[:, 256:384] = key_grad.astype(BF)
    dqkv[:, 384:512] = joined[1].astype(BF)
    flat[:, :512] = mm_tn(ain[...], dqkv[...]).astype(BF)
    ones = jnp.ones((BLK, 128), BF)
    gain_sum = jnp.zeros((ain.shape[1], 128), F32)
    for r in range(4):
        rows = pl.ds(pl.multiple_of(offs[r], BLK), BLK)
        part = mm_nt(dqkv[rows, :], wqkv[...])
        gain_sum += mm_tn((part * ain[rows, :].astype(F32)).astype(BF), ones)
        if r % 2 == 0:
            keep_o[r // 2] = part
        else:
            send_o[r // 2] = part.astype(BF)
    flat[:, 512:] = gain_sum.astype(BF)
    spread(flat, dests, wg_o)


def spread(flat, dests, outs):
    done = 0
    for out in outs:
        shard = out.shape[1]
        for i in range(out.shape[0]):
            at = pl.multiple_of(dests[done + i] * shard, shard)
            out[i] = flat[pl.ds(at, shard), :]
        done += out.shape[0]


def out_grad_kernel(n_blocks, dests, offs, a0, a1, a2, a3, mix, small, *refs):
    outs, (aog, flat) = refs[:n_blocks], refs[n_blocks:]
    for r, piece in enumerate((a0, a1, a2, a3)):
        aog[pl.ds(pl.multiple_of(offs[r], BLK), BLK), :] = piece[...]
    flat[:, :256] = mm_tn(aog[...], mix[...]).astype(BF)
    flat[:, 256:] = small[...].astype(BF)
    spread(flat, dests, outs)


def route_kernel(
    tok, keep, got, cross, gains, wob, routes, cot, after_o, ma_o, mb_o, mc_o, gates_o
):
    after = tok[...].astype(F32) + (keep[0] + got[0].astype(F32) + cross[...].astype(F32))
    after_o[...] = after
    factor = lax.rsqrt(jnp.mean(after * after, axis=-1, keepdims=True) + EPSILON)
    moe_in = (after * factor * gains[1:2, :]).astype(BF)
    logits = mm(moe_in, wob[:, 256:])
    lane = lanes(logits.shape)
    routed = lane < 0
    for k in range(routes.shape[1]):
        routed = routed | (routes[:, k : k + 1] == lane)
    top = jnp.max(jnp.where(routed, logits, FLOOR_SCORE), axis=1, keepdims=True)
    lifted = jnp.where(routed, jnp.exp(jnp.where(routed, logits - top, 0.0)), 0.0)
    gates = lifted / jnp.sum(lifted, axis=1, keepdims=True)
    gates_o[...] = gates
    high = gates.astype(BF).astype(F32)
    middle = (gates - high).astype(BF).astype(F32)
    low = gates - high - middle
    extra = high + pltpu.roll(middle, 32, 1) + pltpu.roll(low, 64, 1)
    for out, (a, b, c, d, at) in zip((ma_o, mb_o, mc_o), cuts(cot.shape[1])):
        out[:, : b - a] = moe_in[:, a:b]
        out[:, at:] = cot[:, c:d]
    mc_o[:, TOK[2] : TOK[2] + NOTES] = extra.astype(BF)


def place_weights(meta, parts, mat, kinds):
    hidden = mat.shape[1] // len(kinds)
    done = 0
    for part in parts:
        shard = part.shape[2]
        for b in range(part.shape[0]):
            block = done + b
            at = meta[5 + block // 16] + block % 16 // 4 * shard if len(parts) > 1 else block // 4 * shard
            at = pl.multiple_of(at, shard)
            for i, m in enumerate(kinds):
                col = i * hidden + block % 4 * 128
                mat[pl.ds(at, shard), col : col + 128] = part[b, m]
        done += part.shape[0]


def one_hot(rank):
    row_ids = lax.broadcasted_iota(jnp.int32, (BLK, rank.shape[-1]), 0)
    return jnp.where(rank == row_ids, 1.0, 0.0).astype(BF)


def expert_kernel(n_mats, first, meta, *refs):
    refs = list(refs)
    take = lambda n: [refs.pop(0) for _ in range(n)]
    tok_k, tok_c = take(3), take(3)
    (rank,) = take(1)
    mats = take(n_mats)
    prev = [] if first else take(6)
    outs = take(6)
    pick_o, dy_o, pre_o, weighted_o, mat = take(5)
    hidden = mat.shape[1] // 3
    own_expert = meta[0]

    @pl.when(pl.program_id(0) == 0)
    def _():
        place_weights(meta, mats, mat, (0, 1, 2))

    pick = one_hot(rank[0])
    half = pick.shape[1] // 2
    pick_k, pick_c = pick[:, :half], pick[:, half:]
    flat = lambda ref: ref[...].reshape(half, ref.shape[-1])
    spans = cuts(pick_o.shape[1])
    for i, (a, b, c, d, at) in enumerate(spans):
        got = mm(pick_k, flat(tok_k[i])) + mm(pick_c, flat(tok_c[i]))
        pick_o[:, a:b] = got[:, : b - a].astype(BF)
        dy_o[:, c:d] = got[:, at:].astype(BF)
    extra = got[:, TOK[2] : TOK[2] + NOTES]
    lane = lanes(extra.shape)
    mine = (lane % 32 == own_expert) & (lane < 96)
    gate = jnp.sum(jnp.where(mine, extra, 0.0), axis=1, keepdims=True)
    picked, dy = pick_o[...], dy_o[...]
    gate_pre = mm(picked, mat[:, :hidden])
    up_pre = mm(picked, mat[:, hidden : 2 * hidden])
    back = mm(dy, mat[:, 2 * hidden :])
    sigma = 1.0 / (1.0 + jnp.exp(-gate_pre))
    active = gate_pre * sigma
    hid = active * up_pre
    gate_dot = jnp.sum(hid.astype(BF).astype(F32) * back, axis=1, keepdims=True)
    weighted_o[...] = (gate * hid).astype(BF)
    back = back * gate
    pre_o[:, :hidden] = (back * up_pre * sigma * (1.0 + gate_pre * (1.0 - sigma))).astype(BF)
    pre_o[:, hidden:] = (back * active).astype(BF)
    picked_grad = mm_nt(pre_o[...], mat[:, : 2 * hidden]).astype(BF)
    expert_out = mm_nt(weighted_o[...], mat[:, 2 * hidden :]).astype(BF)
    dot_high = gate_dot.astype(BF).astype(F32)
    dot_low = gate_dot - dot_high
    note = jnp.where(lane == own_expert, dot_high, 0.0)
    note = jnp.where(lane == own_expert + 32, dot_low, note).astype(BF)
    for side, chosen in ((1, pick_c), (0, pick_k)):
        for i, (a, b, c, d, _) in enumerate(spans):
            part = [picked_grad[:, a:b]] + ([note] if i == 2 else []) + [expert_out[:, c:d]]
            part = jnp.concatenate(part, axis=1)
            index = i + 3 * side
            summed = mm_tn(chosen, part)
            if not first:
                summed += prev[index][...].reshape(summed.shape).astype(F32)
            outs[index][...] = summed.astype(BF).reshape(outs[index].shape)


def weight_grad_kernel(blocks, meta, picked, dy, pre, weighted, *outs):
    shard = outs[0].shape[2]
    grads = (mm_tn(picked[...], pre[...]).astype(BF), mm_tn(dy[...], weighted[...]).astype(BF))
    hidden = weighted.shape[1]
    for step in range(4):

        @pl.when(pl.program_id(0) == step)
        def _(step=step):
            for b in range(blocks):
                block, n = step * blocks + b, 0
                while block >= outs[n].shape[0]:
                    block -= outs[n].shape[0]
                    n += 1
                rows = slice(b // 4 * shard, b // 4 * shard + shard)
                for m in range(3):
                    col = m % 2 * hidden + b % 4 * 128
                    outs[n][block, m] = grads[m // 2][rows, col : col + 128]


def back_kernel(
    after, ak, ar, bk, br, ck, cr, gains, wob, gates, cot, after_grad_o, aog_o, small_o, block_o
):
    both = lambda a, b: a[...].astype(F32) + b[...].astype(F32)
    sums = [both(ak, ar), both(bk, br), both(ck, cr)]
    spans = cuts(after.shape[1])
    upstream = jnp.concatenate([v[:, : b - a] for v, (a, b, *_) in zip(sums, spans)], axis=1)
    moe_out = jnp.concatenate([v[:, span[4] :] for v, span in zip(sums, spans)], axis=1)
    block_o[...] = (after[...] + moe_out).astype(BF)
    extra = sums[2][:, TOK[2] : TOK[2] + NOTES]
    lane = lanes(extra.shape)
    gate_dot = jnp.where(lane < 32, extra + pltpu.roll(extra, 96, 1), 0.0)
    share = gates[...]
    logit_grad = share * (gate_dot - jnp.sum(share * gate_dot, axis=1, keepdims=True))
    high = logit_grad.astype(BF)
    low = (logit_grad - high.astype(F32)).astype(BF)
    router = wob[:, 256:]
    gain = gains[1:2, :]
    upstream += mm_nt(high, router) + mm_nt(low, router)
    value = after[...]
    factor = lax.rsqrt(jnp.mean(value * value, axis=-1, keepdims=True) + EPSILON)
    normed = value * factor
    moe_in = (normed * gain).astype(BF)
    scaled = upstream * gain
    inward = factor * (scaled - normed * jnp.mean(scaled * normed, axis=-1, keepdims=True))
    after_grad = cot[...].astype(F32) + inward
    after_grad_o[...] = after_grad
    aog_o[...] = after_grad.astype(BF)
    column = jnp.where(lane == 32, 1.0, 0.0).astype(BF)
    small_o[...] = (
        mm_tn(moe_in, high) + mm_tn(moe_in, low) + mm_tn((upstream * normed).astype(BF), column)
    )


def finish_kernel(tok, keep, got, cross, gains, after_grad, out):
    upstream = keep[0] + got[0].astype(F32) + cross[...].astype(F32)
    value = tok[...].astype(F32)
    factor = lax.rsqrt(jnp.mean(value * value, axis=-1, keepdims=True) + EPSILON)
    normed = value * factor
    scaled = upstream * gains[0:1, :]
    inward = factor * (scaled - normed * jnp.mean(scaled * normed, axis=-1, keepdims=True))
    out[...] = after_grad[...] + inward


def spec_of(space):
    return pl.BlockSpec(memory_space=space)


def cost(micros):
    return pl.CostEstimate(flops=1, bytes_accessed=int(micros * 750000), transcendentals=0)


def simple_call(kernel, outs, n_scalar, n_in, micros, scratch=()):
    return pl.pallas_call(
        kernel,
        out_shape=[jax.ShapeDtypeStruct(s, d) for s, d in outs],
        in_specs=[spec_of(pltpu.SMEM)] * n_scalar + [spec_of(pltpu.VMEM)] * n_in,
        out_specs=[spec_of(pltpu.VMEM)] * len(outs),
        scratch_shapes=list(scratch),
        compiler_params=pltpu.CompilerParams(vmem_limit_bytes=VMEM_LIMIT),
        cost_estimate=cost(micros),
    )


def gather_pool(pieces, beside):
    bufs = pieces
    for step in range(4):
        moving = beside(step)(*bufs)
        axes = [(order + ("c",))[step] for order in ORDERS]
        came = together([swap(buf, axis) for buf, axis in zip(bufs, axes)], *moving)
        if step < 3:
            bufs = [jnp.stack([buf, new]) for buf, new in zip(bufs, came)]
    return list(bufs), list(came)


def scatter_pool(kept, other, fill):
    add = lambda a, b: (a.astype(F32) + b.astype(F32)).astype(BF)
    bufs = kept
    for step in range(4):
        moving = fill(step, bufs if step else other)
        if step == 0:
            came = [swap(send, "c") for send in other]
        else:
            axes = [order[3 - step] for order in ORDERS]
            came = [swap(buf[1], axis) for buf, axis in zip(bufs, axes)]
            bufs = [buf[0] for buf in bufs]
        came = together(came, *moving)
        if step < 3:
            bufs = together([add(a, b) for a, b in zip(bufs, came)])
    return list(zip(bufs, came))


def gather_tensor(value):
    cross = swap(value, "x")
    return [value, swap(value, "c"), cross, swap(cross, "c")]


def sum_tensor(keep, send):
    got = swap(send, "c")
    cross = swap((keep[1] + got[1].astype(F32)).astype(BF), "x")
    return got, cross


def pool_spec(order, width):
    shape = tuple(2 if axis == "x" else 1 for axis in reversed(order)) + (BLK, width)

    def index(g, meta):
        place = {"x": 0, "u": g // 2, "y": g % 2}
        return tuple(place[axis] for axis in reversed(order)) + (0, 0)

    return pl.BlockSpec(shape, index)


def local(
    tokens, segments, routes, priority, norm_attn, w_query, w_key, w_value, w_out, norm_moe,
    w_router, w_gate, w_up, w_down, cotangent,
):
    _, rows, dim = tokens.shape
    n_outer = lax.axis_size("o")
    n_dp = 4 * n_outer
    shard = w_query.shape[0]
    length = 4 * rows
    top = routes.shape[2]
    experts = w_gate.shape[0]
    per_device = experts // 16
    capacity = length * top // experts
    hidden = 4 * w_gate.shape[2]
    widths = [at + d - c for _, _, c, d, at in cuts(dim)]
    at_x, at_c = lax.axis_index("x"), lax.axis_index("c")
    at_t = at_x * 2 + at_c
    at_pool = lax.axis_index(POOL)

    at_dp, at_z, at_y = lax.axis_index(DP), lax.axis_index(("o", "u")), lax.axis_index("y")
    steps = lambda n: jnp.arange(n, dtype=jnp.int32)

    tok = tokens[0]
    cot = cotangent[0]
    tok_parts = gather_tensor(tok)
    own_mats = []

    def weight_part(j):
        return jnp.stack([w[j * 16 : (j + 1) * 16] for w in (w_gate, w_up, w_down)], axis=1)

    first_mats = lax.all_to_all(weight_part(0), POOL, 0, 0, tiled=True)

    parts_in = []

    def part_in(*markers):
        if n_outer != 2:
            return ()
        j, i = divmod(len(parts_in), 4)
        parts_in.append(swap(after_all(own_mats[j][4 * i : 4 * i + 4], *markers), "o"))
        return (parts_in[-1],)

    seg = segments[0]
    start = jnp.zeros_like(seg)
    for s in range(1, 5):
        start = jnp.where(seg >= s, jnp.sum((seg < s).astype(jnp.int32)), start)
    place = (jnp.arange(length, dtype=jnp.int32) - start).astype(F32)
    lane = jnp.arange(128, dtype=jnp.int32)
    half = HEAD_SIZE // 2
    inverse = jnp.exp((lane % half).astype(F32) * (-2.0 * math.log(10000.0) / HEAD_SIZE))
    angle = place[:, None] * inverse[None, :]
    cosine = jnp.cos(angle)
    sine = jnp.sin(angle) * jnp.where(lane % HEAD_SIZE < half, -1.0, 1.0)
    start_col = start[:, None]

    notes = jnp.pad(jnp.stack([norm_attn, norm_moe]), ((0, 14), (0, 512 - shard)))
    pack = jnp.concatenate([w_query, w_key, w_value], axis=1)
    pack_b = jnp.concatenate([w_out, w_router, jnp.zeros((shard, 128 - experts), BF)], axis=1)
    if n_dp == 8:
        pack = jnp.concatenate(
            [jnp.concatenate([pack, pack_b], axis=1), jnp.pad(notes, ((0, 0), (0, 384)))], axis=0
        )
        rest = [lax.ppermute(pack, ("o", "u"), [(i, i ^ s) for i in range(4)]) for s in (1, 2, 3)]
        near = jnp.stack([pack, *together(rest, cosine, sine, start_col)])
        wa = [near[:, :, :512]]
        wa.append(swap(wa[0], "y"))
        wb = [near[:, :shard, 512:]]
        wb.append(swap(wb[0], "y"))
        table = jnp.bitwise_xor(at_z, steps(8) % 4) * 2 + jnp.bitwise_xor(at_y, steps(8) // 4)
        gains = jnp.zeros((8, dim), F32)
    else:
        wa = [lax.all_gather(pack, DP, axis=0)]
        wb = [lax.all_gather(pack_b, DP, axis=0)]
        table = steps(n_dp)
        gains = jnp.stack([lax.all_gather(g, DP, axis=0, tiled=True) for g in (norm_attn, norm_moe)])
        gains = jnp.pad(gains.astype(F32), ((0, 6), (0, 0)))

    table = table.astype(jnp.int32)
    next_part = weight_part(1)
    own_mats.append(first_mats)
    *tok_parts, next_part = together((*tok_parts, next_part), *wa, first_mats)
    own_mats.append(lax.all_to_all(next_part, POOL, 0, 0, tiled=True))
    moving = part_in(tok_parts[0])
    plan = after_all(jnp.concatenate([routes[0].T, priority], axis=0), tok_parts[0])
    plan = jnp.stack([plan, swap(plan, "y")])
    offs = (jnp.bitwise_xor(at_t, steps(4)) * rows).astype(jnp.int32)
    heads = w_query.shape[1]
    ain, wqkv, gains, q, kd, vd, mix, lse = simple_call(
        functools.partial(attend_forward_kernel, len(wa), shard),
        [
            ((length, dim), BF),
            ((dim, 512), BF),
            ((8, dim), F32),
            ((length, heads), BF),
            ((2, length, 128), BF),
            ((2, length, 128), BF),
            ((length, heads), BF),
            ((length, 128), F32),
        ],
        2,
        8 + len(wa),
        11,
    )(table, offs, *tok_parts, *wa, gains, cosine, sine, start_col)
    keep, send, wob = simple_call(
        functools.partial(project_kernel, len(wb)),
        [((2, rows, dim), F32), ((2, rows, dim), BF), ((dim, 384), BF)],
        2,
        1 + len(wb),
        4,
    )(table, offs, mix, *wb)
    keep, send, wob = together((keep, send, wob), *moving)
    moving = part_in(send)
    got, cross = sum_tensor(keep, send)
    got, cross, own_mats[1], plan = together((got, cross, own_mats[1], plan), *moving)
    route_col = lax.dynamic_slice_in_dim(routes[0], at_t * rows, rows, 0)
    after, ma, mb, mc, gates = simple_call(
        route_kernel,
        [
            ((rows, dim), F32),
            *[((rows, width), BF) for width in widths],
            ((rows, 128), F32),
        ],
        0,
        8,
        4,
    )(tok, keep, got, cross, gains, wob, route_col, cot)

    own = [j * 16 + at_pool for j in range(per_device)]
    plan = jnp.concatenate([plan, swap(plan, "u")], axis=0)
    hits = jnp.stack([jnp.any(plan[:, :top] == e, axis=1) for e in own], axis=1)
    first = plan[:, top]
    less = (first[:, :, None] < first[:, None, :]).astype(BF)
    rank = jnp.einsum("gjs,gst->gjt", hits.astype(BF), less, preferred_element_type=F32)
    rank = rank.astype(jnp.int32)
    rank = jnp.where(hits & (rank < capacity), rank, -1)
    rank = rank.reshape(4, per_device, 2, 2, rows)
    rank = jnp.where(at_x == 1, rank[:, :, ::-1], rank)
    rank = jnp.where(at_c == 1, rank[:, :, :, ::-1], rank)
    rank = rank.swapaxes(2, 3).reshape(4, per_device, length)

    def beside(step):
        return lambda *markers: sum((part_in(*markers) for _ in range((1, 1, 2, 1)[step])), ()) + (
            (plan, plan, rank)[step : step + 1]
        )

    tok_kept, tok_other = gather_pool([ma, mb, mc], beside)
    if n_outer == 2:
        ready_mats = lambda j: [own_mats[j]] + parts_in[4 * j : 4 * j + 4]
    else:
        all_mats = [lax.all_gather(m, "o", axis=0, tiled=True) for m in own_mats]
        ready_mats = lambda j: [all_mats[j]]
    at_o = lax.axis_index("o")
    bases = [at_o * 4 * shard, (1 - at_o) * 4 * shard] if n_outer == 2 else [0, 0]
    bases = jnp.stack([jnp.int32(base) for base in bases])

    params = dict(compiler_params=pltpu.CompilerParams(vmem_limit_bytes=VMEM_LIMIT))
    tok_specs = [pool_spec(o, w) for o, w in zip(ORDERS, widths)]
    slot_spec = lambda width: pl.BlockSpec((BLK, width), lambda g, meta: (g, 0))
    rank_spec = pl.BlockSpec((1, 1, length), lambda g, meta: (g, 0, 0))
    mat_shape = (n_outer * 16, 3, shard, hidden // 4)
    mat_spec = lambda m: pl.BlockSpec(
        m.shape, lambda g, meta: (0, 0, 0, 0), pipeline_mode=pl.Buffered(1)
    )
    down_spec = lambda m: pl.BlockSpec(
        (m.shape[0], 1) + m.shape[2:], lambda g, meta: (0, 2, 0, 0), pipeline_mode=pl.Buffered(1)
    )
    pool_shapes = [jax.ShapeDtypeStruct((2, 2, 2, rows, w), BF) for w in widths]
    slots = 4 * capacity
    groups = steps(4)
    metas = [jnp.concatenate([e[None], groups, bases]).astype(jnp.int32) for e in own]
    chunk = dim // 4
    full = lambda width: pl.BlockSpec((slots, width), lambda i, meta: (0, 0))
    turned = lambda i, meta: jnp.where(meta[5] == 0, i ^ 2, i) if n_outer == 2 else i
    chunk_spec = pl.BlockSpec((slots, chunk), lambda i, meta: (0, turned(i, meta)))
    grad_shape = lambda n: jax.ShapeDtypeStruct((n,) + mat_shape[1:], BF)
    whole = lambda n: pl.BlockSpec((n,) + mat_shape[1:], lambda i, meta: (0, 0, 0, 0))

    def weight_grads_of(meta, saved):
        counts = [4, 4, 4, 4, 16] if n_outer == 2 else [16 * n_outer]
        return pl.pallas_call(
            functools.partial(weight_grad_kernel, chunk // shard * 4),
            grid_spec=pltpu.PrefetchScalarGridSpec(
                num_scalar_prefetch=1,
                grid=(4,),
                in_specs=[chunk_spec, chunk_spec, full(2 * hidden), full(hidden)],
                out_specs=[whole(n) for n in counts],
            ),
            out_shape=[grad_shape(n) for n in counts],
            cost_estimate=cost(9),
            **params,
        )(meta, *saved)

    prev, weighted, saved = [], [], []
    parts_out = []

    def part_out(sends, *markers):
        if n_outer != 2:
            return ()
        parts_out.append(swap(after_all(sends[len(parts_out) % 4], *markers), "o"))
        return (parts_out[-1],)

    for j in range(per_device):
        if j == 0:
            moving = part_in(*tok_other)
        else:
            prev = together(prev, *moving)
            first_grads = weight_grads_of(after_all(metas[0], prev[0]), saved[0])
            metas[j] = after_all(metas[j], first_grads[0])
            moving = part_out(first_grads[:4], first_grads[0])
            moving += part_out(first_grads[:4], first_grads[0])
        result = pl.pallas_call(
            functools.partial(expert_kernel, len(ready_mats(j)), j == 0),
            grid_spec=pltpu.PrefetchScalarGridSpec(
                num_scalar_prefetch=1,
                grid=(4,),
                in_specs=tok_specs * 2
                + [rank_spec]
                + [mat_spec(m) for m in ready_mats(j)]
                + (tok_specs * 2 if prev else []),
                out_specs=tok_specs * 2
                + [slot_spec(dim), slot_spec(dim), slot_spec(2 * hidden), slot_spec(hidden)],
                scratch_shapes=[pltpu.VMEM((dim, 3 * hidden), BF)],
            ),
            out_shape=pool_shapes * 2
            + [jax.ShapeDtypeStruct((slots, w), BF) for w in (dim, dim, 2 * hidden, hidden)],
            cost_estimate=cost(29),
            **params,
        )(
            metas[j], *tok_kept, *tok_other, rank[:, j : j + 1], *ready_mats(j), *prev,
        )
        prev = result[:6]
        weighted.append(result[9])
        saved.append(result[6:10])

    prev = together(prev, *moving)
    last_grads = []

    moved = []

    def total(mine, parts):
        return (mine.astype(F32) + jnp.concatenate(parts, axis=0).astype(F32)).astype(BF)

    def fill(step, bufs):
        if step == 0:
            last_grads.extend(weight_grads_of(after_all(metas[1], prev[0]), saved[1]))
            return part_out(first_grads[:4], *bufs) + (last_grads[0],)
        if step == 2 and n_outer == 2:
            value = total(first_grads[4], parts_out[:4])
            moved.append(lax.all_to_all(after_all(value, *bufs), POOL, 0, 0, tiled=True))
        moving = part_out((first_grads if len(parts_out) < 4 else last_grads)[:4], *bufs)
        return moving + (part_out(last_grads[:4], *bufs) if step == 1 else ())

    pairs = scatter_pool(prev[:3], prev[3:], fill)

    after_grad, aog, small, block_out = simple_call(
        back_kernel,
        [((rows, dim), F32), ((rows, dim), BF), ((dim, 128), F32), ((rows, dim), BF)],
        0,
        11,
        5,
    )(after, *pairs[0], *pairs[1], *pairs[2], gains, wob, gates, cot)
    near, cross = swap(aog, "c"), swap(aog, "x")
    moving = part_out(last_grads[:4], aog)
    near, cross = together((near, cross), *moving)
    aog_parts = [aog, near, cross, swap(cross, "c")]

    n_tails = 2 if n_dp == 8 else 1
    dests = jnp.bitwise_xor(at_z, steps(8) % 4) * 2 + jnp.bitwise_xor(at_y, steps(8) // 4)
    dests = (dests if n_dp == 8 else steps(n_dp)).astype(jnp.int32)
    tail_shape = lambda width: [((n_dp // n_tails, shard, width), BF)] * n_tails
    sides = simple_call(
        functools.partial(out_grad_kernel, n_tails),
        tail_shape(384),
        2,
        6,
        2,
        scratch=[pltpu.VMEM((length, dim), BF), pltpu.VMEM((dim, 384), BF)],
    )(dests, offs, *aog_parts, mix, small)

    aog_parts = together(aog_parts, *sides)
    if n_outer == 2:
        last_sum = after_all(total(last_grads[4], parts_out[4:]), *aog_parts)
    else:
        first_sum, last_sum = (
            lax.psum_scatter(g[0], "o", scatter_dimension=0, tiled=True)
            for g in (first_grads, last_grads)
        )
        moved.append(lax.all_to_all(first_sum, POOL, 0, 0, tiled=True))
    moved.append(lax.all_to_all(last_sum, POOL, 0, 0, tiled=True))
    sides = list(sides)
    if n_tails == 2:
        sides[1] = swap(sides[1], "y")
    keep, send, *tails = simple_call(
        functools.partial(attend_backward_kernel, n_tails),
        [((2, rows, dim), F32), ((2, rows, dim), BF)] + tail_shape(640),
        2,
        14,
        60,
        scratch=[
            pltpu.VMEM((length, dim), BF),
            pltpu.VMEM((length, heads), BF),
            pltpu.VMEM((length, 512), BF),
            pltpu.VMEM((2, length, 128), F32),
            pltpu.VMEM((2, length, 128), F32),
            pltpu.VMEM((dim, 640), BF),
        ],
    )(dests, offs, *aog_parts, wqkv, wob, q, kd, vd, lse, start_col, ain, cosine, sine)
    keep, send, *tails = together((keep, send, *tails), *sides)

    got = swap(send, "c")
    tails = list(tails)
    if n_tails == 2:
        tails[1] = swap(tails[1], "y")
    got, *tails = together((got, *tails))
    cross = swap((keep[1] + got[1].astype(F32)).astype(BF), "x")
    if n_tails == 2:
        ends = [
            jnp.concatenate([sum(p[s].astype(F32) for p in part) for part in (sides, tails)], axis=1)
            for s in range(4)
        ]
        for s in range(1, 4):
            perm = [(i, i ^ s) for i in range(4)]
            ends[s] = lax.ppermute(ends[s].astype(BF), ("o", "u"), perm).astype(F32)
        ends = sum(ends)
    else:
        ends = jnp.concatenate([sides[0], tails[0]], axis=2).astype(F32).reshape(dim, 1024)
        ends = lax.psum_scatter(ends, DP, scatter_dimension=0, tiled=True)
    side, tail = ends[:, :384], ends[:, 384:]
    tokens_grad = simple_call(finish_kernel, [((rows, dim), F32)], 0, 6, 4)(
        tok, keep, got, cross, gains, after_grad
    )[0]

    narrow = jnp.concatenate([side[:, 256 : 256 + experts + 1], tail[:, 512:513]], axis=1)
    narrow = narrow + swap(narrow, "x")
    narrow = narrow + swap(narrow, "c")
    gate_grad, up_grad, down_grad = (
        jnp.concatenate([part[:, m] for part in moved], axis=0).astype(F32) for m in range(3)
    )
    return (
        block_out[None],
        tokens_grad[None],
        narrow[:, experts + 1] / norm_attn.astype(F32),
        tail[:, :256],
        tail[:, 256:384],
        tail[:, 384:512],
        side[:, :256],
        narrow[:, experts],
        narrow[:, :experts],
        gate_grad,
        up_grad,
        down_grad,
    )


def solution(mesh):
    devices = mesh.devices
    fine = Mesh(devices.reshape(devices.shape[0] // 4, 2, 2, 2, 2), ("o", "u", "y", "x", "c"))
    dp, tensor = DP, ("x", "c")
    in_specs = (
        P(dp, tensor, None),
        P(dp, None),
        P(dp, None, None),
        P(dp, None),
        P(dp),
        P(dp, tensor),
        P(dp, tensor),
        P(dp, tensor),
        P(dp, tensor),
        P(dp),
        P(dp, None),
        P(None, dp, tensor),
        P(None, dp, tensor),
        P(None, dp, tensor),
        P(dp, tensor, None),
    )
    out_specs = (
        P(dp, tensor, None),
        P(dp, tensor, None),
        P(dp),
        P(dp, tensor),
        P(dp, tensor),
        P(dp, tensor),
        P(dp, tensor),
        P(dp),
        P(dp, None),
        P(None, dp, tensor),
        P(None, dp, tensor),
        P(None, dp, tensor),
    )
    return jax.shard_map(local, mesh=fine, in_specs=in_specs, out_specs=out_specs, check_vma=False)
```

time: 828 us -> 617 us (0.75)
  waiting for transfers between devices: 432 us -> 304 us
  starting transfers between devices: 129 us -> 82 us
  other arithmetic: 85.3 us -> 60.7 us
  local copies, waits for them, and re-layouts: 43.5 us -> 29.2 us
  Pallas kernels: 114 us -> 128 us
  between operations: 15.6 us -> 2.37 us
    ppermute x66 -> x58, waiting for transfers between devices: 348 us -> 270 us  [swap(): return lax.ppermute(value, axis, [(0, 1), (1, 0)])]
    ppermute x66 -> x58, starting transfers between devices: 82.7 us -> 55.1 us  [swap(): return lax.ppermute(value, axis, [(0, 1), (1, 0)])]
    reduce_scatter x1 -> x0, waiting for transfers between devices: 27 us -> none  [local(): lax.psum_scatter(jnp.concatenate([og, small], axis=1), DP, scatter_dimens...]
    another operation x31 -> x14, other arithmetic: 40.8 us -> 18.7 us  [the longest x9 15.9 us: gather_pool(): bufs = [jnp.stack([buf, new]) for buf, new in zip(bufs, came)]]
    convert_element_type x2 -> x12, other arithmetic: 4.93 us -> 20 us  [the longest x9 13.5 us: scatter_pool(): add = lambda a, b: (a.astype(F32) + b.astype(F32)).astype(BF)]
    pallas_call x6 -> x10, Pallas kernels: 109 us -> 123 us  [the longest x2 54.6 us: local(): pl.pallas_call(functools.partial(expert_kernel, len(ready_mats(j)), j ==...]
    all_to_all x5 -> x4, waiting for transfers between devices: 13.6 us -> 0.01 us  [the longest x1 0.01 us: local(): first_mats = lax.all_to_all(weight_part(0), POOL, 0, 0, tiled=True)]
    ppermute x14 -> x6, starting transfers between devices: 22.4 us -> 8.81 us  [the longest x3 4.58 us: local(): lax.ppermute(pack, ('o', 'u'), [(i, i ^ s) for i in range(4)])]
  transfers between devices with their start and end apart: 86 -> 68, of which waited for: 28 -> 31; matrix products, arithmetic and copies ran while one was open for 14% -> 10% of each run, Pallas kernels for 10% -> 19%
where the time goes in v2:
time: 617 us; the launch traced here: 610 us
  waiting for transfers between devices  304 us (49%)
  Pallas kernels  128 us (21%)
  starting transfers between devices  82 us (13%)
  other arithmetic  60.7 us (10%)
  local copies, waits for them, and re-layouts  29.2 us (5%)
    ppermute x58, waiting for transfers between devices, swap(): return lax.ppermute(value, axis, [(0, 1), (1, 0)])  270 us
    ppermute x58, starting transfers between devices, swap(): return lax.ppermute(value, axis, [(0, 1), (1, 0)])  55.1 us
    pallas_call x2, Pallas kernels, local(): pl.pallas_call(functools.partial(expert_kernel, len(ready_mats(j)), j ==...  54.6 us
    ppermute x3, waiting for transfers between devices, local(): lax.ppermute(pack, ('o', 'u'), [(i, i ^ s) for i in range(4)])  23.2 us
    pallas_call x1, Pallas kernels, local(): simple_call(functools.partial(attend_backward_kernel, n_tails), [((2, row...  22.3 us
    pallas_call x2, Pallas kernels, weight_grads_of(): pl.pallas_call(functools.partial(weight_grad_kernel, chunk // shard * 4),...  18.7 us
    another operation x9, other arithmetic, gather_pool(): bufs = [jnp.stack([buf, new]) for buf, new in zip(bufs, came)]  15.9 us
    convert_element_type x9, other arithmetic, scatter_pool(): add = lambda a, b: (a.astype(F32) + b.astype(F32)).astype(BF)  13.5 us
  transfers between devices with their start and end apart: 68, of which 31 were waited for; matrix products, arithmetic and copies ran while one was open for 10% of the time, Pallas kernels for 19%

profile of v2, /device:TPU:0, one launch (start us, length us, event | category | flops | bytes accessed | tf_op | source)
XLA Modules:
  0.0 610.1 jit_solution(5755347633156829287)
XLA Ops:
  5.4 6.4 %all-to-all-start = ((bf16[16,3,128,128]{3,2,1,0:T(8,128)(2,1)}), bf16[16,3,128,128]{3,2,1,0:T(8,128)(2,1)S(1)}, u32[]{:S(2)}, u32[]{:S(2)}) async-start(bf16[16,3,128,128]{3,2,1,0:T(8,128)(2,1)} %pad_maximum_fusion.5), calls=%async_computation | async-start | bytes 3145728 | tf_op jit(solution)/shard_map/all_to_all | solution.py:517
  24.6 3.1 fusion.13
  27.7 8.2 %collective-permute-done.4 = bf16[144,896]{1,0:T(8,128)(2,1)S(1)} collective-permute-done((bf16[144,896]{1,0:T(8,128)(2,1)S(1)}, bf16[144,896]{1,0:T(8,128)(2,1)S(1)}, u32[]{:S(2)}, u32[]{:S(2)}) %collective-permute-start.4) | collective-permute-done | bytes 258080 | tf_op jit(solution)/shard_map/ppermute | solution.py:548
  35.9 7.8 %collective-permute-done.3 = bf16[144,896]{1,0:T(8,128)(2,1)S(1)} collective-permute-done((bf16[144,896]{1,0:T(8,128)(2,1)S(1)}, bf16[144,896]{1,0:T(8,128)(2,1)S(1)}, u32[]{:S(2)}, u32[]{:S(2)}) %collective-permute-start.3) | collective-permute-done | bytes 258080 | tf_op jit(solution)/shard_map/ppermute | solution.py:548
  43.6 7.2 %collective-permute-done.5 = bf16[144,896]{1,0:T(8,128)(2,1)S(1)} collective-permute-done((bf16[144,896]{1,0:T(8,128)(2,1)S(1)}, bf16[144,896]{1,0:T(8,128)(2,1)S(1)}, u32[]{:S(2)}, u32[]{:S(2)}) %collective-permute-start.5) | collective-permute-done | bytes 258080 | tf_op jit(solution)/shard_map/ppermute | solution.py:548
  55.7 11.2 %collective-permute-done.6.refs_1_ = bf16[4,144,512]{2,1,0:T(8,128)(2,1)S(1)} collective-permute-done((bf16[4,144,512]{2,1,0:T(8,128)(2,1)S(1)}, bf16[4,144,512]{2,1,0:T(8,128)(2,1)S(1)}, u32[]{:S(2)}, u32[]{:S(2)}) %collective-permute-start.6) | collective-permute-done | bytes 589856 | tf_op jit(solution)/shard_map/ppermute | solution.py:44
  67.7 3.9 all-to-all-start.1
  79.1 10.9 %shard_map.238 = (bf16[1024,1024]{1,0:T(8,128)(2,1)}, bf16[1024,512]{1,0:T(8,128)(2,1)}, f32[8,1024]{1,0:T(8,128)}, bf16[1024,256]{1,0:T(8,128)(2,1)}, bf16[2,10...) custom-call(s32[8]{0:T(128)} %fusion.41.table.dests, ...), custom_call_target="tpu_custom_call" | custom-call | flops 1 | bytes 8250000 | tf_op jit(solution)/shard_map/pallas_call | solution.py:573
  90.0 7.7 %collective-permute-done.7.refs_1_ = bf16[4,128,384]{2,1,0:T(8,128)(2,1)} collective-permute-done((bf16[4,128,384]{2,1,0:T(8,128)(2,1)}, bf16[4,128,384]{2,1,0:T(8,128)(2,1)}, u32[]{:S(2)}, u32[]{:S(2)}) %collective-permute-start.7) | collective-permute-done | bytes 393248 | tf_op jit(solution)/shard_map/ppermute | solution.py:44
  97.7 3.9 shard_map.239
  107.0 3.6 collective-permute-start.10
  112.0 3.1 collective-permute-done.11
  115.2 16.0 %collective-permute-done.12.refs_9_ = bf16[4,3,128,128]{3,2,1,0:T(8,128)(2,1)} collective-permute-done((bf16[4,3,128,128]{3,2,1,0:T(8,128)(2,1)}, bf16[4,3,128,128]{3,2,1,0:T(8,128)(2,1)}, u32[]{:S(2)}, u32[]{:S(2)}) %collective-permute-start.12) | collective-permute-done | bytes 393248 | tf_op jit(solution)/shard_map/ppermute | solution.py:44
  131.2 5.2 shard_map.240
  139.0 20.4 %collective-permute-done.17 = s32[2,9,1024]{2,1,0:T(8,128)S(1)} collective-permute-done((s32[2,9,1024]{2,1,0:T(8,128)S(1)}, s32[2,9,1024]{2,1,0:T(8,128)S(1)}, u32[]{:S(2)}, u32[]{:S(2)}) %collective-permute-start.17) | collective-permute-done | bytes 73760 | tf_op jit(solution)/shard_map/ppermute | solution.py:44
  166.0 20.6 %collective-permute-done.21.refs_11_ = bf16[4,3,128,128]{3,2,1,0:T(8,128)(2,1)S(1)} collective-permute-done((bf16[4,3,128,128]{3,2,1,0:T(8,128)(2,1)S(1)}, bf16[4,3,128,128]{3,2,1,0:T(8,128)(2,1)S(1)}, u32[]{:S(2)}, u32[]{:S(2)}) %collective-permute-start.21) | collective-permute-done | bytes 393248 | tf_op jit(solution)/shard_map/ppermute | solution.py:44
  200.9 2.9 and_select_fusion
  207.2 24.6 %collective-permute-done.25.refs_8_ = bf16[4,3,128,128]{3,2,1,0:T(8,128)(2,1)S(1)} collective-permute-done((bf16[4,3,128,128]{3,2,1,0:T(8,128)(2,1)S(1)}, bf16[4,3,128,128]{3,2,1,0:T(8,128)(2,1)S(1)}, u32[]{:S(2)}, u32[]{:S(2)}) %collective-permute-start.25) | collective-permute-done | bytes 393248 | tf_op jit(solution)/shard_map/ppermute | solution.py:44
  231.8 7.1 %collective-permute-done.26.refs_9_ = bf16[4,3,128,128]{3,2,1,0:T(8,128)(2,1)S(1)} collective-permute-done((bf16[4,3,128,128]{3,2,1,0:T(8,128)(2,1)S(1)}, bf16[4,3,128,128]{3,2,1,0:T(8,128)(2,1)S(1)}, u32[]{:S(2)}, u32[]{:S(2)}) %collective-permute-start.26) | collective-permute-done | bytes 393248 | tf_op jit(solution)/shard_map/ppermute | solution.py:44
  241.0 3.0 pad_maximum_fusion.1.refs_2_
  248.1 19.2 %collective-permute-done.30.refs_10_ = bf16[4,3,128,128]{3,2,1,0:T(8,128)(2,1)S(1)} collective-permute-done((bf16[4,3,128,128]{3,2,1,0:T(8,128)(2,1)S(1)}, bf16[4,3,128,128]{3,2,1,0:T(8,128)(2,1)S(1)}, u32[]{:S(2)}, u32[]{:S(2)}) %collective-permute-start.30) | collective-permute-done | bytes 393248 | tf_op jit(solution)/shard_map/ppermute | solution.py:44
  272.2 26.0 %shard_map.241 = (bf16[2,2,2,256,896]{4,3,2,1,0:T(8,128)(2,1)}, bf16[2,2,2,256,512]{4,3,2,1,0:T(8,128)(2,1)}, bf16[2,2,2,256,768]{4,3,2,1,0:T(8,128)(2,1)}, bf16...) custom-call(s32[7]{0:T(128)} %get-tuple-element.215.meta, ...), custom_call_target="tpu_custom_call" | custom-call | flops 1 | bytes 21750000 | tf_op jit(solution)/shard_map/pallas_call | solution.py:696
  298.2 9.2 %shard_map.242 = (bf16[4,3,128,128]{3,2,1,0:T(8,128)(2,1)}, bf16[4,3,128,128]{3,2,1,0:T(8,128)(2,1)}, bf16[4,3,128,128]{3,2,1,0:T(8,128)(2,1)}, bf16[4,3,128,128...) custom-call(s32[7]{0:T(128)} %get-tuple-element.215.meta, bf16[1024,1024]{1,0:T(8,128)(2,1)} %get-tuple-element.216.picked, ...), custom_call_target="tpu_custom_call" | custom-call | flops 1 | bytes 6750000 | tf_op jit(solution)/shard_map/pallas_call | solution.py:665
  307.4 2.9 collective-permute-start.32
  310.4 28.6 %shard_map.243 = (bf16[2,2,2,256,896]{4,3,2,1,0:T(8,128)(2,1)}, bf16[2,2,2,256,512]{4,3,2,1,0:T(8,128)(2,1)}, bf16[2,2,2,256,768]{4,3,2,1,0:T(8,128)(2,1)}, bf16...) custom-call(s32[7]{0:T(128)} %get-tuple-element.242.meta, ...), custom_call_target="tpu_custom_call" | custom-call | flops 1 | bytes 21750000 | tf_op jit(solution)/shard_map/pallas_call | solution.py:696
  339.0 5.7 collective-permute-done.33
  345.4 9.5 %shard_map.244 = (bf16[4,3,128,128]{3,2,1,0:T(8,128)(2,1)}, bf16[4,3,128,128]{3,2,1,0:T(8,128)(2,1)}, bf16[4,3,128,128]{3,2,1,0:T(8,128)(2,1)}, bf16[4,3,128,128...) custom-call(s32[7]{0:T(128)} %get-tuple-element.242.meta, bf16[1024,1024]{1,0:T(8,128)(2,1)} %get-tuple-element.243.picked, ...), custom_call_target="tpu_custom_call" | custom-call | flops 1 | bytes 6750000 | tf_op jit(solution)/shard_map/pallas_call | solution.py:665
  354.9 9.0 %collective-permute-done.37 = bf16[4,3,128,128]{3,2,1,0:T(8,128)(2,1)S(1)} collective-permute-done((bf16[4,3,128,128]{3,2,1,0:T(8,128)(2,1)}, bf16[4,3,128,128]{3,2,1,0:T(8,128)(2,1)S(1)}, u32[]{:S(2)}, u32[]{:S(2)}) %collective-permute-start.37) | collective-permute-done | bytes 393248 | tf_op jit(solution)/shard_map/ppermute | solution.py:44
  363.9 3.1 add_convert_fusion
  374.8 3.2 collective-permute-start.41
  378.1 28.7 %collective-permute-done.41 = bf16[4,3,128,128]{3,2,1,0:T(8,128)(2,1)S(1)} collective-permute-done((bf16[4,3,128,128]{3,2,1,0:T(8,128)(2,1)S(1)}, bf16[4,3,128,128]{3,2,1,0:T(8,128)(2,1)S(1)}, u32[]{:S(2)}, u32[]{:S(2)}) %collective-permute-start.41) | collective-permute-done | bytes 393248 | tf_op jit(solution)/shard_map/ppermute | solution.py:44
  406.8 7.2 %collective-permute-done.42 = bf16[4,3,128,128]{3,2,1,0:T(8,128)(2,1)S(1)} collective-permute-done((bf16[4,3,128,128]{3,2,1,0:T(8,128)(2,1)S(1)}, bf16[4,3,128,128]{3,2,1,0:T(8,128)(2,1)S(1)}, u32[]{:S(2)}, u32[]{:S(2)}) %collective-permute-start.42) | collective-permute-done | bytes 393248 | tf_op jit(solution)/shard_map/ppermute | solution.py:44
  426.8 3.9 all-to-all-start.2
  430.8 18.4 %collective-permute-done.46 = bf16[4,3,128,128]{3,2,1,0:T(8,128)(2,1)} collective-permute-done((bf16[4,3,128,128]{3,2,1,0:T(8,128)(2,1)}, bf16[4,3,128,128]{3,2,1,0:T(8,128)(2,1)}, u32[]{:S(2)}, u32[]{:S(2)}) %collective-permute-start.46) | collective-permute-done | bytes 393248 | tf_op jit(solution)/shard_map/ppermute | solution.py:44
  460.6 9.1 %collective-permute-done.48.br = bf16[256,512]{1,0:T(8,128)(2,1)S(1)} collective-permute-done((bf16[256,512]{1,0:T(8,128)(2,1)S(1)}, bf16[256,512]{1,0:T(8,128)(2,1)S(1)}, u32[]{:S(2)}, u32[]{:S(2)}) %collective-permute-start.48) | collective-permute-done | bytes 262176 | tf_op jit(solution)/shard_map/ppermute | solution.py:44
  469.8 4.6 collective-permute-done.50
  474.3 8.6 %collective-permute-done.47.ar = bf16[256,896]{1,0:T(8,128)(2,1)S(1)} collective-permute-done((bf16[256,896]{1,0:T(8,128)(2,1)S(1)}, bf16[256,896]{1,0:T(8,128)(2,1)S(1)}, u32[]{:S(2)}, u32[]{:S(2)}) %collective-permute-start.47) | collective-permute-done | bytes 458784 | tf_op jit(solution)/shard_map/ppermute | solution.py:44
  483.7 5.1 shard_map.245
  490.6 19.5 %collective-permute-done.53 = bf16[4,3,128,128]{3,2,1,0:T(8,128)(2,1)S(1)} collective-permute-done((bf16[4,3,128,128]{3,2,1,0:T(8,128)(2,1)S(1)}, bf16[4,3,128,128]{3,2,1,0:T(8,128)(2,1)S(1)}, u32[]{:S(2)}, u32[]{:S(2)}) %collective-permute-start.53) | collective-permute-done | bytes 393248 | tf_op jit(solution)/shard_map/ppermute | solution.py:44
  513.6 3.7 shard_map.246
  517.5 22.3 %shard_map.247 = (f32[2,256,1024]{2,1,0:T(8,128)}, bf16[2,256,1024]{2,1,0:T(8,128)(2,1)}, bf16[4,128,640]{2,1,0:T(8,128)(2,1)}, bf16[4,128,640]{2,1,0:T(8,128)(2,1)}) custom-call(s32[8]{0:T(128)} %fusion.41.table.dests, s32[4]{0:T(128)} %xor_multiply_fusion.offs, bf16[256,1024]{1,0:T(8,128)(2,1)} %get-tuple-element.288.a0, bf16[256,1024]{1,0:T(8,128)(2,1)} %copy-done.21, ...), custom_call_target="tpu_custom_call" | custom-call | flops 1 | bytes 45000000 | tf_op jit(solution)/shard_map/pallas_call | solution.py:778
  544.5 3.8 all-to-all-start.3
  550.8 17.5 %collective-permute-done.57 = bf16[4,128,640]{2,1,0:T(8,128)(2,1)} collective-permute-done((bf16[4,128,640]{2,1,0:T(8,128)(2,1)}, bf16[4,128,640]{2,1,0:T(8,128)(2,1)}, u32[]{:S(2)}, u32[]{:S(2)}) %collective-permute-start.57) | collective-permute-done | bytes 655392 | tf_op jit(solution)/shard_map/ppermute | solution.py:44
  569.7 3.5 collective-permute-start.61
  575.9 3.3 collective-permute-start.58
  579.2 9.8 %collective-permute-done.60 = bf16[128,1024]{1,0:T(8,128)(2,1)S(1)} collective-permute-done((bf16[128,1024]{1,0:T(8,128)(2,1)S(1)}, bf16[128,1024]{1,0:T(8,128)(2,1)S(1)}, u32[]{:S(2)}, u32[]{:S(2)}) %collective-permute-start.60) | collective-permute-done | bytes 262176 | tf_op jit(solution)/shard_map/ppermute | solution.py:808
  590.8 3.9 collective-permute-start.62
  600.2 4.0 shard_map.248
  (370 shorter events, 137.6 us)
Async XLA Ops:
  5.4 61.5 %all-to-all-start = ((bf16[16,3,128,128]{3,2,1,0:T(8,128)(2,1)}), bf16[16,3,128,128]{3,2,1,0:T(8,128)(2,1)S(1)}, u32[]{:S(2)}, u32[]{:S(2)}) async-start(bf16[16,3,128,128]{3,2,1,0:T(8,128)(2,1)} %pad_maximum_fusion.5), calls=%async_computation | async-start | bytes 3145728 | tf_op jit(solution)/shard_map/all_to_all | solution.py:517
  12.3 23.6 %collective-permute-start.4 = (bf16[144,896]{1,0:T(8,128)(2,1)S(1)}, bf16[144,896]{1,0:T(8,128)(2,1)S(1)}, u32[]{:S(2)}, u32[]{:S(2)}) collective-permute-start(bf16[144,896]{1,0:T(8,128)(2,1)S(1)} %get-tuple-element.395), channel_id=1, source_target_pairs={{0,16},{8,24},{16,0},{24,8},{1,17},{9,25},{17,1},{25,9},{2,18},{10... | collective-permute-start | bytes 774152 | tf_op jit(solution)/shard_map/ppermute | solution.py:548
  14.9 28.7 %collective-permute-start.3 = (bf16[144,896]{1,0:T(8,128)(2,1)S(1)}, bf16[144,896]{1,0:T(8,128)(2,1)S(1)}, u32[]{:S(2)}, u32[]{:S(2)}) collective-permute-start(bf16[144,896]{1,0:T(8,128)(2,1)S(1)} %get-tuple-element.395), channel_id=1, source_target_pairs={{0,8},{8,0},{16,24},{24,16},{1,9},{9,1},{17,25},{25,17},{2,10},{10... | collective-permute-start | bytes 774152 | tf_op jit(solution)/shard_map/ppermute | solution.py:548
  16.8 34.0 %collective-permute-start.5 = (bf16[144,896]{1,0:T(8,128)(2,1)S(1)}, bf16[144,896]{1,0:T(8,128)(2,1)S(1)}, u32[]{:S(2)}, u32[]{:S(2)}) collective-permute-start(bf16[144,896]{1,0:T(8,128)(2,1)S(1)} %get-tuple-element.395), channel_id=1, source_target_pairs={{0,24},{8,16},{16,8},{24,0},{1,25},{9,17},{17,9},{25,1},{2,26},{10... | collective-permute-start | bytes 774152 | tf_op jit(solution)/shard_map/ppermute | solution.py:548
  16.8 36.9 %collective-permute-start.1 = (bf16[256,1024]{1,0:T(8,128)(2,1)S(1)}, bf16[256,1024]{1,0:T(8,128)(2,1)S(1)}, u32[]{:S(2)}, u32[]{:S(2)}) collective-permute-start(bf16[256,1024]{1,0:T(8,128)(2,1)S(1)} %bitcast.156), channel_id=1, source_target_pairs={{0,2},{2,0},{1,3},{3,1},{4,6},{6,4},{5,7},{7,5},{8,10},{10,8},{9,1... | collective-permute-start | bytes 1572872 | tf_op jit(solution)/shard_map/ppermute | solution.py:44
  67.7 63.5 %all-to-all-start.1 = ((bf16[16,3,128,128]{3,2,1,0:T(8,128)(2,1)}), bf16[16,3,128,128]{3,2,1,0:T(8,128)(2,1)S(1)}, u32[]{:S(2)}, u32[]{:S(2)}) async-start(bf16[16,3,128,128]{3,2,1,0:T(8,128)(2,1)} %pad_maximum_fusion.4), calls=%async_computation.1 | async-start | bytes 3145728 | tf_op jit(solution)/shard_map/all_to_all | solution.py:567
  73.4 24.3 %collective-permute-start.7 = (bf16[4,128,384]{2,1,0:T(8,128)(2,1)}, bf16[4,128,384]{2,1,0:T(8,128)(2,1)}, u32[]{:S(2)}, u32[]{:S(2)}) collective-permute-start(bf16[4,128,384]{2,1,0:T(8,128)(2,1)} %pad_maximum_fusion.12.refs_0_), channel_id=1, source_target_pairs={{0,4},{4,0},{1,5},{5,1},{2,6},{6,2},{3,7},{7,3},{8,12},{12,8},{9,1... | collective-permute-start | bytes 1179656 | tf_op jit(solution)/shard_map/ppermute | solution.py:44
  76.3 25.4 %collective-permute-start.8 = (bf16[4,3,128,128]{3,2,1,0:T(8,128)(2,1)S(1)}, bf16[4,3,128,128]{3,2,1,0:T(8,128)(2,1)S(1)}, u32[]{:S(2)}, u32[]{:S(2)}) collective-permute-start(bf16[4,3,128,128]{3,2,1,0:T(8,128)(2,1)S(1)} %get-tuple-element.174), channel_id=1, source_target_pairs={{0,16},{16,0},{1,17},{17,1},{2,18},{18,2},{3,19},{19,3},{4,20},{20... | collective-permute-start | bytes 1179656 | tf_op jit(solution)/shard_map/ppermute | solution.py:44
  107.0 24.2 %collective-permute-start.10 = (bf16[256,1024]{1,0:T(8,128)(2,1)S(1)}, bf16[256,1024]{1,0:T(8,128)(2,1)}, u32[]{:S(2)}, u32[]{:S(2)}) collective-permute-start(bf16[256,1024]{1,0:T(8,128)(2,1)S(1)} %fusion.14), channel_id=1, source_target_pairs={{0,2},{2,0},{1,3},{3,1},{4,6},{6,4},{5,7},{7,5},{8,10},{10,8},{9,1... | collective-permute-start | bytes 1572872 | tf_op jit(solution)/shard_map/ppermute | solution.py:44
  136.4 23.0 %collective-permute-start.13 = (bf16[256,896]{1,0:T(8,128)(2,1)}, bf16[256,896]{1,0:T(8,128)(2,1)S(1)}, u32[]{:S(2)}, u32[]{:S(2)}) collective-permute-start(bf16[256,896]{1,0:T(8,128)(2,1)} %get-tuple-element.185), channel_id=1, source_target_pairs={{0,8},{8,0},{1,9},{9,1},{2,10},{10,2},{3,11},{11,3},{4,12},{12,4},... | collective-permute-start | bytes 1376264 | tf_op jit(solution)/shard_map/ppermute | solution.py:44
  136.4 23.0 %collective-permute-start.16 = (bf16[4,3,128,128]{3,2,1,0:T(8,128)(2,1)S(1)}, bf16[4,3,128,128]{3,2,1,0:T(8,128)(2,1)S(1)}, u32[]{:S(2)}, u32[]{:S(2)}) collective-permute-start(bf16[4,3,128,128]{3,2,1,0:T(8,128)(2,1)S(1)} %copy-done.50), channel_id=1, source_target_pairs={{0,16},{16,0},{1,17},{17,1},{2,18},{18,2},{3,19},{19,3},{4,20},{20... | collective-permute-start | bytes 1179656 | tf_op jit(solution)/shard_map/ppermute | solution.py:44
  138.1 21.3 %collective-permute-start.15 = (bf16[256,768]{1,0:T(8,128)(2,1)}, bf16[256,768]{1,0:T(8,128)(2,1)S(1)}, u32[]{:S(2)}, u32[]{:S(2)}) collective-permute-start(bf16[256,768]{1,0:T(8,128)(2,1)} %get-tuple-element.187), channel_id=1, source_target_pairs={{0,2},{2,0},{1,3},{3,1},{4,6},{6,4},{5,7},{7,5},{8,10},{10,8},{9,1... | collective-permute-start | bytes 1179656 | tf_op jit(solution)/shard_map/ppermute | solution.py:44
  138.5 20.9 %collective-permute-start.14 = (bf16[256,512]{1,0:T(8,128)(2,1)}, bf16[256,512]{1,0:T(8,128)(2,1)S(1)}, u32[]{:S(2)}, u32[]{:S(2)}) collective-permute-start(bf16[256,512]{1,0:T(8,128)(2,1)} %get-tuple-element.186), channel_id=1, source_target_pairs={{0,4},{4,0},{1,5},{5,1},{2,6},{6,2},{3,7},{7,3},{8,12},{12,8},{9,1... | collective-permute-start | bytes 786440 | tf_op jit(solution)/shard_map/ppermute | solution.py:44
  161.4 27.3 %collective-permute-start.18 = (bf16[2,256,896]{2,1,0:T(8,128)(2,1)S(1)}, bf16[2,256,896]{2,1,0:T(8,128)(2,1)S(1)}, u32[]{:S(2)}, u32[]{:S(2)}) collective-permute-start(bf16[2,256,896]{2,1,0:T(8,128)(2,1)S(1)} %get-tuple-element.377), channel_id=1, source_target_pairs={{0,4},{4,0},{1,5},{5,1},{2,6},{6,2},{3,7},{7,3},{8,12},{12,8},{9,1... | collective-permute-start | bytes 2752520 | tf_op jit(solution)/shard_map/ppermute | solution.py:44
  161.6 27.1 %collective-permute-start.20 = (bf16[2,256,768]{2,1,0:T(8,128)(2,1)S(1)}, bf16[2,256,768]{2,1,0:T(8,128)(2,1)S(1)}, u32[]{:S(2)}, u32[]{:S(2)}) collective-permute-start(bf16[2,256,768]{2,1,0:T(8,128)(2,1)S(1)} %get-tuple-element.385), channel_id=1, source_target_pairs={{0,8},{8,0},{1,9},{9,1},{2,10},{10,2},{3,11},{11,3},{4,12},{12,4},... | collective-permute-start | bytes 2359304 | tf_op jit(solution)/shard_map/ppermute | solution.py:44
  162.8 23.7 %collective-permute-start.19 = (bf16[2,256,512]{2,1,0:T(8,128)(2,1)S(1)}, bf16[2,256,512]{2,1,0:T(8,128)(2,1)S(1)}, u32[]{:S(2)}, u32[]{:S(2)}) collective-permute-start(bf16[2,256,512]{2,1,0:T(8,128)(2,1)S(1)} %get-tuple-element.393), channel_id=1, source_target_pairs={{0,2},{2,0},{1,3},{3,1},{4,6},{6,4},{5,7},{7,5},{8,10},{10,8},{9,1... | collective-permute-start | bytes 1572872 | tf_op jit(solution)/shard_map/ppermute | solution.py:44
  163.4 23.1 %collective-permute-start.21 = (bf16[4,3,128,128]{3,2,1,0:T(8,128)(2,1)S(1)}, bf16[4,3,128,128]{3,2,1,0:T(8,128)(2,1)S(1)}, u32[]{:S(2)}, u32[]{:S(2)}) collective-permute-start(bf16[4,3,128,128]{3,2,1,0:T(8,128)(2,1)S(1)} %copy-done.49), channel_id=1, source_target_pairs={{0,16},{16,0},{1,17},{17,1},{2,18},{18,2},{3,19},{19,3},{4,20},{20... | collective-permute-start | bytes 1179656 | tf_op jit(solution)/shard_map/ppermute | solution.py:44
  190.3 48.6 %collective-permute-start.22 = (bf16[2,2,256,896]{3,2,1,0:T(8,128)(2,1)}, bf16[2,2,256,896]{3,2,1,0:T(8,128)(2,1)}, u32[]{:S(2)}, u32[]{:S(2)}) collective-permute-start(bf16[2,2,256,896]{3,2,1,0:T(8,128)(2,1)} %get-tuple-element.345), channel_id=1, source_target_pairs={{0,2},{2,0},{1,3},{3,1},{4,6},{6,4},{5,7},{7,5},{8,10},{10,8},{9,1... | collective-permute-start | bytes 5505032 | tf_op jit(solution)/shard_map/ppermute | solution.py:44
  193.1 45.8 %collective-permute-start.24 = (bf16[2,2,256,768]{3,2,1,0:T(8,128)(2,1)}, bf16[2,2,256,768]{3,2,1,0:T(8,128)(2,1)}, u32[]{:S(2)}, u32[]{:S(2)}) collective-permute-start(bf16[2,2,256,768]{3,2,1,0:T(8,128)(2,1)} %get-tuple-element.357), channel_id=1, source_target_pairs={{0,4},{4,0},{1,5},{5,1},{2,6},{6,2},{3,7},{7,3},{8,12},{12,8},{9,1... | collective-permute-start | bytes 4718600 | tf_op jit(solution)/shard_map/ppermute | solution.py:44
  197.5 41.3 %collective-permute-start.23 = (bf16[2,2,256,512]{3,2,1,0:T(8,128)(2,1)}, bf16[2,2,256,512]{3,2,1,0:T(8,128)(2,1)}, u32[]{:S(2)}, u32[]{:S(2)}) collective-permute-start(bf16[2,2,256,512]{3,2,1,0:T(8,128)(2,1)} %get-tuple-element.367), channel_id=1, source_target_pairs={{0,8},{8,0},{1,9},{9,1},{2,10},{10,2},{3,11},{11,3},{4,12},{12,4},... | collective-permute-start | bytes 3145736 | tf_op jit(solution)/shard_map/ppermute | solution.py:44
  204.1 27.7 %collective-permute-start.25 = (bf16[4,3,128,128]{3,2,1,0:T(8,128)(2,1)S(1)}, bf16[4,3,128,128]{3,2,1,0:T(8,128)(2,1)S(1)}, u32[]{:S(2)}, u32[]{:S(2)}) collective-permute-start(bf16[4,3,128,128]{3,2,1,0:T(8,128)(2,1)S(1)} %copy-done.63), channel_id=1, source_target_pairs={{0,16},{16,0},{1,17},{17,1},{2,18},{18,2},{3,19},{19,3},{4,20},{20... | collective-permute-start | bytes 1179656 | tf_op jit(solution)/shard_map/ppermute | solution.py:44
  204.7 34.1 %collective-permute-start.26 = (bf16[4,3,128,128]{3,2,1,0:T(8,128)(2,1)S(1)}, bf16[4,3,128,128]{3,2,1,0:T(8,128)(2,1)S(1)}, u32[]{:S(2)}, u32[]{:S(2)}) collective-permute-start(bf16[4,3,128,128]{3,2,1,0:T(8,128)(2,1)S(1)} %copy-done.61), channel_id=1, source_target_pairs={{0,16},{16,0},{1,17},{17,1},{2,18},{18,2},{3,19},{19,3},{4,20},{20... | collective-permute-start | bytes 1179656 | tf_op jit(solution)/shard_map/ppermute | solution.py:44
  240.9 26.3 %collective-permute-start.27 = (bf16[2,2,2,256,896]{4,3,2,1,0:T(8,128)(2,1)S(1)}, bf16[2,2,2,256,896]{4,3,2,1,0:T(8,128)(2,1)S(1)}, u32[]{:S(2)}, u32[]{:S(2)}) collective-permute-start(bf16[2,2,2,256,896]{4,3,2,1,0:T(8,128)(2,1)S(1)} %pad_maximum_fusion.refs_0_), channel_id=1, source_target_pairs={{0,1},{1,0},{2,3},{3,2},{4,5},{5,4},{6,7},{7,6},{8,9},{9,8},{10,11... | collective-permute-start | bytes 11010056 | tf_op jit(solution)/shard_map/ppermute | solution.py:44
  244.0 23.3 %collective-permute-start.29 = (bf16[2,2,2,256,768]{4,3,2,1,0:T(8,128)(2,1)S(1)}, bf16[2,2,2,256,768]{4,3,2,1,0:T(8,128)(2,1)S(1)}, u32[]{:S(2)}, u32[]{:S(2)}) collective-permute-start(bf16[2,2,2,256,768]{4,3,2,1,0:T(8,128)(2,1)S(1)} %pad_maximum_fusion.1.refs_2_), channel_id=1, source_target_pairs={{0,1},{1,0},{2,3},{3,2},{4,5},{5,4},{6,7},{7,6},{8,9},{9,8},{10,11... | collective-permute-start | bytes 9437192 | tf_op jit(solution)/shard_map/ppermute | solution.py:44
  246.4 20.8 %collective-permute-start.28 = (bf16[2,2,2,256,512]{4,3,2,1,0:T(8,128)(2,1)S(1)}, bf16[2,2,2,256,512]{4,3,2,1,0:T(8,128)(2,1)S(1)}, u32[]{:S(2)}, u32[]{:S(2)}) collective-permute-start(bf16[2,2,2,256,512]{4,3,2,1,0:T(8,128)(2,1)S(1)} %pad_maximum_fusion.2.refs_1_), channel_id=1, source_target_pairs={{0,1},{1,0},{2,3},{3,2},{4,5},{5,4},{6,7},{7,6},{8,9},{9,8},{10,11... | collective-permute-start | bytes 6291464 | tf_op jit(solution)/shard_map/ppermute | solution.py:44
  246.5 20.7 %collective-permute-start.30 = (bf16[4,3,128,128]{3,2,1,0:T(8,128)(2,1)S(1)}, bf16[4,3,128,128]{3,2,1,0:T(8,128)(2,1)S(1)}, u32[]{:S(2)}, u32[]{:S(2)}) collective-permute-start(bf16[4,3,128,128]{3,2,1,0:T(8,128)(2,1)S(1)} %copy-done.58), channel_id=1, source_target_pairs={{0,16},{16,0},{1,17},{17,1},{2,18},{18,2},{3,19},{19,3},{4,20},{20... | collective-permute-start | bytes 1179656 | tf_op jit(solution)/shard_map/ppermute | solution.py:44
  270.9 27.3 %collective-permute-start.31 = (bf16[4,3,128,128]{3,2,1,0:T(8,128)(2,1)S(1)}, bf16[4,3,128,128]{3,2,1,0:T(8,128)(2,1)S(1)}, u32[]{:S(2)}, u32[]{:S(2)}) collective-permute-start(bf16[4,3,128,128]{3,2,1,0:T(8,128)(2,1)S(1)} %copy-done.55), channel_id=1, source_target_pairs={{0,16},{16,0},{1,17},{17,1},{2,18},{18,2},{3,19},{19,3},{4,20},{20... | collective-permute-start | bytes 1179656 | tf_op jit(solution)/shard_map/ppermute | solution.py:44
  307.4 31.6 %collective-permute-start.32 = (bf16[4,3,128,128]{3,2,1,0:T(8,128)(2,1)}, bf16[4,3,128,128]{3,2,1,0:T(8,128)(2,1)S(1)}, u32[]{:S(2)}, u32[]{:S(2)}) collective-permute-start(bf16[4,3,128,128]{3,2,1,0:T(8,128)(2,1)} %get-tuple-element.233), channel_id=1, source_target_pairs={{0,16},{16,0},{1,17},{17,1},{2,18},{18,2},{3,19},{19,3},{4,20},{20... | collective-permute-start | bytes 1179656 | tf_op jit(solution)/shard_map/ppermute | solution.py:44
  310.3 34.4 %collective-permute-start.33 = (bf16[4,3,128,128]{3,2,1,0:T(8,128)(2,1)}, bf16[4,3,128,128]{3,2,1,0:T(8,128)(2,1)S(1)}, u32[]{:S(2)}, u32[]{:S(2)}) collective-permute-start(bf16[4,3,128,128]{3,2,1,0:T(8,128)(2,1)} %get-tuple-element.235), channel_id=1, source_target_pairs={{0,16},{16,0},{1,17},{17,1},{2,18},{18,2},{3,19},{19,3},{4,20},{20... | collective-permute-start | bytes 1179656 | tf_op jit(solution)/shard_map/ppermute | solution.py:44
  372.3 43.9 %collective-permute-start.38 = (bf16[2,2,256,896]{3,2,1,0:T(8,128)(2,1)S(1)}, bf16[2,2,256,896]{3,2,1,0:T(8,128)(2,1)S(1)}, u32[]{:S(2)}, u32[]{:S(2)}) collective-permute-start(bf16[2,2,256,896]{3,2,1,0:T(8,128)(2,1)S(1)} %slice_bitcast_fusion), channel_id=1, source_target_pairs={{0,2},{2,0},{1,3},{3,1},{4,6},{6,4},{5,7},{7,5},{8,10},{10,8},{9,1... | collective-permute-start | bytes 5505032 | tf_op jit(solution)/shard_map/ppermute | solution.py:44
  374.1 42.1 %collective-permute-start.40 = (bf16[2,2,256,768]{3,2,1,0:T(8,128)(2,1)S(1)}, bf16[2,2,256,768]{3,2,1,0:T(8,128)(2,1)S(1)}, u32[]{:S(2)}, u32[]{:S(2)}) collective-permute-start(bf16[2,2,256,768]{3,2,1,0:T(8,128)(2,1)S(1)} %slice_bitcast_fusion.1), channel_id=1, source_target_pairs={{0,4},{4,0},{1,5},{5,1},{2,6},{6,2},{3,7},{7,3},{8,12},{12,8},{9,1... | collective-permute-start | bytes 4718600 | tf_op jit(solution)/shard_map/ppermute | solution.py:44
  374.7 41.5 %collective-permute-start.39 = (bf16[2,2,256,512]{3,2,1,0:T(8,128)(2,1)S(1)}, bf16[2,2,256,512]{3,2,1,0:T(8,128)(2,1)S(1)}, u32[]{:S(2)}, u32[]{:S(2)}) collective-permute-start(bf16[2,2,256,512]{3,2,1,0:T(8,128)(2,1)S(1)} %slice_bitcast_fusion.2), channel_id=1, source_target_pairs={{0,8},{8,0},{1,9},{9,1},{2,10},{10,2},{3,11},{11,3},{4,12},{12,4},... | collective-permute-start | bytes 3145736 | tf_op jit(solution)/shard_map/ppermute | solution.py:44
  374.8 32.0 %collective-permute-start.41 = (bf16[4,3,128,128]{3,2,1,0:T(8,128)(2,1)S(1)}, bf16[4,3,128,128]{3,2,1,0:T(8,128)(2,1)S(1)}, u32[]{:S(2)}, u32[]{:S(2)}) collective-permute-start(bf16[4,3,128,128]{3,2,1,0:T(8,128)(2,1)S(1)} %copy-done.84), channel_id=1, source_target_pairs={{0,16},{16,0},{1,17},{17,1},{2,18},{18,2},{3,19},{19,3},{4,20},{20... | collective-permute-start | bytes 1179656 | tf_op jit(solution)/shard_map/ppermute | solution.py:44
  378.0 36.0 %collective-permute-start.42 = (bf16[4,3,128,128]{3,2,1,0:T(8,128)(2,1)S(1)}, bf16[4,3,128,128]{3,2,1,0:T(8,128)(2,1)S(1)}, u32[]{:S(2)}, u32[]{:S(2)}) collective-permute-start(bf16[4,3,128,128]{3,2,1,0:T(8,128)(2,1)S(1)} %copy-done.85), channel_id=1, source_target_pairs={{0,16},{16,0},{1,17},{17,1},{2,18},{18,2},{3,19},{19,3},{4,20},{20... | collective-permute-start | bytes 1179656 | tf_op jit(solution)/shard_map/ppermute | solution.py:44
  418.5 31.7 %collective-permute-start.43 = (bf16[2,256,896]{2,1,0:T(8,128)(2,1)}, bf16[2,256,896]{2,1,0:T(8,128)(2,1)}, u32[]{:S(2)}, u32[]{:S(2)}) collective-permute-start(bf16[2,256,896]{2,1,0:T(8,128)(2,1)} %slice_bitcast_fusion.3), channel_id=1, source_target_pairs={{0,4},{4,0},{1,5},{5,1},{2,6},{6,2},{3,7},{7,3},{8,12},{12,8},{9,1... | collective-permute-start | bytes 2752520 | tf_op jit(solution)/shard_map/ppermute | solution.py:44
  421.0 29.2 %collective-permute-start.45 = (bf16[2,256,768]{2,1,0:T(8,128)(2,1)}, bf16[2,256,768]{2,1,0:T(8,128)(2,1)}, u32[]{:S(2)}, u32[]{:S(2)}) collective-permute-start(bf16[2,256,768]{2,1,0:T(8,128)(2,1)} %slice_bitcast_fusion.4), channel_id=1, source_target_pairs={{0,8},{8,0},{1,9},{9,1},{2,10},{10,2},{3,11},{11,3},{4,12},{12,4},... | collective-permute-start | bytes 2359304 | tf_op jit(solution)/shard_map/ppermute | solution.py:44
  423.2 25.9 %collective-permute-start.44 = (bf16[2,256,512]{2,1,0:T(8,128)(2,1)}, bf16[2,256,512]{2,1,0:T(8,128)(2,1)}, u32[]{:S(2)}, u32[]{:S(2)}) collective-permute-start(bf16[2,256,512]{2,1,0:T(8,128)(2,1)} %slice_bitcast_fusion.11), channel_id=1, source_target_pairs={{0,2},{2,0},{1,3},{3,1},{4,6},{6,4},{5,7},{7,5},{8,10},{10,8},{9,1... | collective-permute-start | bytes 1572872 | tf_op jit(solution)/shard_map/ppermute | solution.py:44
  423.6 25.5 %collective-permute-start.46 = (bf16[4,3,128,128]{3,2,1,0:T(8,128)(2,1)}, bf16[4,3,128,128]{3,2,1,0:T(8,128)(2,1)}, u32[]{:S(2)}, u32[]{:S(2)}) collective-permute-start(bf16[4,3,128,128]{3,2,1,0:T(8,128)(2,1)} %get-tuple-element.266), channel_id=1, source_target_pairs={{0,16},{16,0},{1,17},{17,1},{2,18},{18,2},{3,19},{19,3},{4,20},{20... | collective-permute-start | bytes 1179656 | tf_op jit(solution)/shard_map/ppermute | solution.py:44
  426.8 117.7 %all-to-all-start.2 = ((bf16[16,3,128,128]{3,2,1,0:T(8,128)(2,1)}), bf16[16,3,128,128]{3,2,1,0:T(8,128)(2,1)S(1)}, u32[]{:S(2)}, u32[]{:S(2)}) async-start(bf16[16,3,128,128]{3,2,1,0:T(8,128)(2,1)} %add_convert_fusion.4), calls=%async_computation.2 | async-start | bytes 3145728 | tf_op jit(solution)/shard_map/all_to_all | solution.py:734
  458.9 24.0 %collective-permute-start.47 = (bf16[256,896]{1,0:T(8,128)(2,1)S(1)}, bf16[256,896]{1,0:T(8,128)(2,1)S(1)}, u32[]{:S(2)}, u32[]{:S(2)}) collective-permute-start(bf16[256,896]{1,0:T(8,128)(2,1)S(1)} %get-tuple-element.374), channel_id=1, source_target_pairs={{0,8},{8,0},{1,9},{9,1},{2,10},{10,2},{3,11},{11,3},{4,12},{12,4},... | collective-permute-start | bytes 1376264 | tf_op jit(solution)/shard_map/ppermute | solution.py:44
  488.7 21.4 %collective-permute-start.52 = (bf16[256,1024]{1,0:T(8,128)(2,1)}, bf16[256,1024]{1,0:T(8,128)(2,1)S(1)}, u32[]{:S(2)}, u32[]{:S(2)}) collective-permute-start(bf16[256,1024]{1,0:T(8,128)(2,1)} %get-tuple-element.288.a0), channel_id=1, source_target_pairs={{0,2},{2,0},{1,3},{3,1},{4,6},{6,4},{5,7},{7,5},{8,10},{10,8},{9,1... | collective-permute-start | bytes 1572872 | tf_op jit(solution)/shard_map/ppermute | solution.py:44
  489.2 21.6 %collective-permute-start.51 = (bf16[256,1024]{1,0:T(8,128)(2,1)}, bf16[256,1024]{1,0:T(8,128)(2,1)S(1)}, u32[]{:S(2)}, u32[]{:S(2)}) collective-permute-start(bf16[256,1024]{1,0:T(8,128)(2,1)} %get-tuple-element.288.a0), channel_id=1, source_target_pairs={{0,1},{1,0},{2,3},{3,2},{4,5},{5,4},{6,7},{7,6},{8,9},{9,8},{10,11... | collective-permute-start | bytes 1572872 | tf_op jit(solution)/shard_map/ppermute | solution.py:44
  489.2 20.9 %collective-permute-start.53 = (bf16[4,3,128,128]{3,2,1,0:T(8,128)(2,1)S(1)}, bf16[4,3,128,128]{3,2,1,0:T(8,128)(2,1)S(1)}, u32[]{:S(2)}, u32[]{:S(2)}) collective-permute-start(bf16[4,3,128,128]{3,2,1,0:T(8,128)(2,1)S(1)} %copy-done.82), channel_id=1, source_target_pairs={{0,16},{16,0},{1,17},{17,1},{2,18},{18,2},{3,19},{19,3},{4,20},{20... | collective-permute-start | bytes 1179656 | tf_op jit(solution)/shard_map/ppermute | solution.py:44
  517.2 22.5 %collective-permute-start.55 = (bf16[4,128,384]{2,1,0:T(8,128)(2,1)}, bf16[4,128,384]{2,1,0:T(8,128)(2,1)}, u32[]{:S(2)}, u32[]{:S(2)}) collective-permute-start(bf16[4,128,384]{2,1,0:T(8,128)(2,1)} %get-tuple-element.287), channel_id=1, source_target_pairs={{0,4},{4,0},{1,5},{5,1},{2,6},{6,2},{3,7},{7,3},{8,12},{12,8},{9,1... | collective-permute-start | bytes 1179656 | tf_op jit(solution)/shard_map/ppermute | solution.py:44
  539.8 28.5 %collective-permute-start.56 = (bf16[2,256,1024]{2,1,0:T(8,128)(2,1)}, bf16[2,256,1024]{2,1,0:T(8,128)(2,1)}, u32[]{:S(2)}, u32[]{:S(2)}) collective-permute-start(bf16[2,256,1024]{2,1,0:T(8,128)(2,1)} %get-tuple-element.303), channel_id=1, source_target_pairs={{0,1},{1,0},{2,3},{3,2},{4,5},{5,4},{6,7},{7,6},{8,9},{9,8},{10,11... | collective-permute-start | bytes 3145736 | tf_op jit(solution)/shard_map/ppermute | solution.py:44
  539.8 28.4 %collective-permute-start.57 = (bf16[4,128,640]{2,1,0:T(8,128)(2,1)}, bf16[4,128,640]{2,1,0:T(8,128)(2,1)}, u32[]{:S(2)}, u32[]{:S(2)}) collective-permute-start(bf16[4,128,640]{2,1,0:T(8,128)(2,1)} %get-tuple-element.305), channel_id=1, source_target_pairs={{0,4},{4,0},{1,5},{5,1},{2,6},{6,2},{3,7},{7,3},{8,12},{12,8},{9,1... | collective-permute-start | bytes 1966088 | tf_op jit(solution)/shard_map/ppermute | solution.py:44
  544.5 59.7 %all-to-all-start.3 = ((bf16[16,3,128,128]{3,2,1,0:T(8,128)(2,1)}), bf16[16,3,128,128]{3,2,1,0:T(8,128)(2,1)S(1)}, u32[]{:S(2)}, u32[]{:S(2)}) async-start(bf16[16,3,128,128]{3,2,1,0:T(8,128)(2,1)} %add_convert_fusion.3), calls=%async_computation.3 | async-start | bytes 3145728 | tf_op jit(solution)/shard_map/all_to_all | solution.py:774
  575.9 23.5 %collective-permute-start.58 = (bf16[256,1024]{1,0:T(8,128)(2,1)}, bf16[256,1024]{1,0:T(8,128)(2,1)S(1)}, u32[]{:S(2)}, u32[]{:S(2)}) collective-permute-start(bf16[256,1024]{1,0:T(8,128)(2,1)} %fusion.15), channel_id=1, source_target_pairs={{0,2},{2,0},{1,3},{3,1},{4,6},{6,4},{5,7},{7,5},{8,10},{10,8},{9,1... | collective-permute-start | bytes 1572872 | tf_op jit(solution)/shard_map/ppermute | solution.py:44
  (106 other events, 1063.4 us)

commit v3 on v2

--- a/solution.py
+++ b/solution.py
@@ -297,11 +297,11 @@
 def expert_kernel(n_mats, first, meta, *refs):
     refs = list(refs)
     take = lambda n: [refs.pop(0) for _ in range(n)]
-    tok_k, tok_c = take(3), take(3)
+    pieces = [take(4) for _ in range(3)]
     (rank,) = take(1)
     mats = take(n_mats)
-    prev = [] if first else take(6)
-    outs = take(6)
+    prev_rank, prev = (None, None) if first else (take(1)[0], take(3))
+    outs = take(3 if first else 6)
     pick_o, dy_o, pre_o, weighted_o, mat = take(5)
     hidden = mat.shape[1] // 3
     own_expert = meta[0]
@@ -313,10 +313,17 @@
     pick = one_hot(rank[0])
     half = pick.shape[1] // 2
     pick_k, pick_c = pick[:, :half], pick[:, half:]
-    flat = lambda ref: ref[...].reshape(half, ref.shape[-1])
+    step = pl.program_id(0)
+
+    def rows_of(i, side):
+        low, high = (ref[...].reshape(-1, ref.shape[-1]) for ref in pieces[i][2 * side : 2 * side + 2])
+        if i == 0:
+            return jnp.concatenate([low, high], axis=0)
+        return jnp.where((step // 2 if i == 1 else step % 2) == 0, low, high)
+
     spans = cuts(pick_o.shape[1])
     for i, (a, b, c, d, at) in enumerate(spans):
-        got = mm(pick_k, flat(tok_k[i])) + mm(pick_c, flat(tok_c[i]))
+        got = mm(pick_k, rows_of(i, 0)) + mm(pick_c, rows_of(i, 1))
         pick_o[:, a:b] = got[:, : b - a].astype(BF)
         dy_o[:, c:d] = got[:, at:].astype(BF)
     extra = got[:, TOK[2] : TOK[2] + NOTES]
@@ -341,15 +348,19 @@
     dot_low = gate_dot - dot_high
     note = jnp.where(lane == own_expert, dot_high, 0.0)
     note = jnp.where(lane == own_expert + 32, dot_low, note).astype(BF)
-    for side, chosen in ((1, pick_c), (0, pick_k)):
-        for i, (a, b, c, d, _) in enumerate(spans):
-            part = [picked_grad[:, a:b]] + ([note] if i == 2 else []) + [expert_out[:, c:d]]
-            part = jnp.concatenate(part, axis=1)
-            index = i + 3 * side
-            summed = mm_tn(chosen, part)
-            if not first:
-                summed += prev[index][...].reshape(summed.shape).astype(F32)
-            outs[index][...] = summed.astype(BF).reshape(outs[index].shape)
+    if not first:
+        pick = jnp.concatenate([one_hot(prev_rank[0]), pick], axis=0)
+    for i, (a, b, c, d, _) in enumerate(spans):
+        part = [picked_grad[:, a:b]] + ([note] if i == 2 else []) + [expert_out[:, c:d]]
+        part = jnp.concatenate(part, axis=1)
+        if first:
+            outs[i][...] = part
+            continue
+        part = jnp.concatenate([prev[i][...], part], axis=0)
+        for side in range(2):
+            summed = mm_tn(pick[:, side * half : side * half + half], part)
+            out = outs[i + 3 * side]
+            out[...] = summed.astype(BF).reshape(out.shape)
 
 
 def weight_grad_kernel(blocks, meta, picked, dy, pre, weighted, *outs):
@@ -435,32 +446,36 @@
     )
 
 
-def gather_pool(pieces, beside):
+def gather_pool(pieces, beside, ready):
     bufs = pieces
-    for step in range(4):
-        moving = beside(step)(*bufs)
-        axes = [(order + ("c",))[step] for order in ORDERS]
-        came = together([swap(buf, axis) for buf, axis in zip(bufs, axes)], *moving)
-        if step < 3:
+    came = (ready,)
+    for step in range(3):
+        moving = beside(step)(*came)
+        came = [swap(buf, order[step]) for buf, order in zip(bufs, ORDERS)]
+        came = together(came, *moving)
+        if step < 2:
             bufs = [jnp.stack([buf, new]) for buf, new in zip(bufs, came)]
-    return list(bufs), list(came)
+    moving = beside(3)(*came)
+    near = [swap(after_all(value, *came), "c") for value in bufs]
+    far = [swap(value, "c") for value in came]
+    values = together((*near, *far), *moving)
+    return list(zip(bufs, came, values[:3], values[3:]))
 
 
 def scatter_pool(kept, other, fill):
     add = lambda a, b: (a.astype(F32) + b.astype(F32)).astype(BF)
-    bufs = kept
-    for step in range(4):
-        moving = fill(step, bufs if step else other)
-        if step == 0:
-            came = [swap(send, "c") for send in other]
-        else:
-            axes = [order[3 - step] for order in ORDERS]
-            came = [swap(buf[1], axis) for buf, axis in zip(bufs, axes)]
-            bufs = [buf[0] for buf in bufs]
-        came = together(came, *moving)
-        if step < 3:
-            bufs = together([add(a, b) for a, b in zip(bufs, came)])
-    return list(zip(bufs, came))
+    moving = fill(0, other)
+    came = together([swap(send, "c") for send in other], *moving)
+    before = list(zip(kept, came))
+    for step in range(1, 4):
+        sends = together([add(a[1], b[1]) for a, b in before])
+        moving = fill(step, came)
+        came = [swap(send, order[3 - step]) for send, order in zip(sends, ORDERS)]
+        flat = together([value for pair in before for value in pair], *sends)
+        keeps = [add(flat[2 * i][0], flat[2 * i + 1][0]) for i in range(3)]
+        values = together((*came, *keeps), *moving)
+        before = list(zip(values[3:], values[:3]))
+    return before
 
 
 def gather_tensor(value):
@@ -474,14 +489,19 @@
     return got, cross
 
 
-def pool_spec(order, width):
-    shape = tuple(2 if axis == "x" else 1 for axis in reversed(order)) + (BLK, width)
-
-    def index(g, meta):
-        place = {"x": 0, "u": g // 2, "y": g % 2}
-        return tuple(place[axis] for axis in reversed(order)) + (0, 0)
-
-    return pl.BlockSpec(shape, index)
+def pool_specs(order, width):
+    def spec(axes, half):
+        shape = tuple(2 if axis == "x" else 1 for axis in reversed(axes)) + (BLK, width)
+
+        def index(g, meta):
+            place = {"x": 0, "u": g // 2, "y": g % 2}
+            if half is not None and order[2] == "u":
+                place["y"] = jnp.where(g // 2 == half, g % 2, 1 - half)
+            return tuple(place[axis] for axis in reversed(axes)) + (0, 0)
+
+        return pl.BlockSpec(shape, index)
+
+    return [spec(order[:2], 0), spec(order[:2], 1)], spec(order, None)
 
 
 def local(
@@ -508,13 +528,11 @@
 
     tok = tokens[0]
     cot = cotangent[0]
-    tok_parts = gather_tensor(tok)
+    tok_near, tok_cross = swap(tok, "c"), swap(tok, "x")
     own_mats = []
 
     def weight_part(j):
         return jnp.stack([w[j * 16 : (j + 1) * 16] for w in (w_gate, w_up, w_down)], axis=1)
-
-    first_mats = lax.all_to_all(weight_part(0), POOL, 0, 0, tiled=True)
 
     parts_in = []
 
@@ -524,6 +542,9 @@
         j, i = divmod(len(parts_in), 4)
         parts_in.append(swap(after_all(own_mats[j][4 * i : 4 * i + 4], *markers), "o"))
         return (parts_in[-1],)
+
+    first_mats = after_all(weight_part(0), tok_near)
+    first_mats = lax.all_to_all(first_mats, POOL, 0, 0, tiled=True)
 
     seg = segments[0]
     start = jnp.zeros_like(seg)
@@ -546,7 +567,10 @@
             [jnp.concatenate([pack, pack_b], axis=1), jnp.pad(notes, ((0, 0), (0, 384)))], axis=0
         )
         rest = [lax.ppermute(pack, ("o", "u"), [(i, i ^ s) for i in range(4)]) for s in (1, 2, 3)]
-        near = jnp.stack([pack, *together(rest, cosine, sine, start_col)])
+        *rest, tok_near, tok_cross = together(
+            (*rest, tok_near, tok_cross), cosine, sine, start_col
+        )
+        near = jnp.stack([pack, *rest])
         wa = [near[:, :, :512]]
         wa.append(swap(wa[0], "y"))
         wb = [near[:, :shard, 512:]]
@@ -561,9 +585,11 @@
         gains = jnp.pad(gains.astype(F32), ((0, 6), (0, 0)))
 
     table = table.astype(jnp.int32)
+    own_mats.append(first_mats)
+    moving = part_in(wa[0])
     next_part = weight_part(1)
-    own_mats.append(first_mats)
-    *tok_parts, next_part = together((*tok_parts, next_part), *wa, first_mats)
+    tok_parts = [tok, tok_near, tok_cross, swap(tok_cross, "c")]
+    *tok_parts, next_part = together((*tok_parts, next_part), *wa, *moving)
     own_mats.append(lax.all_to_all(next_part, POOL, 0, 0, tiled=True))
     moving = part_in(tok_parts[0])
     plan = after_all(jnp.concatenate([routes[0].T, priority], axis=0), tok_parts[0])
@@ -594,9 +620,9 @@
         4,
     )(table, offs, mix, *wb)
     keep, send, wob = together((keep, send, wob), *moving)
-    moving = part_in(send)
+    moving = part_in(mix)
     got, cross = sum_tensor(keep, send)
-    got, cross, own_mats[1], plan = together((got, cross, own_mats[1], plan), *moving)
+    got, cross, plan, own_mats[1] = together((got, cross, plan, own_mats[1]), *moving)
     route_col = lax.dynamic_slice_in_dim(routes[0], at_t * rows, rows, 0)
     after, ma, mb, mc, gates = simple_call(
         route_kernel,
@@ -624,11 +650,11 @@
     rank = rank.swapaxes(2, 3).reshape(4, per_device, length)
 
     def beside(step):
-        return lambda *markers: sum((part_in(*markers) for _ in range((1, 1, 2, 1)[step])), ()) + (
+        return lambda *markers: sum((part_in(*markers) for _ in range((1, 1, 2, 0)[step])), ()) + (
             (plan, plan, rank)[step : step + 1]
         )
 
-    tok_kept, tok_other = gather_pool([ma, mb, mc], beside)
+    pool = [value for piece in gather_pool([ma, mb, mc], beside, cross) for value in piece]
     if n_outer == 2:
         ready_mats = lambda j: [own_mats[j]] + parts_in[4 * j : 4 * j + 4]
     else:
@@ -639,7 +665,9 @@
     bases = jnp.stack([jnp.int32(base) for base in bases])
 
     params = dict(compiler_params=pltpu.CompilerParams(vmem_limit_bytes=VMEM_LIMIT))
-    tok_specs = [pool_spec(o, w) for o, w in zip(ORDERS, widths)]
+    specs = [pool_specs(o, w) for o, w in zip(ORDERS, widths)]
+    tok_specs = [spec for halves, _ in specs for spec in halves * 2]
+    sum_specs = [whole for _, whole in specs]
     slot_spec = lambda width: pl.BlockSpec((BLK, width), lambda g, meta: (g, 0))
     rank_spec = pl.BlockSpec((1, 1, length), lambda g, meta: (g, 0, 0))
     mat_shape = (n_outer * 16, 3, shard, hidden // 4)
@@ -686,7 +714,7 @@
 
     for j in range(per_device):
         if j == 0:
-            moving = part_in(*tok_other)
+            moving = part_in(*pool)
         else:
             prev = together(prev, *moving)
             first_grads = weight_grads_of(after_all(metas[0], prev[0]), saved[0])
@@ -698,24 +726,26 @@
             grid_spec=pltpu.PrefetchScalarGridSpec(
                 num_scalar_prefetch=1,
                 grid=(4,),
-                in_specs=tok_specs * 2
+                in_specs=tok_specs
                 + [rank_spec]
                 + [mat_spec(m) for m in ready_mats(j)]
-                + (tok_specs * 2 if prev else []),
-                out_specs=tok_specs * 2
+                + ([rank_spec] + [slot_spec(w) for w in widths] if j else []),
+                out_specs=(sum_specs * 2 if j else [slot_spec(w) for w in widths])
                 + [slot_spec(dim), slot_spec(dim), slot_spec(2 * hidden), slot_spec(hidden)],
                 scratch_shapes=[pltpu.VMEM((dim, 3 * hidden), BF)],
             ),
-            out_shape=pool_shapes * 2
+            out_shape=(
+                pool_shapes * 2 if j else [jax.ShapeDtypeStruct((slots, w), BF) for w in widths]
+            )
             + [jax.ShapeDtypeStruct((slots, w), BF) for w in (dim, dim, 2 * hidden, hidden)],
             cost_estimate=cost(29),
             **params,
         )(
-            metas[j], *tok_kept, *tok_other, rank[:, j : j + 1], *ready_mats(j), *prev,
+            metas[j], *pool, rank[:, j : j + 1], *ready_mats(j),
+            *([rank[:, :1], *prev] if j else []),
         )
-        prev = result[:6]
-        weighted.append(result[9])
-        saved.append(result[6:10])
+        prev, kept = (result[:6], result[6:]) if j else (result[:3], result[3:])
+        saved.append(kept)
 
     prev = together(prev, *moving)
     last_grads = []
@@ -728,12 +758,10 @@
     def fill(step, bufs):
         if step == 0:
             last_grads.extend(weight_grads_of(after_all(metas[1], prev[0]), saved[1]))
-            return part_out(first_grads[:4], *bufs) + (last_grads[0],)
-        if step == 2 and n_outer == 2:
-            value = total(first_grads[4], parts_out[:4])
-            moved.append(lax.all_to_all(after_all(value, *bufs), POOL, 0, 0, tiled=True))
-        moving = part_out((first_grads if len(parts_out) < 4 else last_grads)[:4], *bufs)
-        return moving + (part_out(last_grads[:4], *bufs) if step == 1 else ())
+            return (*part_out(first_grads[:4], *bufs), last_grads[0])
+        if step == 1:
+            return part_out(first_grads[:4], *bufs) + part_out(last_grads[:4], *bufs)
+        return part_out(last_grads[:4], *bufs) if step == 2 else ()
 
     pairs = scatter_pool(prev[:3], prev[3:], fill)
 
@@ -745,7 +773,7 @@
         5,
     )(after, *pairs[0], *pairs[1], *pairs[2], gains, wob, gates, cot)
     near, cross = swap(aog, "c"), swap(aog, "x")
-    moving = part_out(last_grads[:4], aog)
+    moving = part_out(last_grads[:4], pairs[0][1])
     near, cross = together((near, cross), *moving)
     aog_parts = [aog, near, cross, swap(cross, "c")]
 
@@ -763,15 +791,15 @@
     )(dests, offs, *aog_parts, mix, small)
 
     aog_parts = together(aog_parts, *sides)
+    moving = part_out(last_grads[:4], cross)
     if n_outer == 2:
-        last_sum = after_all(total(last_grads[4], parts_out[4:]), *aog_parts)
+        first_sum = after_all(total(first_grads[4], parts_out[:4]), *aog_parts)
     else:
         first_sum, last_sum = (
             lax.psum_scatter(g[0], "o", scatter_dimension=0, tiled=True)
             for g in (first_grads, last_grads)
         )
-        moved.append(lax.all_to_all(first_sum, POOL, 0, 0, tiled=True))
-    moved.append(lax.all_to_all(last_sum, POOL, 0, 0, tiled=True))
+    moved.append(lax.all_to_all(first_sum, POOL, 0, 0, tiled=True))
     sides = list(sides)
     if n_tails == 2:
         sides[1] = swap(sides[1], "y")
@@ -790,34 +818,40 @@
             pltpu.VMEM((dim, 640), BF),
         ],
     )(dests, offs, *aog_parts, wqkv, wob, q, kd, vd, lse, start_col, ain, cosine, sine)
-    keep, send, *tails = together((keep, send, *tails), *sides)
-
+    keep, send, *tails = together((keep, send, *tails), *sides, *moving)
+
+    if n_outer == 2:
+        last_sum = total(last_grads[4], parts_out[4:])
     got = swap(send, "c")
-    tails = list(tails)
-    if n_tails == 2:
-        tails[1] = swap(tails[1], "y")
-    got, *tails = together((got, *tails))
     cross = swap((keep[1] + got[1].astype(F32)).astype(BF), "x")
     if n_tails == 2:
-        ends = [
-            jnp.concatenate([sum(p[s].astype(F32) for p in part) for part in (sides, tails)], axis=1)
-            for s in range(4)
-        ]
-        for s in range(1, 4):
-            perm = [(i, i ^ s) for i in range(4)]
-            ends[s] = lax.ppermute(ends[s].astype(BF), ("o", "u"), perm).astype(F32)
-        ends = sum(ends)
+        add = lambda a, b: (a.astype(F32) + b.astype(F32)).astype(BF)
+        side_sums = add(*sides)
+        tails[1] = swap(tails[1], "y")
+
+        def reduce_z(sums):
+            return [sums[0]] + [
+                lax.ppermute(sums[s], ("o", "u"), [(i, i ^ s) for i in range(4)]) for s in (1, 2, 3)
+            ]
+
+        side_parts = reduce_z(side_sums)
+        *tails, cross, got, moved[0] = together((*tails, cross, got, moved[0]), *side_parts)
+        tail_parts = reduce_z(add(*tails))
+        side, tail = (sum(p.astype(F32) for p in parts) for parts in (side_parts, tail_parts))
     else:
-        ends = jnp.concatenate([sides[0], tails[0]], axis=2).astype(F32).reshape(dim, 1024)
-        ends = lax.psum_scatter(ends, DP, scatter_dimension=0, tiled=True)
-    side, tail = ends[:, :384], ends[:, 384:]
+        side, tail = (
+            lax.psum_scatter(part[0].astype(F32).reshape(dim, -1), DP, scatter_dimension=0, tiled=True)
+            for part in (sides, tails)
+        )
+    moved.append(lax.all_to_all(after_all(last_sum, *tails), POOL, 0, 0, tiled=True))
     tokens_grad = simple_call(finish_kernel, [((rows, dim), F32)], 0, 6, 4)(
         tok, keep, got, cross, gains, after_grad
     )[0]
 
     narrow = jnp.concatenate([side[:, 256 : 256 + experts + 1], tail[:, 512:513]], axis=1)
-    narrow = narrow + swap(narrow, "x")
-    narrow = narrow + swap(narrow, "c")
+    narrow = narrow + sum(
+        lax.ppermute(narrow, ("x", "c"), [(i, i ^ s) for i in range(4)]) for s in range(1, 4)
+    )
     gate_grad, up_grad, down_grad = (
         jnp.concatenate([part[:, m] for part in moved], axis=0).astype(F32) for m in range(3)
     )

time: 617 us -> 582 us (0.943)
  waiting for transfers between devices: 304 us -> 268 us
  starting transfers between devices: 82 us -> 99.3 us
  other arithmetic: 60.7 us -> 51.2 us
    ppermute x58 -> x59, waiting for transfers between devices: 270 us -> 224 us  [swap(): return lax.ppermute(value, axis, [(0, 1), (1, 0)])]
    ppermute x3 -> x9, waiting for transfers between devices: 11.3 us -> 24.5 us  [the longest x6 22.8 us: reduce_z(): lax.ppermute(sums[s], ('o', 'u'), [(i, i ^ s) for i in range(4)])]
    another operation x9 -> x6, other arithmetic: 15.9 us -> 2.74 us  [gather_pool(): bufs = [jnp.stack([buf, new]) for buf, new in zip(bufs, came)]]
    ppermute x58 -> x59, starting transfers between devices: 55.1 us -> 63.1 us  [swap(): return lax.ppermute(value, axis, [(0, 1), (1, 0)])]
    ppermute x3 -> x9, starting transfers between devices: 4.23 us -> 11.7 us  [the longest x6 9.13 us: reduce_z(): lax.ppermute(sums[s], ('o', 'u'), [(i, i ^ s) for i in range(4)])]
    unnamed x175 -> x155, local copies, waits for them, and re-layouts: 10.5 us -> 13.5 us
    convert_element_type x9 -> x18, other arithmetic: 13.5 us -> 14.9 us  [scatter_pool(): add = lambda a, b: (a.astype(F32) + b.astype(F32)).astype(BF)]
  transfers between devices with their start and end apart: 68 -> 75, of which waited for: 31 -> 30; matrix products, arithmetic and copies ran while one was open for 10% -> 10% of each run, Pallas kernels for 19% -> 18%
where the time goes in v3:
time: 582 us; the launch traced here: 578 us
  waiting for transfers between devices  268 us (46%)
  Pallas kernels  127 us (22%)
  starting transfers between devices  99.3 us (17%)
  other arithmetic  51.2 us (9%)
  local copies, waits for them, and re-layouts  28.4 us (5%)
    ppermute x59, waiting for transfers between devices, swap(): return lax.ppermute(value, axis, [(0, 1), (1, 0)])  224 us
    ppermute x59, starting transfers between devices, swap(): return lax.ppermute(value, axis, [(0, 1), (1, 0)])  63.1 us
    pallas_call x2, Pallas kernels, local(): pl.pallas_call(functools.partial(expert_kernel, len(ready_mats(j)), j ==...  53 us
    ppermute x6, waiting for transfers between devices, reduce_z(): lax.ppermute(sums[s], ('o', 'u'), [(i, i ^ s) for i in range(4)])  22.8 us
    pallas_call x1, Pallas kernels, local(): simple_call(functools.partial(attend_backward_kernel, n_tails), [((2, row...  22 us
    ppermute x3, waiting for transfers between devices, local(): lax.ppermute(pack, ('o', 'u'), [(i, i ^ s) for i in range(4)])  19.5 us
    pallas_call x2, Pallas kernels, weight_grads_of(): pl.pallas_call(functools.partial(weight_grad_kernel, chunk // shard * 4),...  18.9 us
    convert_element_type x18, other arithmetic, scatter_pool(): add = lambda a, b: (a.astype(F32) + b.astype(F32)).astype(BF)  14.9 us
  transfers between devices with their start and end apart: 75, of which 30 were waited for; matrix products, arithmetic and copies ran while one was open for 10% of the time, Pallas kernels for 18%

profile of v3, /device:TPU:0, one launch (start us, length us, event | category | flops | bytes accessed | tf_op | source)
XLA Modules:
  0.0 578.2 jit_solution(15140161289299446813)
XLA Ops:
  5.0 6.4 %all-to-all-start = ((bf16[16,3,128,128]{3,2,1,0:T(8,128)(2,1)}), bf16[16,3,128,128]{3,2,1,0:T(8,128)(2,1)S(1)}, u32[]{:S(2)}, u32[]{:S(2)}) async-start(bf16[16,3,128,128]{3,2,1,0:T(8,128)(2,1)} %pad_maximum_fusion.2), calls=%async_computation | async-start | bytes 3145728 | tf_op jit(solution)/shard_map/all_to_all | solution.py:547
  13.3 4.0 collective-permute-start.2
  23.0 2.6 compare_select_fusion.3
  25.6 3.1 fusion.17
  28.7 11.1 %collective-permute-done.2 = bf16[144,896]{1,0:T(8,128)(2,1)S(1)} collective-permute-done((bf16[144,896]{1,0:T(8,128)(2,1)S(1)}, bf16[144,896]{1,0:T(8,128)(2,1)S(1)}, u32[]{:S(2)}, u32[]{:S(2)}) %collective-permute-start.2) | collective-permute-done | bytes 258080 | tf_op jit(solution)/shard_map/ppermute | solution.py:569
  40.9 7.4 %collective-permute-done = bf16[144,896]{1,0:T(8,128)(2,1)S(1)} collective-permute-done((bf16[144,896]{1,0:T(8,128)(2,1)S(1)}, bf16[144,896]{1,0:T(8,128)(2,1)S(1)}, u32[]{:S(2)}, u32[]{:S(2)}) %collective-permute-start) | collective-permute-done | bytes 258080 | tf_op jit(solution)/shard_map/ppermute | solution.py:569
  52.1 3.2 collective-permute-start.7
  56.6 8.2 %collective-permute-done.6.refs_1_ = bf16[4,144,512]{2,1,0:T(8,128)(2,1)} collective-permute-done((bf16[4,144,512]{2,1,0:T(8,128)(2,1)S(1)}, bf16[4,144,512]{2,1,0:T(8,128)(2,1)}, u32[]{:S(2)}, u32[]{:S(2)}) %collective-permute-start.6) | collective-permute-done | bytes 589856 | tf_op jit(solution)/shard_map/ppermute | solution.py:44
  64.8 8.2 %collective-permute-done.7.refs_14_ = bf16[4,3,128,128]{3,2,1,0:T(8,128)(2,1)} collective-permute-done((bf16[4,3,128,128]{3,2,1,0:T(8,128)(2,1)S(1)}, bf16[4,3,128,128]{3,2,1,0:T(8,128)(2,1)}, u32[]{:S(2)}, u32[]{:S(2)}) %collective-permute-start.7) | collective-permute-done | bytes 393248 | tf_op jit(solution)/shard_map/ppermute | solution.py:44
  73.0 4.2 all-to-all-start.1
  83.0 10.9 %shard_map.238 = (bf16[1024,1024]{1,0:T(8,128)(2,1)}, bf16[1024,512]{1,0:T(8,128)(2,1)}, f32[8,1024]{1,0:T(8,128)}, bf16[1024,256]{1,0:T(8,128)(2,1)}, bf16[2,10...) custom-call(s32[8]{0:T(128)} %fusion.47.table.dests, ...), custom_call_target="tpu_custom_call" | custom-call | flops 1 | bytes 8250000 | tf_op jit(solution)/shard_map/pallas_call | solution.py:599
  93.9 8.9 %collective-permute-done.8.refs_1_ = bf16[4,128,384]{2,1,0:T(8,128)(2,1)S(1)} collective-permute-done((bf16[4,128,384]{2,1,0:T(8,128)(2,1)S(1)}, bf16[4,128,384]{2,1,0:T(8,128)(2,1)S(1)}, u32[]{:S(2)}, u32[]{:S(2)}) %collective-permute-start.8) | collective-permute-done | bytes 393248 | tf_op jit(solution)/shard_map/ppermute | solution.py:44
  103.7 3.9 shard_map.239
  108.3 2.9 collective-permute-done.10.got
  112.9 3.6 collective-permute-start.11
  119.0 3.1 collective-permute-done.12
  122.1 15.0 %collective-permute-done.13.refs_16_ = bf16[4,3,128,128]{3,2,1,0:T(8,128)(2,1)} collective-permute-done((bf16[4,3,128,128]{3,2,1,0:T(8,128)(2,1)}, bf16[4,3,128,128]{3,2,1,0:T(8,128)(2,1)}, u32[]{:S(2)}, u32[]{:S(2)}) %collective-permute-start.13) | collective-permute-done | bytes 393248 | tf_op jit(solution)/shard_map/ppermute | solution.py:44
  137.1 5.2 shard_map.240
  142.3 2.6 collective-permute-start.17
  145.4 19.9 %collective-permute-done.18 = s32[2,9,1024]{2,1,0:T(8,128)S(1)} collective-permute-done((s32[2,9,1024]{2,1,0:T(8,128)S(1)}, s32[2,9,1024]{2,1,0:T(8,128)S(1)}, u32[]{:S(2)}, u32[]{:S(2)}) %collective-permute-start.18) | collective-permute-done | bytes 73760 | tf_op jit(solution)/shard_map/ppermute | solution.py:44
  172.4 19.4 %collective-permute-done.22.refs_14_ = bf16[4,3,128,128]{3,2,1,0:T(8,128)(2,1)S(1)} collective-permute-done((bf16[4,3,128,128]{3,2,1,0:T(8,128)(2,1)S(1)}, bf16[4,3,128,128]{3,2,1,0:T(8,128)(2,1)S(1)}, u32[]{:S(2)}, u32[]{:S(2)}) %collective-permute-start.22) | collective-permute-done | bytes 393248 | tf_op jit(solution)/shard_map/ppermute | solution.py:44
  203.0 2.9 and_select_fusion
  209.2 24.1 %collective-permute-done.26.refs_15_ = bf16[4,3,128,128]{3,2,1,0:T(8,128)(2,1)} collective-permute-done((bf16[4,3,128,128]{3,2,1,0:T(8,128)(2,1)}, bf16[4,3,128,128]{3,2,1,0:T(8,128)(2,1)}, u32[]{:S(2)}, u32[]{:S(2)}) %collective-permute-start.26) | collective-permute-done | bytes 393248 | tf_op jit(solution)/shard_map/ppermute | solution.py:44
  233.3 8.1 %collective-permute-done.27.refs_16_ = bf16[4,3,128,128]{3,2,1,0:T(8,128)(2,1)} collective-permute-done((bf16[4,3,128,128]{3,2,1,0:T(8,128)(2,1)}, bf16[4,3,128,128]{3,2,1,0:T(8,128)(2,1)}, u32[]{:S(2)}, u32[]{:S(2)}) %collective-permute-start.27) | collective-permute-done | bytes 393248 | tf_op jit(solution)/shard_map/ppermute | solution.py:44
  245.2 10.5 %collective-permute-done.32.refs_7_ = bf16[2,2,256,512]{3,2,1,0:T(8,128)(2,1)S(1)} collective-permute-done((bf16[2,2,256,512]{3,2,1,0:T(8,128)(2,1)}, bf16[2,2,256,512]{3,2,1,0:T(8,128)(2,1)S(1)}, u32[]{:S(2)}, u32[]{:S(2)}) %collective-permute-start.32) | collective-permute-done | bytes 1048608 | tf_op jit(solution)/shard_map/ppermute | solution.py:44
  260.8 20.5 %shard_map.241 = (bf16[1024,896]{1,0:T(8,128)(2,1)}, bf16[1024,512]{1,0:T(8,128)(2,1)}, bf16[1024,768]{1,0:T(8,128)(2,1)}, bf16[1024,1024]{1,0:T(8,128)(2,1)}, b...) custom-call(s32[7]{0:T(128)} %get-tuple-element.253.meta, ...), custom_call_target="tpu_custom_call" | custom-call | flops 1 | bytes 21750000 | tf_op jit(solution)/shard_map/pallas_call | solution.py:724
  281.3 9.2 %shard_map.242 = (bf16[4,3,128,128]{3,2,1,0:T(8,128)(2,1)}, bf16[4,3,128,128]{3,2,1,0:T(8,128)(2,1)}, bf16[4,3,128,128]{3,2,1,0:T(8,128)(2,1)}, bf16[4,3,128,128...) custom-call(s32[7]{0:T(128)} %get-tuple-element.253.meta, bf16[1024,1024]{1,0:T(8,128)(2,1)} %get-tuple-element.254.picked, ...), custom_call_target="tpu_custom_call" | custom-call | flops 1 | bytes 6750000 | tf_op jit(solution)/shard_map/pallas_call | solution.py:693
  293.4 32.5 %shard_map.243 = (bf16[2,2,2,256,896]{4,3,2,1,0:T(8,128)(2,1)}, bf16[2,2,2,256,512]{4,3,2,1,0:T(8,128)(2,1)}, bf16[2,2,2,256,768]{4,3,2,1,0:T(8,128)(2,1)}, bf16...) custom-call(s32[7]{0:T(128)} %get-tuple-element.277.meta, ...), custom_call_target="tpu_custom_call" | custom-call | flops 1 | bytes 21750000 | tf_op jit(solution)/shard_map/pallas_call | solution.py:724
  328.9 9.7 %shard_map.244 = (bf16[4,3,128,128]{3,2,1,0:T(8,128)(2,1)}, bf16[4,3,128,128]{3,2,1,0:T(8,128)(2,1)}, bf16[4,3,128,128]{3,2,1,0:T(8,128)(2,1)}, bf16[4,3,128,128...) custom-call(s32[7]{0:T(128)} %get-tuple-element.277.meta, bf16[1024,1024]{1,0:T(8,128)(2,1)} %get-tuple-element.278.picked, ...), custom_call_target="tpu_custom_call" | custom-call | flops 1 | bytes 6750000 | tf_op jit(solution)/shard_map/pallas_call | solution.py:693
  338.6 8.6 %collective-permute-done.40 = bf16[4,3,128,128]{3,2,1,0:T(8,128)(2,1)} collective-permute-done((bf16[4,3,128,128]{3,2,1,0:T(8,128)(2,1)}, bf16[4,3,128,128]{3,2,1,0:T(8,128)(2,1)}, u32[]{:S(2)}, u32[]{:S(2)}) %collective-permute-start.40) | collective-permute-done | bytes 393248 | tf_op jit(solution)/shard_map/ppermute | solution.py:44
  355.8 3.2 collective-permute-start.44
  364.4 23.4 %collective-permute-done.44 = bf16[4,3,128,128]{3,2,1,0:T(8,128)(2,1)S(1)} collective-permute-done((bf16[4,3,128,128]{3,2,1,0:T(8,128)(2,1)S(1)}, bf16[4,3,128,128]{3,2,1,0:T(8,128)(2,1)S(1)}, u32[]{:S(2)}, u32[]{:S(2)}) %collective-permute-start.44) | collective-permute-done | bytes 393248 | tf_op jit(solution)/shard_map/ppermute | solution.py:44
  387.8 7.2 %collective-permute-done.45 = bf16[4,3,128,128]{3,2,1,0:T(8,128)(2,1)S(1)} collective-permute-done((bf16[4,3,128,128]{3,2,1,0:T(8,128)(2,1)S(1)}, bf16[4,3,128,128]{3,2,1,0:T(8,128)(2,1)S(1)}, u32[]{:S(2)}, u32[]{:S(2)}) %collective-permute-start.45) | collective-permute-done | bytes 393248 | tf_op jit(solution)/shard_map/ppermute | solution.py:44
  403.2 21.5 %collective-permute-done.49 = bf16[4,3,128,128]{3,2,1,0:T(8,128)(2,1)S(1)} collective-permute-done((bf16[4,3,128,128]{3,2,1,0:T(8,128)(2,1)S(1)}, bf16[4,3,128,128]{3,2,1,0:T(8,128)(2,1)S(1)}, u32[]{:S(2)}, u32[]{:S(2)}) %collective-permute-start.49) | collective-permute-done | bytes 393248 | tf_op jit(solution)/shard_map/ppermute | solution.py:44
  433.0 3.2 collective-permute-done.52.cr
  436.2 2.7 collective-permute-done.50.ar
  439.7 5.1 shard_map.245
  446.8 19.6 %collective-permute-done.55 = bf16[4,3,128,128]{3,2,1,0:T(8,128)(2,1)S(1)} collective-permute-done((bf16[4,3,128,128]{3,2,1,0:T(8,128)(2,1)}, bf16[4,3,128,128]{3,2,1,0:T(8,128)(2,1)S(1)}, u32[]{:S(2)}, u32[]{:S(2)}) %collective-permute-start.55) | collective-permute-done | bytes 393248 | tf_op jit(solution)/shard_map/ppermute | solution.py:44
  467.1 3.5 add_convert_fusion.3
  471.4 3.7 shard_map.246
  475.1 4.4 all-to-all-start.2
  483.9 22.0 %shard_map.247 = (f32[2,256,1024]{2,1,0:T(8,128)}, bf16[2,256,1024]{2,1,0:T(8,128)(2,1)}, bf16[4,128,640]{2,1,0:T(8,128)(2,1)}, bf16[4,128,640]{2,1,0:T(8,128)(2,1)}) custom-call(s32[8]{0:T(128)} %fusion.47.table.dests, s32[4]{0:T(128)} %xor_multiply_fusion.offs, bf16[256,1024]{1,0:T(8,128)(2,1)} %get-tuple-element.348.a0, bf16[256,1024]{1,0:T(8,128)(2,1)} %copy-done.19, ...), custom_call_target="tpu_custom_call" | custom-call | flops 1 | bytes 45000000 | tf_op jit(solution)/shard_map/pallas_call | solution.py:806
  506.8 2.7 collective-permute-start.59
  515.1 3.3 collective-permute-start.64
  522.5 5.4 collective-permute-done.63
  529.4 4.8 all-to-all-start.3
  542.6 4.0 shard_map.248
  547.8 17.3 %collective-permute-done.65 = bf16[128,640]{1,0:T(8,128)(2,1)S(1)} collective-permute-done((bf16[128,640]{1,0:T(8,128)(2,1)}, bf16[128,640]{1,0:T(8,128)(2,1)S(1)}, u32[]{:S(2)}, u32[]{:S(2)}) %collective-permute-start.65) | collective-permute-done | bytes 163872 | tf_op jit(solution)/shard_map/ppermute | solution.py:834
  (361 shorter events, 139.4 us)
Async XLA Ops:
  5.0 46.1 %all-to-all-start = ((bf16[16,3,128,128]{3,2,1,0:T(8,128)(2,1)}), bf16[16,3,128,128]{3,2,1,0:T(8,128)(2,1)S(1)}, u32[]{:S(2)}, u32[]{:S(2)}) async-start(bf16[16,3,128,128]{3,2,1,0:T(8,128)(2,1)} %pad_maximum_fusion.2), calls=%async_computation | async-start | bytes 3145728 | tf_op jit(solution)/shard_map/all_to_all | solution.py:547
  13.3 26.5 %collective-permute-start.2 = (bf16[144,896]{1,0:T(8,128)(2,1)S(1)}, bf16[144,896]{1,0:T(8,128)(2,1)S(1)}, u32[]{:S(2)}, u32[]{:S(2)}) collective-permute-start(bf16[144,896]{1,0:T(8,128)(2,1)S(1)} %get-tuple-element.443), channel_id=1, source_target_pairs={{0,24},{8,16},{16,8},{24,0},{1,25},{9,17},{17,9},{25,1},{2,26},{10... | collective-permute-start | bytes 774152 | tf_op jit(solution)/shard_map/ppermute | solution.py:569
  17.3 23.5 %collective-permute-start.1 = (bf16[144,896]{1,0:T(8,128)(2,1)S(1)}, bf16[144,896]{1,0:T(8,128)(2,1)S(1)}, u32[]{:S(2)}, u32[]{:S(2)}) collective-permute-start(bf16[144,896]{1,0:T(8,128)(2,1)S(1)} %get-tuple-element.443), channel_id=1, source_target_pairs={{0,16},{8,24},{16,0},{24,8},{1,17},{9,25},{17,1},{25,9},{2,18},{10... | collective-permute-start | bytes 774152 | tf_op jit(solution)/shard_map/ppermute | solution.py:569
  17.3 30.9 %collective-permute-start = (bf16[144,896]{1,0:T(8,128)(2,1)S(1)}, bf16[144,896]{1,0:T(8,128)(2,1)S(1)}, u32[]{:S(2)}, u32[]{:S(2)}) collective-permute-start(bf16[144,896]{1,0:T(8,128)(2,1)S(1)} %get-tuple-element.443), channel_id=1, source_target_pairs={{0,8},{8,0},{16,24},{24,16},{1,9},{9,1},{17,25},{25,17},{2,10},{10... | collective-permute-start | bytes 774152 | tf_op jit(solution)/shard_map/ppermute | solution.py:569
  18.0 30.3 %collective-permute-start.4 = (bf16[256,1024]{1,0:T(8,128)(2,1)S(1)}, bf16[256,1024]{1,0:T(8,128)(2,1)}, u32[]{:S(2)}, u32[]{:S(2)}) collective-permute-start(bf16[256,1024]{1,0:T(8,128)(2,1)S(1)} %bitcast.141), channel_id=1, source_target_pairs={{0,2},{2,0},{1,3},{3,1},{4,6},{6,4},{5,7},{7,5},{8,10},{10,8},{9,1... | collective-permute-start | bytes 1572872 | tf_op jit(solution)/shard_map/ppermute | solution.py:44
  52.1 20.9 %collective-permute-start.7 = (bf16[4,3,128,128]{3,2,1,0:T(8,128)(2,1)S(1)}, bf16[4,3,128,128]{3,2,1,0:T(8,128)(2,1)}, u32[]{:S(2)}, u32[]{:S(2)}) collective-permute-start(bf16[4,3,128,128]{3,2,1,0:T(8,128)(2,1)S(1)} %get-tuple-element.201), channel_id=1, source_target_pairs={{0,16},{16,0},{1,17},{17,1},{2,18},{18,2},{3,19},{19,3},{4,20},{20... | collective-permute-start | bytes 1179656 | tf_op jit(solution)/shard_map/ppermute | solution.py:44
  73.0 64.1 %all-to-all-start.1 = ((bf16[16,3,128,128]{3,2,1,0:T(8,128)(2,1)}), bf16[16,3,128,128]{3,2,1,0:T(8,128)(2,1)S(1)}, u32[]{:S(2)}, u32[]{:S(2)}) async-start(bf16[16,3,128,128]{3,2,1,0:T(8,128)(2,1)} %pad_maximum_fusion.1), calls=%async_computation.1 | async-start | bytes 3145728 | tf_op jit(solution)/shard_map/all_to_all | solution.py:593
  77.3 25.6 %collective-permute-start.8 = (bf16[4,128,384]{2,1,0:T(8,128)(2,1)S(1)}, bf16[4,128,384]{2,1,0:T(8,128)(2,1)S(1)}, u32[]{:S(2)}, u32[]{:S(2)}) collective-permute-start(bf16[4,128,384]{2,1,0:T(8,128)(2,1)S(1)} %pad_maximum_fusion.9.refs_0_), channel_id=1, source_target_pairs={{0,4},{4,0},{1,5},{5,1},{2,6},{6,2},{3,7},{7,3},{8,12},{12,8},{9,1... | collective-permute-start | bytes 1179656 | tf_op jit(solution)/shard_map/ppermute | solution.py:44
  79.2 28.4 %collective-permute-start.9 = (bf16[4,3,128,128]{3,2,1,0:T(8,128)(2,1)}, bf16[4,3,128,128]{3,2,1,0:T(8,128)(2,1)S(1)}, u32[]{:S(2)}, u32[]{:S(2)}) collective-permute-start(bf16[4,3,128,128]{3,2,1,0:T(8,128)(2,1)} %get-tuple-element.210), channel_id=1, source_target_pairs={{0,16},{16,0},{1,17},{17,1},{2,18},{18,2},{3,19},{19,3},{4,20},{20... | collective-permute-start | bytes 1179656 | tf_op jit(solution)/shard_map/ppermute | solution.py:44
  112.9 24.2 %collective-permute-start.11 = (bf16[256,1024]{1,0:T(8,128)(2,1)S(1)}, bf16[256,1024]{1,0:T(8,128)(2,1)}, u32[]{:S(2)}, u32[]{:S(2)}) collective-permute-start(bf16[256,1024]{1,0:T(8,128)(2,1)S(1)} %fusion.18), channel_id=1, source_target_pairs={{0,2},{2,0},{1,3},{3,1},{4,6},{6,4},{5,7},{7,5},{8,10},{10,8},{9,1... | collective-permute-start | bytes 1572872 | tf_op jit(solution)/shard_map/ppermute | solution.py:44
  116.6 20.5 %collective-permute-start.13 = (bf16[4,3,128,128]{3,2,1,0:T(8,128)(2,1)}, bf16[4,3,128,128]{3,2,1,0:T(8,128)(2,1)}, u32[]{:S(2)}, u32[]{:S(2)}) collective-permute-start(bf16[4,3,128,128]{3,2,1,0:T(8,128)(2,1)} %get-tuple-element.215), channel_id=1, source_target_pairs={{0,16},{16,0},{1,17},{17,1},{2,18},{18,2},{3,19},{19,3},{4,20},{20... | collective-permute-start | bytes 1179656 | tf_op jit(solution)/shard_map/ppermute | solution.py:44
  142.3 23.0 %collective-permute-start.14 = (bf16[256,896]{1,0:T(8,128)(2,1)}, bf16[256,896]{1,0:T(8,128)(2,1)S(1)}, u32[]{:S(2)}, u32[]{:S(2)}) collective-permute-start(bf16[256,896]{1,0:T(8,128)(2,1)} %get-tuple-element.221), channel_id=1, source_target_pairs={{0,8},{8,0},{1,9},{9,1},{2,10},{10,2},{3,11},{11,3},{4,12},{12,4},... | collective-permute-start | bytes 1376264 | tf_op jit(solution)/shard_map/ppermute | solution.py:44
  142.3 23.0 %collective-permute-start.17 = (bf16[4,3,128,128]{3,2,1,0:T(8,128)(2,1)S(1)}, bf16[4,3,128,128]{3,2,1,0:T(8,128)(2,1)S(1)}, u32[]{:S(2)}, u32[]{:S(2)}) collective-permute-start(bf16[4,3,128,128]{3,2,1,0:T(8,128)(2,1)S(1)} %copy-done.41), channel_id=1, source_target_pairs={{0,16},{16,0},{1,17},{17,1},{2,18},{18,2},{3,19},{19,3},{4,20},{20... | collective-permute-start | bytes 1179656 | tf_op jit(solution)/shard_map/ppermute | solution.py:44
  144.9 20.4 %collective-permute-start.16 = (bf16[256,768]{1,0:T(8,128)(2,1)}, bf16[256,768]{1,0:T(8,128)(2,1)S(1)}, u32[]{:S(2)}, u32[]{:S(2)}) collective-permute-start(bf16[256,768]{1,0:T(8,128)(2,1)} %get-tuple-element.223), channel_id=1, source_target_pairs={{0,2},{2,0},{1,3},{3,1},{4,6},{6,4},{5,7},{7,5},{8,10},{10,8},{9,1... | collective-permute-start | bytes 1179656 | tf_op jit(solution)/shard_map/ppermute | solution.py:44
  167.3 26.8 %collective-permute-start.19 = (bf16[2,256,896]{2,1,0:T(8,128)(2,1)S(1)}, bf16[2,256,896]{2,1,0:T(8,128)(2,1)S(1)}, u32[]{:S(2)}, u32[]{:S(2)}) collective-permute-start(bf16[2,256,896]{2,1,0:T(8,128)(2,1)S(1)} %get-tuple-element.429), channel_id=1, source_target_pairs={{0,4},{4,0},{1,5},{5,1},{2,6},{6,2},{3,7},{7,3},{8,12},{12,8},{9,1... | collective-permute-start | bytes 2752520 | tf_op jit(solution)/shard_map/ppermute | solution.py:44
  167.5 26.6 %collective-permute-start.21 = (bf16[2,256,768]{2,1,0:T(8,128)(2,1)S(1)}, bf16[2,256,768]{2,1,0:T(8,128)(2,1)S(1)}, u32[]{:S(2)}, u32[]{:S(2)}) collective-permute-start(bf16[2,256,768]{2,1,0:T(8,128)(2,1)S(1)} %get-tuple-element.431), channel_id=1, source_target_pairs={{0,8},{8,0},{1,9},{9,1},{2,10},{10,2},{3,11},{11,3},{4,12},{12,4},... | collective-permute-start | bytes 2359304 | tf_op jit(solution)/shard_map/ppermute | solution.py:44
  168.3 23.6 %collective-permute-start.20 = (bf16[2,256,512]{2,1,0:T(8,128)(2,1)S(1)}, bf16[2,256,512]{2,1,0:T(8,128)(2,1)S(1)}, u32[]{:S(2)}, u32[]{:S(2)}) collective-permute-start(bf16[2,256,512]{2,1,0:T(8,128)(2,1)S(1)} %get-tuple-element.436), channel_id=1, source_target_pairs={{0,2},{2,0},{1,3},{3,1},{4,6},{6,4},{5,7},{7,5},{8,10},{10,8},{9,1... | collective-permute-start | bytes 1572872 | tf_op jit(solution)/shard_map/ppermute | solution.py:44
  170.0 21.9 %collective-permute-start.22 = (bf16[4,3,128,128]{3,2,1,0:T(8,128)(2,1)S(1)}, bf16[4,3,128,128]{3,2,1,0:T(8,128)(2,1)S(1)}, u32[]{:S(2)}, u32[]{:S(2)}) collective-permute-start(bf16[4,3,128,128]{3,2,1,0:T(8,128)(2,1)S(1)} %get-tuple-element.230), channel_id=1, source_target_pairs={{0,16},{16,0},{1,17},{17,1},{2,18},{18,2},{3,19},{19,3},{4,20},{20... | collective-permute-start | bytes 1179656 | tf_op jit(solution)/shard_map/ppermute | solution.py:44
  194.3 47.2 %collective-permute-start.23 = (bf16[2,2,256,896]{3,2,1,0:T(8,128)(2,1)S(1)}, bf16[2,2,256,896]{3,2,1,0:T(8,128)(2,1)}, u32[]{:S(2)}, u32[]{:S(2)}) collective-permute-start(bf16[2,2,256,896]{3,2,1,0:T(8,128)(2,1)S(1)} %pad_maximum_fusion.refs_0_), channel_id=1, source_target_pairs={{0,2},{2,0},{1,3},{3,1},{4,6},{6,4},{5,7},{7,5},{8,10},{10,8},{9,1... | collective-permute-start | bytes 5505032 | tf_op jit(solution)/shard_map/ppermute | solution.py:44
  195.5 46.0 %collective-permute-start.25 = (bf16[2,2,256,768]{3,2,1,0:T(8,128)(2,1)S(1)}, bf16[2,2,256,768]{3,2,1,0:T(8,128)(2,1)}, u32[]{:S(2)}, u32[]{:S(2)}) collective-permute-start(bf16[2,2,256,768]{3,2,1,0:T(8,128)(2,1)S(1)} %pad_maximum_fusion.3.refs_8_), channel_id=1, source_target_pairs={{0,4},{4,0},{1,5},{5,1},{2,6},{6,2},{3,7},{7,3},{8,12},{12,8},{9,1... | collective-permute-start | bytes 4718600 | tf_op jit(solution)/shard_map/ppermute | solution.py:44
  198.5 42.9 %collective-permute-start.24 = (bf16[2,2,256,512]{3,2,1,0:T(8,128)(2,1)}, bf16[2,2,256,512]{3,2,1,0:T(8,128)(2,1)}, u32[]{:S(2)}, u32[]{:S(2)}) collective-permute-start(bf16[2,2,256,512]{3,2,1,0:T(8,128)(2,1)} %pad_maximum_fusion.4.refs_4_), channel_id=1, source_target_pairs={{0,8},{8,0},{1,9},{9,1},{2,10},{10,2},{3,11},{11,3},{4,12},{12,4},... | collective-permute-start | bytes 3145736 | tf_op jit(solution)/shard_map/ppermute | solution.py:44
  206.1 27.2 %collective-permute-start.26 = (bf16[4,3,128,128]{3,2,1,0:T(8,128)(2,1)}, bf16[4,3,128,128]{3,2,1,0:T(8,128)(2,1)}, u32[]{:S(2)}, u32[]{:S(2)}) collective-permute-start(bf16[4,3,128,128]{3,2,1,0:T(8,128)(2,1)} %get-tuple-element.234), channel_id=1, source_target_pairs={{0,16},{16,0},{1,17},{17,1},{2,18},{18,2},{3,19},{19,3},{4,20},{20... | collective-permute-start | bytes 1179656 | tf_op jit(solution)/shard_map/ppermute | solution.py:44
  207.0 34.4 %collective-permute-start.27 = (bf16[4,3,128,128]{3,2,1,0:T(8,128)(2,1)}, bf16[4,3,128,128]{3,2,1,0:T(8,128)(2,1)}, u32[]{:S(2)}, u32[]{:S(2)}) collective-permute-start(bf16[4,3,128,128]{3,2,1,0:T(8,128)(2,1)} %get-tuple-element.235), channel_id=1, source_target_pairs={{0,16},{16,0},{1,17},{17,1},{2,18},{18,2},{3,19},{19,3},{4,20},{20... | collective-permute-start | bytes 1179656 | tf_op jit(solution)/shard_map/ppermute | solution.py:44
  258.8 22.5 %collective-permute-start.34 = (bf16[4,3,128,128]{3,2,1,0:T(8,128)(2,1)}, bf16[4,3,128,128]{3,2,1,0:T(8,128)(2,1)S(1)}, u32[]{:S(2)}, u32[]{:S(2)}) collective-permute-start(bf16[4,3,128,128]{3,2,1,0:T(8,128)(2,1)} %get-tuple-element.251), channel_id=1, source_target_pairs={{0,16},{16,0},{1,17},{17,1},{2,18},{18,2},{3,19},{19,3},{4,20},{20... | collective-permute-start | bytes 1179656 | tf_op jit(solution)/shard_map/ppermute | solution.py:44
  290.5 35.4 %collective-permute-start.35 = (bf16[4,3,128,128]{3,2,1,0:T(8,128)(2,1)}, bf16[4,3,128,128]{3,2,1,0:T(8,128)(2,1)S(1)}, u32[]{:S(2)}, u32[]{:S(2)}) collective-permute-start(bf16[4,3,128,128]{3,2,1,0:T(8,128)(2,1)} %get-tuple-element.268), channel_id=1, source_target_pairs={{0,16},{16,0},{1,17},{17,1},{2,18},{18,2},{3,19},{19,3},{4,20},{20... | collective-permute-start | bytes 1179656 | tf_op jit(solution)/shard_map/ppermute | solution.py:44
  292.8 34.0 %collective-permute-start.36 = (bf16[4,3,128,128]{3,2,1,0:T(8,128)(2,1)}, bf16[4,3,128,128]{3,2,1,0:T(8,128)(2,1)S(1)}, u32[]{:S(2)}, u32[]{:S(2)}) collective-permute-start(bf16[4,3,128,128]{3,2,1,0:T(8,128)(2,1)} %get-tuple-element.270), channel_id=1, source_target_pairs={{0,16},{16,0},{1,17},{17,1},{2,18},{18,2},{3,19},{19,3},{4,20},{20... | collective-permute-start | bytes 1179656 | tf_op jit(solution)/shard_map/ppermute | solution.py:44
  326.8 20.4 %collective-permute-start.37 = (bf16[2,2,2,256,896]{4,3,2,1,0:T(8,128)(2,1)}, bf16[2,2,2,256,896]{4,3,2,1,0:T(8,128)(2,1)}, u32[]{:S(2)}, u32[]{:S(2)}) collective-permute-start(bf16[2,2,2,256,896]{4,3,2,1,0:T(8,128)(2,1)} %get-tuple-element.272), channel_id=1, source_target_pairs={{0,1},{1,0},{2,3},{3,2},{4,5},{5,4},{6,7},{7,6},{8,9},{9,8},{10,11... | collective-permute-start | bytes 11010056 | tf_op jit(solution)/shard_map/ppermute | solution.py:44
  326.8 20.4 %collective-permute-start.39 = (bf16[2,2,2,256,768]{4,3,2,1,0:T(8,128)(2,1)}, bf16[2,2,2,256,768]{4,3,2,1,0:T(8,128)(2,1)}, u32[]{:S(2)}, u32[]{:S(2)}) collective-permute-start(bf16[2,2,2,256,768]{4,3,2,1,0:T(8,128)(2,1)} %get-tuple-element.274), channel_id=1, source_target_pairs={{0,1},{1,0},{2,3},{3,2},{4,5},{5,4},{6,7},{7,6},{8,9},{9,8},{10,11... | collective-permute-start | bytes 9437192 | tf_op jit(solution)/shard_map/ppermute | solution.py:44
  353.5 43.8 %collective-permute-start.41 = (bf16[2,2,256,896]{3,2,1,0:T(8,128)(2,1)S(1)}, bf16[2,2,256,896]{3,2,1,0:T(8,128)(2,1)S(1)}, u32[]{:S(2)}, u32[]{:S(2)}) collective-permute-start(bf16[2,2,256,896]{3,2,1,0:T(8,128)(2,1)S(1)} %fusion.4), channel_id=1, source_target_pairs={{0,2},{2,0},{1,3},{3,1},{4,6},{6,4},{5,7},{7,5},{8,10},{10,8},{9,1... | collective-permute-start | bytes 5505032 | tf_op jit(solution)/shard_map/ppermute | solution.py:44
  355.3 42.0 %collective-permute-start.43 = (bf16[2,2,256,768]{3,2,1,0:T(8,128)(2,1)S(1)}, bf16[2,2,256,768]{3,2,1,0:T(8,128)(2,1)S(1)}, u32[]{:S(2)}, u32[]{:S(2)}) collective-permute-start(bf16[2,2,256,768]{3,2,1,0:T(8,128)(2,1)S(1)} %fusion.6), channel_id=1, source_target_pairs={{0,4},{4,0},{1,5},{5,1},{2,6},{6,2},{3,7},{7,3},{8,12},{12,8},{9,1... | collective-permute-start | bytes 4718600 | tf_op jit(solution)/shard_map/ppermute | solution.py:44
  355.8 41.4 %collective-permute-start.42 = (bf16[2,2,256,512]{3,2,1,0:T(8,128)(2,1)S(1)}, bf16[2,2,256,512]{3,2,1,0:T(8,128)(2,1)S(1)}, u32[]{:S(2)}, u32[]{:S(2)}) collective-permute-start(bf16[2,2,256,512]{3,2,1,0:T(8,128)(2,1)S(1)} %fusion.11), channel_id=1, source_target_pairs={{0,8},{8,0},{1,9},{9,1},{2,10},{10,2},{3,11},{11,3},{4,12},{12,4},... | collective-permute-start | bytes 3145736 | tf_op jit(solution)/shard_map/ppermute | solution.py:44
  355.8 32.0 %collective-permute-start.44 = (bf16[4,3,128,128]{3,2,1,0:T(8,128)(2,1)S(1)}, bf16[4,3,128,128]{3,2,1,0:T(8,128)(2,1)S(1)}, u32[]{:S(2)}, u32[]{:S(2)}) collective-permute-start(bf16[4,3,128,128]{3,2,1,0:T(8,128)(2,1)S(1)} %copy-done.72), channel_id=1, source_target_pairs={{0,16},{16,0},{1,17},{17,1},{2,18},{18,2},{3,19},{19,3},{4,20},{20... | collective-permute-start | bytes 1179656 | tf_op jit(solution)/shard_map/ppermute | solution.py:44
  359.0 36.0 %collective-permute-start.45 = (bf16[4,3,128,128]{3,2,1,0:T(8,128)(2,1)S(1)}, bf16[4,3,128,128]{3,2,1,0:T(8,128)(2,1)S(1)}, u32[]{:S(2)}, u32[]{:S(2)}) collective-permute-start(bf16[4,3,128,128]{3,2,1,0:T(8,128)(2,1)S(1)} %copy-done.74), channel_id=1, source_target_pairs={{0,16},{16,0},{1,17},{17,1},{2,18},{18,2},{3,19},{19,3},{4,20},{20... | collective-permute-start | bytes 1179656 | tf_op jit(solution)/shard_map/ppermute | solution.py:44
  397.9 28.3 %collective-permute-start.46 = (bf16[2,256,896]{2,1,0:T(8,128)(2,1)S(1)}, bf16[2,256,896]{2,1,0:T(8,128)(2,1)S(1)}, u32[]{:S(2)}, u32[]{:S(2)}) collective-permute-start(bf16[2,256,896]{2,1,0:T(8,128)(2,1)S(1)} %fusion.13), channel_id=1, source_target_pairs={{0,4},{4,0},{1,5},{5,1},{2,6},{6,2},{3,7},{7,3},{8,12},{12,8},{9,1... | collective-permute-start | bytes 2752520 | tf_op jit(solution)/shard_map/ppermute | solution.py:44
  399.4 25.3 %collective-permute-start.47 = (bf16[2,256,512]{2,1,0:T(8,128)(2,1)S(1)}, bf16[2,256,512]{2,1,0:T(8,128)(2,1)S(1)}, u32[]{:S(2)}, u32[]{:S(2)}) collective-permute-start(bf16[2,256,512]{2,1,0:T(8,128)(2,1)S(1)} %fusion.19), channel_id=1, source_target_pairs={{0,2},{2,0},{1,3},{3,1},{4,6},{6,4},{5,7},{7,5},{8,10},{10,8},{9,1... | collective-permute-start | bytes 1572872 | tf_op jit(solution)/shard_map/ppermute | solution.py:44
  399.7 26.4 %collective-permute-start.48 = (bf16[2,256,768]{2,1,0:T(8,128)(2,1)S(1)}, bf16[2,256,768]{2,1,0:T(8,128)(2,1)S(1)}, u32[]{:S(2)}, u32[]{:S(2)}) collective-permute-start(bf16[2,256,768]{2,1,0:T(8,128)(2,1)S(1)} %fusion.15), channel_id=1, source_target_pairs={{0,8},{8,0},{1,9},{9,1},{2,10},{10,2},{3,11},{11,3},{4,12},{12,4},... | collective-permute-start | bytes 2359304 | tf_op jit(solution)/shard_map/ppermute | solution.py:44
  401.3 23.4 %collective-permute-start.49 = (bf16[4,3,128,128]{3,2,1,0:T(8,128)(2,1)S(1)}, bf16[4,3,128,128]{3,2,1,0:T(8,128)(2,1)S(1)}, u32[]{:S(2)}, u32[]{:S(2)}) collective-permute-start(bf16[4,3,128,128]{3,2,1,0:T(8,128)(2,1)S(1)} %copy-done.73), channel_id=1, source_target_pairs={{0,16},{16,0},{1,17},{17,1},{2,18},{18,2},{3,19},{19,3},{4,20},{20... | collective-permute-start | bytes 1179656 | tf_op jit(solution)/shard_map/ppermute | solution.py:44
  444.8 21.6 %collective-permute-start.54 = (bf16[256,1024]{1,0:T(8,128)(2,1)}, bf16[256,1024]{1,0:T(8,128)(2,1)S(1)}, u32[]{:S(2)}, u32[]{:S(2)}) collective-permute-start(bf16[256,1024]{1,0:T(8,128)(2,1)} %get-tuple-element.348.a0), channel_id=1, source_target_pairs={{0,2},{2,0},{1,3},{3,1},{4,6},{6,4},{5,7},{7,5},{8,10},{10,8},{9,1... | collective-permute-start | bytes 1572872 | tf_op jit(solution)/shard_map/ppermute | solution.py:44
  445.3 21.8 %collective-permute-start.53 = (bf16[256,1024]{1,0:T(8,128)(2,1)}, bf16[256,1024]{1,0:T(8,128)(2,1)S(1)}, u32[]{:S(2)}, u32[]{:S(2)}) collective-permute-start(bf16[256,1024]{1,0:T(8,128)(2,1)} %get-tuple-element.348.a0), channel_id=1, source_target_pairs={{0,1},{1,0},{2,3},{3,2},{4,5},{5,4},{6,7},{7,6},{8,9},{9,8},{10,11... | collective-permute-start | bytes 1572872 | tf_op jit(solution)/shard_map/ppermute | solution.py:44
  445.3 21.1 %collective-permute-start.55 = (bf16[4,3,128,128]{3,2,1,0:T(8,128)(2,1)}, bf16[4,3,128,128]{3,2,1,0:T(8,128)(2,1)S(1)}, u32[]{:S(2)}, u32[]{:S(2)}) collective-permute-start(bf16[4,3,128,128]{3,2,1,0:T(8,128)(2,1)} %get-tuple-element.342), channel_id=1, source_target_pairs={{0,16},{16,0},{1,17},{17,1},{2,18},{18,2},{3,19},{19,3},{4,20},{20... | collective-permute-start | bytes 1179656 | tf_op jit(solution)/shard_map/ppermute | solution.py:44
  475.1 54.3 %all-to-all-start.2 = ((bf16[16,3,128,128]{3,2,1,0:T(8,128)(2,1)}), bf16[16,3,128,128]{3,2,1,0:T(8,128)(2,1)S(1)}, u32[]{:S(2)}, u32[]{:S(2)}) async-start(bf16[16,3,128,128]{3,2,1,0:T(8,128)(2,1)} %add_convert_fusion.3), calls=%async_computation.2 | async-start | bytes 3145728 | tf_op jit(solution)/shard_map/all_to_all | solution.py:802
  479.6 26.3 %collective-permute-start.58 = (bf16[4,3,128,128]{3,2,1,0:T(8,128)(2,1)S(1)}, bf16[4,3,128,128]{3,2,1,0:T(8,128)(2,1)S(1)}, u32[]{:S(2)}, u32[]{:S(2)}) collective-permute-start(bf16[4,3,128,128]{3,2,1,0:T(8,128)(2,1)S(1)} %copy-done.71), channel_id=1, source_target_pairs={{0,16},{16,0},{1,17},{17,1},{2,18},{18,2},{3,19},{19,3},{4,20},{20... | collective-permute-start | bytes 1179656 | tf_op jit(solution)/shard_map/ppermute | solution.py:44
  482.1 23.9 %collective-permute-start.57 = (bf16[4,128,384]{2,1,0:T(8,128)(2,1)S(1)}, bf16[4,128,384]{2,1,0:T(8,128)(2,1)S(1)}, u32[]{:S(2)}, u32[]{:S(2)}) collective-permute-start(bf16[4,128,384]{2,1,0:T(8,128)(2,1)S(1)} %copy-done.75), channel_id=1, source_target_pairs={{0,4},{4,0},{1,5},{5,1},{2,6},{6,2},{3,7},{7,3},{8,12},{12,8},{9,1... | collective-permute-start | bytes 1179656 | tf_op jit(solution)/shard_map/ppermute | solution.py:44
  506.8 21.2 %collective-permute-start.59 = (bf16[4,128,640]{2,1,0:T(8,128)(2,1)}, bf16[4,128,640]{2,1,0:T(8,128)(2,1)S(1)}, u32[]{:S(2)}, u32[]{:S(2)}) collective-permute-start(bf16[4,128,640]{2,1,0:T(8,128)(2,1)} %get-tuple-element.366), channel_id=1, source_target_pairs={{0,4},{4,0},{1,5},{5,1},{2,6},{6,2},{3,7},{7,3},{8,12},{12,8},{9,1... | collective-permute-start | bytes 1966088 | tf_op jit(solution)/shard_map/ppermute | solution.py:44
  529.4 44.0 %all-to-all-start.3 = ((bf16[16,3,128,128]{3,2,1,0:T(8,128)(2,1)}), bf16[16,3,128,128]{3,2,1,0:T(8,128)(2,1)S(1)}, u32[]{:S(2)}, u32[]{:S(2)}) async-start(bf16[16,3,128,128]{3,2,1,0:T(8,128)(2,1)} %add_convert_fusion.2), calls=%async_computation.3 | async-start | bytes 3145728 | tf_op jit(solution)/shard_map/all_to_all | solution.py:846
  539.1 26.0 %collective-permute-start.65 = (bf16[128,640]{1,0:T(8,128)(2,1)}, bf16[128,640]{1,0:T(8,128)(2,1)S(1)}, u32[]{:S(2)}, u32[]{:S(2)}) collective-permute-start(bf16[128,640]{1,0:T(8,128)(2,1)} %get-tuple-element.432), channel_id=1, source_target_pairs={{0,8},{8,0},{16,24},{24,16},{1,9},{9,1},{17,25},{25,17},{2,10},{10... | collective-permute-start | bytes 491528 | tf_op jit(solution)/shard_map/ppermute | solution.py:834
  541.0 24.1 %collective-permute-start.67 = (bf16[128,640]{1,0:T(8,128)(2,1)S(1)}, bf16[128,640]{1,0:T(8,128)(2,1)S(1)}, u32[]{:S(2)}, u32[]{:S(2)}) collective-permute-start(bf16[128,640]{1,0:T(8,128)(2,1)S(1)} %get-tuple-element.433), channel_id=1, source_target_pairs={{0,24},{8,16},{16,8},{24,0},{1,25},{9,17},{17,9},{25,1},{2,26},{10... | collective-permute-start | bytes 491528 | tf_op jit(solution)/shard_map/ppermute | solution.py:834
  541.2 23.9 %collective-permute-start.66 = (bf16[128,640]{1,0:T(8,128)(2,1)S(1)}, bf16[128,640]{1,0:T(8,128)(2,1)}, u32[]{:S(2)}, u32[]{:S(2)}) collective-permute-start(bf16[128,640]{1,0:T(8,128)(2,1)S(1)} %get-tuple-element.434), channel_id=1, source_target_pairs={{0,16},{8,24},{16,0},{24,8},{1,17},{9,25},{17,1},{25,9},{2,18},{10... | collective-permute-start | bytes 491528 | tf_op jit(solution)/shard_map/ppermute | solution.py:834
  (103 other events, 922.8 us)

commit v4 on v3

--- a/solution.py
+++ b/solution.py
@@ -18,6 +18,8 @@
 TOK = (512, 256, 256)
 SECOND = (384, 256, 384)
 NOTES = 128
+PARTS_IN = ((3, 4, 4, 2, 3), (8, 3, 5))
+PARTS_OUT = ((7, 3, 6), (2, 4, 2, 3, 5))
 BLK = 256
 BF = jnp.bfloat16
 F32 = jnp.float32
@@ -102,9 +104,9 @@
             at = pl.multiple_of(table[base + b] * shard, shard)
             wqkv_o[pl.ds(at, shard), :] = part[b, :shard, :]
             if shard == 128:
-                note = part[b, shard:, :].astype(F32)
+                note = part[b, shard:, :128].astype(F32)
                 for row in range(2):
-                    gains_o[row : row + 1, pl.ds(at, 128)] = note[row : row + 1, :128]
+                    gains_o[row : row + 1, pl.ds(at, 128)] = note[row : row + 1]
         base += part.shape[0]
     gain = gains_o[0:1, :]
     for r, piece in enumerate((t0, t1, t2, t3)):
@@ -150,13 +152,13 @@
         lse_o[rows, :] = logs
 
 
-def project_kernel(n_parts, table, offs, mix, *refs):
+def project_kernel(n_parts, shard, table, offs, mix, *refs):
     parts, (keep_o, send_o, wob) = refs[:n_parts], refs[n_parts:]
     base = 0
     for part in parts:
-        shard = part.shape[1]
         for b in range(part.shape[0]):
-            wob[pl.ds(pl.multiple_of(table[base + b] * shard, shard), shard), :] = part[b]
+            at = pl.multiple_of(table[base + b] * shard, shard)
+            wob[pl.ds(at, shard), :] = part[b]
         base += part.shape[0]
     for r in range(4):
         rows = pl.ds(pl.multiple_of(offs[r], BLK), BLK)
@@ -534,14 +536,17 @@
     def weight_part(j):
         return jnp.stack([w[j * 16 : (j + 1) * 16] for w in (w_gate, w_up, w_down)], axis=1)
 
-    parts_in = []
+    parts_in = [[], []]
 
     def part_in(*markers):
         if n_outer != 2:
             return ()
-        j, i = divmod(len(parts_in), 4)
-        parts_in.append(swap(after_all(own_mats[j][4 * i : 4 * i + 4], *markers), "o"))
-        return (parts_in[-1],)
+        j = 1 if len(parts_in[0]) == len(PARTS_IN[0]) else 0
+        count, i = PARTS_IN[j], len(parts_in[j])
+        at = sum(count[:i])
+        part = after_all(own_mats[j][at : at + count[i]], *markers)
+        parts_in[j].append(swap(part, "o"))
+        return (parts_in[j][-1],)
 
     first_mats = after_all(weight_part(0), tok_near)
     first_mats = lax.all_to_all(first_mats, POOL, 0, 0, tiled=True)
@@ -574,7 +579,7 @@
         wa = [near[:, :, :512]]
         wa.append(swap(wa[0], "y"))
         wb = [near[:, :shard, 512:]]
-        wb.append(swap(wb[0], "y"))
+        wb.append(swap(after_all(wb[0], wa[1]), "y"))
         table = jnp.bitwise_xor(at_z, steps(8) % 4) * 2 + jnp.bitwise_xor(at_y, steps(8) // 4)
         gains = jnp.zeros((8, dim), F32)
     else:
@@ -613,7 +618,7 @@
         11,
     )(table, offs, *tok_parts, *wa, gains, cosine, sine, start_col)
     keep, send, wob = simple_call(
-        functools.partial(project_kernel, len(wb)),
+        functools.partial(project_kernel, len(wb), shard),
         [((2, rows, dim), F32), ((2, rows, dim), BF), ((dim, 384), BF)],
         2,
         1 + len(wb),
@@ -650,13 +655,13 @@
     rank = rank.swapaxes(2, 3).reshape(4, per_device, length)
 
     def beside(step):
-        return lambda *markers: sum((part_in(*markers) for _ in range((1, 1, 2, 0)[step])), ()) + (
+        return lambda *markers: part_in(*markers) + (
             (plan, plan, rank)[step : step + 1]
         )
 
     pool = [value for piece in gather_pool([ma, mb, mc], beside, cross) for value in piece]
     if n_outer == 2:
-        ready_mats = lambda j: [own_mats[j]] + parts_in[4 * j : 4 * j + 4]
+        ready_mats = lambda j: [own_mats[j]] + parts_in[j]
     else:
         all_mats = [lax.all_gather(m, "o", axis=0, tiled=True) for m in own_mats]
         ready_mats = lambda j: [all_mats[j]]
@@ -688,8 +693,8 @@
     grad_shape = lambda n: jax.ShapeDtypeStruct((n,) + mat_shape[1:], BF)
     whole = lambda n: pl.BlockSpec((n,) + mat_shape[1:], lambda i, meta: (0, 0, 0, 0))
 
-    def weight_grads_of(meta, saved):
-        counts = [4, 4, 4, 4, 16] if n_outer == 2 else [16 * n_outer]
+    def weight_grads_of(meta, saved, j):
+        counts = [*PARTS_OUT[j], 16] if n_outer == 2 else [16 * n_outer]
         return pl.pallas_call(
             functools.partial(weight_grad_kernel, chunk // shard * 4),
             grid_spec=pltpu.PrefetchScalarGridSpec(
@@ -704,23 +709,24 @@
         )(meta, *saved)
 
     prev, weighted, saved = [], [], []
-    parts_out = []
-
-    def part_out(sends, *markers):
+    parts_out, all_grads = [[], []], [[], []]
+
+    def part_out(j, *markers):
         if n_outer != 2:
             return ()
-        parts_out.append(swap(after_all(sends[len(parts_out) % 4], *markers), "o"))
-        return (parts_out[-1],)
+        part = all_grads[j][len(parts_out[j])]
+        parts_out[j].append(swap(after_all(part, *markers), "o"))
+        return (parts_out[j][-1],)
 
     for j in range(per_device):
         if j == 0:
             moving = part_in(*pool)
         else:
             prev = together(prev, *moving)
-            first_grads = weight_grads_of(after_all(metas[0], prev[0]), saved[0])
+            first_grads = weight_grads_of(after_all(metas[0], prev[0]), saved[0], 0)
             metas[j] = after_all(metas[j], first_grads[0])
-            moving = part_out(first_grads[:4], first_grads[0])
-            moving += part_out(first_grads[:4], first_grads[0])
+            all_grads[0].extend(first_grads)
+            moving = part_out(0, first_grads[0])
         result = pl.pallas_call(
             functools.partial(expert_kernel, len(ready_mats(j)), j == 0),
             grid_spec=pltpu.PrefetchScalarGridSpec(
@@ -748,7 +754,7 @@
         saved.append(kept)
 
     prev = together(prev, *moving)
-    last_grads = []
+    last_grads = all_grads[1]
 
     moved = []
 
@@ -757,11 +763,9 @@
 
     def fill(step, bufs):
         if step == 0:
-            last_grads.extend(weight_grads_of(after_all(metas[1], prev[0]), saved[1]))
-            return (*part_out(first_grads[:4], *bufs), last_grads[0])
-        if step == 1:
-            return part_out(first_grads[:4], *bufs) + part_out(last_grads[:4], *bufs)
-        return part_out(last_grads[:4], *bufs) if step == 2 else ()
+            last_grads.extend(weight_grads_of(after_all(metas[1], prev[0]), saved[1], 1))
+            return (*part_out(0, *bufs), last_grads[0])
+        return (part_out(0, *bufs) if step == 1 else ()) + part_out(1, *bufs)
 
     pairs = scatter_pool(prev[:3], prev[3:], fill)
 
@@ -773,7 +777,7 @@
         5,
     )(after, *pairs[0], *pairs[1], *pairs[2], gains, wob, gates, cot)
     near, cross = swap(aog, "c"), swap(aog, "x")
-    moving = part_out(last_grads[:4], pairs[0][1])
+    moving = part_out(1, pairs[0][1])
     near, cross = together((near, cross), *moving)
     aog_parts = [aog, near, cross, swap(cross, "c")]
 
@@ -791,9 +795,9 @@
     )(dests, offs, *aog_parts, mix, small)
 
     aog_parts = together(aog_parts, *sides)
-    moving = part_out(last_grads[:4], cross)
+    moving = part_out(1, cross)
     if n_outer == 2:
-        first_sum = after_all(total(first_grads[4], parts_out[:4]), *aog_parts)
+        first_sum = after_all(total(first_grads[-1], parts_out[0]), *aog_parts)
     else:
         first_sum, last_sum = (
             lax.psum_scatter(g[0], "o", scatter_dimension=0, tiled=True)
@@ -820,9 +824,9 @@
     )(dests, offs, *aog_parts, wqkv, wob, q, kd, vd, lse, start_col, ain, cosine, sine)
     keep, send, *tails = together((keep, send, *tails), *sides, *moving)
 
+    got = swap(send, "c")
     if n_outer == 2:
-        last_sum = total(last_grads[4], parts_out[4:])
-    got = swap(send, "c")
+        last_sum = total(last_grads[-1], [*parts_out[1][:-1], after_all(parts_out[1][-1], got)])
     cross = swap((keep[1] + got[1].astype(F32)).astype(BF), "x")
     if n_tails == 2:
         add = lambda a, b: (a.astype(F32) + b.astype(F32)).astype(BF)

time: 582 us -> 574 us (0.986)
  waiting for transfers between devices: 268 us -> 258 us
    ppermute x59, waiting for transfers between devices: 224 us -> 213 us  [swap(): return lax.ppermute(value, axis, [(0, 1), (1, 0)])]
    unnamed x155 -> x153, local copies, waits for them, and re-layouts: 13.5 us -> 12.6 us
  transfers between devices with their start and end apart: 75 -> 75, of which waited for: 30 -> 31; matrix products, arithmetic and copies ran while one was open for 10% -> 10% of each run, Pallas kernels for 18% -> 18%
where the time goes in v4:
time: 574 us; the launch traced here: 570 us
  waiting for transfers between devices  258 us (45%)
  Pallas kernels  127 us (22%)
  starting transfers between devices  98.6 us (17%)
  other arithmetic  51.9 us (9%)
  local copies, waits for them, and re-layouts  29.3 us (5%)
    ppermute x59, waiting for transfers between devices, swap(): return lax.ppermute(value, axis, [(0, 1), (1, 0)])  213 us
    ppermute x59, starting transfers between devices, swap(): return lax.ppermute(value, axis, [(0, 1), (1, 0)])  60.6 us
    pallas_call x2, Pallas kernels, local(): pl.pallas_call(functools.partial(expert_kernel, len(ready_mats(j)), j ==...  53 us
    ppermute x6, waiting for transfers between devices, reduce_z(): lax.ppermute(sums[s], ('o', 'u'), [(i, i ^ s) for i in range(4)])  22.3 us
    pallas_call x1, Pallas kernels, local(): simple_call(functools.partial(attend_backward_kernel, n_tails), [((2, row...  22.1 us
    ppermute x3, waiting for transfers between devices, local(): lax.ppermute(pack, ('o', 'u'), [(i, i ^ s) for i in range(4)])  21.1 us
    pallas_call x2, Pallas kernels, weight_grads_of(): pl.pallas_call(functools.partial(weight_grad_kernel, chunk // shard * 4),...  18.9 us
    convert_element_type x18, other arithmetic, scatter_pool(): add = lambda a, b: (a.astype(F32) + b.astype(F32)).astype(BF)  14.9 us
  transfers between devices with their start and end apart: 75, of which 31 were waited for; matrix products, arithmetic and copies ran while one was open for 10% of the time, Pallas kernels for 18%

profile of v4, /device:TPU:0, one launch (start us, length us, event | category | flops | bytes accessed | tf_op | source)
XLA Modules:
  0.0 569.5 jit_solution(3269249011661377684)
XLA Ops:
  5.1 6.4 %all-to-all-start = ((bf16[16,3,128,128]{3,2,1,0:T(8,128)(2,1)}), bf16[16,3,128,128]{3,2,1,0:T(8,128)(2,1)S(1)}, u32[]{:S(2)}, u32[]{:S(2)}) async-start(bf16[16,3,128,128]{3,2,1,0:T(8,128)(2,1)} %pad_maximum_fusion.2), calls=%async_computation | async-start | bytes 3145728 | tf_op jit(solution)/shard_map/all_to_all | solution.py:552
  11.9 4.0 collective-permute-start.2
  21.5 2.6 compare_select_fusion.3
  24.2 3.1 fusion.17
  27.3 12.7 %collective-permute-done.2 = bf16[144,896]{1,0:T(8,128)(2,1)S(1)} collective-permute-done((bf16[144,896]{1,0:T(8,128)(2,1)S(1)}, bf16[144,896]{1,0:T(8,128)(2,1)S(1)}, u32[]{:S(2)}, u32[]{:S(2)}) %collective-permute-start.2) | collective-permute-done | bytes 258080 | tf_op jit(solution)/shard_map/ppermute | solution.py:574
  41.0 7.4 %collective-permute-done = bf16[144,896]{1,0:T(8,128)(2,1)S(1)} collective-permute-done((bf16[144,896]{1,0:T(8,128)(2,1)S(1)}, bf16[144,896]{1,0:T(8,128)(2,1)S(1)}, u32[]{:S(2)}, u32[]{:S(2)}) %collective-permute-start) | collective-permute-done | bytes 258080 | tf_op jit(solution)/shard_map/ppermute | solution.py:574
  48.6 2.6 collective-permute-start.6
  52.1 2.7 collective-permute-start.7
  57.4 7.1 %collective-permute-done.6.refs_1_ = bf16[4,144,512]{2,1,0:T(8,128)(2,1)} collective-permute-done((bf16[4,144,512]{2,1,0:T(8,128)(2,1)S(1)}, bf16[4,144,512]{2,1,0:T(8,128)(2,1)}, u32[]{:S(2)}, u32[]{:S(2)}) %collective-permute-start.6) | collective-permute-done | bytes 589856 | tf_op jit(solution)/shard_map/ppermute | solution.py:46
  64.5 4.3 collective-permute-done.7.refs_14_
  69.5 4.2 all-to-all-start.1
  82.2 10.9 %shard_map.238 = (bf16[1024,1024]{1,0:T(8,128)(2,1)}, bf16[1024,512]{1,0:T(8,128)(2,1)}, f32[8,1024]{1,0:T(8,128)}, bf16[1024,256]{1,0:T(8,128)(2,1)}, bf16[2,10...) custom-call(s32[8]{0:T(128)} %fusion.47.table.dests, ...), custom_call_target="tpu_custom_call" | custom-call | flops 1 | bytes 8250000 | tf_op jit(solution)/shard_map/pallas_call | solution.py:604
  93.1 6.3 %collective-permute-done.8.refs_1_ = bf16[4,128,384]{2,1,0:T(8,128)(2,1)S(1)} collective-permute-done((bf16[4,128,384]{2,1,0:T(8,128)(2,1)}, bf16[4,128,384]{2,1,0:T(8,128)(2,1)S(1)}, u32[]{:S(2)}, u32[]{:S(2)}) %collective-permute-start.8) | collective-permute-done | bytes 393248 | tf_op jit(solution)/shard_map/ppermute | solution.py:46
  100.2 3.9 shard_map.239
  104.1 2.9 collective-permute-done.10.got
  110.1 3.6 collective-permute-start.11
  119.9 14.3 %collective-permute-done.13.refs_16_ = bf16[4,3,128,128]{3,2,1,0:T(8,128)(2,1)} collective-permute-done((bf16[4,3,128,128]{3,2,1,0:T(8,128)(2,1)}, bf16[4,3,128,128]{3,2,1,0:T(8,128)(2,1)}, u32[]{:S(2)}, u32[]{:S(2)}) %collective-permute-start.13) | collective-permute-done | bytes 393248 | tf_op jit(solution)/shard_map/ppermute | solution.py:46
  134.2 5.1 shard_map.240
  142.4 15.6 %collective-permute-done.18 = s32[2,9,1024]{2,1,0:T(8,128)S(1)} collective-permute-done((s32[2,9,1024]{2,1,0:T(8,128)S(1)}, s32[2,9,1024]{2,1,0:T(8,128)S(1)}, u32[]{:S(2)}, u32[]{:S(2)}) %collective-permute-start.18) | collective-permute-done | bytes 73760 | tf_op jit(solution)/shard_map/ppermute | solution.py:46
  164.0 20.7 %collective-permute-done.22.refs_18_ = bf16[3,3,128,128]{3,2,1,0:T(8,128)(2,1)S(1)} collective-permute-done((bf16[3,3,128,128]{3,2,1,0:T(8,128)(2,1)S(1)}, bf16[3,3,128,128]{3,2,1,0:T(8,128)(2,1)S(1)}, u32[]{:S(2)}, u32[]{:S(2)}) %collective-permute-start.22) | collective-permute-done | bytes 294944 | tf_op jit(solution)/shard_map/ppermute | solution.py:46
  196.4 2.9 and_select_fusion
  199.7 30.3 %collective-permute-done.26.refs_14_ = bf16[8,3,128,128]{3,2,1,0:T(8,128)(2,1)} collective-permute-done((bf16[8,3,128,128]{3,2,1,0:T(8,128)(2,1)}, bf16[8,3,128,128]{3,2,1,0:T(8,128)(2,1)}, u32[]{:S(2)}, u32[]{:S(2)}) %collective-permute-start.26) | collective-permute-done | bytes 786464 | tf_op jit(solution)/shard_map/ppermute | solution.py:46
  230.8 2.8 collective-permute-start.33
  234.3 13.3 %collective-permute-done.33.refs_15_ = bf16[3,3,128,128]{3,2,1,0:T(8,128)(2,1)S(1)} collective-permute-done((bf16[3,3,128,128]{3,2,1,0:T(8,128)(2,1)S(1)}, bf16[3,3,128,128]{3,2,1,0:T(8,128)(2,1)S(1)}, u32[]{:S(2)}, u32[]{:S(2)}) %collective-permute-start.33) | collective-permute-done | bytes 294944 | tf_op jit(solution)/shard_map/ppermute | solution.py:46
  249.1 3.5 collective-permute-done.31.refs_7_
  257.9 20.5 %shard_map.241 = (bf16[1024,896]{1,0:T(8,128)(2,1)}, bf16[1024,512]{1,0:T(8,128)(2,1)}, bf16[1024,768]{1,0:T(8,128)(2,1)}, bf16[1024,1024]{1,0:T(8,128)(2,1)}, b...) custom-call(s32[7]{0:T(128)} %get-tuple-element.256.meta, ...), custom_call_target="tpu_custom_call" | custom-call | flops 1 | bytes 21750000 | tf_op jit(solution)/shard_map/pallas_call | solution.py:730
  278.4 3.0 collective-permute-done.34.refs_16_
  281.5 9.2 %shard_map.242 = (bf16[7,3,128,128]{3,2,1,0:T(8,128)(2,1)}, bf16[3,3,128,128]{3,2,1,0:T(8,128)(2,1)}, bf16[6,3,128,128]{3,2,1,0:T(8,128)(2,1)}, bf16[16,3,128,128]{3,2,1,0:T(8,128)(2,1)}) custom-call(s32[7]{0:T(128)} %get-tuple-element.256.meta, bf16[1024,1024]{1,0:T(8,128)(2,1)} %get-tuple-element.257.picked, bf16[1024,1024]{1,0:T(8,128)(2,1)} %get-tuple-element.258.dy, ...), custom_call_target="tpu_custom_call" | custom-call | flops 1 | bytes 6750000 | tf_op jit(solution)/shard_map/pallas_call | solution.py:698
  290.6 32.5 %shard_map.243 = (bf16[2,2,2,256,896]{4,3,2,1,0:T(8,128)(2,1)}, bf16[2,2,2,256,512]{4,3,2,1,0:T(8,128)(2,1)}, bf16[2,2,2,256,768]{4,3,2,1,0:T(8,128)(2,1)}, bf16...) custom-call(s32[7]{0:T(128)} %get-tuple-element.278.meta, ...), custom_call_target="tpu_custom_call" | custom-call | flops 1 | bytes 21750000 | tf_op jit(solution)/shard_map/pallas_call | solution.py:730
  323.8 2.8 collective-permute-start.39
  326.7 9.8 %shard_map.244 = (bf16[2,3,128,128]{3,2,1,0:T(8,128)(2,1)}, bf16[4,3,128,128]{3,2,1,0:T(8,128)(2,1)}, bf16[2,3,128,128]{3,2,1,0:T(8,128)(2,1)}, bf16[3,3,128,128...) custom-call(s32[7]{0:T(128)} %get-tuple-element.278.meta, ...), custom_call_target="tpu_custom_call" | custom-call | flops 1 | bytes 6750000 | tf_op jit(solution)/shard_map/pallas_call | solution.py:698
  336.4 4.4 collective-permute-done.39
  349.3 2.8 collective-permute-start.44
  357.5 19.6 %collective-permute-done.44 = bf16[2,3,128,128]{3,2,1,0:T(8,128)(2,1)S(1)} collective-permute-done((bf16[2,3,128,128]{3,2,1,0:T(8,128)(2,1)S(1)}, bf16[2,3,128,128]{3,2,1,0:T(8,128)(2,1)S(1)}, u32[]{:S(2)}, u32[]{:S(2)}) %collective-permute-start.44) | collective-permute-done | bytes 196640 | tf_op jit(solution)/shard_map/ppermute | solution.py:46
  377.1 11.2 %collective-permute-done.43 = bf16[6,3,128,128]{3,2,1,0:T(8,128)(2,1)S(1)} collective-permute-done((bf16[6,3,128,128]{3,2,1,0:T(8,128)(2,1)S(1)}, bf16[6,3,128,128]{3,2,1,0:T(8,128)(2,1)S(1)}, u32[]{:S(2)}, u32[]{:S(2)}) %collective-permute-start.43) | collective-permute-done | bytes 589856 | tf_op jit(solution)/shard_map/ppermute | solution.py:46
  396.3 21.4 %collective-permute-done.48 = bf16[4,3,128,128]{3,2,1,0:T(8,128)(2,1)S(1)} collective-permute-done((bf16[4,3,128,128]{3,2,1,0:T(8,128)(2,1)S(1)}, bf16[4,3,128,128]{3,2,1,0:T(8,128)(2,1)S(1)}, u32[]{:S(2)}, u32[]{:S(2)}) %collective-permute-start.48) | collective-permute-done | bytes 393248 | tf_op jit(solution)/shard_map/ppermute | solution.py:46
  427.2 7.3 %collective-permute-done.52 = bf16[2,3,128,128]{3,2,1,0:T(8,128)(2,1)S(1)} collective-permute-done((bf16[2,3,128,128]{3,2,1,0:T(8,128)(2,1)S(1)}, bf16[2,3,128,128]{3,2,1,0:T(8,128)(2,1)S(1)}, u32[]{:S(2)}, u32[]{:S(2)}) %collective-permute-start.52) | collective-permute-done | bytes 196640 | tf_op jit(solution)/shard_map/ppermute | solution.py:46
  437.4 5.2 shard_map.245
  444.5 15.4 %collective-permute-done.55 = bf16[3,3,128,128]{3,2,1,0:T(8,128)(2,1)S(1)} collective-permute-done((bf16[3,3,128,128]{3,2,1,0:T(8,128)(2,1)}, bf16[3,3,128,128]{3,2,1,0:T(8,128)(2,1)S(1)}, u32[]{:S(2)}, u32[]{:S(2)}) %collective-permute-start.55) | collective-permute-done | bytes 294944 | tf_op jit(solution)/shard_map/ppermute | solution.py:46
  462.8 3.7 shard_map.246
  466.5 4.2 all-to-all-start.2
  475.1 22.1 %shard_map.247 = (f32[2,256,1024]{2,1,0:T(8,128)}, bf16[2,256,1024]{2,1,0:T(8,128)(2,1)}, bf16[4,128,640]{2,1,0:T(8,128)(2,1)}, bf16[4,128,640]{2,1,0:T(8,128)(2,1)}) custom-call(s32[8]{0:T(128)} %fusion.47.table.dests, s32[4]{0:T(128)} %xor_multiply_fusion.offs, bf16[256,1024]{1,0:T(8,128)(2,1)} %get-tuple-element.351.a0, bf16[256,1024]{1,0:T(8,128)(2,1)} %copy-done.20, ...), custom_call_target="tpu_custom_call" | custom-call | flops 1 | bytes 45000000 | tf_op jit(solution)/shard_map/pallas_call | solution.py:810
  499.5 2.7 collective-permute-start.59
  504.7 3.9 collective-permute-start.64
  512.8 5.0 collective-permute-done.63
  519.3 6.5 %all-to-all-start.3 = ((bf16[16,3,128,128]{3,2,1,0:T(8,128)(2,1)}), bf16[16,3,128,128]{3,2,1,0:T(8,128)(2,1)S(1)}, u32[]{:S(2)}, u32[]{:S(2)}) async-start(bf16[16,3,128,128]{3,2,1,0:T(8,128)(2,1)} %add_convert_fusion.2), calls=%async_computation.3 | async-start | bytes 3145728 | tf_op jit(solution)/shard_map/all_to_all | solution.py:850
  534.1 4.0 shard_map.248
  539.3 17.3 %collective-permute-done.65 = bf16[128,640]{1,0:T(8,128)(2,1)S(1)} collective-permute-done((bf16[128,640]{1,0:T(8,128)(2,1)}, bf16[128,640]{1,0:T(8,128)(2,1)S(1)}, u32[]{:S(2)}, u32[]{:S(2)}) %collective-permute-start.65) | collective-permute-done | bytes 163872 | tf_op jit(solution)/shard_map/ppermute | solution.py:838
  (364 shorter events, 140.0 us)
Async XLA Ops:
  5.1 46.1 %all-to-all-start = ((bf16[16,3,128,128]{3,2,1,0:T(8,128)(2,1)}), bf16[16,3,128,128]{3,2,1,0:T(8,128)(2,1)S(1)}, u32[]{:S(2)}, u32[]{:S(2)}) async-start(bf16[16,3,128,128]{3,2,1,0:T(8,128)(2,1)} %pad_maximum_fusion.2), calls=%async_computation | async-start | bytes 3145728 | tf_op jit(solution)/shard_map/all_to_all | solution.py:552
  11.9 28.1 %collective-permute-start.2 = (bf16[144,896]{1,0:T(8,128)(2,1)S(1)}, bf16[144,896]{1,0:T(8,128)(2,1)S(1)}, u32[]{:S(2)}, u32[]{:S(2)}) collective-permute-start(bf16[144,896]{1,0:T(8,128)(2,1)S(1)} %get-tuple-element.443), channel_id=1, source_target_pairs={{0,24},{8,16},{16,8},{24,0},{1,25},{9,17},{17,9},{25,1},{2,26},{10... | collective-permute-start | bytes 774152 | tf_op jit(solution)/shard_map/ppermute | solution.py:574
  15.9 25.1 %collective-permute-start.1 = (bf16[144,896]{1,0:T(8,128)(2,1)S(1)}, bf16[144,896]{1,0:T(8,128)(2,1)S(1)}, u32[]{:S(2)}, u32[]{:S(2)}) collective-permute-start(bf16[144,896]{1,0:T(8,128)(2,1)S(1)} %get-tuple-element.443), channel_id=1, source_target_pairs={{0,16},{8,24},{16,0},{24,8},{1,17},{9,25},{17,1},{25,9},{2,18},{10... | collective-permute-start | bytes 774152 | tf_op jit(solution)/shard_map/ppermute | solution.py:574
  15.9 32.5 %collective-permute-start = (bf16[144,896]{1,0:T(8,128)(2,1)S(1)}, bf16[144,896]{1,0:T(8,128)(2,1)S(1)}, u32[]{:S(2)}, u32[]{:S(2)}) collective-permute-start(bf16[144,896]{1,0:T(8,128)(2,1)S(1)} %get-tuple-element.443), channel_id=1, source_target_pairs={{0,8},{8,0},{16,24},{24,16},{1,9},{9,1},{17,25},{25,17},{2,10},{10... | collective-permute-start | bytes 774152 | tf_op jit(solution)/shard_map/ppermute | solution.py:574
  16.5 31.8 %collective-permute-start.4 = (bf16[256,1024]{1,0:T(8,128)(2,1)S(1)}, bf16[256,1024]{1,0:T(8,128)(2,1)}, u32[]{:S(2)}, u32[]{:S(2)}) collective-permute-start(bf16[256,1024]{1,0:T(8,128)(2,1)S(1)} %bitcast.141), channel_id=1, source_target_pairs={{0,2},{2,0},{1,3},{3,1},{4,6},{6,4},{5,7},{7,5},{8,10},{10,8},{9,1... | collective-permute-start | bytes 1572872 | tf_op jit(solution)/shard_map/ppermute | solution.py:46
  69.5 64.6 %all-to-all-start.1 = ((bf16[16,3,128,128]{3,2,1,0:T(8,128)(2,1)}), bf16[16,3,128,128]{3,2,1,0:T(8,128)(2,1)S(1)}, u32[]{:S(2)}, u32[]{:S(2)}) async-start(bf16[16,3,128,128]{3,2,1,0:T(8,128)(2,1)} %pad_maximum_fusion.1), calls=%async_computation.1 | async-start | bytes 3145728 | tf_op jit(solution)/shard_map/all_to_all | solution.py:598
  75.5 23.9 %collective-permute-start.8 = (bf16[4,128,384]{2,1,0:T(8,128)(2,1)}, bf16[4,128,384]{2,1,0:T(8,128)(2,1)S(1)}, u32[]{:S(2)}, u32[]{:S(2)}) collective-permute-start(bf16[4,128,384]{2,1,0:T(8,128)(2,1)} %pad_maximum_fusion.9.refs_0_), channel_id=1, source_target_pairs={{0,4},{4,0},{1,5},{5,1},{2,6},{6,2},{3,7},{7,3},{8,12},{12,8},{9,1... | collective-permute-start | bytes 1179656 | tf_op jit(solution)/shard_map/ppermute | solution.py:46
  78.3 25.7 %collective-permute-start.9 = (bf16[4,3,128,128]{3,2,1,0:T(8,128)(2,1)}, bf16[4,3,128,128]{3,2,1,0:T(8,128)(2,1)}, u32[]{:S(2)}, u32[]{:S(2)}) collective-permute-start(bf16[4,3,128,128]{3,2,1,0:T(8,128)(2,1)} %get-tuple-element.213), channel_id=1, source_target_pairs={{0,16},{16,0},{1,17},{17,1},{2,18},{18,2},{3,19},{19,3},{4,20},{20... | collective-permute-start | bytes 1179656 | tf_op jit(solution)/shard_map/ppermute | solution.py:46
  110.1 24.1 %collective-permute-start.11 = (bf16[256,1024]{1,0:T(8,128)(2,1)}, bf16[256,1024]{1,0:T(8,128)(2,1)}, u32[]{:S(2)}, u32[]{:S(2)}) collective-permute-start(bf16[256,1024]{1,0:T(8,128)(2,1)} %fusion.18), channel_id=1, source_target_pairs={{0,2},{2,0},{1,3},{3,1},{4,6},{6,4},{5,7},{7,5},{8,10},{10,8},{9,1... | collective-permute-start | bytes 1572872 | tf_op jit(solution)/shard_map/ppermute | solution.py:46
  113.6 20.5 %collective-permute-start.13 = (bf16[4,3,128,128]{3,2,1,0:T(8,128)(2,1)}, bf16[4,3,128,128]{3,2,1,0:T(8,128)(2,1)}, u32[]{:S(2)}, u32[]{:S(2)}) collective-permute-start(bf16[4,3,128,128]{3,2,1,0:T(8,128)(2,1)} %get-tuple-element.218), channel_id=1, source_target_pairs={{0,16},{16,0},{1,17},{17,1},{2,18},{18,2},{3,19},{19,3},{4,20},{20... | collective-permute-start | bytes 1179656 | tf_op jit(solution)/shard_map/ppermute | solution.py:46
  139.3 18.8 %collective-permute-start.14 = (bf16[256,896]{1,0:T(8,128)(2,1)}, bf16[256,896]{1,0:T(8,128)(2,1)S(1)}, u32[]{:S(2)}, u32[]{:S(2)}) collective-permute-start(bf16[256,896]{1,0:T(8,128)(2,1)} %get-tuple-element.224), channel_id=1, source_target_pairs={{0,8},{8,0},{1,9},{9,1},{2,10},{10,2},{3,11},{11,3},{4,12},{12,4},... | collective-permute-start | bytes 1376264 | tf_op jit(solution)/shard_map/ppermute | solution.py:46
  139.3 18.8 %collective-permute-start.16 = (bf16[256,768]{1,0:T(8,128)(2,1)}, bf16[256,768]{1,0:T(8,128)(2,1)S(1)}, u32[]{:S(2)}, u32[]{:S(2)}) collective-permute-start(bf16[256,768]{1,0:T(8,128)(2,1)} %get-tuple-element.226), channel_id=1, source_target_pairs={{0,2},{2,0},{1,3},{3,1},{4,6},{6,4},{5,7},{7,5},{8,10},{10,8},{9,1... | collective-permute-start | bytes 1179656 | tf_op jit(solution)/shard_map/ppermute | solution.py:46
  139.7 18.4 %collective-permute-start.15 = (bf16[256,512]{1,0:T(8,128)(2,1)}, bf16[256,512]{1,0:T(8,128)(2,1)S(1)}, u32[]{:S(2)}, u32[]{:S(2)}) collective-permute-start(bf16[256,512]{1,0:T(8,128)(2,1)} %get-tuple-element.225), channel_id=1, source_target_pairs={{0,4},{4,0},{1,5},{5,1},{2,6},{6,2},{3,7},{7,3},{8,12},{12,8},{9,1... | collective-permute-start | bytes 786440 | tf_op jit(solution)/shard_map/ppermute | solution.py:46
  139.7 18.3 %collective-permute-start.18 = (s32[2,9,1024]{2,1,0:T(8,128)S(1)}, s32[2,9,1024]{2,1,0:T(8,128)S(1)}, u32[]{:S(2)}, u32[]{:S(2)}) collective-permute-start(s32[2,9,1024]{2,1,0:T(8,128)S(1)} %pad_add_fusion), channel_id=1, source_target_pairs={{0,8},{8,0},{1,9},{9,1},{2,10},{10,2},{3,11},{11,3},{4,12},{12,4},... | collective-permute-start | bytes 221192 | tf_op jit(solution)/shard_map/ppermute | solution.py:46
  159.9 25.5 %collective-permute-start.19 = (bf16[2,256,896]{2,1,0:T(8,128)(2,1)S(1)}, bf16[2,256,896]{2,1,0:T(8,128)(2,1)S(1)}, u32[]{:S(2)}, u32[]{:S(2)}) collective-permute-start(bf16[2,256,896]{2,1,0:T(8,128)(2,1)S(1)} %get-tuple-element.429), channel_id=1, source_target_pairs={{0,4},{4,0},{1,5},{5,1},{2,6},{6,2},{3,7},{7,3},{8,12},{12,8},{9,1... | collective-permute-start | bytes 2752520 | tf_op jit(solution)/shard_map/ppermute | solution.py:46
  160.2 25.3 %collective-permute-start.21 = (bf16[2,256,768]{2,1,0:T(8,128)(2,1)S(1)}, bf16[2,256,768]{2,1,0:T(8,128)(2,1)S(1)}, u32[]{:S(2)}, u32[]{:S(2)}) collective-permute-start(bf16[2,256,768]{2,1,0:T(8,128)(2,1)S(1)} %get-tuple-element.431), channel_id=1, source_target_pairs={{0,8},{8,0},{1,9},{9,1},{2,10},{10,2},{3,11},{11,3},{4,12},{12,4},... | collective-permute-start | bytes 2359304 | tf_op jit(solution)/shard_map/ppermute | solution.py:46
  162.0 22.7 %collective-permute-start.20 = (bf16[2,256,512]{2,1,0:T(8,128)(2,1)S(1)}, bf16[2,256,512]{2,1,0:T(8,128)(2,1)S(1)}, u32[]{:S(2)}, u32[]{:S(2)}) collective-permute-start(bf16[2,256,512]{2,1,0:T(8,128)(2,1)S(1)} %get-tuple-element.436), channel_id=1, source_target_pairs={{0,2},{2,0},{1,3},{3,1},{4,6},{6,4},{5,7},{7,5},{8,10},{10,8},{9,1... | collective-permute-start | bytes 1572872 | tf_op jit(solution)/shard_map/ppermute | solution.py:46
  162.2 22.5 %collective-permute-start.22 = (bf16[3,3,128,128]{3,2,1,0:T(8,128)(2,1)S(1)}, bf16[3,3,128,128]{3,2,1,0:T(8,128)(2,1)S(1)}, u32[]{:S(2)}, u32[]{:S(2)}) collective-permute-start(bf16[3,3,128,128]{3,2,1,0:T(8,128)(2,1)S(1)} %copy-done.46), channel_id=1, source_target_pairs={{0,16},{16,0},{1,17},{17,1},{2,18},{18,2},{3,19},{19,3},{4,20},{20... | collective-permute-start | bytes 884744 | tf_op jit(solution)/shard_map/ppermute | solution.py:46
  185.6 45.1 %collective-permute-start.23 = (bf16[2,2,256,896]{3,2,1,0:T(8,128)(2,1)S(1)}, bf16[2,2,256,896]{3,2,1,0:T(8,128)(2,1)}, u32[]{:S(2)}, u32[]{:S(2)}) collective-permute-start(bf16[2,2,256,896]{3,2,1,0:T(8,128)(2,1)S(1)} %pad_maximum_fusion.refs_0_), channel_id=1, source_target_pairs={{0,2},{2,0},{1,3},{3,1},{4,6},{6,4},{5,7},{7,5},{8,10},{10,8},{9,1... | collective-permute-start | bytes 5505032 | tf_op jit(solution)/shard_map/ppermute | solution.py:46
  187.2 43.6 %collective-permute-start.25 = (bf16[2,2,256,768]{3,2,1,0:T(8,128)(2,1)}, bf16[2,2,256,768]{3,2,1,0:T(8,128)(2,1)}, u32[]{:S(2)}, u32[]{:S(2)}) collective-permute-start(bf16[2,2,256,768]{3,2,1,0:T(8,128)(2,1)} %pad_maximum_fusion.3.refs_8_), channel_id=1, source_target_pairs={{0,4},{4,0},{1,5},{5,1},{2,6},{6,2},{3,7},{7,3},{8,12},{12,8},{9,1... | collective-permute-start | bytes 4718600 | tf_op jit(solution)/shard_map/ppermute | solution.py:46
  190.1 40.6 %collective-permute-start.24 = (bf16[2,2,256,512]{3,2,1,0:T(8,128)(2,1)}, bf16[2,2,256,512]{3,2,1,0:T(8,128)(2,1)}, u32[]{:S(2)}, u32[]{:S(2)}) collective-permute-start(bf16[2,2,256,512]{3,2,1,0:T(8,128)(2,1)} %pad_maximum_fusion.4.refs_4_), channel_id=1, source_target_pairs={{0,8},{8,0},{1,9},{9,1},{2,10},{10,2},{3,11},{11,3},{4,12},{12,4},... | collective-permute-start | bytes 3145736 | tf_op jit(solution)/shard_map/ppermute | solution.py:46
  194.2 35.8 %collective-permute-start.26 = (bf16[8,3,128,128]{3,2,1,0:T(8,128)(2,1)}, bf16[8,3,128,128]{3,2,1,0:T(8,128)(2,1)}, u32[]{:S(2)}, u32[]{:S(2)}) collective-permute-start(bf16[8,3,128,128]{3,2,1,0:T(8,128)(2,1)} %slice.266), channel_id=1, source_target_pairs={{0,16},{16,0},{1,17},{17,1},{2,18},{18,2},{3,19},{19,3},{4,20},{20... | collective-permute-start | bytes 2359304 | tf_op jit(solution)/shard_map/ppermute | solution.py:46
  233.6 19.1 %collective-permute-start.27 = (bf16[2,2,256,896]{3,2,1,0:T(8,128)(2,1)S(1)}, bf16[2,2,256,896]{3,2,1,0:T(8,128)(2,1)S(1)}, u32[]{:S(2)}, u32[]{:S(2)}) collective-permute-start(bf16[2,2,256,896]{3,2,1,0:T(8,128)(2,1)S(1)} %pad_maximum_fusion.refs_0_), channel_id=1, source_target_pairs={{0,1},{1,0},{2,3},{3,2},{4,5},{5,4},{6,7},{7,6},{8,9},{9,8},{10,11... | collective-permute-start | bytes 5505032 | tf_op jit(solution)/shard_map/ppermute | solution.py:46
  233.8 20.2 %collective-permute-start.30 = (bf16[2,2,256,896]{3,2,1,0:T(8,128)(2,1)}, bf16[2,2,256,896]{3,2,1,0:T(8,128)(2,1)S(1)}, u32[]{:S(2)}, u32[]{:S(2)}) collective-permute-start(bf16[2,2,256,896]{3,2,1,0:T(8,128)(2,1)} %collective-permute-done.23.refs_1_), channel_id=1, source_target_pairs={{0,1},{1,0},{2,3},{3,2},{4,5},{5,4},{6,7},{7,6},{8,9},{9,8},{10,11... | collective-permute-start | bytes 5505032 | tf_op jit(solution)/shard_map/ppermute | solution.py:46
  234.1 18.6 %collective-permute-start.29 = (bf16[2,2,256,768]{3,2,1,0:T(8,128)(2,1)}, bf16[2,2,256,768]{3,2,1,0:T(8,128)(2,1)S(1)}, u32[]{:S(2)}, u32[]{:S(2)}) collective-permute-start(bf16[2,2,256,768]{3,2,1,0:T(8,128)(2,1)} %pad_maximum_fusion.3.refs_8_), channel_id=1, source_target_pairs={{0,1},{1,0},{2,3},{3,2},{4,5},{5,4},{6,7},{7,6},{8,9},{9,8},{10,11... | collective-permute-start | bytes 4718600 | tf_op jit(solution)/shard_map/ppermute | solution.py:46
  256.6 24.9 %collective-permute-start.34 = (bf16[5,3,128,128]{3,2,1,0:T(8,128)(2,1)}, bf16[5,3,128,128]{3,2,1,0:T(8,128)(2,1)S(1)}, u32[]{:S(2)}, u32[]{:S(2)}) collective-permute-start(bf16[5,3,128,128]{3,2,1,0:T(8,128)(2,1)} %slice.271), channel_id=1, source_target_pairs={{0,16},{16,0},{1,17},{17,1},{2,18},{18,2},{3,19},{19,3},{4,20},{20... | collective-permute-start | bytes 1474568 | tf_op jit(solution)/shard_map/ppermute | solution.py:46
  290.6 32.7 %collective-permute-start.35 = (bf16[7,3,128,128]{3,2,1,0:T(8,128)(2,1)}, bf16[7,3,128,128]{3,2,1,0:T(8,128)(2,1)S(1)}, u32[]{:S(2)}, u32[]{:S(2)}) collective-permute-start(bf16[7,3,128,128]{3,2,1,0:T(8,128)(2,1)} %get-tuple-element.271), channel_id=1, source_target_pairs={{0,16},{16,0},{1,17},{17,1},{2,18},{18,2},{3,19},{19,3},{4,20},{20... | collective-permute-start | bytes 2064392 | tf_op jit(solution)/shard_map/ppermute | solution.py:46
  323.3 17.5 %collective-permute-start.36 = (bf16[2,2,2,256,896]{4,3,2,1,0:T(8,128)(2,1)}, bf16[2,2,2,256,896]{4,3,2,1,0:T(8,128)(2,1)}, u32[]{:S(2)}, u32[]{:S(2)}) collective-permute-start(bf16[2,2,2,256,896]{4,3,2,1,0:T(8,128)(2,1)} %get-tuple-element.273), channel_id=1, source_target_pairs={{0,1},{1,0},{2,3},{3,2},{4,5},{5,4},{6,7},{7,6},{8,9},{9,8},{10,11... | collective-permute-start | bytes 11010056 | tf_op jit(solution)/shard_map/ppermute | solution.py:46
  323.3 17.5 %collective-permute-start.38 = (bf16[2,2,2,256,768]{4,3,2,1,0:T(8,128)(2,1)}, bf16[2,2,2,256,768]{4,3,2,1,0:T(8,128)(2,1)}, u32[]{:S(2)}, u32[]{:S(2)}) collective-permute-start(bf16[2,2,2,256,768]{4,3,2,1,0:T(8,128)(2,1)} %get-tuple-element.275), channel_id=1, source_target_pairs={{0,1},{1,0},{2,3},{3,2},{4,5},{5,4},{6,7},{7,6},{8,9},{9,8},{10,11... | collective-permute-start | bytes 9437192 | tf_op jit(solution)/shard_map/ppermute | solution.py:46
  323.8 17.0 %collective-permute-start.37 = (bf16[2,2,2,256,512]{4,3,2,1,0:T(8,128)(2,1)}, bf16[2,2,2,256,512]{4,3,2,1,0:T(8,128)(2,1)}, u32[]{:S(2)}, u32[]{:S(2)}) collective-permute-start(bf16[2,2,2,256,512]{4,3,2,1,0:T(8,128)(2,1)} %get-tuple-element.274), channel_id=1, source_target_pairs={{0,1},{1,0},{2,3},{3,2},{4,5},{5,4},{6,7},{7,6},{8,9},{9,8},{10,11... | collective-permute-start | bytes 6291464 | tf_op jit(solution)/shard_map/ppermute | solution.py:46
  347.1 43.4 %collective-permute-start.40 = (bf16[2,2,256,896]{3,2,1,0:T(8,128)(2,1)S(1)}, bf16[2,2,256,896]{3,2,1,0:T(8,128)(2,1)S(1)}, u32[]{:S(2)}, u32[]{:S(2)}) collective-permute-start(bf16[2,2,256,896]{3,2,1,0:T(8,128)(2,1)S(1)} %fusion.4), channel_id=1, source_target_pairs={{0,2},{2,0},{1,3},{3,1},{4,6},{6,4},{5,7},{7,5},{8,10},{10,8},{9,1... | collective-permute-start | bytes 5505032 | tf_op jit(solution)/shard_map/ppermute | solution.py:46
  348.7 41.8 %collective-permute-start.42 = (bf16[2,2,256,768]{3,2,1,0:T(8,128)(2,1)S(1)}, bf16[2,2,256,768]{3,2,1,0:T(8,128)(2,1)S(1)}, u32[]{:S(2)}, u32[]{:S(2)}) collective-permute-start(bf16[2,2,256,768]{3,2,1,0:T(8,128)(2,1)S(1)} %fusion.6), channel_id=1, source_target_pairs={{0,4},{4,0},{1,5},{5,1},{2,6},{6,2},{3,7},{7,3},{8,12},{12,8},{9,1... | collective-permute-start | bytes 4718600 | tf_op jit(solution)/shard_map/ppermute | solution.py:46
  349.3 41.2 %collective-permute-start.41 = (bf16[2,2,256,512]{3,2,1,0:T(8,128)(2,1)S(1)}, bf16[2,2,256,512]{3,2,1,0:T(8,128)(2,1)S(1)}, u32[]{:S(2)}, u32[]{:S(2)}) collective-permute-start(bf16[2,2,256,512]{3,2,1,0:T(8,128)(2,1)S(1)} %fusion.11), channel_id=1, source_target_pairs={{0,8},{8,0},{1,9},{9,1},{2,10},{10,2},{3,11},{11,3},{4,12},{12,4},... | collective-permute-start | bytes 3145736 | tf_op jit(solution)/shard_map/ppermute | solution.py:46
  349.3 27.8 %collective-permute-start.44 = (bf16[2,3,128,128]{3,2,1,0:T(8,128)(2,1)S(1)}, bf16[2,3,128,128]{3,2,1,0:T(8,128)(2,1)S(1)}, u32[]{:S(2)}, u32[]{:S(2)}) collective-permute-start(bf16[2,3,128,128]{3,2,1,0:T(8,128)(2,1)S(1)} %copy-done.72), channel_id=1, source_target_pairs={{0,16},{16,0},{1,17},{17,1},{2,18},{18,2},{3,19},{19,3},{4,20},{20... | collective-permute-start | bytes 589832 | tf_op jit(solution)/shard_map/ppermute | solution.py:46
  352.1 36.2 %collective-permute-start.43 = (bf16[6,3,128,128]{3,2,1,0:T(8,128)(2,1)S(1)}, bf16[6,3,128,128]{3,2,1,0:T(8,128)(2,1)S(1)}, u32[]{:S(2)}, u32[]{:S(2)}) collective-permute-start(bf16[6,3,128,128]{3,2,1,0:T(8,128)(2,1)S(1)} %copy-done.69), channel_id=1, source_target_pairs={{0,16},{16,0},{1,17},{17,1},{2,18},{18,2},{3,19},{19,3},{4,20},{20... | collective-permute-start | bytes 1769480 | tf_op jit(solution)/shard_map/ppermute | solution.py:46
  391.1 28.3 %collective-permute-start.45 = (bf16[2,256,896]{2,1,0:T(8,128)(2,1)S(1)}, bf16[2,256,896]{2,1,0:T(8,128)(2,1)S(1)}, u32[]{:S(2)}, u32[]{:S(2)}) collective-permute-start(bf16[2,256,896]{2,1,0:T(8,128)(2,1)S(1)} %fusion.13), channel_id=1, source_target_pairs={{0,4},{4,0},{1,5},{5,1},{2,6},{6,2},{3,7},{7,3},{8,12},{12,8},{9,1... | collective-permute-start | bytes 2752520 | tf_op jit(solution)/shard_map/ppermute | solution.py:46
  392.5 25.2 %collective-permute-start.46 = (bf16[2,256,512]{2,1,0:T(8,128)(2,1)S(1)}, bf16[2,256,512]{2,1,0:T(8,128)(2,1)S(1)}, u32[]{:S(2)}, u32[]{:S(2)}) collective-permute-start(bf16[2,256,512]{2,1,0:T(8,128)(2,1)S(1)} %fusion.19), channel_id=1, source_target_pairs={{0,2},{2,0},{1,3},{3,1},{4,6},{6,4},{5,7},{7,5},{8,10},{10,8},{9,1... | collective-permute-start | bytes 1572872 | tf_op jit(solution)/shard_map/ppermute | solution.py:46
  393.1 26.4 %collective-permute-start.47 = (bf16[2,256,768]{2,1,0:T(8,128)(2,1)S(1)}, bf16[2,256,768]{2,1,0:T(8,128)(2,1)S(1)}, u32[]{:S(2)}, u32[]{:S(2)}) collective-permute-start(bf16[2,256,768]{2,1,0:T(8,128)(2,1)S(1)} %fusion.15), channel_id=1, source_target_pairs={{0,8},{8,0},{1,9},{9,1},{2,10},{10,2},{3,11},{11,3},{4,12},{12,4},... | collective-permute-start | bytes 2359304 | tf_op jit(solution)/shard_map/ppermute | solution.py:46
  394.4 23.3 %collective-permute-start.48 = (bf16[4,3,128,128]{3,2,1,0:T(8,128)(2,1)S(1)}, bf16[4,3,128,128]{3,2,1,0:T(8,128)(2,1)S(1)}, u32[]{:S(2)}, u32[]{:S(2)}) collective-permute-start(bf16[4,3,128,128]{3,2,1,0:T(8,128)(2,1)S(1)} %copy-done.70), channel_id=1, source_target_pairs={{0,16},{16,0},{1,17},{17,1},{2,18},{18,2},{3,19},{19,3},{4,20},{20... | collective-permute-start | bytes 1179656 | tf_op jit(solution)/shard_map/ppermute | solution.py:46
  442.6 17.3 %collective-permute-start.54 = (bf16[256,1024]{1,0:T(8,128)(2,1)}, bf16[256,1024]{1,0:T(8,128)(2,1)S(1)}, u32[]{:S(2)}, u32[]{:S(2)}) collective-permute-start(bf16[256,1024]{1,0:T(8,128)(2,1)} %get-tuple-element.351.a0), channel_id=1, source_target_pairs={{0,2},{2,0},{1,3},{3,1},{4,6},{6,4},{5,7},{7,5},{8,10},{10,8},{9,1... | collective-permute-start | bytes 1572872 | tf_op jit(solution)/shard_map/ppermute | solution.py:46
  466.5 52.8 %all-to-all-start.2 = ((bf16[16,3,128,128]{3,2,1,0:T(8,128)(2,1)}), bf16[16,3,128,128]{3,2,1,0:T(8,128)(2,1)S(1)}, u32[]{:S(2)}, u32[]{:S(2)}) async-start(bf16[16,3,128,128]{3,2,1,0:T(8,128)(2,1)} %add_convert_fusion.3), calls=%async_computation.2 | async-start | bytes 3145728 | tf_op jit(solution)/shard_map/all_to_all | solution.py:806
  470.7 28.5 %collective-permute-start.58 = (bf16[5,3,128,128]{3,2,1,0:T(8,128)(2,1)}, bf16[5,3,128,128]{3,2,1,0:T(8,128)(2,1)S(1)}, u32[]{:S(2)}, u32[]{:S(2)}) collective-permute-start(bf16[5,3,128,128]{3,2,1,0:T(8,128)(2,1)} %get-tuple-element.366), channel_id=1, source_target_pairs={{0,16},{16,0},{1,17},{17,1},{2,18},{18,2},{3,19},{19,3},{4,20},{20... | collective-permute-start | bytes 1474568 | tf_op jit(solution)/shard_map/ppermute | solution.py:46
  473.2 26.1 %collective-permute-start.57 = (bf16[4,128,384]{2,1,0:T(8,128)(2,1)}, bf16[4,128,384]{2,1,0:T(8,128)(2,1)S(1)}, u32[]{:S(2)}, u32[]{:S(2)}) collective-permute-start(bf16[4,128,384]{2,1,0:T(8,128)(2,1)} %get-tuple-element.350), channel_id=1, source_target_pairs={{0,4},{4,0},{1,5},{5,1},{2,6},{6,2},{3,7},{7,3},{8,12},{12,8},{9,1... | collective-permute-start | bytes 1179656 | tf_op jit(solution)/shard_map/ppermute | solution.py:46
  499.5 18.3 %collective-permute-start.59 = (bf16[4,128,640]{2,1,0:T(8,128)(2,1)}, bf16[4,128,640]{2,1,0:T(8,128)(2,1)S(1)}, u32[]{:S(2)}, u32[]{:S(2)}) collective-permute-start(bf16[4,128,640]{2,1,0:T(8,128)(2,1)} %get-tuple-element.369), channel_id=1, source_target_pairs={{0,4},{4,0},{1,5},{5,1},{2,6},{6,2},{3,7},{7,3},{8,12},{12,8},{9,1... | collective-permute-start | bytes 1966088 | tf_op jit(solution)/shard_map/ppermute | solution.py:46
  519.3 45.5 %all-to-all-start.3 = ((bf16[16,3,128,128]{3,2,1,0:T(8,128)(2,1)}), bf16[16,3,128,128]{3,2,1,0:T(8,128)(2,1)S(1)}, u32[]{:S(2)}, u32[]{:S(2)}) async-start(bf16[16,3,128,128]{3,2,1,0:T(8,128)(2,1)} %add_convert_fusion.2), calls=%async_computation.3 | async-start | bytes 3145728 | tf_op jit(solution)/shard_map/all_to_all | solution.py:850
  530.6 26.0 %collective-permute-start.65 = (bf16[128,640]{1,0:T(8,128)(2,1)}, bf16[128,640]{1,0:T(8,128)(2,1)S(1)}, u32[]{:S(2)}, u32[]{:S(2)}) collective-permute-start(bf16[128,640]{1,0:T(8,128)(2,1)} %get-tuple-element.432), channel_id=1, source_target_pairs={{0,8},{8,0},{16,24},{24,16},{1,9},{9,1},{17,25},{25,17},{2,10},{10... | collective-permute-start | bytes 491528 | tf_op jit(solution)/shard_map/ppermute | solution.py:838
  532.5 24.1 %collective-permute-start.67 = (bf16[128,640]{1,0:T(8,128)(2,1)S(1)}, bf16[128,640]{1,0:T(8,128)(2,1)S(1)}, u32[]{:S(2)}, u32[]{:S(2)}) collective-permute-start(bf16[128,640]{1,0:T(8,128)(2,1)S(1)} %get-tuple-element.433), channel_id=1, source_target_pairs={{0,24},{8,16},{16,8},{24,0},{1,25},{9,17},{17,9},{25,1},{2,26},{10... | collective-permute-start | bytes 491528 | tf_op jit(solution)/shard_map/ppermute | solution.py:838
  532.5 24.1 %collective-permute-start.66 = (bf16[128,640]{1,0:T(8,128)(2,1)S(1)}, bf16[128,640]{1,0:T(8,128)(2,1)}, u32[]{:S(2)}, u32[]{:S(2)}) collective-permute-start(bf16[128,640]{1,0:T(8,128)(2,1)S(1)} %get-tuple-element.434), channel_id=1, source_target_pairs={{0,16},{8,24},{16,0},{24,8},{1,17},{9,25},{17,1},{25,9},{2,18},{10... | collective-permute-start | bytes 491528 | tf_op jit(solution)/shard_map/ppermute | solution.py:838
  (100 other events, 905.8 us)

commit v5 on v4

--- a/solution.py
+++ b/solution.py
@@ -18,7 +18,7 @@
 TOK = (512, 256, 256)
 SECOND = (384, 256, 384)
 NOTES = 128
-PARTS_IN = ((3, 4, 4, 2, 3), (8, 3, 5))
+PARTS_IN = ((3, 6, 3, 2, 2), (8, 3, 5))
 PARTS_OUT = ((7, 3, 6), (2, 4, 2, 3, 5))
 BLK = 256
 BF = jnp.bfloat16
@@ -470,7 +470,7 @@
     came = together([swap(send, "c") for send in other], *moving)
     before = list(zip(kept, came))
     for step in range(1, 4):
-        sends = together([add(a[1], b[1]) for a, b in before])
+        sends = [add(a[1], b[1]) for a, b in before]
         moving = fill(step, came)
         came = [swap(send, order[3 - step]) for send, order in zip(sends, ORDERS)]
         flat = together([value for pair in before for value in pair], *sends)
@@ -778,7 +778,9 @@
     )(after, *pairs[0], *pairs[1], *pairs[2], gains, wob, gates, cot)
     near, cross = swap(aog, "c"), swap(aog, "x")
     moving = part_out(1, pairs[0][1])
-    near, cross = together((near, cross), *moving)
+    if n_outer == 2:
+        first_sum = total(first_grads[-1], parts_out[0])
+        near, cross, first_sum = together((near, cross, first_sum), *moving)
     aog_parts = [aog, near, cross, swap(cross, "c")]
 
     n_tails = 2 if n_dp == 8 else 1
@@ -797,7 +799,7 @@
     aog_parts = together(aog_parts, *sides)
     moving = part_out(1, cross)
     if n_outer == 2:
-        first_sum = after_all(total(first_grads[-1], parts_out[0]), *aog_parts)
+        first_sum = after_all(first_sum, *aog_parts)
     else:
         first_sum, last_sum = (
             lax.psum_scatter(g[0], "o", scatter_dimension=0, tiled=True)

time: 574 us -> 566 us (0.986)
  waiting for transfers between devices: 258 us -> 244 us
  starting transfers between devices: 98.6 us -> 105 us
    ppermute x59, waiting for transfers between devices: 213 us -> 198 us  [swap(): return lax.ppermute(value, axis, [(0, 1), (1, 0)])]
    ppermute x59, starting transfers between devices: 60.6 us -> 67.8 us  [swap(): return lax.ppermute(value, axis, [(0, 1), (1, 0)])]
  transfers between devices with their start and end apart: 75 -> 75, of which waited for: 31 -> 34; matrix products, arithmetic and copies ran while one was open for 10% -> 11% of each run, Pallas kernels for 18% -> 18%
where the time goes in v5:
time: 566 us; the launch traced here: 561 us
  waiting for transfers between devices  244 us (43%)
  Pallas kernels  127 us (22%)
  starting transfers between devices  105 us (19%)
  other arithmetic  52.5 us (9%)
  local copies, waits for them, and re-layouts  28.3 us (5%)
    ppermute x59, waiting for transfers between devices, swap(): return lax.ppermute(value, axis, [(0, 1), (1, 0)])  198 us
    ppermute x59, starting transfers between devices, swap(): return lax.ppermute(value, axis, [(0, 1), (1, 0)])  67.8 us
    pallas_call x2, Pallas kernels, local(): pl.pallas_call(functools.partial(expert_kernel, len(ready_mats(j)), j ==...  53 us
    ppermute x6, waiting for transfers between devices, reduce_z(): lax.ppermute(sums[s], ('o', 'u'), [(i, i ^ s) for i in range(4)])  22.5 us
    pallas_call x1, Pallas kernels, local(): simple_call(functools.partial(attend_backward_kernel, n_tails), [((2, row...  22.1 us
    ppermute x3, waiting for transfers between devices, local(): lax.ppermute(pack, ('o', 'u'), [(i, i ^ s) for i in range(4)])  21.1 us
    pallas_call x2, Pallas kernels, weight_grads_of(): pl.pallas_call(functools.partial(weight_grad_kernel, chunk // shard * 4),...  18.9 us
    convert_element_type x18, other arithmetic, scatter_pool(): add = lambda a, b: (a.astype(F32) + b.astype(F32)).astype(BF)  14.7 us
  transfers between devices with their start and end apart: 75, of which 34 were waited for; matrix products, arithmetic and copies ran while one was open for 11% of the time, Pallas kernels for 18%

profile of v5, /device:TPU:0, one launch (start us, length us, event | category | flops | bytes accessed | tf_op | source)
XLA Modules:
  0.0 561.4 jit_solution(3259863661471109496)
XLA Ops:
  5.1 6.4 %all-to-all-start = ((bf16[16,3,128,128]{3,2,1,0:T(8,128)(2,1)}), bf16[16,3,128,128]{3,2,1,0:T(8,128)(2,1)S(1)}, u32[]{:S(2)}, u32[]{:S(2)}) async-start(bf16[16,3,128,128]{3,2,1,0:T(8,128)(2,1)} %pad_maximum_fusion.2), calls=%async_computation | async-start | bytes 3145728 | tf_op jit(solution)/shard_map/all_to_all | solution.py:552
  11.9 4.0 collective-permute-start.2
  21.5 2.6 compare_select_fusion.3
  24.2 3.1 fusion.17
  27.2 12.7 %collective-permute-done.2 = bf16[144,896]{1,0:T(8,128)(2,1)S(1)} collective-permute-done((bf16[144,896]{1,0:T(8,128)(2,1)S(1)}, bf16[144,896]{1,0:T(8,128)(2,1)S(1)}, u32[]{:S(2)}, u32[]{:S(2)}) %collective-permute-start.2) | collective-permute-done | bytes 258080 | tf_op jit(solution)/shard_map/ppermute | solution.py:574
  41.0 7.4 %collective-permute-done = bf16[144,896]{1,0:T(8,128)(2,1)S(1)} collective-permute-done((bf16[144,896]{1,0:T(8,128)(2,1)S(1)}, bf16[144,896]{1,0:T(8,128)(2,1)S(1)}, u32[]{:S(2)}, u32[]{:S(2)}) %collective-permute-start) | collective-permute-done | bytes 258080 | tf_op jit(solution)/shard_map/ppermute | solution.py:574
  48.6 2.6 collective-permute-start.6
  52.1 2.7 collective-permute-start.7
  57.3 7.2 %collective-permute-done.6.refs_1_ = bf16[4,144,512]{2,1,0:T(8,128)(2,1)} collective-permute-done((bf16[4,144,512]{2,1,0:T(8,128)(2,1)S(1)}, bf16[4,144,512]{2,1,0:T(8,128)(2,1)}, u32[]{:S(2)}, u32[]{:S(2)}) %collective-permute-start.6) | collective-permute-done | bytes 589856 | tf_op jit(solution)/shard_map/ppermute | solution.py:46
  64.5 4.3 collective-permute-done.7.refs_14_
  69.5 4.2 all-to-all-start.1
  82.0 11.0 %shard_map.238 = (bf16[1024,1024]{1,0:T(8,128)(2,1)}, bf16[1024,512]{1,0:T(8,128)(2,1)}, f32[8,1024]{1,0:T(8,128)}, bf16[1024,256]{1,0:T(8,128)(2,1)}, bf16[2,10...) custom-call(s32[8]{0:T(128)} %fusion.47.table.dests, ...), custom_call_target="tpu_custom_call" | custom-call | flops 1 | bytes 8250000 | tf_op jit(solution)/shard_map/pallas_call | solution.py:604
  95.9 3.9 shard_map.239
  99.8 4.2 collective-permute-done.9.refs_15_
  104.0 2.9 collective-permute-done.10.got
  112.5 3.4 collective-permute-start.13
  121.0 8.6 %collective-permute-done.13.refs_16_ = bf16[3,3,128,128]{3,2,1,0:T(8,128)(2,1)} collective-permute-done((bf16[3,3,128,128]{3,2,1,0:T(8,128)(2,1)}, bf16[3,3,128,128]{3,2,1,0:T(8,128)(2,1)}, u32[]{:S(2)}, u32[]{:S(2)}) %collective-permute-start.13) | collective-permute-done | bytes 294944 | tf_op jit(solution)/shard_map/ppermute | solution.py:46
  129.6 5.1 shard_map.240
  140.0 15.5 %collective-permute-done.18 = s32[2,9,1024]{2,1,0:T(8,128)S(1)} collective-permute-done((s32[2,9,1024]{2,1,0:T(8,128)S(1)}, s32[2,9,1024]{2,1,0:T(8,128)S(1)}, u32[]{:S(2)}, u32[]{:S(2)}) %collective-permute-start.18) | collective-permute-done | bytes 73760 | tf_op jit(solution)/shard_map/ppermute | solution.py:46
  162.7 15.9 %collective-permute-done.22.refs_18_ = bf16[2,3,128,128]{3,2,1,0:T(8,128)(2,1)S(1)} collective-permute-done((bf16[2,3,128,128]{3,2,1,0:T(8,128)(2,1)S(1)}, bf16[2,3,128,128]{3,2,1,0:T(8,128)(2,1)S(1)}, u32[]{:S(2)}, u32[]{:S(2)}) %collective-permute-start.22) | collective-permute-done | bytes 196640 | tf_op jit(solution)/shard_map/ppermute | solution.py:46
  190.4 2.9 and_select_fusion
  193.6 28.8 %collective-permute-done.26.refs_14_ = bf16[8,3,128,128]{3,2,1,0:T(8,128)(2,1)} collective-permute-done((bf16[8,3,128,128]{3,2,1,0:T(8,128)(2,1)}, bf16[8,3,128,128]{3,2,1,0:T(8,128)(2,1)}, u32[]{:S(2)}, u32[]{:S(2)}) %collective-permute-start.26) | collective-permute-done | bytes 786464 | tf_op jit(solution)/shard_map/ppermute | solution.py:46
  226.7 13.4 %collective-permute-done.33.refs_15_ = bf16[3,3,128,128]{3,2,1,0:T(8,128)(2,1)S(1)} collective-permute-done((bf16[3,3,128,128]{3,2,1,0:T(8,128)(2,1)S(1)}, bf16[3,3,128,128]{3,2,1,0:T(8,128)(2,1)S(1)}, u32[]{:S(2)}, u32[]{:S(2)}) %collective-permute-start.33) | collective-permute-done | bytes 294944 | tf_op jit(solution)/shard_map/ppermute | solution.py:46
  241.8 3.6 collective-permute-done.31.refs_7_
  250.5 20.6 %shard_map.241 = (bf16[1024,896]{1,0:T(8,128)(2,1)}, bf16[1024,512]{1,0:T(8,128)(2,1)}, bf16[1024,768]{1,0:T(8,128)(2,1)}, bf16[1024,1024]{1,0:T(8,128)(2,1)}, b...) custom-call(s32[7]{0:T(128)} %get-tuple-element.248.meta, ...), custom_call_target="tpu_custom_call" | custom-call | flops 1 | bytes 21750000 | tf_op jit(solution)/shard_map/pallas_call | solution.py:730
  271.1 3.0 collective-permute-done.34.refs_16_
  274.1 9.1 %shard_map.242 = (bf16[7,3,128,128]{3,2,1,0:T(8,128)(2,1)}, bf16[3,3,128,128]{3,2,1,0:T(8,128)(2,1)}, bf16[6,3,128,128]{3,2,1,0:T(8,128)(2,1)}, bf16[16,3,128,128]{3,2,1,0:T(8,128)(2,1)}) custom-call(s32[7]{0:T(128)} %get-tuple-element.248.meta, bf16[1024,1024]{1,0:T(8,128)(2,1)} %get-tuple-element.249.picked, bf16[1024,1024]{1,0:T(8,128)(2,1)} %get-tuple-element.250.dy, ...), custom_call_target="tpu_custom_call" | custom-call | flops 1 | bytes 6750000 | tf_op jit(solution)/shard_map/pallas_call | solution.py:698
  283.2 32.5 %shard_map.243 = (bf16[2,2,2,256,896]{4,3,2,1,0:T(8,128)(2,1)}, bf16[2,2,2,256,512]{4,3,2,1,0:T(8,128)(2,1)}, bf16[2,2,2,256,768]{4,3,2,1,0:T(8,128)(2,1)}, bf16...) custom-call(s32[7]{0:T(128)} %get-tuple-element.270.meta, ...), custom_call_target="tpu_custom_call" | custom-call | flops 1 | bytes 21750000 | tf_op jit(solution)/shard_map/pallas_call | solution.py:730
  316.6 2.7 collective-permute-start.39
  319.3 9.8 %shard_map.244 = (bf16[2,3,128,128]{3,2,1,0:T(8,128)(2,1)}, bf16[4,3,128,128]{3,2,1,0:T(8,128)(2,1)}, bf16[2,3,128,128]{3,2,1,0:T(8,128)(2,1)}, bf16[3,3,128,128...) custom-call(s32[7]{0:T(128)} %get-tuple-element.270.meta, ...), custom_call_target="tpu_custom_call" | custom-call | flops 1 | bytes 6750000 | tf_op jit(solution)/shard_map/pallas_call | solution.py:698
  329.0 4.4 collective-permute-done.39
  341.4 3.3 collective-permute-start.44
  350.0 19.2 %collective-permute-done.44 = bf16[2,3,128,128]{3,2,1,0:T(8,128)(2,1)S(1)} collective-permute-done((bf16[2,3,128,128]{3,2,1,0:T(8,128)(2,1)S(1)}, bf16[2,3,128,128]{3,2,1,0:T(8,128)(2,1)S(1)}, u32[]{:S(2)}, u32[]{:S(2)}) %collective-permute-start.44) | collective-permute-done | bytes 196640 | tf_op jit(solution)/shard_map/ppermute | solution.py:46
  369.2 10.9 %collective-permute-done.43 = bf16[6,3,128,128]{3,2,1,0:T(8,128)(2,1)S(1)} collective-permute-done((bf16[6,3,128,128]{3,2,1,0:T(8,128)(2,1)S(1)}, bf16[6,3,128,128]{3,2,1,0:T(8,128)(2,1)S(1)}, u32[]{:S(2)}, u32[]{:S(2)}) %collective-permute-start.43) | collective-permute-done | bytes 589856 | tf_op jit(solution)/shard_map/ppermute | solution.py:46
  388.6 21.0 %collective-permute-done.48 = bf16[4,3,128,128]{3,2,1,0:T(8,128)(2,1)S(1)} collective-permute-done((bf16[4,3,128,128]{3,2,1,0:T(8,128)(2,1)S(1)}, bf16[4,3,128,128]{3,2,1,0:T(8,128)(2,1)S(1)}, u32[]{:S(2)}, u32[]{:S(2)}) %collective-permute-start.48) | collective-permute-done | bytes 393248 | tf_op jit(solution)/shard_map/ppermute | solution.py:46
  419.8 7.1 %collective-permute-done.52 = bf16[2,3,128,128]{3,2,1,0:T(8,128)(2,1)S(1)} collective-permute-done((bf16[2,3,128,128]{3,2,1,0:T(8,128)(2,1)S(1)}, bf16[2,3,128,128]{3,2,1,0:T(8,128)(2,1)S(1)}, u32[]{:S(2)}, u32[]{:S(2)}) %collective-permute-start.52) | collective-permute-done | bytes 196640 | tf_op jit(solution)/shard_map/ppermute | solution.py:46
  429.3 5.2 shard_map.245
  437.6 2.9 add_convert_fusion.3
  440.5 11.6 %collective-permute-done.55 = bf16[3,3,128,128]{3,2,1,0:T(8,128)(2,1)S(1)} collective-permute-done((bf16[3,3,128,128]{3,2,1,0:T(8,128)(2,1)}, bf16[3,3,128,128]{3,2,1,0:T(8,128)(2,1)S(1)}, u32[]{:S(2)}, u32[]{:S(2)}) %collective-permute-start.55) | collective-permute-done | bytes 294944 | tf_op jit(solution)/shard_map/ppermute | solution.py:46
  454.9 3.7 shard_map.246
  458.6 4.3 all-to-all-start.2
  466.8 22.1 %shard_map.247 = (f32[2,256,1024]{2,1,0:T(8,128)}, bf16[2,256,1024]{2,1,0:T(8,128)(2,1)}, bf16[4,128,640]{2,1,0:T(8,128)(2,1)}, bf16[4,128,640]{2,1,0:T(8,128)(2,1)}) custom-call(s32[8]{0:T(128)} %fusion.47.table.dests, s32[4]{0:T(128)} %xor_multiply_fusion.offs, bf16[256,1024]{1,0:T(8,128)(2,1)} %get-tuple-element.335.a0, bf16[256,1024]{1,0:T(8,128)(2,1)} %copy-done.20, ...), custom_call_target="tpu_custom_call" | custom-call | flops 1 | bytes 45000000 | tf_op jit(solution)/shard_map/pallas_call | solution.py:812
  491.7 2.7 collective-permute-start.59
  496.9 3.4 collective-permute-start.64
  504.5 5.2 collective-permute-done.63
  511.2 6.3 %all-to-all-start.3 = ((bf16[16,3,128,128]{3,2,1,0:T(8,128)(2,1)}), bf16[16,3,128,128]{3,2,1,0:T(8,128)(2,1)S(1)}, u32[]{:S(2)}, u32[]{:S(2)}) async-start(bf16[16,3,128,128]{3,2,1,0:T(8,128)(2,1)} %add_convert_fusion.2), calls=%async_computation.3 | async-start | bytes 3145728 | tf_op jit(solution)/shard_map/all_to_all | solution.py:852
  525.8 4.0 shard_map.248
  531.0 17.3 %collective-permute-done.65 = bf16[128,640]{1,0:T(8,128)(2,1)S(1)} collective-permute-done((bf16[128,640]{1,0:T(8,128)(2,1)}, bf16[128,640]{1,0:T(8,128)(2,1)S(1)}, u32[]{:S(2)}, u32[]{:S(2)}) %collective-permute-start.65) | collective-permute-done | bytes 163872 | tf_op jit(solution)/shard_map/ppermute | solution.py:840
  (364 shorter events, 151.1 us)
Async XLA Ops:
  5.1 46.1 %all-to-all-start = ((bf16[16,3,128,128]{3,2,1,0:T(8,128)(2,1)}), bf16[16,3,128,128]{3,2,1,0:T(8,128)(2,1)S(1)}, u32[]{:S(2)}, u32[]{:S(2)}) async-start(bf16[16,3,128,128]{3,2,1,0:T(8,128)(2,1)} %pad_maximum_fusion.2), calls=%async_computation | async-start | bytes 3145728 | tf_op jit(solution)/shard_map/all_to_all | solution.py:552
  11.9 28.1 %collective-permute-start.2 = (bf16[144,896]{1,0:T(8,128)(2,1)S(1)}, bf16[144,896]{1,0:T(8,128)(2,1)S(1)}, u32[]{:S(2)}, u32[]{:S(2)}) collective-permute-start(bf16[144,896]{1,0:T(8,128)(2,1)S(1)} %get-tuple-element.427), channel_id=1, source_target_pairs={{0,24},{8,16},{16,8},{24,0},{1,25},{9,17},{17,9},{25,1},{2,26},{10... | collective-permute-start | bytes 774152 | tf_op jit(solution)/shard_map/ppermute | solution.py:574
  15.9 25.1 %collective-permute-start.1 = (bf16[144,896]{1,0:T(8,128)(2,1)S(1)}, bf16[144,896]{1,0:T(8,128)(2,1)S(1)}, u32[]{:S(2)}, u32[]{:S(2)}) collective-permute-start(bf16[144,896]{1,0:T(8,128)(2,1)S(1)} %get-tuple-element.427), channel_id=1, source_target_pairs={{0,16},{8,24},{16,0},{24,8},{1,17},{9,25},{17,1},{25,9},{2,18},{10... | collective-permute-start | bytes 774152 | tf_op jit(solution)/shard_map/ppermute | solution.py:574
  15.9 32.5 %collective-permute-start = (bf16[144,896]{1,0:T(8,128)(2,1)S(1)}, bf16[144,896]{1,0:T(8,128)(2,1)S(1)}, u32[]{:S(2)}, u32[]{:S(2)}) collective-permute-start(bf16[144,896]{1,0:T(8,128)(2,1)S(1)} %get-tuple-element.427), channel_id=1, source_target_pairs={{0,8},{8,0},{16,24},{24,16},{1,9},{9,1},{17,25},{25,17},{2,10},{10... | collective-permute-start | bytes 774152 | tf_op jit(solution)/shard_map/ppermute | solution.py:574
  16.5 31.8 %collective-permute-start.4 = (bf16[256,1024]{1,0:T(8,128)(2,1)S(1)}, bf16[256,1024]{1,0:T(8,128)(2,1)}, u32[]{:S(2)}, u32[]{:S(2)}) collective-permute-start(bf16[256,1024]{1,0:T(8,128)(2,1)S(1)} %bitcast.141), channel_id=1, source_target_pairs={{0,2},{2,0},{1,3},{3,1},{4,6},{6,4},{5,7},{7,5},{8,10},{10,8},{9,1... | collective-permute-start | bytes 1572872 | tf_op jit(solution)/shard_map/ppermute | solution.py:46
  69.5 60.1 %all-to-all-start.1 = ((bf16[16,3,128,128]{3,2,1,0:T(8,128)(2,1)}), bf16[16,3,128,128]{3,2,1,0:T(8,128)(2,1)S(1)}, u32[]{:S(2)}, u32[]{:S(2)}) async-start(bf16[16,3,128,128]{3,2,1,0:T(8,128)(2,1)} %pad_maximum_fusion.1), calls=%async_computation.1 | async-start | bytes 3145728 | tf_op jit(solution)/shard_map/all_to_all | solution.py:598
  74.6 29.5 %collective-permute-start.9 = (bf16[6,3,128,128]{3,2,1,0:T(8,128)(2,1)}, bf16[6,3,128,128]{3,2,1,0:T(8,128)(2,1)}, u32[]{:S(2)}, u32[]{:S(2)}) collective-permute-start(bf16[6,3,128,128]{3,2,1,0:T(8,128)(2,1)} %slice.336), channel_id=1, source_target_pairs={{0,16},{16,0},{1,17},{17,1},{2,18},{18,2},{3,19},{19,3},{4,20},{20... | collective-permute-start | bytes 1769480 | tf_op jit(solution)/shard_map/ppermute | solution.py:46
  77.4 17.7 %collective-permute-start.8 = (bf16[4,128,384]{2,1,0:T(8,128)(2,1)}, bf16[4,128,384]{2,1,0:T(8,128)(2,1)S(1)}, u32[]{:S(2)}, u32[]{:S(2)}) collective-permute-start(bf16[4,128,384]{2,1,0:T(8,128)(2,1)} %pad_maximum_fusion.9.refs_0_), channel_id=1, source_target_pairs={{0,4},{4,0},{1,5},{5,1},{2,6},{6,2},{3,7},{7,3},{8,12},{12,8},{9,1... | collective-permute-start | bytes 1179656 | tf_op jit(solution)/shard_map/ppermute | solution.py:46
  110.0 19.5 %collective-permute-start.11 = (bf16[256,1024]{1,0:T(8,128)(2,1)}, bf16[256,1024]{1,0:T(8,128)(2,1)}, u32[]{:S(2)}, u32[]{:S(2)}) collective-permute-start(bf16[256,1024]{1,0:T(8,128)(2,1)} %fusion.18), channel_id=1, source_target_pairs={{0,2},{2,0},{1,3},{3,1},{4,6},{6,4},{5,7},{7,5},{8,10},{10,8},{9,1... | collective-permute-start | bytes 1572872 | tf_op jit(solution)/shard_map/ppermute | solution.py:46
  112.5 17.0 %collective-permute-start.13 = (bf16[3,3,128,128]{3,2,1,0:T(8,128)(2,1)}, bf16[3,3,128,128]{3,2,1,0:T(8,128)(2,1)}, u32[]{:S(2)}, u32[]{:S(2)}) collective-permute-start(bf16[3,3,128,128]{3,2,1,0:T(8,128)(2,1)} %get-tuple-element.210), channel_id=1, source_target_pairs={{0,16},{16,0},{1,17},{17,1},{2,18},{18,2},{3,19},{19,3},{4,20},{20... | collective-permute-start | bytes 884744 | tf_op jit(solution)/shard_map/ppermute | solution.py:46
  134.7 20.8 %collective-permute-start.15 = (bf16[256,512]{1,0:T(8,128)(2,1)}, bf16[256,512]{1,0:T(8,128)(2,1)S(1)}, u32[]{:S(2)}, u32[]{:S(2)}) collective-permute-start(bf16[256,512]{1,0:T(8,128)(2,1)} %get-tuple-element.217), channel_id=1, source_target_pairs={{0,4},{4,0},{1,5},{5,1},{2,6},{6,2},{3,7},{7,3},{8,12},{12,8},{9,1... | collective-permute-start | bytes 786440 | tf_op jit(solution)/shard_map/ppermute | solution.py:46
  135.9 19.6 %collective-permute-start.16 = (bf16[256,768]{1,0:T(8,128)(2,1)}, bf16[256,768]{1,0:T(8,128)(2,1)S(1)}, u32[]{:S(2)}, u32[]{:S(2)}) collective-permute-start(bf16[256,768]{1,0:T(8,128)(2,1)} %get-tuple-element.218), channel_id=1, source_target_pairs={{0,2},{2,0},{1,3},{3,1},{4,6},{6,4},{5,7},{7,5},{8,10},{10,8},{9,1... | collective-permute-start | bytes 1179656 | tf_op jit(solution)/shard_map/ppermute | solution.py:46
  137.1 18.5 %collective-permute-start.14 = (bf16[256,896]{1,0:T(8,128)(2,1)}, bf16[256,896]{1,0:T(8,128)(2,1)S(1)}, u32[]{:S(2)}, u32[]{:S(2)}) collective-permute-start(bf16[256,896]{1,0:T(8,128)(2,1)} %get-tuple-element.216), channel_id=1, source_target_pairs={{0,8},{8,0},{1,9},{9,1},{2,10},{10,2},{3,11},{11,3},{4,12},{12,4},... | collective-permute-start | bytes 1376264 | tf_op jit(solution)/shard_map/ppermute | solution.py:46
  137.1 18.4 %collective-permute-start.18 = (s32[2,9,1024]{2,1,0:T(8,128)S(1)}, s32[2,9,1024]{2,1,0:T(8,128)S(1)}, u32[]{:S(2)}, u32[]{:S(2)}) collective-permute-start(s32[2,9,1024]{2,1,0:T(8,128)S(1)} %pad_add_fusion), channel_id=1, source_target_pairs={{0,8},{8,0},{1,9},{9,1},{2,10},{10,2},{3,11},{11,3},{4,12},{12,4},... | collective-permute-start | bytes 221192 | tf_op jit(solution)/shard_map/ppermute | solution.py:46
  157.4 22.1 %collective-permute-start.19 = (bf16[2,256,896]{2,1,0:T(8,128)(2,1)S(1)}, bf16[2,256,896]{2,1,0:T(8,128)(2,1)S(1)}, u32[]{:S(2)}, u32[]{:S(2)}) collective-permute-start(bf16[2,256,896]{2,1,0:T(8,128)(2,1)S(1)} %get-tuple-element.413), channel_id=1, source_target_pairs={{0,4},{4,0},{1,5},{5,1},{2,6},{6,2},{3,7},{7,3},{8,12},{12,8},{9,1... | collective-permute-start | bytes 2752520 | tf_op jit(solution)/shard_map/ppermute | solution.py:46
  157.9 21.5 %collective-permute-start.21 = (bf16[2,256,768]{2,1,0:T(8,128)(2,1)S(1)}, bf16[2,256,768]{2,1,0:T(8,128)(2,1)S(1)}, u32[]{:S(2)}, u32[]{:S(2)}) collective-permute-start(bf16[2,256,768]{2,1,0:T(8,128)(2,1)S(1)} %get-tuple-element.415), channel_id=1, source_target_pairs={{0,8},{8,0},{1,9},{9,1},{2,10},{10,2},{3,11},{11,3},{4,12},{12,4},... | collective-permute-start | bytes 2359304 | tf_op jit(solution)/shard_map/ppermute | solution.py:46
  159.4 19.3 %collective-permute-start.20 = (bf16[2,256,512]{2,1,0:T(8,128)(2,1)S(1)}, bf16[2,256,512]{2,1,0:T(8,128)(2,1)S(1)}, u32[]{:S(2)}, u32[]{:S(2)}) collective-permute-start(bf16[2,256,512]{2,1,0:T(8,128)(2,1)S(1)} %get-tuple-element.420), channel_id=1, source_target_pairs={{0,2},{2,0},{1,3},{3,1},{4,6},{6,4},{5,7},{7,5},{8,10},{10,8},{9,1... | collective-permute-start | bytes 1572872 | tf_op jit(solution)/shard_map/ppermute | solution.py:46
  160.9 17.8 %collective-permute-start.22 = (bf16[2,3,128,128]{3,2,1,0:T(8,128)(2,1)S(1)}, bf16[2,3,128,128]{3,2,1,0:T(8,128)(2,1)S(1)}, u32[]{:S(2)}, u32[]{:S(2)}) collective-permute-start(bf16[2,3,128,128]{3,2,1,0:T(8,128)(2,1)S(1)} %get-tuple-element.224), channel_id=1, source_target_pairs={{0,16},{16,0},{1,17},{17,1},{2,18},{18,2},{3,19},{19,3},{4,20},{20... | collective-permute-start | bytes 589832 | tf_op jit(solution)/shard_map/ppermute | solution.py:46
  179.7 43.8 %collective-permute-start.23 = (bf16[2,2,256,896]{3,2,1,0:T(8,128)(2,1)S(1)}, bf16[2,2,256,896]{3,2,1,0:T(8,128)(2,1)}, u32[]{:S(2)}, u32[]{:S(2)}) collective-permute-start(bf16[2,2,256,896]{3,2,1,0:T(8,128)(2,1)S(1)} %pad_maximum_fusion.refs_0_), channel_id=1, source_target_pairs={{0,2},{2,0},{1,3},{3,1},{4,6},{6,4},{5,7},{7,5},{8,10},{10,8},{9,1... | collective-permute-start | bytes 5505032 | tf_op jit(solution)/shard_map/ppermute | solution.py:46
  182.1 41.3 %collective-permute-start.25 = (bf16[2,2,256,768]{3,2,1,0:T(8,128)(2,1)}, bf16[2,2,256,768]{3,2,1,0:T(8,128)(2,1)}, u32[]{:S(2)}, u32[]{:S(2)}) collective-permute-start(bf16[2,2,256,768]{3,2,1,0:T(8,128)(2,1)} %pad_maximum_fusion.3.refs_8_), channel_id=1, source_target_pairs={{0,4},{4,0},{1,5},{5,1},{2,6},{6,2},{3,7},{7,3},{8,12},{12,8},{9,1... | collective-permute-start | bytes 4718600 | tf_op jit(solution)/shard_map/ppermute | solution.py:46
  184.6 38.9 %collective-permute-start.24 = (bf16[2,2,256,512]{3,2,1,0:T(8,128)(2,1)}, bf16[2,2,256,512]{3,2,1,0:T(8,128)(2,1)}, u32[]{:S(2)}, u32[]{:S(2)}) collective-permute-start(bf16[2,2,256,512]{3,2,1,0:T(8,128)(2,1)} %pad_maximum_fusion.4.refs_4_), channel_id=1, source_target_pairs={{0,8},{8,0},{1,9},{9,1},{2,10},{10,2},{3,11},{11,3},{4,12},{12,4},... | collective-permute-start | bytes 3145736 | tf_op jit(solution)/shard_map/ppermute | solution.py:46
  188.5 34.0 %collective-permute-start.26 = (bf16[8,3,128,128]{3,2,1,0:T(8,128)(2,1)}, bf16[8,3,128,128]{3,2,1,0:T(8,128)(2,1)}, u32[]{:S(2)}, u32[]{:S(2)}) collective-permute-start(bf16[8,3,128,128]{3,2,1,0:T(8,128)(2,1)} %slice.266), channel_id=1, source_target_pairs={{0,16},{16,0},{1,17},{17,1},{2,18},{18,2},{3,19},{19,3},{4,20},{20... | collective-permute-start | bytes 2359304 | tf_op jit(solution)/shard_map/ppermute | solution.py:46
  226.0 19.3 %collective-permute-start.27 = (bf16[2,2,256,896]{3,2,1,0:T(8,128)(2,1)S(1)}, bf16[2,2,256,896]{3,2,1,0:T(8,128)(2,1)S(1)}, u32[]{:S(2)}, u32[]{:S(2)}) collective-permute-start(bf16[2,2,256,896]{3,2,1,0:T(8,128)(2,1)S(1)} %pad_maximum_fusion.refs_0_), channel_id=1, source_target_pairs={{0,1},{1,0},{2,3},{3,2},{4,5},{5,4},{6,7},{7,6},{8,9},{9,8},{10,11... | collective-permute-start | bytes 5505032 | tf_op jit(solution)/shard_map/ppermute | solution.py:46
  226.2 20.5 %collective-permute-start.30 = (bf16[2,2,256,896]{3,2,1,0:T(8,128)(2,1)}, bf16[2,2,256,896]{3,2,1,0:T(8,128)(2,1)S(1)}, u32[]{:S(2)}, u32[]{:S(2)}) collective-permute-start(bf16[2,2,256,896]{3,2,1,0:T(8,128)(2,1)} %collective-permute-done.23.refs_1_), channel_id=1, source_target_pairs={{0,1},{1,0},{2,3},{3,2},{4,5},{5,4},{6,7},{7,6},{8,9},{9,8},{10,11... | collective-permute-start | bytes 5505032 | tf_op jit(solution)/shard_map/ppermute | solution.py:46
  226.5 18.8 %collective-permute-start.29 = (bf16[2,2,256,768]{3,2,1,0:T(8,128)(2,1)}, bf16[2,2,256,768]{3,2,1,0:T(8,128)(2,1)S(1)}, u32[]{:S(2)}, u32[]{:S(2)}) collective-permute-start(bf16[2,2,256,768]{3,2,1,0:T(8,128)(2,1)} %pad_maximum_fusion.3.refs_8_), channel_id=1, source_target_pairs={{0,1},{1,0},{2,3},{3,2},{4,5},{5,4},{6,7},{7,6},{8,9},{9,8},{10,11... | collective-permute-start | bytes 4718600 | tf_op jit(solution)/shard_map/ppermute | solution.py:46
  249.2 24.9 %collective-permute-start.34 = (bf16[5,3,128,128]{3,2,1,0:T(8,128)(2,1)}, bf16[5,3,128,128]{3,2,1,0:T(8,128)(2,1)S(1)}, u32[]{:S(2)}, u32[]{:S(2)}) collective-permute-start(bf16[5,3,128,128]{3,2,1,0:T(8,128)(2,1)} %slice.271), channel_id=1, source_target_pairs={{0,16},{16,0},{1,17},{17,1},{2,18},{18,2},{3,19},{19,3},{4,20},{20... | collective-permute-start | bytes 1474568 | tf_op jit(solution)/shard_map/ppermute | solution.py:46
  283.2 32.9 %collective-permute-start.35 = (bf16[7,3,128,128]{3,2,1,0:T(8,128)(2,1)}, bf16[7,3,128,128]{3,2,1,0:T(8,128)(2,1)S(1)}, u32[]{:S(2)}, u32[]{:S(2)}) collective-permute-start(bf16[7,3,128,128]{3,2,1,0:T(8,128)(2,1)} %get-tuple-element.263), channel_id=1, source_target_pairs={{0,16},{16,0},{1,17},{17,1},{2,18},{18,2},{3,19},{19,3},{4,20},{20... | collective-permute-start | bytes 2064392 | tf_op jit(solution)/shard_map/ppermute | solution.py:46
  316.1 17.4 %collective-permute-start.36 = (bf16[2,2,2,256,896]{4,3,2,1,0:T(8,128)(2,1)}, bf16[2,2,2,256,896]{4,3,2,1,0:T(8,128)(2,1)}, u32[]{:S(2)}, u32[]{:S(2)}) collective-permute-start(bf16[2,2,2,256,896]{4,3,2,1,0:T(8,128)(2,1)} %get-tuple-element.265), channel_id=1, source_target_pairs={{0,1},{1,0},{2,3},{3,2},{4,5},{5,4},{6,7},{7,6},{8,9},{9,8},{10,11... | collective-permute-start | bytes 11010056 | tf_op jit(solution)/shard_map/ppermute | solution.py:46
  316.1 17.4 %collective-permute-start.38 = (bf16[2,2,2,256,768]{4,3,2,1,0:T(8,128)(2,1)}, bf16[2,2,2,256,768]{4,3,2,1,0:T(8,128)(2,1)}, u32[]{:S(2)}, u32[]{:S(2)}) collective-permute-start(bf16[2,2,2,256,768]{4,3,2,1,0:T(8,128)(2,1)} %get-tuple-element.267), channel_id=1, source_target_pairs={{0,1},{1,0},{2,3},{3,2},{4,5},{5,4},{6,7},{7,6},{8,9},{9,8},{10,11... | collective-permute-start | bytes 9437192 | tf_op jit(solution)/shard_map/ppermute | solution.py:46
  335.6 46.7 %collective-permute-start.40 = (bf16[2,2,256,896]{3,2,1,0:T(8,128)(2,1)S(1)}, bf16[2,2,256,896]{3,2,1,0:T(8,128)(2,1)S(1)}, u32[]{:S(2)}, u32[]{:S(2)}) collective-permute-start(bf16[2,2,256,896]{3,2,1,0:T(8,128)(2,1)S(1)} %fusion.4), channel_id=1, source_target_pairs={{0,2},{2,0},{1,3},{3,1},{4,6},{6,4},{5,7},{7,5},{8,10},{10,8},{9,1... | collective-permute-start | bytes 5505032 | tf_op jit(solution)/shard_map/ppermute | solution.py:46
  338.8 43.5 %collective-permute-start.42 = (bf16[2,2,256,768]{3,2,1,0:T(8,128)(2,1)S(1)}, bf16[2,2,256,768]{3,2,1,0:T(8,128)(2,1)S(1)}, u32[]{:S(2)}, u32[]{:S(2)}) collective-permute-start(bf16[2,2,256,768]{3,2,1,0:T(8,128)(2,1)S(1)} %fusion.6), channel_id=1, source_target_pairs={{0,4},{4,0},{1,5},{5,1},{2,6},{6,2},{3,7},{7,3},{8,12},{12,8},{9,1... | collective-permute-start | bytes 4718600 | tf_op jit(solution)/shard_map/ppermute | solution.py:46
  341.1 41.2 %collective-permute-start.41 = (bf16[2,2,256,512]{3,2,1,0:T(8,128)(2,1)S(1)}, bf16[2,2,256,512]{3,2,1,0:T(8,128)(2,1)S(1)}, u32[]{:S(2)}, u32[]{:S(2)}) collective-permute-start(bf16[2,2,256,512]{3,2,1,0:T(8,128)(2,1)S(1)} %fusion.11), channel_id=1, source_target_pairs={{0,8},{8,0},{1,9},{9,1},{2,10},{10,2},{3,11},{11,3},{4,12},{12,4},... | collective-permute-start | bytes 3145736 | tf_op jit(solution)/shard_map/ppermute | solution.py:46
  341.4 27.8 %collective-permute-start.44 = (bf16[2,3,128,128]{3,2,1,0:T(8,128)(2,1)S(1)}, bf16[2,3,128,128]{3,2,1,0:T(8,128)(2,1)S(1)}, u32[]{:S(2)}, u32[]{:S(2)}) collective-permute-start(bf16[2,3,128,128]{3,2,1,0:T(8,128)(2,1)S(1)} %copy-done.72), channel_id=1, source_target_pairs={{0,16},{16,0},{1,17},{17,1},{2,18},{18,2},{3,19},{19,3},{4,20},{20... | collective-permute-start | bytes 589832 | tf_op jit(solution)/shard_map/ppermute | solution.py:46
  344.7 35.4 %collective-permute-start.43 = (bf16[6,3,128,128]{3,2,1,0:T(8,128)(2,1)S(1)}, bf16[6,3,128,128]{3,2,1,0:T(8,128)(2,1)S(1)}, u32[]{:S(2)}, u32[]{:S(2)}) collective-permute-start(bf16[6,3,128,128]{3,2,1,0:T(8,128)(2,1)S(1)} %copy-done.69), channel_id=1, source_target_pairs={{0,16},{16,0},{1,17},{17,1},{2,18},{18,2},{3,19},{19,3},{4,20},{20... | collective-permute-start | bytes 1769480 | tf_op jit(solution)/shard_map/ppermute | solution.py:46
  382.4 27.2 %collective-permute-start.46 = (bf16[2,256,512]{2,1,0:T(8,128)(2,1)S(1)}, bf16[2,256,512]{2,1,0:T(8,128)(2,1)S(1)}, u32[]{:S(2)}, u32[]{:S(2)}) collective-permute-start(bf16[2,256,512]{2,1,0:T(8,128)(2,1)S(1)} %fusion.19), channel_id=1, source_target_pairs={{0,2},{2,0},{1,3},{3,1},{4,6},{6,4},{5,7},{7,5},{8,10},{10,8},{9,1... | collective-permute-start | bytes 1572872 | tf_op jit(solution)/shard_map/ppermute | solution.py:46
  383.6 28.0 %collective-permute-start.45 = (bf16[2,256,896]{2,1,0:T(8,128)(2,1)S(1)}, bf16[2,256,896]{2,1,0:T(8,128)(2,1)S(1)}, u32[]{:S(2)}, u32[]{:S(2)}) collective-permute-start(bf16[2,256,896]{2,1,0:T(8,128)(2,1)S(1)} %fusion.13), channel_id=1, source_target_pairs={{0,4},{4,0},{1,5},{5,1},{2,6},{6,2},{3,7},{7,3},{8,12},{12,8},{9,1... | collective-permute-start | bytes 2752520 | tf_op jit(solution)/shard_map/ppermute | solution.py:46
  385.2 26.3 %collective-permute-start.47 = (bf16[2,256,768]{2,1,0:T(8,128)(2,1)S(1)}, bf16[2,256,768]{2,1,0:T(8,128)(2,1)S(1)}, u32[]{:S(2)}, u32[]{:S(2)}) collective-permute-start(bf16[2,256,768]{2,1,0:T(8,128)(2,1)S(1)} %fusion.15), channel_id=1, source_target_pairs={{0,8},{8,0},{1,9},{9,1},{2,10},{10,2},{3,11},{11,3},{4,12},{12,4},... | collective-permute-start | bytes 2359304 | tf_op jit(solution)/shard_map/ppermute | solution.py:46
  386.3 23.3 %collective-permute-start.48 = (bf16[4,3,128,128]{3,2,1,0:T(8,128)(2,1)S(1)}, bf16[4,3,128,128]{3,2,1,0:T(8,128)(2,1)S(1)}, u32[]{:S(2)}, u32[]{:S(2)}) collective-permute-start(bf16[4,3,128,128]{3,2,1,0:T(8,128)(2,1)S(1)} %copy-done.70), channel_id=1, source_target_pairs={{0,16},{16,0},{1,17},{17,1},{2,18},{18,2},{3,19},{19,3},{4,20},{20... | collective-permute-start | bytes 1179656 | tf_op jit(solution)/shard_map/ppermute | solution.py:46
  434.5 17.6 %collective-permute-start.54 = (bf16[256,1024]{1,0:T(8,128)(2,1)}, bf16[256,1024]{1,0:T(8,128)(2,1)S(1)}, u32[]{:S(2)}, u32[]{:S(2)}) collective-permute-start(bf16[256,1024]{1,0:T(8,128)(2,1)} %get-tuple-element.335.a0), channel_id=1, source_target_pairs={{0,2},{2,0},{1,3},{3,1},{4,6},{6,4},{5,7},{7,5},{8,10},{10,8},{9,1... | collective-permute-start | bytes 1572872 | tf_op jit(solution)/shard_map/ppermute | solution.py:46
  435.2 16.9 %collective-permute-start.53 = (bf16[256,1024]{1,0:T(8,128)(2,1)}, bf16[256,1024]{1,0:T(8,128)(2,1)S(1)}, u32[]{:S(2)}, u32[]{:S(2)}) collective-permute-start(bf16[256,1024]{1,0:T(8,128)(2,1)} %get-tuple-element.335.a0), channel_id=1, source_target_pairs={{0,1},{1,0},{2,3},{3,2},{4,5},{5,4},{6,7},{7,6},{8,9},{9,8},{10,11... | collective-permute-start | bytes 1572872 | tf_op jit(solution)/shard_map/ppermute | solution.py:46
  458.6 52.6 %all-to-all-start.2 = ((bf16[16,3,128,128]{3,2,1,0:T(8,128)(2,1)}), bf16[16,3,128,128]{3,2,1,0:T(8,128)(2,1)S(1)}, u32[]{:S(2)}, u32[]{:S(2)}) async-start(bf16[16,3,128,128]{3,2,1,0:T(8,128)(2,1)} %add_convert_fusion.3), calls=%async_computation.2 | async-start | bytes 3145728 | tf_op jit(solution)/shard_map/all_to_all | solution.py:808
  462.9 28.5 %collective-permute-start.58 = (bf16[5,3,128,128]{3,2,1,0:T(8,128)(2,1)}, bf16[5,3,128,128]{3,2,1,0:T(8,128)(2,1)S(1)}, u32[]{:S(2)}, u32[]{:S(2)}) collective-permute-start(bf16[5,3,128,128]{3,2,1,0:T(8,128)(2,1)} %get-tuple-element.350), channel_id=1, source_target_pairs={{0,16},{16,0},{1,17},{17,1},{2,18},{18,2},{3,19},{19,3},{4,20},{20... | collective-permute-start | bytes 1474568 | tf_op jit(solution)/shard_map/ppermute | solution.py:46
  464.9 26.6 %collective-permute-start.57 = (bf16[4,128,384]{2,1,0:T(8,128)(2,1)}, bf16[4,128,384]{2,1,0:T(8,128)(2,1)S(1)}, u32[]{:S(2)}, u32[]{:S(2)}) collective-permute-start(bf16[4,128,384]{2,1,0:T(8,128)(2,1)} %get-tuple-element.334), channel_id=1, source_target_pairs={{0,4},{4,0},{1,5},{5,1},{2,6},{6,2},{3,7},{7,3},{8,12},{12,8},{9,1... | collective-permute-start | bytes 1179656 | tf_op jit(solution)/shard_map/ppermute | solution.py:46
  491.7 18.3 %collective-permute-start.59 = (bf16[4,128,640]{2,1,0:T(8,128)(2,1)}, bf16[4,128,640]{2,1,0:T(8,128)(2,1)S(1)}, u32[]{:S(2)}, u32[]{:S(2)}) collective-permute-start(bf16[4,128,640]{2,1,0:T(8,128)(2,1)} %get-tuple-element.353), channel_id=1, source_target_pairs={{0,4},{4,0},{1,5},{5,1},{2,6},{6,2},{3,7},{7,3},{8,12},{12,8},{9,1... | collective-permute-start | bytes 1966088 | tf_op jit(solution)/shard_map/ppermute | solution.py:46
  511.2 45.5 %all-to-all-start.3 = ((bf16[16,3,128,128]{3,2,1,0:T(8,128)(2,1)}), bf16[16,3,128,128]{3,2,1,0:T(8,128)(2,1)S(1)}, u32[]{:S(2)}, u32[]{:S(2)}) async-start(bf16[16,3,128,128]{3,2,1,0:T(8,128)(2,1)} %add_convert_fusion.2), calls=%async_computation.3 | async-start | bytes 3145728 | tf_op jit(solution)/shard_map/all_to_all | solution.py:852
  522.3 26.0 %collective-permute-start.65 = (bf16[128,640]{1,0:T(8,128)(2,1)}, bf16[128,640]{1,0:T(8,128)(2,1)S(1)}, u32[]{:S(2)}, u32[]{:S(2)}) collective-permute-start(bf16[128,640]{1,0:T(8,128)(2,1)} %get-tuple-element.416), channel_id=1, source_target_pairs={{0,8},{8,0},{16,24},{24,16},{1,9},{9,1},{17,25},{25,17},{2,10},{10... | collective-permute-start | bytes 491528 | tf_op jit(solution)/shard_map/ppermute | solution.py:840
  524.2 24.1 %collective-permute-start.67 = (bf16[128,640]{1,0:T(8,128)(2,1)S(1)}, bf16[128,640]{1,0:T(8,128)(2,1)S(1)}, u32[]{:S(2)}, u32[]{:S(2)}) collective-permute-start(bf16[128,640]{1,0:T(8,128)(2,1)S(1)} %get-tuple-element.417), channel_id=1, source_target_pairs={{0,24},{8,16},{16,8},{24,0},{1,25},{9,17},{17,9},{25,1},{2,26},{10... | collective-permute-start | bytes 491528 | tf_op jit(solution)/shard_map/ppermute | solution.py:840
  524.2 24.1 %collective-permute-start.66 = (bf16[128,640]{1,0:T(8,128)(2,1)S(1)}, bf16[128,640]{1,0:T(8,128)(2,1)}, u32[]{:S(2)}, u32[]{:S(2)}) collective-permute-start(bf16[128,640]{1,0:T(8,128)(2,1)S(1)} %get-tuple-element.418), channel_id=1, source_target_pairs={{0,16},{8,24},{16,0},{24,8},{1,17},{9,25},{17,1},{25,9},{2,18},{10... | collective-permute-start | bytes 491528 | tf_op jit(solution)/shard_map/ppermute | solution.py:840
  (100 other events, 851.3 us)

commit v6 on v5

--- a/solution.py
+++ b/solution.py
@@ -18,7 +18,7 @@
 TOK = (512, 256, 256)
 SECOND = (384, 256, 384)
 NOTES = 128
-PARTS_IN = ((3, 6, 3, 2, 2), (8, 3, 5))
+PARTS_IN = ((3, 5, 3, 2, 3), (8, 3, 5))
 PARTS_OUT = ((7, 3, 6), (2, 4, 2, 3, 5))
 BLK = 256
 BF = jnp.bfloat16

time: 566 us -> 569 us (level)
    unnamed x153 -> x155, local copies, waits for them, and re-layouts: 11.8 us -> 11.9 us
where the time goes in v6:
time: 569 us; the launch traced here: 565 us
  waiting for transfers between devices  248 us (44%)
  Pallas kernels  127 us (22%)
  starting transfers between devices  104 us (18%)
  other arithmetic  52.7 us (9%)
  local copies, waits for them, and re-layouts  28.6 us (5%)
    ppermute x59, waiting for transfers between devices, swap(): return lax.ppermute(value, axis, [(0, 1), (1, 0)])  203 us
    ppermute x59, starting transfers between devices, swap(): return lax.ppermute(value, axis, [(0, 1), (1, 0)])  66 us
    pallas_call x2, Pallas kernels, local(): pl.pallas_call(functools.partial(expert_kernel, len(ready_mats(j)), j ==...  53 us
    ppermute x6, waiting for transfers between devices, reduce_z(): lax.ppermute(sums[s], ('o', 'u'), [(i, i ^ s) for i in range(4)])  22.3 us
    pallas_call x1, Pallas kernels, local(): simple_call(functools.partial(attend_backward_kernel, n_tails), [((2, row...  22.1 us
    ppermute x3, waiting for transfers between devices, local(): lax.ppermute(pack, ('o', 'u'), [(i, i ^ s) for i in range(4)])  21.1 us
    pallas_call x2, Pallas kernels, weight_grads_of(): pl.pallas_call(functools.partial(weight_grad_kernel, chunk // shard * 4),...  18.9 us
    convert_element_type x18, other arithmetic, scatter_pool(): add = lambda a, b: (a.astype(F32) + b.astype(F32)).astype(BF)  14.7 us
  transfers between devices with their start and end apart: 75, of which 34 were waited for; matrix products, arithmetic and copies ran while one was open for 11% of the time, Pallas kernels for 18%

profile of v6, /device:TPU:0, one launch (start us, length us, event | category | flops | bytes accessed | tf_op | source)
XLA Modules:
  0.0 565.2 jit_solution(14874643545074806672)
XLA Ops:
  5.1 6.4 %all-to-all-start = ((bf16[16,3,128,128]{3,2,1,0:T(8,128)(2,1)}), bf16[16,3,128,128]{3,2,1,0:T(8,128)(2,1)S(1)}, u32[]{:S(2)}, u32[]{:S(2)}) async-start(bf16[16,3,128,128]{3,2,1,0:T(8,128)(2,1)} %pad_maximum_fusion.2), calls=%async_computation | async-start | bytes 3145728 | tf_op jit(solution)/shard_map/all_to_all | solution.py:552
  11.9 4.0 collective-permute-start.2
  24.2 3.1 fusion.17
  27.2 12.7 %collective-permute-done.2 = bf16[144,896]{1,0:T(8,128)(2,1)S(1)} collective-permute-done((bf16[144,896]{1,0:T(8,128)(2,1)S(1)}, bf16[144,896]{1,0:T(8,128)(2,1)S(1)}, u32[]{:S(2)}, u32[]{:S(2)}) %collective-permute-start.2) | collective-permute-done | bytes 258080 | tf_op jit(solution)/shard_map/ppermute | solution.py:574
  41.0 7.4 %collective-permute-done = bf16[144,896]{1,0:T(8,128)(2,1)S(1)} collective-permute-done((bf16[144,896]{1,0:T(8,128)(2,1)S(1)}, bf16[144,896]{1,0:T(8,128)(2,1)S(1)}, u32[]{:S(2)}, u32[]{:S(2)}) %collective-permute-start) | collective-permute-done | bytes 258080 | tf_op jit(solution)/shard_map/ppermute | solution.py:574
  52.3 2.7 collective-permute-start.7
  57.5 7.0 %collective-permute-done.6.refs_1_ = bf16[4,144,512]{2,1,0:T(8,128)(2,1)} collective-permute-done((bf16[4,144,512]{2,1,0:T(8,128)(2,1)S(1)}, bf16[4,144,512]{2,1,0:T(8,128)(2,1)}, u32[]{:S(2)}, u32[]{:S(2)}) %collective-permute-start.6) | collective-permute-done | bytes 589856 | tf_op jit(solution)/shard_map/ppermute | solution.py:46
  64.5 4.5 collective-permute-done.7.refs_14_
  69.6 4.2 all-to-all-start.1
  82.2 11.0 %shard_map.238 = (bf16[1024,1024]{1,0:T(8,128)(2,1)}, bf16[1024,512]{1,0:T(8,128)(2,1)}, f32[8,1024]{1,0:T(8,128)}, bf16[1024,256]{1,0:T(8,128)(2,1)}, bf16[2,10...) custom-call(s32[8]{0:T(128)} %fusion.47.table.dests, ...), custom_call_target="tpu_custom_call" | custom-call | flops 1 | bytes 8250000 | tf_op jit(solution)/shard_map/pallas_call | solution.py:604
  93.1 3.2 collective-permute-done.8.refs_1_
  97.1 3.9 shard_map.239
  102.1 2.9 collective-permute-done.10.got
  108.1 4.0 collective-permute-start.11
  112.1 2.9 collective-permute-start.13
  120.0 8.7 %collective-permute-done.13.refs_16_ = bf16[3,3,128,128]{3,2,1,0:T(8,128)(2,1)} collective-permute-done((bf16[3,3,128,128]{3,2,1,0:T(8,128)(2,1)}, bf16[3,3,128,128]{3,2,1,0:T(8,128)(2,1)}, u32[]{:S(2)}, u32[]{:S(2)}) %collective-permute-start.13) | collective-permute-done | bytes 294944 | tf_op jit(solution)/shard_map/ppermute | solution.py:46
  128.7 5.1 shard_map.240
  138.4 14.4 %collective-permute-done.18 = s32[2,9,1024]{2,1,0:T(8,128)S(1)} collective-permute-done((s32[2,9,1024]{2,1,0:T(8,128)S(1)}, s32[2,9,1024]{2,1,0:T(8,128)S(1)}, u32[]{:S(2)}, u32[]{:S(2)}) %collective-permute-start.18) | collective-permute-done | bytes 73760 | tf_op jit(solution)/shard_map/ppermute | solution.py:46
  160.0 20.7 %collective-permute-done.22.refs_18_ = bf16[3,3,128,128]{3,2,1,0:T(8,128)(2,1)S(1)} collective-permute-done((bf16[3,3,128,128]{3,2,1,0:T(8,128)(2,1)S(1)}, bf16[3,3,128,128]{3,2,1,0:T(8,128)(2,1)S(1)}, u32[]{:S(2)}, u32[]{:S(2)}) %collective-permute-start.22) | collective-permute-done | bytes 294944 | tf_op jit(solution)/shard_map/ppermute | solution.py:46
  192.5 2.9 and_select_fusion
  195.8 30.3 %collective-permute-done.26.refs_14_ = bf16[8,3,128,128]{3,2,1,0:T(8,128)(2,1)} collective-permute-done((bf16[8,3,128,128]{3,2,1,0:T(8,128)(2,1)}, bf16[8,3,128,128]{3,2,1,0:T(8,128)(2,1)}, u32[]{:S(2)}, u32[]{:S(2)}) %collective-permute-start.26) | collective-permute-done | bytes 786464 | tf_op jit(solution)/shard_map/ppermute | solution.py:46
  226.9 2.8 collective-permute-start.33
  230.4 13.3 %collective-permute-done.33.refs_15_ = bf16[3,3,128,128]{3,2,1,0:T(8,128)(2,1)S(1)} collective-permute-done((bf16[3,3,128,128]{3,2,1,0:T(8,128)(2,1)S(1)}, bf16[3,3,128,128]{3,2,1,0:T(8,128)(2,1)S(1)}, u32[]{:S(2)}, u32[]{:S(2)}) %collective-permute-start.33) | collective-permute-done | bytes 294944 | tf_op jit(solution)/shard_map/ppermute | solution.py:46
  245.2 3.6 collective-permute-done.31.refs_7_
  253.9 20.6 %shard_map.241 = (bf16[1024,896]{1,0:T(8,128)(2,1)}, bf16[1024,512]{1,0:T(8,128)(2,1)}, bf16[1024,768]{1,0:T(8,128)(2,1)}, bf16[1024,1024]{1,0:T(8,128)(2,1)}, b...) custom-call(s32[7]{0:T(128)} %get-tuple-element.248.meta, ...), custom_call_target="tpu_custom_call" | custom-call | flops 1 | bytes 21750000 | tf_op jit(solution)/shard_map/pallas_call | solution.py:730
  274.5 3.1 collective-permute-done.34.refs_16_
  277.6 9.1 %shard_map.242 = (bf16[7,3,128,128]{3,2,1,0:T(8,128)(2,1)}, bf16[3,3,128,128]{3,2,1,0:T(8,128)(2,1)}, bf16[6,3,128,128]{3,2,1,0:T(8,128)(2,1)}, bf16[16,3,128,128]{3,2,1,0:T(8,128)(2,1)}) custom-call(s32[7]{0:T(128)} %get-tuple-element.248.meta, bf16[1024,1024]{1,0:T(8,128)(2,1)} %get-tuple-element.249.picked, bf16[1024,1024]{1,0:T(8,128)(2,1)} %get-tuple-element.250.dy, ...), custom_call_target="tpu_custom_call" | custom-call | flops 1 | bytes 6750000 | tf_op jit(solution)/shard_map/pallas_call | solution.py:698
  286.7 32.5 %shard_map.243 = (bf16[2,2,2,256,896]{4,3,2,1,0:T(8,128)(2,1)}, bf16[2,2,2,256,512]{4,3,2,1,0:T(8,128)(2,1)}, bf16[2,2,2,256,768]{4,3,2,1,0:T(8,128)(2,1)}, bf16...) custom-call(s32[7]{0:T(128)} %get-tuple-element.270.meta, ...), custom_call_target="tpu_custom_call" | custom-call | flops 1 | bytes 21750000 | tf_op jit(solution)/shard_map/pallas_call | solution.py:730
  319.8 2.9 collective-permute-start.39
  322.7 9.8 %shard_map.244 = (bf16[2,3,128,128]{3,2,1,0:T(8,128)(2,1)}, bf16[4,3,128,128]{3,2,1,0:T(8,128)(2,1)}, bf16[2,3,128,128]{3,2,1,0:T(8,128)(2,1)}, bf16[3,3,128,128...) custom-call(s32[7]{0:T(128)} %get-tuple-element.270.meta, ...), custom_call_target="tpu_custom_call" | custom-call | flops 1 | bytes 6750000 | tf_op jit(solution)/shard_map/pallas_call | solution.py:698
  332.5 4.3 collective-permute-done.39
  344.7 2.8 collective-permute-start.44
  353.0 19.5 %collective-permute-done.44 = bf16[2,3,128,128]{3,2,1,0:T(8,128)(2,1)S(1)} collective-permute-done((bf16[2,3,128,128]{3,2,1,0:T(8,128)(2,1)S(1)}, bf16[2,3,128,128]{3,2,1,0:T(8,128)(2,1)S(1)}, u32[]{:S(2)}, u32[]{:S(2)}) %collective-permute-start.44) | collective-permute-done | bytes 196640 | tf_op jit(solution)/shard_map/ppermute | solution.py:46
  372.5 11.1 %collective-permute-done.43 = bf16[6,3,128,128]{3,2,1,0:T(8,128)(2,1)S(1)} collective-permute-done((bf16[6,3,128,128]{3,2,1,0:T(8,128)(2,1)S(1)}, bf16[6,3,128,128]{3,2,1,0:T(8,128)(2,1)S(1)}, u32[]{:S(2)}, u32[]{:S(2)}) %collective-permute-start.43) | collective-permute-done | bytes 589856 | tf_op jit(solution)/shard_map/ppermute | solution.py:46
  392.1 21.3 %collective-permute-done.48 = bf16[4,3,128,128]{3,2,1,0:T(8,128)(2,1)S(1)} collective-permute-done((bf16[4,3,128,128]{3,2,1,0:T(8,128)(2,1)S(1)}, bf16[4,3,128,128]{3,2,1,0:T(8,128)(2,1)S(1)}, u32[]{:S(2)}, u32[]{:S(2)}) %collective-permute-start.48) | collective-permute-done | bytes 393248 | tf_op jit(solution)/shard_map/ppermute | solution.py:46
  422.6 7.4 %collective-permute-done.52 = bf16[2,3,128,128]{3,2,1,0:T(8,128)(2,1)S(1)} collective-permute-done((bf16[2,3,128,128]{3,2,1,0:T(8,128)(2,1)S(1)}, bf16[2,3,128,128]{3,2,1,0:T(8,128)(2,1)S(1)}, u32[]{:S(2)}, u32[]{:S(2)}) %collective-permute-start.52) | collective-permute-done | bytes 196640 | tf_op jit(solution)/shard_map/ppermute | solution.py:46
  433.1 5.2 shard_map.245
  440.4 2.9 add_convert_fusion.3
  443.3 12.5 %collective-permute-done.55 = bf16[3,3,128,128]{3,2,1,0:T(8,128)(2,1)S(1)} collective-permute-done((bf16[3,3,128,128]{3,2,1,0:T(8,128)(2,1)}, bf16[3,3,128,128]{3,2,1,0:T(8,128)(2,1)S(1)}, u32[]{:S(2)}, u32[]{:S(2)}) %collective-permute-start.55) | collective-permute-done | bytes 294944 | tf_op jit(solution)/shard_map/ppermute | solution.py:46
  458.6 3.7 shard_map.246
  462.3 4.2 all-to-all-start.2
  470.6 22.1 %shard_map.247 = (f32[2,256,1024]{2,1,0:T(8,128)}, bf16[2,256,1024]{2,1,0:T(8,128)(2,1)}, bf16[4,128,640]{2,1,0:T(8,128)(2,1)}, bf16[4,128,640]{2,1,0:T(8,128)(2,1)}) custom-call(s32[8]{0:T(128)} %fusion.47.table.dests, s32[4]{0:T(128)} %xor_multiply_fusion.offs, bf16[256,1024]{1,0:T(8,128)(2,1)} %get-tuple-element.335.a0, bf16[256,1024]{1,0:T(8,128)(2,1)} %copy-done.20, ...), custom_call_target="tpu_custom_call" | custom-call | flops 1 | bytes 45000000 | tf_op jit(solution)/shard_map/pallas_call | solution.py:812
  495.1 2.8 collective-permute-start.59
  500.4 3.8 collective-permute-start.64
  508.3 5.0 collective-permute-done.63
  514.8 6.5 %all-to-all-start.3 = ((bf16[16,3,128,128]{3,2,1,0:T(8,128)(2,1)}), bf16[16,3,128,128]{3,2,1,0:T(8,128)(2,1)S(1)}, u32[]{:S(2)}, u32[]{:S(2)}) async-start(bf16[16,3,128,128]{3,2,1,0:T(8,128)(2,1)} %add_convert_fusion.2), calls=%async_computation.3 | async-start | bytes 3145728 | tf_op jit(solution)/shard_map/all_to_all | solution.py:852
  529.6 4.0 shard_map.248
  534.8 17.3 %collective-permute-done.65 = bf16[128,640]{1,0:T(8,128)(2,1)S(1)} collective-permute-done((bf16[128,640]{1,0:T(8,128)(2,1)}, bf16[128,640]{1,0:T(8,128)(2,1)S(1)}, u32[]{:S(2)}, u32[]{:S(2)}) %collective-permute-start.65) | collective-permute-done | bytes 163872 | tf_op jit(solution)/shard_map/ppermute | solution.py:840
  (366 shorter events, 147.7 us)
Async XLA Ops:
  5.1 46.1 %all-to-all-start = ((bf16[16,3,128,128]{3,2,1,0:T(8,128)(2,1)}), bf16[16,3,128,128]{3,2,1,0:T(8,128)(2,1)S(1)}, u32[]{:S(2)}, u32[]{:S(2)}) async-start(bf16[16,3,128,128]{3,2,1,0:T(8,128)(2,1)} %pad_maximum_fusion.2), calls=%async_computation | async-start | bytes 3145728 | tf_op jit(solution)/shard_map/all_to_all | solution.py:552
  11.9 28.1 %collective-permute-start.2 = (bf16[144,896]{1,0:T(8,128)(2,1)S(1)}, bf16[144,896]{1,0:T(8,128)(2,1)S(1)}, u32[]{:S(2)}, u32[]{:S(2)}) collective-permute-start(bf16[144,896]{1,0:T(8,128)(2,1)S(1)} %get-tuple-element.426), channel_id=1, source_target_pairs={{0,24},{8,16},{16,8},{24,0},{1,25},{9,17},{17,9},{25,1},{2,26},{10... | collective-permute-start | bytes 774152 | tf_op jit(solution)/shard_map/ppermute | solution.py:574
  15.9 25.1 %collective-permute-start.1 = (bf16[144,896]{1,0:T(8,128)(2,1)S(1)}, bf16[144,896]{1,0:T(8,128)(2,1)S(1)}, u32[]{:S(2)}, u32[]{:S(2)}) collective-permute-start(bf16[144,896]{1,0:T(8,128)(2,1)S(1)} %get-tuple-element.426), channel_id=1, source_target_pairs={{0,16},{8,24},{16,0},{24,8},{1,17},{9,25},{17,1},{25,9},{2,18},{10... | collective-permute-start | bytes 774152 | tf_op jit(solution)/shard_map/ppermute | solution.py:574
  15.9 32.5 %collective-permute-start = (bf16[144,896]{1,0:T(8,128)(2,1)S(1)}, bf16[144,896]{1,0:T(8,128)(2,1)S(1)}, u32[]{:S(2)}, u32[]{:S(2)}) collective-permute-start(bf16[144,896]{1,0:T(8,128)(2,1)S(1)} %get-tuple-element.426), channel_id=1, source_target_pairs={{0,8},{8,0},{16,24},{24,16},{1,9},{9,1},{17,25},{25,17},{2,10},{10... | collective-permute-start | bytes 774152 | tf_op jit(solution)/shard_map/ppermute | solution.py:574
  16.5 31.8 %collective-permute-start.4 = (bf16[256,1024]{1,0:T(8,128)(2,1)S(1)}, bf16[256,1024]{1,0:T(8,128)(2,1)}, u32[]{:S(2)}, u32[]{:S(2)}) collective-permute-start(bf16[256,1024]{1,0:T(8,128)(2,1)S(1)} %bitcast.141), channel_id=1, source_target_pairs={{0,2},{2,0},{1,3},{3,1},{4,6},{6,4},{5,7},{7,5},{8,10},{10,8},{9,1... | collective-permute-start | bytes 1572872 | tf_op jit(solution)/shard_map/ppermute | solution.py:46
  69.6 59.0 %all-to-all-start.1 = ((bf16[16,3,128,128]{3,2,1,0:T(8,128)(2,1)}), bf16[16,3,128,128]{3,2,1,0:T(8,128)(2,1)S(1)}, u32[]{:S(2)}, u32[]{:S(2)}) async-start(bf16[16,3,128,128]{3,2,1,0:T(8,128)(2,1)} %pad_maximum_fusion.1), calls=%async_computation.1 | async-start | bytes 3145728 | tf_op jit(solution)/shard_map/all_to_all | solution.py:598
  74.7 27.4 %collective-permute-start.9 = (bf16[5,3,128,128]{3,2,1,0:T(8,128)(2,1)}, bf16[5,3,128,128]{3,2,1,0:T(8,128)(2,1)}, u32[]{:S(2)}, u32[]{:S(2)}) collective-permute-start(bf16[5,3,128,128]{3,2,1,0:T(8,128)(2,1)} %slice.336), channel_id=1, source_target_pairs={{0,16},{16,0},{1,17},{17,1},{2,18},{18,2},{3,19},{19,3},{4,20},{20... | collective-permute-start | bytes 1474568 | tf_op jit(solution)/shard_map/ppermute | solution.py:46
  77.6 18.7 %collective-permute-start.8 = (bf16[4,128,384]{2,1,0:T(8,128)(2,1)}, bf16[4,128,384]{2,1,0:T(8,128)(2,1)S(1)}, u32[]{:S(2)}, u32[]{:S(2)}) collective-permute-start(bf16[4,128,384]{2,1,0:T(8,128)(2,1)} %pad_maximum_fusion.9.refs_0_), channel_id=1, source_target_pairs={{0,4},{4,0},{1,5},{5,1},{2,6},{6,2},{3,7},{7,3},{8,12},{12,8},{9,1... | collective-permute-start | bytes 1179656 | tf_op jit(solution)/shard_map/ppermute | solution.py:46
  108.1 20.6 %collective-permute-start.11 = (bf16[256,1024]{1,0:T(8,128)(2,1)}, bf16[256,1024]{1,0:T(8,128)(2,1)}, u32[]{:S(2)}, u32[]{:S(2)}) collective-permute-start(bf16[256,1024]{1,0:T(8,128)(2,1)} %fusion.18), channel_id=1, source_target_pairs={{0,2},{2,0},{1,3},{3,1},{4,6},{6,4},{5,7},{7,5},{8,10},{10,8},{9,1... | collective-permute-start | bytes 1572872 | tf_op jit(solution)/shard_map/ppermute | solution.py:46
  133.8 19.0 %collective-permute-start.14 = (bf16[256,896]{1,0:T(8,128)(2,1)}, bf16[256,896]{1,0:T(8,128)(2,1)S(1)}, u32[]{:S(2)}, u32[]{:S(2)}) collective-permute-start(bf16[256,896]{1,0:T(8,128)(2,1)} %get-tuple-element.216), channel_id=1, source_target_pairs={{0,8},{8,0},{1,9},{9,1},{2,10},{10,2},{3,11},{11,3},{4,12},{12,4},... | collective-permute-start | bytes 1376264 | tf_op jit(solution)/shard_map/ppermute | solution.py:46
  134.5 18.3 %collective-permute-start.16 = (bf16[256,768]{1,0:T(8,128)(2,1)}, bf16[256,768]{1,0:T(8,128)(2,1)S(1)}, u32[]{:S(2)}, u32[]{:S(2)}) collective-permute-start(bf16[256,768]{1,0:T(8,128)(2,1)} %get-tuple-element.218), channel_id=1, source_target_pairs={{0,2},{2,0},{1,3},{3,1},{4,6},{6,4},{5,7},{7,5},{8,10},{10,8},{9,1... | collective-permute-start | bytes 1179656 | tf_op jit(solution)/shard_map/ppermute | solution.py:46
  134.8 18.0 %collective-permute-start.15 = (bf16[256,512]{1,0:T(8,128)(2,1)}, bf16[256,512]{1,0:T(8,128)(2,1)S(1)}, u32[]{:S(2)}, u32[]{:S(2)}) collective-permute-start(bf16[256,512]{1,0:T(8,128)(2,1)} %get-tuple-element.217), channel_id=1, source_target_pairs={{0,4},{4,0},{1,5},{5,1},{2,6},{6,2},{3,7},{7,3},{8,12},{12,8},{9,1... | collective-permute-start | bytes 786440 | tf_op jit(solution)/shard_map/ppermute | solution.py:46
  135.5 17.3 %collective-permute-start.18 = (s32[2,9,1024]{2,1,0:T(8,128)S(1)}, s32[2,9,1024]{2,1,0:T(8,128)S(1)}, u32[]{:S(2)}, u32[]{:S(2)}) collective-permute-start(s32[2,9,1024]{2,1,0:T(8,128)S(1)} %pad_add_fusion), channel_id=1, source_target_pairs={{0,8},{8,0},{1,9},{9,1},{2,10},{10,2},{3,11},{11,3},{4,12},{12,4},... | collective-permute-start | bytes 221192 | tf_op jit(solution)/shard_map/ppermute | solution.py:46
  154.7 26.7 %collective-permute-start.19 = (bf16[2,256,896]{2,1,0:T(8,128)(2,1)S(1)}, bf16[2,256,896]{2,1,0:T(8,128)(2,1)S(1)}, u32[]{:S(2)}, u32[]{:S(2)}) collective-permute-start(bf16[2,256,896]{2,1,0:T(8,128)(2,1)S(1)} %get-tuple-element.412), channel_id=1, source_target_pairs={{0,4},{4,0},{1,5},{5,1},{2,6},{6,2},{3,7},{7,3},{8,12},{12,8},{9,1... | collective-permute-start | bytes 2752520 | tf_op jit(solution)/shard_map/ppermute | solution.py:46
  155.2 26.1 %collective-permute-start.21 = (bf16[2,256,768]{2,1,0:T(8,128)(2,1)S(1)}, bf16[2,256,768]{2,1,0:T(8,128)(2,1)S(1)}, u32[]{:S(2)}, u32[]{:S(2)}) collective-permute-start(bf16[2,256,768]{2,1,0:T(8,128)(2,1)S(1)} %get-tuple-element.414), channel_id=1, source_target_pairs={{0,8},{8,0},{1,9},{9,1},{2,10},{10,2},{3,11},{11,3},{4,12},{12,4},... | collective-permute-start | bytes 2359304 | tf_op jit(solution)/shard_map/ppermute | solution.py:46
  158.0 22.7 %collective-permute-start.20 = (bf16[2,256,512]{2,1,0:T(8,128)(2,1)S(1)}, bf16[2,256,512]{2,1,0:T(8,128)(2,1)S(1)}, u32[]{:S(2)}, u32[]{:S(2)}) collective-permute-start(bf16[2,256,512]{2,1,0:T(8,128)(2,1)S(1)} %get-tuple-element.419), channel_id=1, source_target_pairs={{0,2},{2,0},{1,3},{3,1},{4,6},{6,4},{5,7},{7,5},{8,10},{10,8},{9,1... | collective-permute-start | bytes 1572872 | tf_op jit(solution)/shard_map/ppermute | solution.py:46
  158.1 22.5 %collective-permute-start.22 = (bf16[3,3,128,128]{3,2,1,0:T(8,128)(2,1)S(1)}, bf16[3,3,128,128]{3,2,1,0:T(8,128)(2,1)S(1)}, u32[]{:S(2)}, u32[]{:S(2)}) collective-permute-start(bf16[3,3,128,128]{3,2,1,0:T(8,128)(2,1)S(1)} %copy-done.47), channel_id=1, source_target_pairs={{0,16},{16,0},{1,17},{17,1},{2,18},{18,2},{3,19},{19,3},{4,20},{20... | collective-permute-start | bytes 884744 | tf_op jit(solution)/shard_map/ppermute | solution.py:46
  181.6 45.2 %collective-permute-start.23 = (bf16[2,2,256,896]{3,2,1,0:T(8,128)(2,1)S(1)}, bf16[2,2,256,896]{3,2,1,0:T(8,128)(2,1)}, u32[]{:S(2)}, u32[]{:S(2)}) collective-permute-start(bf16[2,2,256,896]{3,2,1,0:T(8,128)(2,1)S(1)} %pad_maximum_fusion.refs_0_), channel_id=1, source_target_pairs={{0,2},{2,0},{1,3},{3,1},{4,6},{6,4},{5,7},{7,5},{8,10},{10,8},{9,1... | collective-permute-start | bytes 5505032 | tf_op jit(solution)/shard_map/ppermute | solution.py:46
  183.2 43.6 %collective-permute-start.25 = (bf16[2,2,256,768]{3,2,1,0:T(8,128)(2,1)}, bf16[2,2,256,768]{3,2,1,0:T(8,128)(2,1)}, u32[]{:S(2)}, u32[]{:S(2)}) collective-permute-start(bf16[2,2,256,768]{3,2,1,0:T(8,128)(2,1)} %pad_maximum_fusion.3.refs_8_), channel_id=1, source_target_pairs={{0,4},{4,0},{1,5},{5,1},{2,6},{6,2},{3,7},{7,3},{8,12},{12,8},{9,1... | collective-permute-start | bytes 4718600 | tf_op jit(solution)/shard_map/ppermute | solution.py:46
  186.2 40.6 %collective-permute-start.24 = (bf16[2,2,256,512]{3,2,1,0:T(8,128)(2,1)}, bf16[2,2,256,512]{3,2,1,0:T(8,128)(2,1)}, u32[]{:S(2)}, u32[]{:S(2)}) collective-permute-start(bf16[2,2,256,512]{3,2,1,0:T(8,128)(2,1)} %pad_maximum_fusion.4.refs_4_), channel_id=1, source_target_pairs={{0,8},{8,0},{1,9},{9,1},{2,10},{10,2},{3,11},{11,3},{4,12},{12,4},... | collective-permute-start | bytes 3145736 | tf_op jit(solution)/shard_map/ppermute | solution.py:46
  190.3 35.8 %collective-permute-start.26 = (bf16[8,3,128,128]{3,2,1,0:T(8,128)(2,1)}, bf16[8,3,128,128]{3,2,1,0:T(8,128)(2,1)}, u32[]{:S(2)}, u32[]{:S(2)}) collective-permute-start(bf16[8,3,128,128]{3,2,1,0:T(8,128)(2,1)} %slice.266), channel_id=1, source_target_pairs={{0,16},{16,0},{1,17},{17,1},{2,18},{18,2},{3,19},{19,3},{4,20},{20... | collective-permute-start | bytes 2359304 | tf_op jit(solution)/shard_map/ppermute | solution.py:46
  229.7 19.1 %collective-permute-start.27 = (bf16[2,2,256,896]{3,2,1,0:T(8,128)(2,1)S(1)}, bf16[2,2,256,896]{3,2,1,0:T(8,128)(2,1)S(1)}, u32[]{:S(2)}, u32[]{:S(2)}) collective-permute-start(bf16[2,2,256,896]{3,2,1,0:T(8,128)(2,1)S(1)} %pad_maximum_fusion.refs_0_), channel_id=1, source_target_pairs={{0,1},{1,0},{2,3},{3,2},{4,5},{5,4},{6,7},{7,6},{8,9},{9,8},{10,11... | collective-permute-start | bytes 5505032 | tf_op jit(solution)/shard_map/ppermute | solution.py:46
  229.9 20.3 %collective-permute-start.30 = (bf16[2,2,256,896]{3,2,1,0:T(8,128)(2,1)}, bf16[2,2,256,896]{3,2,1,0:T(8,128)(2,1)S(1)}, u32[]{:S(2)}, u32[]{:S(2)}) collective-permute-start(bf16[2,2,256,896]{3,2,1,0:T(8,128)(2,1)} %collective-permute-done.23.refs_1_), channel_id=1, source_target_pairs={{0,1},{1,0},{2,3},{3,2},{4,5},{5,4},{6,7},{7,6},{8,9},{9,8},{10,11... | collective-permute-start | bytes 5505032 | tf_op jit(solution)/shard_map/ppermute | solution.py:46
  230.2 18.6 %collective-permute-start.29 = (bf16[2,2,256,768]{3,2,1,0:T(8,128)(2,1)}, bf16[2,2,256,768]{3,2,1,0:T(8,128)(2,1)S(1)}, u32[]{:S(2)}, u32[]{:S(2)}) collective-permute-start(bf16[2,2,256,768]{3,2,1,0:T(8,128)(2,1)} %pad_maximum_fusion.3.refs_8_), channel_id=1, source_target_pairs={{0,1},{1,0},{2,3},{3,2},{4,5},{5,4},{6,7},{7,6},{8,9},{9,8},{10,11... | collective-permute-start | bytes 4718600 | tf_op jit(solution)/shard_map/ppermute | solution.py:46
  252.6 24.9 %collective-permute-start.34 = (bf16[5,3,128,128]{3,2,1,0:T(8,128)(2,1)}, bf16[5,3,128,128]{3,2,1,0:T(8,128)(2,1)S(1)}, u32[]{:S(2)}, u32[]{:S(2)}) collective-permute-start(bf16[5,3,128,128]{3,2,1,0:T(8,128)(2,1)} %slice.271), channel_id=1, source_target_pairs={{0,16},{16,0},{1,17},{17,1},{2,18},{18,2},{3,19},{19,3},{4,20},{20... | collective-permute-start | bytes 1474568 | tf_op jit(solution)/shard_map/ppermute | solution.py:46
  286.6 32.6 %collective-permute-start.35 = (bf16[7,3,128,128]{3,2,1,0:T(8,128)(2,1)}, bf16[7,3,128,128]{3,2,1,0:T(8,128)(2,1)S(1)}, u32[]{:S(2)}, u32[]{:S(2)}) collective-permute-start(bf16[7,3,128,128]{3,2,1,0:T(8,128)(2,1)} %get-tuple-element.263), channel_id=1, source_target_pairs={{0,16},{16,0},{1,17},{17,1},{2,18},{18,2},{3,19},{19,3},{4,20},{20... | collective-permute-start | bytes 2064392 | tf_op jit(solution)/shard_map/ppermute | solution.py:46
  319.3 17.5 %collective-permute-start.36 = (bf16[2,2,2,256,896]{4,3,2,1,0:T(8,128)(2,1)}, bf16[2,2,2,256,896]{4,3,2,1,0:T(8,128)(2,1)}, u32[]{:S(2)}, u32[]{:S(2)}) collective-permute-start(bf16[2,2,2,256,896]{4,3,2,1,0:T(8,128)(2,1)} %get-tuple-element.265), channel_id=1, source_target_pairs={{0,1},{1,0},{2,3},{3,2},{4,5},{5,4},{6,7},{7,6},{8,9},{9,8},{10,11... | collective-permute-start | bytes 11010056 | tf_op jit(solution)/shard_map/ppermute | solution.py:46
  319.3 17.5 %collective-permute-start.38 = (bf16[2,2,2,256,768]{4,3,2,1,0:T(8,128)(2,1)}, bf16[2,2,2,256,768]{4,3,2,1,0:T(8,128)(2,1)}, u32[]{:S(2)}, u32[]{:S(2)}) collective-permute-start(bf16[2,2,2,256,768]{4,3,2,1,0:T(8,128)(2,1)} %get-tuple-element.267), channel_id=1, source_target_pairs={{0,1},{1,0},{2,3},{3,2},{4,5},{5,4},{6,7},{7,6},{8,9},{9,8},{10,11... | collective-permute-start | bytes 9437192 | tf_op jit(solution)/shard_map/ppermute | solution.py:46
  319.8 17.0 %collective-permute-start.37 = (bf16[2,2,2,256,512]{4,3,2,1,0:T(8,128)(2,1)}, bf16[2,2,2,256,512]{4,3,2,1,0:T(8,128)(2,1)}, u32[]{:S(2)}, u32[]{:S(2)}) collective-permute-start(bf16[2,2,2,256,512]{4,3,2,1,0:T(8,128)(2,1)} %get-tuple-element.266), channel_id=1, source_target_pairs={{0,1},{1,0},{2,3},{3,2},{4,5},{5,4},{6,7},{7,6},{8,9},{9,8},{10,11... | collective-permute-start | bytes 6291464 | tf_op jit(solution)/shard_map/ppermute | solution.py:46
  319.8 17.0 %collective-permute-start.39 = (bf16[3,3,128,128]{3,2,1,0:T(8,128)(2,1)}, bf16[3,3,128,128]{3,2,1,0:T(8,128)(2,1)S(1)}, u32[]{:S(2)}, u32[]{:S(2)}) collective-permute-start(bf16[3,3,128,128]{3,2,1,0:T(8,128)(2,1)} %get-tuple-element.269), channel_id=1, source_target_pairs={{0,16},{16,0},{1,17},{17,1},{2,18},{18,2},{3,19},{19,3},{4,20},{20... | collective-permute-start | bytes 884744 | tf_op jit(solution)/shard_map/ppermute | solution.py:46
  339.0 46.9 %collective-permute-start.40 = (bf16[2,2,256,896]{3,2,1,0:T(8,128)(2,1)S(1)}, bf16[2,2,256,896]{3,2,1,0:T(8,128)(2,1)S(1)}, u32[]{:S(2)}, u32[]{:S(2)}) collective-permute-start(bf16[2,2,256,896]{3,2,1,0:T(8,128)(2,1)S(1)} %fusion.4), channel_id=1, source_target_pairs={{0,2},{2,0},{1,3},{3,1},{4,6},{6,4},{5,7},{7,5},{8,10},{10,8},{9,1... | collective-permute-start | bytes 5505032 | tf_op jit(solution)/shard_map/ppermute | solution.py:46
  342.4 43.4 %collective-permute-start.42 = (bf16[2,2,256,768]{3,2,1,0:T(8,128)(2,1)S(1)}, bf16[2,2,256,768]{3,2,1,0:T(8,128)(2,1)S(1)}, u32[]{:S(2)}, u32[]{:S(2)}) collective-permute-start(bf16[2,2,256,768]{3,2,1,0:T(8,128)(2,1)S(1)} %fusion.6), channel_id=1, source_target_pairs={{0,4},{4,0},{1,5},{5,1},{2,6},{6,2},{3,7},{7,3},{8,12},{12,8},{9,1... | collective-permute-start | bytes 4718600 | tf_op jit(solution)/shard_map/ppermute | solution.py:46
  344.6 41.2 %collective-permute-start.41 = (bf16[2,2,256,512]{3,2,1,0:T(8,128)(2,1)S(1)}, bf16[2,2,256,512]{3,2,1,0:T(8,128)(2,1)S(1)}, u32[]{:S(2)}, u32[]{:S(2)}) collective-permute-start(bf16[2,2,256,512]{3,2,1,0:T(8,128)(2,1)S(1)} %fusion.11), channel_id=1, source_target_pairs={{0,8},{8,0},{1,9},{9,1},{2,10},{10,2},{3,11},{11,3},{4,12},{12,4},... | collective-permute-start | bytes 3145736 | tf_op jit(solution)/shard_map/ppermute | solution.py:46
  344.7 27.8 %collective-permute-start.44 = (bf16[2,3,128,128]{3,2,1,0:T(8,128)(2,1)S(1)}, bf16[2,3,128,128]{3,2,1,0:T(8,128)(2,1)S(1)}, u32[]{:S(2)}, u32[]{:S(2)}) collective-permute-start(bf16[2,3,128,128]{3,2,1,0:T(8,128)(2,1)S(1)} %copy-done.73), channel_id=1, source_target_pairs={{0,16},{16,0},{1,17},{17,1},{2,18},{18,2},{3,19},{19,3},{4,20},{20... | collective-permute-start | bytes 589832 | tf_op jit(solution)/shard_map/ppermute | solution.py:46
  347.5 36.2 %collective-permute-start.43 = (bf16[6,3,128,128]{3,2,1,0:T(8,128)(2,1)S(1)}, bf16[6,3,128,128]{3,2,1,0:T(8,128)(2,1)S(1)}, u32[]{:S(2)}, u32[]{:S(2)}) collective-permute-start(bf16[6,3,128,128]{3,2,1,0:T(8,128)(2,1)S(1)} %copy-done.70), channel_id=1, source_target_pairs={{0,16},{16,0},{1,17},{17,1},{2,18},{18,2},{3,19},{19,3},{4,20},{20... | collective-permute-start | bytes 1769480 | tf_op jit(solution)/shard_map/ppermute | solution.py:46
  386.0 27.4 %collective-permute-start.46 = (bf16[2,256,512]{2,1,0:T(8,128)(2,1)S(1)}, bf16[2,256,512]{2,1,0:T(8,128)(2,1)S(1)}, u32[]{:S(2)}, u32[]{:S(2)}) collective-permute-start(bf16[2,256,512]{2,1,0:T(8,128)(2,1)S(1)} %fusion.19), channel_id=1, source_target_pairs={{0,2},{2,0},{1,3},{3,1},{4,6},{6,4},{5,7},{7,5},{8,10},{10,8},{9,1... | collective-permute-start | bytes 1572872 | tf_op jit(solution)/shard_map/ppermute | solution.py:46
  387.1 28.0 %collective-permute-start.45 = (bf16[2,256,896]{2,1,0:T(8,128)(2,1)S(1)}, bf16[2,256,896]{2,1,0:T(8,128)(2,1)S(1)}, u32[]{:S(2)}, u32[]{:S(2)}) collective-permute-start(bf16[2,256,896]{2,1,0:T(8,128)(2,1)S(1)} %fusion.13), channel_id=1, source_target_pairs={{0,4},{4,0},{1,5},{5,1},{2,6},{6,2},{3,7},{7,3},{8,12},{12,8},{9,1... | collective-permute-start | bytes 2752520 | tf_op jit(solution)/shard_map/ppermute | solution.py:46
  388.8 26.3 %collective-permute-start.47 = (bf16[2,256,768]{2,1,0:T(8,128)(2,1)S(1)}, bf16[2,256,768]{2,1,0:T(8,128)(2,1)S(1)}, u32[]{:S(2)}, u32[]{:S(2)}) collective-permute-start(bf16[2,256,768]{2,1,0:T(8,128)(2,1)S(1)} %fusion.15), channel_id=1, source_target_pairs={{0,8},{8,0},{1,9},{9,1},{2,10},{10,2},{3,11},{11,3},{4,12},{12,4},... | collective-permute-start | bytes 2359304 | tf_op jit(solution)/shard_map/ppermute | solution.py:46
  389.8 23.6 %collective-permute-start.48 = (bf16[4,3,128,128]{3,2,1,0:T(8,128)(2,1)S(1)}, bf16[4,3,128,128]{3,2,1,0:T(8,128)(2,1)S(1)}, u32[]{:S(2)}, u32[]{:S(2)}) collective-permute-start(bf16[4,3,128,128]{3,2,1,0:T(8,128)(2,1)S(1)} %copy-done.71), channel_id=1, source_target_pairs={{0,16},{16,0},{1,17},{17,1},{2,18},{18,2},{3,19},{19,3},{4,20},{20... | collective-permute-start | bytes 1179656 | tf_op jit(solution)/shard_map/ppermute | solution.py:46
  438.2 17.5 %collective-permute-start.54 = (bf16[256,1024]{1,0:T(8,128)(2,1)}, bf16[256,1024]{1,0:T(8,128)(2,1)S(1)}, u32[]{:S(2)}, u32[]{:S(2)}) collective-permute-start(bf16[256,1024]{1,0:T(8,128)(2,1)} %get-tuple-element.335.a0), channel_id=1, source_target_pairs={{0,2},{2,0},{1,3},{3,1},{4,6},{6,4},{5,7},{7,5},{8,10},{10,8},{9,1... | collective-permute-start | bytes 1572872 | tf_op jit(solution)/shard_map/ppermute | solution.py:46
  462.3 52.5 %all-to-all-start.2 = ((bf16[16,3,128,128]{3,2,1,0:T(8,128)(2,1)}), bf16[16,3,128,128]{3,2,1,0:T(8,128)(2,1)S(1)}, u32[]{:S(2)}, u32[]{:S(2)}) async-start(bf16[16,3,128,128]{3,2,1,0:T(8,128)(2,1)} %add_convert_fusion.3), calls=%async_computation.2 | async-start | bytes 3145728 | tf_op jit(solution)/shard_map/all_to_all | solution.py:808
  466.5 28.4 %collective-permute-start.58 = (bf16[5,3,128,128]{3,2,1,0:T(8,128)(2,1)}, bf16[5,3,128,128]{3,2,1,0:T(8,128)(2,1)S(1)}, u32[]{:S(2)}, u32[]{:S(2)}) collective-permute-start(bf16[5,3,128,128]{3,2,1,0:T(8,128)(2,1)} %get-tuple-element.350), channel_id=1, source_target_pairs={{0,16},{16,0},{1,17},{17,1},{2,18},{18,2},{3,19},{19,3},{4,20},{20... | collective-permute-start | bytes 1474568 | tf_op jit(solution)/shard_map/ppermute | solution.py:46
  468.7 26.1 %collective-permute-start.57 = (bf16[4,128,384]{2,1,0:T(8,128)(2,1)}, bf16[4,128,384]{2,1,0:T(8,128)(2,1)S(1)}, u32[]{:S(2)}, u32[]{:S(2)}) collective-permute-start(bf16[4,128,384]{2,1,0:T(8,128)(2,1)} %get-tuple-element.334), channel_id=1, source_target_pairs={{0,4},{4,0},{1,5},{5,1},{2,6},{6,2},{3,7},{7,3},{8,12},{12,8},{9,1... | collective-permute-start | bytes 1179656 | tf_op jit(solution)/shard_map/ppermute | solution.py:46
  495.1 18.4 %collective-permute-start.59 = (bf16[4,128,640]{2,1,0:T(8,128)(2,1)}, bf16[4,128,640]{2,1,0:T(8,128)(2,1)S(1)}, u32[]{:S(2)}, u32[]{:S(2)}) collective-permute-start(bf16[4,128,640]{2,1,0:T(8,128)(2,1)} %get-tuple-element.353), channel_id=1, source_target_pairs={{0,4},{4,0},{1,5},{5,1},{2,6},{6,2},{3,7},{7,3},{8,12},{12,8},{9,1... | collective-permute-start | bytes 1966088 | tf_op jit(solution)/shard_map/ppermute | solution.py:46
  514.8 45.6 %all-to-all-start.3 = ((bf16[16,3,128,128]{3,2,1,0:T(8,128)(2,1)}), bf16[16,3,128,128]{3,2,1,0:T(8,128)(2,1)S(1)}, u32[]{:S(2)}, u32[]{:S(2)}) async-start(bf16[16,3,128,128]{3,2,1,0:T(8,128)(2,1)} %add_convert_fusion.2), calls=%async_computation.3 | async-start | bytes 3145728 | tf_op jit(solution)/shard_map/all_to_all | solution.py:852
  526.1 26.0 %collective-permute-start.65 = (bf16[128,640]{1,0:T(8,128)(2,1)}, bf16[128,640]{1,0:T(8,128)(2,1)S(1)}, u32[]{:S(2)}, u32[]{:S(2)}) collective-permute-start(bf16[128,640]{1,0:T(8,128)(2,1)} %get-tuple-element.415), channel_id=1, source_target_pairs={{0,8},{8,0},{16,24},{24,16},{1,9},{9,1},{17,25},{25,17},{2,10},{10... | collective-permute-start | bytes 491528 | tf_op jit(solution)/shard_map/ppermute | solution.py:840
  528.0 24.1 %collective-permute-start.67 = (bf16[128,640]{1,0:T(8,128)(2,1)S(1)}, bf16[128,640]{1,0:T(8,128)(2,1)S(1)}, u32[]{:S(2)}, u32[]{:S(2)}) collective-permute-start(bf16[128,640]{1,0:T(8,128)(2,1)S(1)} %get-tuple-element.416), channel_id=1, source_target_pairs={{0,24},{8,16},{16,8},{24,0},{1,25},{9,17},{17,9},{25,1},{2,26},{10... | collective-permute-start | bytes 491528 | tf_op jit(solution)/shard_map/ppermute | solution.py:840
  528.1 24.1 %collective-permute-start.66 = (bf16[128,640]{1,0:T(8,128)(2,1)S(1)}, bf16[128,640]{1,0:T(8,128)(2,1)}, u32[]{:S(2)}, u32[]{:S(2)}) collective-permute-start(bf16[128,640]{1,0:T(8,128)(2,1)S(1)} %get-tuple-element.417), channel_id=1, source_target_pairs={{0,16},{8,24},{16,0},{24,8},{1,17},{9,25},{17,1},{25,9},{2,18},{10... | collective-permute-start | bytes 491528 | tf_op jit(solution)/shard_map/ppermute | solution.py:840
  (101 other events, 848.4 us)
